TPU v7x, 256 devices: a whole 4x4x8 slice. The times are simulated.
256 devices in a mesh: table: 64 (over x, z, core), row: 4 (over y).
Axes of the slice: x: 4, y: 4, z: 8, core: 2. Of those that a mesh axis runs over, the one named last changes fastest.
Arguments:
- emb_rows: float32 [512, 512, 256], P('table', 'row'), may hold values from -3 to 3
- entry_ids: int32 [512, 4096], P('table'), may hold values from 0 to 511
- entry_sample: int32 [512, 4096], P('table'), may hold values from 0 to 1023, never falling along the last dimension, each value on 1 to 16 neighbouring positions
- cross_v: bfloat16 [2, 131072, 512], P(None, 'table'), may hold values from -0.015625 to 0.015625
- cross_u: bfloat16 [2, 512, 131072], P(None, None, 'table'), may hold values from -0.25 to 0.25
- cross_bias: float32 [2, 131072], P(None, 'table'), may hold values from -3 to 3
- cotangent: bfloat16 [1024, 131072], P('row', 'table'), may hold values from -6 to 6
Outputs:
- crossed: bfloat16 [1024, 131072], P('row', 'table')
- row_grads: float32 [512, 512, 256], P('table', 'row')
Inputs may be any that keep to these rules, and one draw needn't show every extreme that they name: entry_sample never falls along a table's entries, and each sample has 1 to 16 entries in every table.
All inputs are finite; a program needn't handle non-finite values.
Results may differ from a plain program's by a relative error of at most 0.035.
Values may be sent and summed in bfloat16 or wider, within the bound.
No kernel may reach another device: no remote copies, remote signals or barrier semaphores. Data moves between devices by JAX's collectives and lax.ppermute only.
A program may use at most 128 MiB of HBM per device.

v0:
```python
import math

import jax
import jax.numpy as jnp
from jax import lax
from jax.sharding import PartitionSpec as P


def build_counts(entry_ids, entry_sample, sample_count, row_lo, row_count):
    tab_dev, entries = entry_ids.shape
    block = math.gcd(entries, 512)
    nblocks = entries // block
    ids_blocks = jnp.transpose(entry_ids.reshape(tab_dev, nblocks, block), (1, 0, 2))
    sample_blocks = jnp.transpose(entry_sample.reshape(tab_dev, nblocks, block), (1, 0, 2))
    sample_grid = lax.broadcasted_iota(jnp.int32, (1, 1, sample_count), 2)
    row_grid = lax.broadcasted_iota(jnp.int32, (1, 1, row_count), 2) + row_lo

    def step(total, pieces):
        ids, owners = pieces
        sample_hot = (owners[:, :, None] == sample_grid).astype(jnp.bfloat16)
        row_hot = (ids[:, :, None] == row_grid).astype(jnp.bfloat16)
        total = total + jnp.einsum(
            "tes,ter->tsr", sample_hot, row_hot, preferred_element_type=jnp.float32
        )
        return (total, None)

    start = jnp.zeros((tab_dev, sample_count, row_count), jnp.float32)
    counts, _ = lax.scan(step, start, (ids_blocks, sample_blocks))
    return counts


def widen(layer_in, v_layer, u_layer, bias_layer):
    part = jnp.dot(layer_in, v_layer, preferred_element_type=jnp.float32)
    narrow = lax.psum(part, "table").astype(jnp.bfloat16)
    return jnp.dot(narrow, u_layer, preferred_element_type=jnp.float32) + bias_layer


def contract_last(left, right):
    return lax.dot_general(
        left, right, (((1,), (1,)), ((), ())), preferred_element_type=jnp.float32
    )


def local(emb_rows, entry_ids, entry_sample, cross_v, cross_u, cross_bias, cotangent):
    tab_dev, rows_dev, emb = emb_rows.shape
    parts = lax.axis_size("row")
    mine = lax.axis_index("row")
    samp_dev, feat_dev = cotangent.shape
    samples = samp_dev * parts
    layers = cross_v.shape[0]
    three_pass = lax.Precision.HIGH
    counts = build_counts(entry_ids, entry_sample, samples, mine * rows_dev, rows_dev)
    piece = counts
    term = jnp.einsum("tsr,tre->ste", piece, emb_rows, precision=three_pass)
    pooled = lax.psum_scatter(
        term.reshape(samp_dev * lax.axis_size("row"), feat_dev).astype(jnp.bfloat16),
        "row",
        scatter_dimension=0,
        tiled=True,
    )
    counts_low = counts.astype(jnp.bfloat16)
    base = pooled.astype(jnp.float32)
    saved = []
    layer_in = pooled
    for layer in range(layers):
        wide = widen(layer_in, cross_v[layer], cross_u[layer], cross_bias[layer])
        saved.append(wide)
        layer_in = (base * wide + layer_in.astype(jnp.float32)).astype(jnp.bfloat16)
    grad = cotangent.astype(jnp.float32)
    accum = jnp.zeros((samp_dev, feat_dev), jnp.float32)
    for layer in reversed(range(layers)):
        grad_wide = (grad * base).astype(jnp.bfloat16)
        part = contract_last(grad_wide, cross_u[layer])
        grad_narrow = lax.psum(part, "table").astype(jnp.bfloat16)
        accum = accum + grad * saved[layer]
        grad = grad + contract_last(grad_narrow, cross_v[layer])
    grad_pooled = (accum + grad).astype(jnp.bfloat16)
    piece = lax.all_gather(grad_pooled, "row", axis=0, tiled=True)
    count = piece.shape[0]
    values = piece.reshape(count, tab_dev, emb)
    row_grads = jnp.einsum("tsr,ste->tre", counts_low, values, preferred_element_type=jnp.float32)
    return (layer_in, row_grads)


def solution(mesh):
    placed = (
        P("table", "row", None),
        P("table", None),
        P("table", None),
        P(None, "table", None),
        P(None, None, "table"),
        P(None, "table"),
        P("row", "table"),
    )
    return jax.shard_map(
        local,
        mesh=mesh,
        in_specs=placed,
        out_specs=(P("row", "table"), P("table", "row", None)),
        check_vma=False,
    )
```

profile of v0, /device:TPU:1, one launch (start us, length us, event | category | flops | bytes accessed | tf_op | source)
XLA Modules:
  0.0 724.5 jit_solution(11096729755917099012)
XLA Ops:
  7.2 57.7 %while.11 = (s32[]{:T(128)}, f32[8,1024,128]{2,1,0:T(8,128)}, s32[8,8,512]{2,1,0:T(8,128)}, s32[8,8,512]{2,1,0:T(8,128)}, s32[]{:T(128)}, /*index=5*/s32[]{:T(128)}, s32[]{:T(128)}) while((s32[]{:T(128)}, f32[8,1024,128]{2,1,0:T(8,128)}, s32[8,8,512]{2,1,0:T(8,128)}, s32[8,8,512]{2,1,0:T(8,128)}, s32[]{:T(128)}, ...), condition=%wide.region_1.2_spmd.clone, body=%wide.region_0.1_spmd.clone.sunk | while | flops 1080557696 | bytes 8488039 | solution.py:28
  7.3 0.8 dynamic-slice_bitcast_fusion.3
  8.1 5.1 select_add_fusion.2
  13.2 0.7 dynamic-slice_bitcast_fusion.3
  13.9 6.7 select_add_fusion.2
  20.6 0.7 dynamic-slice_bitcast_fusion.3
  21.3 6.7 select_add_fusion.2
  28.0 0.7 dynamic-slice_bitcast_fusion.3
  28.7 6.6 select_add_fusion.2
  35.4 0.7 dynamic-slice_bitcast_fusion.3
  36.1 6.7 select_add_fusion.2
  42.8 0.7 dynamic-slice_bitcast_fusion.3
  43.5 6.7 select_add_fusion.2
  50.2 0.7 dynamic-slice_bitcast_fusion.3
  50.9 6.7 select_add_fusion.2
  58.3 6.6 select_add_fusion.2
  65.0 7.3 %convolution_convert_fusion = bf16[8,1024,256]{1,2,0:T(8,128)(2,1)} fusion(f32[8,1024,128]{2,1,0:T(8,128)} %get-tuple-element.34, f32[8,128,256]{2,1,0:T(8,128)S(1)} %copy-done), kind=kOutput, calls=%fused_computation.26 | convolution fusion | flops 1612709888 | bytes 9437184 | tf_op jit(solution)/shard_map/tsr,tre->ste/dot_general | solution.py:54
  72.2 6.5 copy.10
  79.5 52.7 %reduce-scatter.2.cloned.1.call-done = bf16[256,2048]{1,0:T(8,128)(2,1)} async-done(((bf16[1024,2048]{1,0:T(8,128)(2,1)}), bf16[256,2048]{1,0:T(8,128)(2,1)}) %reduce-scatter.2.cloned.1.call-update) | async-done | bytes 1048592 | tf_op jit(solution)/shard_map/reduce_scatter | solution.py:55
  132.3 2.8 fusion.22
  136.4 255.3 %all-reduce.4 = (bf16[256,512]{1,0:T(8,128)(2,1)S(1)}, bf16[256,512]{1,0:T(8,128)(2,1)}) all-reduce(f32[256,512]{1,0:T(8,128)S(1)} %fusion.32, f32[256,512]{1,0:T(8,128)S(1)} %fusion.22), channel_id=1, replica_groups=mesh['table'=64,'row'=4] {'table'}, use_global_device_ids=true, to_apply=%region_3.4 | all-reduce | flops 262144 | bytes 1572864 | tf_op jit(solution)/shard_map/psum | solution.py:34
  391.7 2.4 convolution_add_fusion.2
  394.2 3.3 fusion.26
  397.5 0.7 convert_add_fusion.1
  398.2 1.3 copy-done.1
  399.6 0.8 copy-done.3
  400.4 1.5 fusion.28
  402.0 256.0 %all-reduce.5 = (bf16[256,512]{1,0:T(8,128)(2,1)S(1)}, bf16[256,512]{1,0:T(8,128)(2,1)}) all-reduce(f32[256,512]{1,0:T(8,128)} %fusion.26, f32[256,512]{1,0:T(8,128)} %fusion.28), channel_id=1, replica_groups=mesh['table'=64,'row'=4] {'table'}, use_global_device_ids=true, to_apply=%region_4.5 | all-reduce | flops 262144 | bytes 1572864 | tf_op jit(solution)/shard_map/psum | solution.py:34
  658.0 3.9 fusion.19
  662.4 1.8 fusion.15
  664.2 48.1 %all-gather.2.cloned.1.call-done = bf16[1024,2048]{1,0:T(8,128)(2,1)} async-done(((bf16[256,2048]{1,0:T(8,128)(2,1)}), bf16[1024,2048]{1,0:T(8,128)(2,1)}) %all-gather.2.cloned.1.call-update) | async-done | bytes 4194320 | tf_op jit(solution)/shard_map/all_gather | solution.py:78
  712.3 5.3 fusion.11
  (44 shorter events, 3.5 us)
Async XLA Ops:
  7.2 57.8 %copy-start = (f32[8,128,256]{2,1,0:T(8,128)S(1)}, f32[8,128,256]{2,1,0:T(8,128)}, u32[]{:S(2)}) copy-start(f32[8,128,256]{2,1,0:T(8,128)} %param.9) | copy-start | bytes 3145732
  7.2 125.1 %reduce-scatter.2.cloned.1.call-start = ((), (), s32[]{:S(2)}) async-start(), calls=%async_computation.1 | async-start | bytes 5242880 | tf_op jit(solution)/shard_map/reduce_scatter | solution.py:55
  78.8 0.7 copy-start.14
  78.8 53.5 %copy-start.9 = (bf16[256,2048]{1,0:T(8,128)(2,1)S(1)}, bf16[256,2048]{1,0:T(8,128)(2,1)}, u32[]{:S(2)}) copy-start(bf16[256,2048]{1,0:T(8,128)(2,1)} %param.15) | copy-start | bytes 3145732
  78.8 633.5 %all-gather.2.cloned.1.call-start = ((), (), s32[]{:S(2)}) async-start(), calls=%async_computation.2 | async-start | bytes 5242880 | tf_op jit(solution)/shard_map/all_gather | solution.py:78
  132.3 2.8 copy-start.4
  132.3 3.5 copy-start.6
  391.7 2.4 copy-start.5
  394.1 3.3 copy-start.7
  394.2 3.3 copy-start.10
  394.2 3.3 copy-start.12
  397.5 2.9 copy-start.3
  398.2 1.3 copy-start.1
  658.0 3.9 copy-start.2
  658.0 3.9 copy-start.8
  658.0 4.4 copy-start.11
  658.0 4.4 copy-start.13
Sparse Core Ops, SparseCore 0:
  78.9 53.2 reduce-scatter.1
  664.3 47.9 all-gather.1
where the time goes:
time: 726 us; the launch traced here: 724 us
  blocking collectives  511 us (70%)
  waiting for transfers between devices  101 us (14%)
  matrix products  81.4 us (11%)
  local copies, waits for them, and re-layouts  16.6 us (2%)
  between operations  14.2 us (2%)
    psum x2, blocking collectives, widen(): narrow = lax.psum(part, 'table').astype(jnp.bfloat16)  511 us
    reduce_scatter x1, waiting for transfers between devices, local(): lax.psum_scatter(term.reshape(samp_dev * lax.axis_size('row'), feat_dev)....  52.7 us
    dot_general x8, matrix products, step(): jnp.einsum('tes,ter->tsr', sample_hot, row_hot, preferred_element_type=jn...  51.7 us
    all_gather x1, waiting for transfers between devices, local(): piece = lax.all_gather(grad_pooled, 'row', axis=0, tiled=True)  48.1 us
  transfers between devices with their start and end apart: 2, of which 2 were waited for; matrix products, arithmetic and copies ran while one was open for 0% of the time, Pallas kernels for 0%

commit v1 on v0

v1 whole, which is shorter than its diff:
```python
import functools

import jax
import jax.numpy as jnp
from jax import lax
from jax.experimental import pallas as pl
from jax.experimental.pallas import tpu as pltpu
from jax.sharding import PartitionSpec as P

F32 = jnp.float32
BF16 = jnp.bfloat16
EB = 512
NT = (((1,), (1,)), ((), ()))
TN = (((0,), (0,)), ((), ()))


def vmem():
    return pl.BlockSpec(memory_space=pltpu.VMEM)


def smem():
    return pl.BlockSpec(memory_space=pltpu.SMEM)


def params(mib):
    return pltpu.CompilerParams(vmem_limit_bytes=mib * 2**20)


def cost(flops, moved):
    return pl.CostEstimate(flops=flops, bytes_accessed=moved, transcendentals=0)


def cast_kernel(in_ref, out_ref):
    out_ref[...] = in_ref[...].astype(BF16)


def cast_half(emb_rows, side):
    tabs, rows, emb = emb_rows.shape
    block = (tabs // 2, rows, emb)
    return pl.pallas_call(
        cast_kernel,
        grid=(1,),
        in_specs=[pl.BlockSpec(block, lambda t: (side, 0, 0))],
        out_specs=pl.BlockSpec(block, lambda t: (0, 0, 0)),
        out_shape=jax.ShapeDtypeStruct(block, BF16),
        compiler_params=params(16),
        cost_estimate=cost(1 << 17, 3 << 18),
        name="cast",
    )(emb_rows)


def counts_kernel(mine_ref, ids_ref, own_ref, *refs, first_table):
    out_ref, turned_ref, acc_ref = refs[-3:]
    t = pl.program_id(0) + first_table
    samp, rows = acc_ref.shape
    mine = mine_ref[0]
    low = mine * samp
    turn = mine * (rows // 4)
    owners = own_ref[pl.ds(t, 1), :]
    first = jnp.sum((owners < low).astype(jnp.int32))
    last = jnp.sum((owners < low + samp).astype(jnp.int32))
    acc_ref[...] = jnp.zeros_like(acc_ref)

    def step(block, carry):
        at = pl.ds(pl.multiple_of(block * EB, EB), EB)
        who = own_ref[pl.ds(t, 1), at] - low
        row = (ids_ref[pl.ds(t, 1), at] - turn) & (rows - 1)
        who_hot = lax.broadcasted_iota(jnp.int32, (samp, EB), 0) == who
        row_hot = lax.broadcasted_iota(jnp.int32, (rows, EB), 0) == row
        acc_ref[...] += lax.dot_general(
            who_hot.astype(F32).astype(BF16), row_hot.astype(F32).astype(BF16), NT, preferred_element_type=F32
        )
        return carry

    lax.fori_loop(first // EB, (last + EB - 1) // EB, step, 0)
    total = acc_ref[...]
    out_ref[0] = total.astype(BF16)
    turned_ref[0] = total.T.astype(BF16)


def make_counts(mine, ids, owners, samp, rows, side, before):
    tabs, entries = ids.shape
    half = tabs // 2
    at = half * side
    whole = pl.BlockSpec((tabs, entries), lambda t: (0, 0))
    return pl.pallas_call(
        functools.partial(counts_kernel, first_table=at),
        grid=(half,),
        in_specs=[smem(), whole, whole] + [pl.BlockSpec(memory_space=pl.ANY)] * len(before),
        out_specs=[
            pl.BlockSpec((1, samp, rows), lambda t: (t + at, 0, 0)),
            pl.BlockSpec((1, rows, samp), lambda t: (t + at, 0, 0)),
        ],
        out_shape=[
            jax.ShapeDtypeStruct((tabs, samp, rows), BF16),
            jax.ShapeDtypeStruct((tabs, rows, samp), BF16),
        ],
        scratch_shapes=[pltpu.VMEM((samp, rows), F32)],
        input_output_aliases={3: 0, 4: 1} if before else {},
        compiler_params=params(56),
        cost_estimate=cost(half * samp * rows * 3072, 3 << 20),
        name="counts",
    )(mine, ids, owners, *before)


def chunk_at(i):
    x, z = i // 8, i % 8
    return (x & 1) * 128 + (x >> 1) * 64 + (z & 1) * 32 + ((z >> 1) & 1) * 16, (z >> 2) * 256


def add_sums(core_ref, z, g, z_ref, g_ref, keep_ref, send_ref):
    t = pl.program_id(0)

    @pl.when(t == 0)
    def _():
        z_ref[...] = z
        g_ref[...] = g

    @pl.when(t > 0)
    def _():
        z_ref[...] += z
        g_ref[...] += g

    @pl.when(t == pl.num_programs(0) - 1)
    def _():
        even = core_ref[0] == 0
        z, g = z_ref[...], g_ref[...]
        keep_ref[...] = jnp.where(even, z, g)
        send_ref[...] = jnp.where(even, g, z).astype(BF16)


def first_kernel(core_ref, counts_ref, *refs):
    (oa, ob, ra, rb, pa, pb, la, lb, cot_ref, v_ref, u_ref, pooled_ref, keep_ref, send_ref, z_ref, g_ref) = refs
    front = pl.program_id(0) < pl.num_programs(0) // 2
    parts = []
    for i in range(counts_ref.shape[0]):
        rows = jnp.concatenate(
            [jnp.where(front, a[i], b[i]) for a, b in ((oa, ob), (ra, rb), (pa, pb), (la, lb))], axis=0
        )
        parts.append(jnp.dot(counts_ref[i], rows, preferred_element_type=F32).astype(BF16))
    pooled = jnp.concatenate(parts, axis=1)
    pooled_ref[...] = pooled
    wide = (cot_ref[...].astype(F32) * pooled.astype(F32)).astype(BF16)
    z = jnp.dot(pooled, v_ref[0], preferred_element_type=F32)
    g = lax.dot_general(wide, u_ref[0], NT, preferred_element_type=F32)
    add_sums(core_ref, z, g, z_ref, g_ref, keep_ref, send_ref)


def first_sums(core, counts, embs, cot, v, u):
    tabs, samp, rows = counts.shape
    emb = embs[0].shape[-1]
    rank = v.shape[-1]
    steps = tabs // 2
    half = steps // 2
    block = (2, rows // 4, emb)
    a_spec = pl.BlockSpec(block, lambda t: (jnp.minimum(t, half - 1), 0, 0))
    b_spec = pl.BlockSpec(block, lambda t: (jnp.maximum(t - half, 0), 0, 0))
    feat = pl.BlockSpec((samp, 2 * emb), lambda t: (0, t))
    sums = pl.BlockSpec((samp, rank), lambda t: (0, 0))
    return pl.pallas_call(
        first_kernel,
        grid=(steps,),
        in_specs=[smem(), pl.BlockSpec((2, samp, rows), lambda t: (t, 0, 0))]
        + [a_spec, b_spec] * 4
        + [
            feat,
            pl.BlockSpec((1, 2 * emb, rank), lambda t: (0, t, 0)),
            pl.BlockSpec((1, rank, 2 * emb), lambda t: (1, 0, t)),
        ],
        out_specs=[feat, sums, sums],
        out_shape=[
            jax.ShapeDtypeStruct((samp, tabs * emb), BF16),
            jax.ShapeDtypeStruct((samp, rank), F32),
            jax.ShapeDtypeStruct((samp, rank), BF16),
        ],
        scratch_shapes=[pltpu.VMEM((samp, rank), F32)] * 2,
        compiler_params=params(48),
        cost_estimate=cost(3 << 29, 10 << 20),
        name="first_sums",
    )(core, counts, *embs, cot, v, u)


def to_core(arr):
    return lax.ppermute(arr, "c", [(0, 1), (1, 0)])


def along(arr, axis, bit):
    size = 4 if axis == "x" else 8
    return lax.ppermute(arr, axis, [(i, i ^ bit) for i in range(size)])


def small(kernel, out_shape, name, *args, scalars=0):
    return pl.pallas_call(
        kernel,
        in_specs=[smem()] * scalars + [vmem()] * (len(args) - scalars),
        out_specs=jax.tree.map(lambda _: vmem(), out_shape),
        out_shape=out_shape,
        compiler_params=params(8),
        cost_estimate=cost(1 << 20, 1 << 20),
        name=name,
    )(*args)


def cut_kernel(keep_ref, got_ref, out_ref):
    for i in range(out_ref.shape[0]):
        r, c = chunk_at(i)
        at = (slice(r, r + 16), slice(c, c + 256))
        out_ref[i] = (keep_ref[at] + got_ref[at].astype(F32)).astype(BF16)


def total_kernel(in_ref, out_ref):
    total = in_ref[0].astype(F32)
    for i in range(1, in_ref.shape[0]):
        total = total + in_ref[i].astype(F32)
    total = total.astype(BF16)
    for i in range(out_ref.shape[0]):
        out_ref[i] = total


def copies_kernel(in_ref, out_ref):
    for i in range(out_ref.shape[0]):
        out_ref[i] = in_ref[...]


def halve_kernel(bit_ref, keep_ref, got_ref, kept_ref, send_ref):
    rows, cols = kept_ref.shape
    total = keep_ref[...] + got_ref[...].astype(F32)
    if rows == total.shape[0]:
        low, high = total[:, :cols], total[:, cols:]
    else:
        low, high = total[:rows], total[rows:]
    even = bit_ref[0] == 0
    kept_ref[...] = jnp.where(even, low, high)
    send_ref[...] = jnp.where(even, high, low).astype(BF16)


def sum_by_exchange(keep, send):
    chunks = small(cut_kernel, jax.ShapeDtypeStruct((32, 16, 256), BF16), "cut", keep, to_core(send))
    parts = lax.all_to_all(chunks, ("x", "z"), 0, 0, tiled=True)
    copies = small(total_kernel, jax.ShapeDtypeStruct((32, 16, 256), BF16), "total", parts)
    mine = lax.all_to_all(copies, ("x", "z"), 0, 0, tiled=True)
    return mine, to_core(mine)


def sum_by_halves(xpos, zpos, keep, send):
    got = to_core(send)
    for axis, bit, pos in (("x", 1, xpos), ("x", 2, xpos >> 1), ("z", 1, zpos), ("z", 2, zpos >> 1), ("z", 4, zpos >> 2)):
        rows, cols = keep.shape
        shape = (rows, cols // 2) if (axis, bit) == ("z", 4) else (rows // 2, cols)
        keep, send = small(
            halve_kernel,
            [jax.ShapeDtypeStruct(shape, F32), jax.ShapeDtypeStruct(shape, BF16)],
            "halve",
            pos & 1,
            keep,
            got,
            scalars=1,
        )
        got = along(send, axis, bit)
    done = small(
        lambda a, b, out: copies_kernel((a[...] + b[...].astype(F32)).astype(BF16), out),
        jax.ShapeDtypeStruct((8, 16, 256), BF16),
        "done",
        keep,
        got,
    )
    part = lax.all_to_all(done, "z", 0, 0, tiled=True)
    copies = small(copies_kernel, jax.ShapeDtypeStruct((4, 8, 16, 256), BF16), "copies", part)
    mine = lax.all_to_all(copies, "x", 0, 0, tiled=True).reshape(32, 16, 256)
    return mine, to_core(mine)


def spread(core_ref, mine_ref, other_ref, in_ref):
    core = core_ref[0]
    for side, ref in ((core, mine_ref), (1 - core, other_ref)):
        for i in range(32):
            r, c = chunk_at(i)
            in_ref[side, r : r + 16, c : c + 256] = ref[i]


def middle_kernel(core_ref, mine_ref, other_ref, pooled_ref, cot_ref, u_ref, b_ref, v_ref, *refs):
    x1_ref, a_ref, keep_ref, send_ref, in_ref, z_ref, g_ref = refs

    @pl.when(pl.program_id(0) == 0)
    def _():
        spread(core_ref, mine_ref, other_ref, in_ref)

    u, v = u_ref[0], v_ref[0]
    pooled = pooled_ref[...].astype(F32)
    cot = cot_ref[...].astype(F32)
    h0 = jnp.dot(in_ref[0], u, preferred_element_type=F32) + b_ref[0:1, :]
    x1 = (pooled * h0 + pooled).astype(BF16)
    x1_ref[...] = x1
    g1 = cot + lax.dot_general(in_ref[1], v, NT, preferred_element_type=F32)
    a_ref[...] = (g1 * h0 + g1).astype(BF16)
    wide = (g1 * pooled).astype(BF16)
    z = jnp.dot(x1, v, preferred_element_type=F32)
    g = lax.dot_general(wide, u, NT, preferred_element_type=F32)
    add_sums(core_ref, z, g, z_ref, g_ref, keep_ref, send_ref)


def middle(core, mine, other, pooled, cot, u, bias, v):
    samp, feats = pooled.shape
    rank = v.shape[-1]
    step = 512
    wide = pl.BlockSpec((samp, step), lambda t: (0, t))
    whole = pl.BlockSpec(mine.shape, lambda t: (0, 0, 0))
    sums = pl.BlockSpec((samp, rank), lambda t: (0, 0))
    feat = jax.ShapeDtypeStruct((samp, feats), BF16)
    return pl.pallas_call(
        middle_kernel,
        grid=(feats // step,),
        in_specs=[
            smem(),
            whole,
            whole,
            wide,
            wide,
            pl.BlockSpec((1, rank, step), lambda t: (0, 0, t)),
            pl.BlockSpec((2, step), lambda t: (0, t)),
            pl.BlockSpec((1, step, rank), lambda t: (1, t, 0)),
        ],
        out_specs=[wide, wide, sums, sums],
        out_shape=[feat, feat, jax.ShapeDtypeStruct((samp, rank), F32), jax.ShapeDtypeStruct((samp, rank), BF16)],
        scratch_shapes=[pltpu.VMEM((2, samp, rank), BF16)] + [pltpu.VMEM((samp, rank), F32)] * 2,
        compiler_params=params(56),
        cost_estimate=cost(1 << 31, 8 << 20),
        name="middle",
    )(core, mine, other, pooled, cot, u, bias, v)


def last_kernel(core_ref, mine_ref, other_ref, turned_ref, pooled_ref, cot_ref, x1_ref, a_ref, u_ref, b_ref, v_ref, *refs):
    crossed_ref, p0, p1a, p1b, p2a, p2b, p3a, p3b, in_ref = refs
    t = pl.program_id(0)
    half = pl.num_programs(0) // 2

    @pl.when(t == 0)
    def _():
        spread(core_ref, mine_ref, other_ref, in_ref)

    pooled = pooled_ref[...].astype(F32)
    cot = cot_ref[...].astype(F32)
    h1 = jnp.dot(in_ref[0], u_ref[0], preferred_element_type=F32) + b_ref[1:2, :]
    crossed_ref[...] = (pooled * h1 + x1_ref[...].astype(F32)).astype(BF16)
    grad = cot * h1 + a_ref[...].astype(F32) + lax.dot_general(in_ref[1], v_ref[0], NT, preferred_element_type=F32)
    grad = grad.astype(BF16)
    tables, rows, emb = p0.shape
    for i in range(tables):
        part = jnp.dot(turned_ref[i], grad[:, i * emb : (i + 1) * emb], preferred_element_type=F32)
        p0[i] = part[:rows]

        @pl.when(t < half)
        def _():
            for k, ref in enumerate((p1a, p2a, p3a)):
                ref[i] = part[(k + 1) * rows : (k + 2) * rows].astype(BF16)

        @pl.when(t >= half)
        def _():
            for k, ref in enumerate((p1b, p2b, p3b)):
                ref[i] = part[(k + 1) * rows : (k + 2) * rows].astype(BF16)


def last(core, mine, other, turned, pooled, cot, x1, a, u, bias, v):
    tabs, rows, samp = turned.shape
    rank = v.shape[-1]
    emb = pooled.shape[1] // tabs
    steps = tabs // 2
    half = steps // 2
    whole = pl.BlockSpec(mine.shape, lambda t: (0, 0, 0))
    feat = pl.BlockSpec((samp, 2 * emb), lambda t: (0, t))
    block = (2, rows // 4, emb)
    a_spec = pl.BlockSpec(block, lambda t: (jnp.minimum(t, half - 1), 0, 0))
    b_spec = pl.BlockSpec(block, lambda t: (jnp.maximum(t - half, 0), 0, 0))
    piece = jax.ShapeDtypeStruct((tabs // 2, rows // 4, emb), BF16)
    return pl.pallas_call(
        last_kernel,
        grid=(steps,),
        in_specs=[smem(), whole, whole, pl.BlockSpec((2, rows, samp), lambda t: (t, 0, 0))]
        + [feat] * 4
        + [
            pl.BlockSpec((1, rank, 2 * emb), lambda t: (1, 0, t)),
            pl.BlockSpec((2, 2 * emb), lambda t: (0, t)),
            pl.BlockSpec((1, 2 * emb, rank), lambda t: (0, t, 0)),
        ],
        out_specs=[feat, pl.BlockSpec(block, lambda t: (t, 0, 0))] + [a_spec, b_spec] * 3,
        out_shape=[
            jax.ShapeDtypeStruct((samp, tabs * emb), BF16),
            jax.ShapeDtypeStruct((tabs, rows // 4, emb), F32),
        ]
        + [piece] * 6,
        scratch_shapes=[pltpu.VMEM((2, samp, rank), BF16)],
        compiler_params=params(56),
        cost_estimate=cost(3 << 29, 14 << 20),
        name="last",
    )(core, mine, other, turned, pooled, cot, x1, a, u, bias, v)


def right(arr):
    return lax.ppermute(arr, "row", [(i, (i + 1) & 3) for i in range(4)])


def left(arr):
    return lax.ppermute(arr, "row", [(i, (i + 3) & 3) for i in range(4)])


def scatter_rows(p0, p1a, p1b, p2a, p2b, p3a, p3b):
    from_left, from_right = right(p2a), left(p2b)
    sum_b, sum_a = right(p1b), left(p3a)
    far_a = right((p1a.astype(F32) + from_left.astype(F32)).astype(BF16))
    far_b = left((p3b.astype(F32) + from_right.astype(F32)).astype(BF16))
    others = jnp.concatenate(
        [sum_a.astype(F32) + far_a.astype(F32), sum_b.astype(F32) + far_b.astype(F32)], axis=0
    )
    return p0 + others


def scalar(axis):
    return lax.axis_index(axis).astype(jnp.int32).reshape(1)


def local(emb_rows, entry_ids, entry_sample, cross_v, cross_u, cross_bias, cotangent):
    samp = cotangent.shape[0]
    rows = emb_rows.shape[1] * lax.axis_size("row")
    mine, core, xpos, zpos = scalar("row"), scalar("c"), scalar("x"), scalar("z")
    own_a, own_b = cast_half(emb_rows, 0), cast_half(emb_rows, 1)
    left_a, right_b = right(own_a), left(own_b)
    left_b, right_a = right(own_b), left(own_a)
    counted = make_counts(mine, entry_ids, entry_sample, samp, rows, 0, ())
    left_a, right_b, *counted = lax.optimization_barrier((left_a, right_b, *counted))
    far_a, far_b = right(left_a), left(right_b)
    counts, turned = make_counts(mine, entry_ids, entry_sample, samp, rows, 1, counted)
    embs = (own_a, own_b, right_a, right_b, far_a, far_b, left_a, left_b)
    pooled, keep, send = first_sums(core, counts, embs, cotangent, cross_v, cross_u)
    sums = sum_by_exchange(keep, send)
    x1, a, keep, send = middle(core, *sums, pooled, cotangent, cross_u, cross_bias, cross_v)
    sums = sum_by_halves(xpos, zpos, keep, send)
    crossed, *pieces = last(core, *sums, turned, pooled, cotangent, x1, a, cross_u, cross_bias, cross_v)
    return crossed, scatter_rows(*pieces)


def solution(mesh):
    fine = jax.sharding.Mesh(mesh.devices.reshape(4, 8, 2, 4), ("x", "z", "c", "row"))
    table = ("x", "z", "c")
    placed = (
        P(table, "row", None),
        P(table, None),
        P(table, None),
        P(None, table, None),
        P(None, None, table),
        P(None, table),
        P("row", table),
    )
    return jax.shard_map(
        local,
        mesh=fine,
        in_specs=placed,
        out_specs=(P("row", table), P(table, "row", None)),
        check_vma=False,
    )
```

time: 726 us -> 170 us (0.23)
  blocking collectives: 511 us -> 52.1 us
  matrix products: 81.4 us -> 0 us
  waiting for transfers between devices: 101 us -> 35.4 us
  starting transfers between devices: 0.08 us -> 38.3 us
  Pallas kernels: 0 us -> 35 us
  between operations: 14.2 us -> 0.81 us
  local copies, waits for them, and re-layouts: 16.6 us -> 4.63 us
    psum x2 -> x0, blocking collectives: 511 us -> none  [widen(): narrow = lax.psum(part, 'table').astype(jnp.bfloat16)]
    dot_general x18 -> x0, matrix products: 81.4 us -> none  [the longest x8 51.7 us: step(): jnp.einsum('tes,ter->tsr', sample_hot, row_hot, preferred_element_type=jn...]
    reduce_scatter x1 -> x0, waiting for transfers between devices: 52.7 us -> none  [local(): lax.psum_scatter(term.reshape(samp_dev * lax.axis_size('row'), feat_dev)....]
    all_to_all x0 -> x4, blocking collectives: none -> 52.1 us  [the longest x1 17.9 us: sum_by_exchange(): parts = lax.all_to_all(chunks, ('x', 'z'), 0, 0, tiled=True)]
    all_gather x1 -> x0, waiting for transfers between devices: 48.1 us -> none  [local(): piece = lax.all_gather(grad_pooled, 'row', axis=0, tiled=True)]
    ppermute x0 -> x21, starting transfers between devices: none -> 38.3 us  [the longest x4 16.8 us: to_core(): return lax.ppermute(arr, 'c', [(0, 1), (1, 0)])]
    ppermute x0 -> x21, waiting for transfers between devices: none -> 35.4 us  [the longest x5 15.6 us: along(): return lax.ppermute(arr, axis, [(i, i ^ bit) for i in range(size)])]
    pallas_call x0 -> x16, Pallas kernels: none -> 35 us  [the longest x2 13.7 us: make_counts(): pl.pallas_call(functools.partial(counts_kernel, first_table=at), grid=(ha...]
  transfers between devices with their start and end apart: 2 -> 21, of which waited for: 2 -> 12; matrix products, arithmetic and copies ran while one was open for 0% -> 1% of each run, Pallas kernels for 0% -> 8%
where the time goes in v1:
time: 170 us
  blocking collectives  52.1 us (31%)
  starting transfers between devices  38.3 us (23%)
  waiting for transfers between devices  35.4 us (21%)
  Pallas kernels  35 us (21%)
  local copies, waits for them, and re-layouts  4.63 us (3%)
  other arithmetic  3.26 us (2%)
    all_to_all x1, blocking collectives, sum_by_exchange(): parts = lax.all_to_all(chunks, ('x', 'z'), 0, 0, tiled=True)  17.9 us
    ppermute x4, starting transfers between devices, to_core(): return lax.ppermute(arr, 'c', [(0, 1), (1, 0)])  16.8 us
    all_to_all x1, blocking collectives, sum_by_exchange(): mine = lax.all_to_all(copies, ('x', 'z'), 0, 0, tiled=True)  16.2 us
    ppermute x5, waiting for transfers between devices, along(): return lax.ppermute(arr, axis, [(i, i ^ bit) for i in range(size)])  15.6 us
    ppermute x6, waiting for transfers between devices, right(): return lax.ppermute(arr, 'row', [(i, i + 1 & 3) for i in range(4)])  15 us
    pallas_call x2, Pallas kernels, make_counts(): pl.pallas_call(functools.partial(counts_kernel, first_table=at), grid=(ha...  13.7 us
    ppermute x6, starting transfers between devices, left(): return lax.ppermute(arr, 'row', [(i, i + 3 & 3) for i in range(4)])  11 us
    all_to_all x1, blocking collectives, sum_by_halves(): part = lax.all_to_all(done, 'z', 0, 0, tiled=True)  10.1 us
  transfers between devices with their start and end apart: 21, of which 12 were waited for; matrix products, arithmetic and copies ran while one was open for 1% of the time, Pallas kernels for 8%

profile of v1, /device:TPU:1, one launch (start us, length us, event | category | flops | bytes accessed | tf_op | source)
XLA Modules:
  0.0 169.5 jit_solution(16738548189911320557)
XLA Ops:
  0.6 1.2 copy-done.1
  1.9 2.2 %collective-permute-start = (bf16[4,128,256]{2,1,0:T(8,128)(2,1)S(1)}, bf16[4,128,256]{2,1,0:T(8,128)(2,1)S(1)}, u32[]{:S(2)}, u32[]{:S(2)}) collective-permute-start(bf16[4,128,256]{2,1,0:T(8,128)(2,1)S(1)} %cast.2.refs_0_), channel_id=1, source_target_pairs={{0,1},{1,2},{2,3},{3,0},{4,5},{5,6},{6,7},{7,4},{8,9},{9,10},{10,1... | collective-permute-start | bytes 786440 | tf_op jit(solution)/shard_map/ppermute | solution.py:399
  4.1 1.5 collective-permute-start.1
  5.7 1.4 collective-permute-start.2
  7.1 7.2 %counts.2 = (bf16[8,256,512]{2,1,0:T(8,128)(2,1)}, bf16[8,512,256]{2,1,0:T(8,128)(2,1)}) custom-call(s32[1]{0:T(128)} %bitcast.6.mine_ref, s32[8,4096]{1,0:T(8,128)} %ids_ref.3, s32[8,4096]{1,0:T(8,128)} %own_ref.3), custom_call_target="tpu_custom_call" | custom-call | flops 1610612736 | bytes 3145728 | tf_op jit(solution)/shard_map/counts/pallas_call | solution.py:86
  14.4 2.7 %collective-permute-start.4 = (bf16[4,128,256]{2,1,0:T(8,128)(2,1)S(1)}, bf16[4,128,256]{2,1,0:T(8,128)(2,1)S(1)}, u32[]{:S(2)}, u32[]{:S(2)}) collective-permute-start(bf16[4,128,256]{2,1,0:T(8,128)(2,1)S(1)} %collective-permute-done.1.refs_3_), channel_id=1, source_target_pairs={{0,3},{1,0},{2,1},{3,2},{4,7},{5,4},{6,5},{7,6},{8,11},{9,8},{10,9... | collective-permute-start | bytes 786440 | tf_op jit(solution)/shard_map/ppermute | solution.py:403
  17.0 6.6 %counts.3 = (bf16[8,256,512]{2,1,0:T(8,128)(2,1)}, bf16[8,512,256]{2,1,0:T(8,128)(2,1)}) custom-call(s32[1]{0:T(128)} %bitcast.6.mine_ref, s32[8,4096]{1,0:T(8,128)} %ids_ref.3, s32[8,4096]{1,0:T(8,128)} %own_ref.3, bf16[8,256,512]{2,1,0:T(8,128)(2,1)} %get-tuple-element.37.refs_0_, ...), custom_call_target="tpu_custom_call", output_to_operand_aliasing={{0}: (3, {}), {1}: (4, {})} | custom-call | flops 1610612736 | bytes 3145728 | tf_op jit(solution)/shard_map/counts/pallas_call | solution.py:86
  23.7 5.3 %first_sums.1 = (bf16[256,2048]{1,0:T(8,128)(2,1)S(1)}, f32[256,512]{1,0:T(8,128)S(1)}, bf16[256,512]{1,0:T(8,128)(2,1)S(1)}) custom-call(s32[1]{0:T(128)} %bitcast.core_ref, bf16[8,256,512]{2,1,0:T(8,128)(2,1)} %get-tuple-element.39.counts_ref, bf16[4,128,256]{2,1,0:T(8,128)(2,1)S(1)} %cast.2.refs_0_, bf16[4,128,256]{2,1,0:T(8,128)(2,1)S(1)} %cast.3.refs_1_, ...), custom_call_target="tpu_custom_call" | custom-call | flops 1610612736 | bytes 10485760 | tf_op jit(solution)/shard_map/first_sums/pallas_call | solution.py:160
  29.9 4.4 %collective-permute-start.6 = (bf16[256,512]{1,0:T(8,128)(2,1)S(1)}, bf16[256,512]{1,0:T(8,128)(2,1)S(1)}, u32[]{:S(2)}, u32[]{:S(2)}) collective-permute-start(bf16[256,512]{1,0:T(8,128)(2,1)S(1)} %get-tuple-element.43), channel_id=1, source_target_pairs={{0,4},{4,0},{1,5},{5,1},{2,6},{6,2},{3,7},{7,3},{8,12},{12,8},{9,1... | collective-permute-start | bytes 786440 | tf_op jit(solution)/shard_map/ppermute | solution.py:184
  35.5 17.9 %all_to_all.20.in_ref = bf16[32,16,256]{2,1,0:T(8,128)(2,1)S(1)} all-to-all(bf16[32,16,256]{2,1,0:T(8,128)(2,1)S(1)} %cut.1), channel_id=1, replica_groups=mesh['x'=4,'z'=8,'c'=2,'row'=4] {'x','z'}, dimensions={0} | all-to-all | bytes 524288 | tf_op jit(solution)/shard_map/all_to_all | solution.py:239
  53.5 16.2 %all_to_all.21.mine_ref = bf16[32,16,256]{2,1,0:T(8,128)(2,1)S(1)} all-to-all(bf16[32,16,256]{2,1,0:T(8,128)(2,1)S(1)} %total.1), channel_id=1, replica_groups=mesh['x'=4,'z'=8,'c'=2,'row'=4] {'x','z'}, dimensions={0} | all-to-all | bytes 524288 | tf_op jit(solution)/shard_map/all_to_all | solution.py:241
  69.7 3.6 %collective-permute-start.7 = (bf16[32,16,256]{2,1,0:T(8,128)(2,1)S(1)}, bf16[32,16,256]{2,1,0:T(8,128)(2,1)S(1)}, u32[]{:S(2)}, u32[]{:S(2)}) collective-permute-start(bf16[32,16,256]{2,1,0:T(8,128)(2,1)S(1)} %all_to_all.21.mine_ref), channel_id=1, source_target_pairs={{0,4},{4,0},{1,5},{5,1},{2,6},{6,2},{3,7},{7,3},{8,12},{12,8},{9,1... | collective-permute-start | bytes 786440 | tf_op jit(solution)/shard_map/ppermute | solution.py:184
  75.1 7.1 %middle.1 = (bf16[256,2048]{1,0:T(8,128)(2,1)}, bf16[256,2048]{1,0:T(8,128)(2,1)}, f32[256,512]{1,0:T(8,128)}, bf16[256,512]{1,0:T(8,128)(2,1)}) custom-call(s32[1]{0:T(128)} %bitcast.core_ref, bf16[32,16,256]{2,1,0:T(8,128)(2,1)} %copy-done.6, bf16[32,16,256]{2,1,0:T(8,128)(2,1)} %copy-done.8, bf16[256,2048]{1,0:T(8,128)(2,1)} %copy-done.2, ...), custom_call_target="tpu_custom_call" | custom-call | flops 2147483648 | bytes 8388608 | tf_op jit(solution)/shard_map/middle/pallas_call | solution.py:310
  82.7 1.4 collective-permute-done.8.got_ref
  85.6 4.4 %collective-permute-done.9.got_ref = bf16[128,512]{1,0:T(8,128)(2,1)S(1)} collective-permute-done((bf16[128,512]{1,0:T(8,128)(2,1)S(1)}, bf16[128,512]{1,0:T(8,128)(2,1)S(1)}, u32[]{:S(2)}, u32[]{:S(2)}) %collective-permute-start.9) | collective-permute-done | bytes 131104 | tf_op jit(solution)/shard_map/ppermute | solution.py:189
  90.0 1.3 collective-permute-start.10
  91.4 3.4 %collective-permute-done.10.got_ref = bf16[64,512]{1,0:T(8,128)(2,1)S(1)} collective-permute-done((bf16[64,512]{1,0:T(8,128)(2,1)S(1)}, bf16[64,512]{1,0:T(8,128)(2,1)S(1)}, u32[]{:S(2)}, u32[]{:S(2)}) %collective-permute-start.10) | collective-permute-done | bytes 65568 | tf_op jit(solution)/shard_map/ppermute | solution.py:189
  94.8 1.6 collective-permute-start.11
  96.4 1.3 collective-permute-done.11.got_ref
  97.7 1.9 %collective-permute-start.12 = (bf16[16,512]{1,0:T(8,128)(2,1)S(1)}, bf16[16,512]{1,0:T(8,128)(2,1)S(1)}, u32[]{:S(2)}, u32[]{:S(2)}) collective-permute-start(bf16[16,512]{1,0:T(8,128)(2,1)S(1)} %get-tuple-element.54), channel_id=1, source_target_pairs={{0,16},{8,24},{16,0},{24,8},{32,48},{40,56},{48,32},{56,40},{1,17}... | collective-permute-start | bytes 49160 | tf_op jit(solution)/shard_map/ppermute | solution.py:189
  99.6 1.8 %collective-permute-done.12.got_ref = bf16[16,512]{1,0:T(8,128)(2,1)S(1)} collective-permute-done((bf16[16,512]{1,0:T(8,128)(2,1)S(1)}, bf16[16,512]{1,0:T(8,128)(2,1)S(1)}, u32[]{:S(2)}, u32[]{:S(2)}) %collective-permute-start.12) | collective-permute-done | bytes 16416 | tf_op jit(solution)/shard_map/ppermute | solution.py:189
  101.5 1.8 %collective-permute-start.13 = (bf16[16,256]{1,0:T(8,128)(2,1)S(1)}, bf16[16,256]{1,0:T(8,128)(2,1)S(1)}, u32[]{:S(2)}, u32[]{:S(2)}) collective-permute-start(bf16[16,256]{1,0:T(8,128)(2,1)S(1)} %get-tuple-element.56), channel_id=1, source_target_pairs={{0,32},{8,40},{16,48},{24,56},{32,0},{40,8},{48,16},{56,24},{1,33}... | collective-permute-start | bytes 24584 | tf_op jit(solution)/shard_map/ppermute | solution.py:189
  103.3 4.7 %collective-permute-done.13.b = bf16[16,256]{1,0:T(8,128)(2,1)S(1)} collective-permute-done((bf16[16,256]{1,0:T(8,128)(2,1)S(1)}, bf16[16,256]{1,0:T(8,128)(2,1)S(1)}, u32[]{:S(2)}, u32[]{:S(2)}) %collective-permute-start.13) | collective-permute-done | bytes 8224 | tf_op jit(solution)/shard_map/ppermute | solution.py:189
  108.0 10.1 %all_to_all.22.in_ref = bf16[8,16,256]{2,1,0:T(8,128)(2,1)S(1)} all-to-all(bf16[8,16,256]{2,1,0:T(8,128)(2,1)S(1)} %done.1), channel_id=1, replica_groups=mesh['x'=4,'z'=8,'c'=2,'row'=4] {'z'}, dimensions={0} | all-to-all | bytes 131072 | tf_op jit(solution)/shard_map/all_to_all | solution.py:267
  118.1 7.9 %all_to_all.23 = bf16[4,8,16,256]{3,2,1,0:T(8,128)(2,1)S(1)} all-to-all(bf16[4,8,16,256]{3,2,1,0:T(8,128)(2,1)S(1)} %copies.1), channel_id=1, replica_groups=mesh['x'=4,'z'=8,'c'=2,'row'=4] {'x'}, dimensions={0} | all-to-all | bytes 524288 | tf_op jit(solution)/shard_map/all_to_all | solution.py:269
  126.0 8.4 %collective-permute-start.14 = (bf16[32,16,256]{2,1,0:T(8,128)(2,1)S(1)}, bf16[32,16,256]{2,1,0:T(8,128)(2,1)S(1)}, u32[]{:S(2)}, u32[]{:S(2)}) collective-permute-start(bf16[32,16,256]{2,1,0:T(8,128)(2,1)S(1)} %bitcast.8), channel_id=1, source_target_pairs={{0,4},{4,0},{1,5},{5,1},{2,6},{6,2},{3,7},{7,3},{8,12},{12,8},{9,1... | collective-permute-start | bytes 786440 | tf_op jit(solution)/shard_map/ppermute | solution.py:184
  136.3 8.5 %last.1 = (bf16[256,2048]{1,0:T(8,128)(2,1)}, f32[8,128,256]{2,1,0:T(8,128)}, bf16[4,128,256]{2,1,0:T(8,128)(2,1)}, bf16[4,128,256]{2,1,0:T(8,128)(2,1)}, bf16[4...) custom-call(s32[1]{0:T(128)} %bitcast.core_ref, ...), custom_call_target="tpu_custom_call" | custom-call | flops 1610612736 | bytes 14680064 | tf_op jit(solution)/shard_map/last/pallas_call | solution.py:375
  145.7 1.8 %collective-permute-start.19 = (bf16[4,128,256]{2,1,0:T(8,128)(2,1)}, bf16[4,128,256]{2,1,0:T(8,128)(2,1)S(1)}, u32[]{:S(2)}, u32[]{:S(2)}) collective-permute-start(bf16[4,128,256]{2,1,0:T(8,128)(2,1)} %get-tuple-element.67), channel_id=1, source_target_pairs={{0,3},{1,0},{2,1},{3,2},{4,7},{5,4},{6,5},{7,6},{8,11},{9,8},{10,9... | collective-permute-start | bytes 786440 | tf_op jit(solution)/shard_map/ppermute | solution.py:403
  148.4 5.5 %collective-permute-done.16 = bf16[4,128,256]{2,1,0:T(8,128)(2,1)S(1)} collective-permute-done((bf16[4,128,256]{2,1,0:T(8,128)(2,1)}, bf16[4,128,256]{2,1,0:T(8,128)(2,1)S(1)}, u32[]{:S(2)}, u32[]{:S(2)}) %collective-permute-start.16) | collective-permute-done | bytes 262176 | tf_op jit(solution)/shard_map/ppermute | solution.py:399
  156.1 2.7 %collective-permute-start.20 = (bf16[4,128,256]{2,1,0:T(8,128)(2,1)S(1)}, bf16[4,128,256]{2,1,0:T(8,128)(2,1)S(1)}, u32[]{:S(2)}, u32[]{:S(2)}) collective-permute-start(bf16[4,128,256]{2,1,0:T(8,128)(2,1)S(1)} %add_convert_fusion), channel_id=1, source_target_pairs={{0,3},{1,0},{2,1},{3,2},{4,7},{5,4},{6,5},{7,6},{8,11},{9,8},{10,9... | collective-permute-start | bytes 786440 | tf_op jit(solution)/shard_map/ppermute | solution.py:403
  158.8 3.9 %collective-permute-done.17 = bf16[4,128,256]{2,1,0:T(8,128)(2,1)S(1)} collective-permute-done((bf16[4,128,256]{2,1,0:T(8,128)(2,1)S(1)}, bf16[4,128,256]{2,1,0:T(8,128)(2,1)S(1)}, u32[]{:S(2)}, u32[]{:S(2)}) %collective-permute-start.17) | collective-permute-done | bytes 262176 | tf_op jit(solution)/shard_map/ppermute | solution.py:399
  162.8 5.6 %collective-permute-done.18 = bf16[4,128,256]{2,1,0:T(8,128)(2,1)S(1)} collective-permute-done((bf16[4,128,256]{2,1,0:T(8,128)(2,1)}, bf16[4,128,256]{2,1,0:T(8,128)(2,1)S(1)}, u32[]{:S(2)}, u32[]{:S(2)}) %collective-permute-start.18) | collective-permute-done | bytes 262176 | tf_op jit(solution)/shard_map/ppermute | solution.py:399
  (53 shorter events, 13.4 us)
Async XLA Ops:
  0.6 1.2 copy-start.1
  1.9 12.4 %collective-permute-start = (bf16[4,128,256]{2,1,0:T(8,128)(2,1)S(1)}, bf16[4,128,256]{2,1,0:T(8,128)(2,1)S(1)}, u32[]{:S(2)}, u32[]{:S(2)}) collective-permute-start(bf16[4,128,256]{2,1,0:T(8,128)(2,1)S(1)} %cast.2.refs_0_), channel_id=1, source_target_pairs={{0,1},{1,2},{2,3},{3,0},{4,5},{5,6},{6,7},{7,4},{8,9},{9,10},{10,1... | collective-permute-start | bytes 786440 | tf_op jit(solution)/shard_map/ppermute | solution.py:399
  4.1 10.2 %collective-permute-start.1 = (bf16[4,128,256]{2,1,0:T(8,128)(2,1)S(1)}, bf16[4,128,256]{2,1,0:T(8,128)(2,1)S(1)}, u32[]{:S(2)}, u32[]{:S(2)}) collective-permute-start(bf16[4,128,256]{2,1,0:T(8,128)(2,1)S(1)} %cast.3.refs_1_), channel_id=1, source_target_pairs={{0,3},{1,0},{2,1},{3,2},{4,7},{5,4},{6,5},{7,6},{8,11},{9,8},{10,9... | collective-permute-start | bytes 786440 | tf_op jit(solution)/shard_map/ppermute | solution.py:403
  5.7 18.0 %collective-permute-start.2 = (bf16[4,128,256]{2,1,0:T(8,128)(2,1)S(1)}, bf16[4,128,256]{2,1,0:T(8,128)(2,1)S(1)}, u32[]{:S(2)}, u32[]{:S(2)}) collective-permute-start(bf16[4,128,256]{2,1,0:T(8,128)(2,1)S(1)} %cast.2.refs_0_), channel_id=1, source_target_pairs={{0,3},{1,0},{2,1},{3,2},{4,7},{5,4},{6,5},{7,6},{8,11},{9,8},{10,9... | collective-permute-start | bytes 786440 | tf_op jit(solution)/shard_map/ppermute | solution.py:403
  7.1 16.5 %collective-permute-start.5 = (bf16[4,128,256]{2,1,0:T(8,128)(2,1)S(1)}, bf16[4,128,256]{2,1,0:T(8,128)(2,1)S(1)}, u32[]{:S(2)}, u32[]{:S(2)}) collective-permute-start(bf16[4,128,256]{2,1,0:T(8,128)(2,1)S(1)} %cast.3.refs_1_), channel_id=1, source_target_pairs={{0,1},{1,2},{2,3},{3,0},{4,5},{5,6},{6,7},{7,4},{8,9},{9,10},{10,1... | collective-permute-start | bytes 786440 | tf_op jit(solution)/shard_map/ppermute | solution.py:399
  14.3 9.3 %collective-permute-start.3 = (bf16[4,128,256]{2,1,0:T(8,128)(2,1)S(1)}, bf16[4,128,256]{2,1,0:T(8,128)(2,1)S(1)}, u32[]{:S(2)}, u32[]{:S(2)}) collective-permute-start(bf16[4,128,256]{2,1,0:T(8,128)(2,1)S(1)} %collective-permute-done.refs_6_), channel_id=1, source_target_pairs={{0,1},{1,2},{2,3},{3,0},{4,5},{5,6},{6,7},{7,4},{8,9},{9,10},{10,1... | collective-permute-start | bytes 786440 | tf_op jit(solution)/shard_map/ppermute | solution.py:399
  14.4 9.3 %collective-permute-start.4 = (bf16[4,128,256]{2,1,0:T(8,128)(2,1)S(1)}, bf16[4,128,256]{2,1,0:T(8,128)(2,1)S(1)}, u32[]{:S(2)}, u32[]{:S(2)}) collective-permute-start(bf16[4,128,256]{2,1,0:T(8,128)(2,1)S(1)} %collective-permute-done.1.refs_3_), channel_id=1, source_target_pairs={{0,3},{1,0},{2,1},{3,2},{4,7},{5,4},{6,5},{7,6},{8,11},{9,8},{10,9... | collective-permute-start | bytes 786440 | tf_op jit(solution)/shard_map/ppermute | solution.py:403
  17.0 6.6 %copy-start = (bf16[256,2048]{1,0:T(8,128)(2,1)S(1)}, bf16[256,2048]{1,0:T(8,128)(2,1)}, u32[]{:S(2)}) copy-start(bf16[256,2048]{1,0:T(8,128)(2,1)} %cot_ref.3) | copy-start | bytes 3145732
  28.9 1.0 copy-start.2
  29.9 5.5 %collective-permute-start.6 = (bf16[256,512]{1,0:T(8,128)(2,1)S(1)}, bf16[256,512]{1,0:T(8,128)(2,1)S(1)}, u32[]{:S(2)}, u32[]{:S(2)}) collective-permute-start(bf16[256,512]{1,0:T(8,128)(2,1)S(1)} %get-tuple-element.43), channel_id=1, source_target_pairs={{0,4},{4,0},{1,5},{5,1},{2,6},{6,2},{3,7},{7,3},{8,12},{12,8},{9,1... | collective-permute-start | bytes 786440 | tf_op jit(solution)/shard_map/ppermute | solution.py:184
  69.7 4.8 %copy-start.6 = (bf16[32,16,256]{2,1,0:T(8,128)(2,1)}, bf16[32,16,256]{2,1,0:T(8,128)(2,1)S(1)}, u32[]{:S(2)}) copy-start(bf16[32,16,256]{2,1,0:T(8,128)(2,1)S(1)} %all_to_all.21.mine_ref) | copy-start | bytes 786436
  69.7 4.8 %collective-permute-start.7 = (bf16[32,16,256]{2,1,0:T(8,128)(2,1)S(1)}, bf16[32,16,256]{2,1,0:T(8,128)(2,1)S(1)}, u32[]{:S(2)}, u32[]{:S(2)}) collective-permute-start(bf16[32,16,256]{2,1,0:T(8,128)(2,1)S(1)} %all_to_all.21.mine_ref), channel_id=1, source_target_pairs={{0,4},{4,0},{1,5},{5,1},{2,6},{6,2},{3,7},{7,3},{8,12},{12,8},{9,1... | collective-permute-start | bytes 786440 | tf_op jit(solution)/shard_map/ppermute | solution.py:184
  74.4 0.7 copy-start.8
  82.3 1.8 %collective-permute-start.8 = (bf16[256,512]{1,0:T(8,128)(2,1)}, bf16[256,512]{1,0:T(8,128)(2,1)S(1)}, u32[]{:S(2)}, u32[]{:S(2)}) collective-permute-start(bf16[256,512]{1,0:T(8,128)(2,1)} %get-tuple-element.46), channel_id=1, source_target_pairs={{0,4},{4,0},{1,5},{5,1},{2,6},{6,2},{3,7},{7,3},{8,12},{12,8},{9,1... | collective-permute-start | bytes 786440 | tf_op jit(solution)/shard_map/ppermute | solution.py:184
  84.1 1.0 copy-start.3
  85.2 4.8 %collective-permute-start.9 = (bf16[128,512]{1,0:T(8,128)(2,1)S(1)}, bf16[128,512]{1,0:T(8,128)(2,1)S(1)}, u32[]{:S(2)}, u32[]{:S(2)}) collective-permute-start(bf16[128,512]{1,0:T(8,128)(2,1)S(1)} %get-tuple-element.48), channel_id=1, source_target_pairs={{0,64},{64,0},{128,192},{192,128},{1,65},{65,1},{129,193},{193,129... | collective-permute-start | bytes 393224 | tf_op jit(solution)/shard_map/ppermute | solution.py:189
  90.0 4.7 %collective-permute-start.10 = (bf16[64,512]{1,0:T(8,128)(2,1)S(1)}, bf16[64,512]{1,0:T(8,128)(2,1)S(1)}, u32[]{:S(2)}, u32[]{:S(2)}) collective-permute-start(bf16[64,512]{1,0:T(8,128)(2,1)S(1)} %get-tuple-element.50), channel_id=1, source_target_pairs={{0,128},{64,192},{128,0},{192,64},{1,129},{65,193},{129,1},{193,65... | collective-permute-start | bytes 196616 | tf_op jit(solution)/shard_map/ppermute | solution.py:189
  94.8 2.9 %collective-permute-start.11 = (bf16[32,512]{1,0:T(8,128)(2,1)S(1)}, bf16[32,512]{1,0:T(8,128)(2,1)S(1)}, u32[]{:S(2)}, u32[]{:S(2)}) collective-permute-start(bf16[32,512]{1,0:T(8,128)(2,1)S(1)} %get-tuple-element.52), channel_id=1, source_target_pairs={{0,8},{8,0},{16,24},{24,16},{32,40},{40,32},{48,56},{56,48},{1,9},... | collective-permute-start | bytes 98312 | tf_op jit(solution)/shard_map/ppermute | solution.py:189
  97.7 3.8 %collective-permute-start.12 = (bf16[16,512]{1,0:T(8,128)(2,1)S(1)}, bf16[16,512]{1,0:T(8,128)(2,1)S(1)}, u32[]{:S(2)}, u32[]{:S(2)}) collective-permute-start(bf16[16,512]{1,0:T(8,128)(2,1)S(1)} %get-tuple-element.54), channel_id=1, source_target_pairs={{0,16},{8,24},{16,0},{24,8},{32,48},{40,56},{48,32},{56,40},{1,17}... | collective-permute-start | bytes 49160 | tf_op jit(solution)/shard_map/ppermute | solution.py:189
  101.5 6.5 %collective-permute-start.13 = (bf16[16,256]{1,0:T(8,128)(2,1)S(1)}, bf16[16,256]{1,0:T(8,128)(2,1)S(1)}, u32[]{:S(2)}, u32[]{:S(2)}) collective-permute-start(bf16[16,256]{1,0:T(8,128)(2,1)S(1)} %get-tuple-element.56), channel_id=1, source_target_pairs={{0,32},{8,40},{16,48},{24,56},{32,0},{40,8},{48,16},{56,24},{1,33}... | collective-permute-start | bytes 24584 | tf_op jit(solution)/shard_map/ppermute | solution.py:189
  126.0 9.6 %copy-start.4 = (bf16[4,8,16,256]{3,2,1,0:T(8,128)(2,1)}, bf16[4,8,16,256]{3,2,1,0:T(8,128)(2,1)S(1)}, u32[]{:S(2)}) copy-start(bf16[4,8,16,256]{3,2,1,0:T(8,128)(2,1)S(1)} %all_to_all.23) | copy-start | bytes 786436
  126.0 9.6 %collective-permute-start.14 = (bf16[32,16,256]{2,1,0:T(8,128)(2,1)S(1)}, bf16[32,16,256]{2,1,0:T(8,128)(2,1)S(1)}, u32[]{:S(2)}, u32[]{:S(2)}) collective-permute-start(bf16[32,16,256]{2,1,0:T(8,128)(2,1)S(1)} %bitcast.8), channel_id=1, source_target_pairs={{0,4},{4,0},{1,5},{5,1},{2,6},{6,2},{3,7},{7,3},{8,12},{12,8},{9,1... | collective-permute-start | bytes 786440 | tf_op jit(solution)/shard_map/ppermute | solution.py:184
  135.6 0.7 copy-start.7
  144.8 23.6 %copy-start.5 = (f32[8,128,256]{2,1,0:T(8,128)S(1)}, f32[8,128,256]{2,1,0:T(8,128)}, u32[]{:S(2)}) copy-start(f32[8,128,256]{2,1,0:T(8,128)} %get-tuple-element.61) | copy-start | bytes 3145732
  144.8 9.0 %collective-permute-start.16 = (bf16[4,128,256]{2,1,0:T(8,128)(2,1)}, bf16[4,128,256]{2,1,0:T(8,128)(2,1)S(1)}, u32[]{:S(2)}, u32[]{:S(2)}) collective-permute-start(bf16[4,128,256]{2,1,0:T(8,128)(2,1)} %get-tuple-element.64), channel_id=1, source_target_pairs={{0,1},{1,2},{2,3},{3,0},{4,5},{5,6},{6,7},{7,4},{8,9},{9,10},{10,1... | collective-permute-start | bytes 786440 | tf_op jit(solution)/shard_map/ppermute | solution.py:399
  145.7 9.3 %collective-permute-start.19 = (bf16[4,128,256]{2,1,0:T(8,128)(2,1)}, bf16[4,128,256]{2,1,0:T(8,128)(2,1)S(1)}, u32[]{:S(2)}, u32[]{:S(2)}) collective-permute-start(bf16[4,128,256]{2,1,0:T(8,128)(2,1)} %get-tuple-element.67), channel_id=1, source_target_pairs={{0,3},{1,0},{2,1},{3,2},{4,7},{5,4},{6,5},{7,6},{8,11},{9,8},{10,9... | collective-permute-start | bytes 786440 | tf_op jit(solution)/shard_map/ppermute | solution.py:403
  147.6 11.2 %collective-permute-start.15 = (bf16[4,128,256]{2,1,0:T(8,128)(2,1)}, bf16[4,128,256]{2,1,0:T(8,128)(2,1)S(1)}, u32[]{:S(2)}, u32[]{:S(2)}) collective-permute-start(bf16[4,128,256]{2,1,0:T(8,128)(2,1)} %get-tuple-element.62), channel_id=1, source_target_pairs={{0,3},{1,0},{2,1},{3,2},{4,7},{5,4},{6,5},{7,6},{8,11},{9,8},{10,9... | collective-permute-start | bytes 786440 | tf_op jit(solution)/shard_map/ppermute | solution.py:403
  154.8 7.9 %collective-permute-start.17 = (bf16[4,128,256]{2,1,0:T(8,128)(2,1)S(1)}, bf16[4,128,256]{2,1,0:T(8,128)(2,1)S(1)}, u32[]{:S(2)}, u32[]{:S(2)}) collective-permute-start(bf16[4,128,256]{2,1,0:T(8,128)(2,1)S(1)} %add_convert_fusion.1), channel_id=1, source_target_pairs={{0,1},{1,2},{2,3},{3,0},{4,5},{5,6},{6,7},{7,4},{8,9},{9,10},{10,1... | collective-permute-start | bytes 786440 | tf_op jit(solution)/shard_map/ppermute | solution.py:399
  154.9 13.4 %collective-permute-start.18 = (bf16[4,128,256]{2,1,0:T(8,128)(2,1)}, bf16[4,128,256]{2,1,0:T(8,128)(2,1)S(1)}, u32[]{:S(2)}, u32[]{:S(2)}) collective-permute-start(bf16[4,128,256]{2,1,0:T(8,128)(2,1)} %get-tuple-element.65), channel_id=1, source_target_pairs={{0,1},{1,2},{2,3},{3,0},{4,5},{5,6},{6,7},{7,4},{8,9},{9,10},{10,1... | collective-permute-start | bytes 786440 | tf_op jit(solution)/shard_map/ppermute | solution.py:399
  156.1 12.3 %collective-permute-start.20 = (bf16[4,128,256]{2,1,0:T(8,128)(2,1)S(1)}, bf16[4,128,256]{2,1,0:T(8,128)(2,1)S(1)}, u32[]{:S(2)}, u32[]{:S(2)}) collective-permute-start(bf16[4,128,256]{2,1,0:T(8,128)(2,1)S(1)} %add_convert_fusion), channel_id=1, source_target_pairs={{0,3},{1,0},{2,1},{3,2},{4,7},{5,4},{6,5},{7,6},{8,11},{9,8},{10,9... | collective-permute-start | bytes 786440 | tf_op jit(solution)/shard_map/ppermute | solution.py:403

commit v2 on v0

v2 whole, which is shorter than its diff:
```python
import functools

import jax
import jax.numpy as jnp
from jax import lax
from jax.experimental import pallas as pl
from jax.experimental.pallas import tpu as pltpu
from jax.sharding import PartitionSpec as P

F32 = jnp.float32
BF16 = jnp.bfloat16
EB = 512
NT = (((1,), (1,)), ((), ()))
TN = (((0,), (0,)), ((), ()))


def vmem():
    return pl.BlockSpec(memory_space=pltpu.VMEM)


def smem():
    return pl.BlockSpec(memory_space=pltpu.SMEM)


def params(mib):
    return pltpu.CompilerParams(vmem_limit_bytes=mib * 2**20)


def cost(flops, moved):
    return pl.CostEstimate(flops=flops, bytes_accessed=moved, transcendentals=0)


def pinned(arr):
    return pltpu.with_memory_space_constraint(arr, pltpu.HBM)


def hbm():
    return pl.BlockSpec(memory_space=pltpu.HBM)


def cast_kernel(in_ref, a_ref, b_ref, held, sems):
    half = a_ref.shape[0]
    outs = (a_ref, b_ref)
    copies = fetch(sems, [(in_ref.at[pl.ds(i * half, half)], held.at[i]) for i in range(2)])
    for i in range(2):
        copies[i].wait()
        outs[i][...] = held[i].astype(BF16)


def cast_halves(emb_rows):
    tabs, rows, emb = emb_rows.shape
    half = (tabs // 2, rows, emb)
    return pl.pallas_call(
        cast_kernel,
        in_specs=[hbm()],
        out_specs=[vmem()] * 2,
        out_shape=[jax.ShapeDtypeStruct(half, BF16)] * 2,
        scratch_shapes=[pltpu.VMEM((2,) + half, F32), pltpu.SemaphoreType.DMA((2,))],
        compiler_params=params(16),
        cost_estimate=cost(1 << 18, 3 << 19),
        name="cast",
    )(pinned(emb_rows))


def counts_kernel(mine_ref, ids_ref, own_ref, *refs, first_table):
    step = pl.program_id(0)
    t = step + first_table
    if first_table:
        edges_ref, out_ref, turned_ref, acc_ref, ids, own, sems = refs
    else:
        out_ref, turned_ref, edges_ref, acc_ref, ids, own, sems = refs
    samp, rows = acc_ref.shape
    tabs, entries = own.shape
    mine = mine_ref[0]
    low = mine * samp
    turn = mine * (rows // 4)

    @pl.when(step == 0)
    def _():
        copies = fetch(sems, [(own_ref, own), (ids_ref, ids)])
        copies[0].wait()
        if not first_table:
            owners = own[...]
            first = jnp.sum((owners < low).astype(jnp.int32), axis=1, keepdims=True)
            last = jnp.sum((owners < low + samp).astype(jnp.int32), axis=1, keepdims=True)
            for i in range(tabs):
                edges_ref[i] = first[i, 0]
                edges_ref[tabs + i] = last[i, 0]
        copies[1].wait()

    start = edges_ref[t] // 128
    steps = (edges_ref[tabs + t] - start * 128 + EB - 1) // EB
    start = jnp.minimum(start, (entries - steps * EB) // 128)
    acc_ref[...] = jnp.zeros_like(acc_ref)
    grid = lax.broadcasted_iota(jnp.int32, (samp, EB), 0).astype(F32).astype(BF16)
    one, zero = jnp.ones((), BF16), jnp.zeros((), BF16)

    def body(block, carry):
        at = pl.ds(pl.multiple_of(start * 128 + block * EB, 128), EB)
        who = own[pl.ds(t, 1), at] - low
        row = (ids[pl.ds(t, 1), at] - turn) & (rows - 1)
        hot = [
            jnp.where(grid == values.astype(F32).astype(BF16), one, zero) for values in (who, row, row - samp)
        ]
        acc_ref[...] += lax.dot_general(
            hot[0], jnp.concatenate(hot[1:], axis=0), NT, preferred_element_type=F32
        )
        return carry

    lax.fori_loop(0, steps, body, 0)
    total = acc_ref[...].astype(BF16)
    out_ref[0] = total
    turned_ref[0] = total.T


def make_counts(mine, ids, owners, samp, rows, side, edges=None):
    tabs, entries = ids.shape
    assert rows == 2 * samp and samp <= 256
    half = tabs // 2
    first = edges is None
    out_specs = [
        pl.BlockSpec((1, samp, rows), lambda t: (t, 0, 0)),
        pl.BlockSpec((1, rows, samp), lambda t: (t, 0, 0)),
    ]
    out_shape = [pltpu.HBM((half, samp, rows), BF16), pltpu.HBM((half, rows, samp), BF16)]
    if first:
        out_specs.append(smem())
        out_shape.append(jax.ShapeDtypeStruct((2 * tabs,), jnp.int32))
    return pl.pallas_call(
        functools.partial(counts_kernel, first_table=half * side),
        grid=(half,),
        in_specs=[smem(), hbm(), hbm()] + ([] if first else [smem()]),
        out_specs=out_specs,
        out_shape=out_shape,
        scratch_shapes=[
            pltpu.VMEM((samp, rows), F32),
            pltpu.VMEM((tabs, entries), jnp.int32),
            pltpu.VMEM((tabs, entries), jnp.int32),
            pltpu.SemaphoreType.DMA((2,)),
        ],
        compiler_params=params(16),
        cost_estimate=cost(half * samp * rows * 3072, 3 << 20),
        name="counts",
    )(mine, pinned(ids), pinned(owners), *([] if first else [edges]))


WIDE = 512


def fetch(sems, pairs):
    copies = [pltpu.make_async_copy(src, dst, sems.at[i]) for i, (src, dst) in enumerate(pairs)]
    for copy in copies:
        copy.start()
    return copies


def features(f):
    return pl.ds(f * WIDE, WIDE)


def emit(core_ref, z, g, keep_ref, send_ref):
    even = core_ref[0] == 0
    keep_ref[...] = jnp.where(even, z, g)
    send_ref[...] = jnp.where(even, g, z).astype(BF16)


def anyspace():
    return pl.BlockSpec(memory_space=pl.ANY)


def first_kernel(core_ref, counts_a, counts_b, *refs):
    embs, refs = refs[:8], refs[8:]
    (cot_ref, v_ref, u_ref, pooled_ref, keep_ref, send_ref, counts, cot, v, u, sems) = refs
    steps = counts.shape[0]
    pairs = []
    for f in range(steps):
        pairs += [
            ((counts_a, counts_b)[2 * f // steps].at[pl.ds(2 * f % steps, 2)], counts.at[f]),
            (cot_ref.at[:, features(f)], cot.at[f]),
            (v_ref.at[0, features(f), :], v.at[f]),
            (u_ref.at[1, :, features(f)], u.at[f]),
        ]
    copies = fetch(sems, pairs)
    z = g = None
    for f in range(steps):
        for copy in copies[4 * f : 4 * f + 4]:
            copy.wait()
        parts = []
        for i in range(2):
            half, at = divmod(2 * f + i, steps)
            rows = jnp.concatenate([embs[2 * k + half][at] for k in range(4)], axis=0)
            parts.append(jnp.dot(counts[f, i], rows, preferred_element_type=F32).astype(BF16))
        pooled = jnp.concatenate(parts, axis=1)
        pooled_ref[:, f * WIDE : (f + 1) * WIDE] = pooled
        wide = (cot[f].astype(F32) * pooled.astype(F32)).astype(BF16)
        more_z = jnp.dot(pooled, v[f], preferred_element_type=F32)
        more_g = lax.dot_general(wide, u[f], NT, preferred_element_type=F32)
        z, g = (more_z, more_g) if f == 0 else (z + more_z, g + more_g)
    emit(core_ref, z, g, keep_ref, send_ref)


def first_sums(core, counts, embs, cot, v, u):
    half, samp, rows = counts[0].shape
    tabs = 2 * half
    emb = embs[0].shape[-1]
    rank = v.shape[-1]
    steps = tabs * emb // WIDE
    assert 2 * emb == WIDE and steps == tabs // 2
    return pl.pallas_call(
        first_kernel,
        in_specs=[smem(), hbm(), hbm()] + [vmem()] * 8 + [hbm()] * 3,
        out_specs=[vmem()] * 3,
        out_shape=[
            jax.ShapeDtypeStruct((samp, tabs * emb), BF16),
            jax.ShapeDtypeStruct((samp, rank), F32),
            jax.ShapeDtypeStruct((samp, rank), BF16),
        ],
        scratch_shapes=[
            pltpu.VMEM((steps, 2, samp, rows), BF16),
            pltpu.VMEM((steps, samp, WIDE), BF16),
            pltpu.VMEM((steps, WIDE, rank), BF16),
            pltpu.VMEM((steps, rank, WIDE), BF16),
            pltpu.SemaphoreType.DMA((4 * steps,)),
        ],
        compiler_params=params(24),
        cost_estimate=cost(3 << 29, 10 << 20),
        name="first_sums",
    )(core, *map(pinned, counts), *embs, pinned(cot), pinned(v), pinned(u))


def to_core(arr):
    return lax.ppermute(arr, "c", [(0, 1), (1, 0)])


def small(kernel, out_shape, name, *args):
    return pl.pallas_call(
        kernel,
        in_specs=[vmem()] * len(args),
        out_specs=vmem(),
        out_shape=out_shape,
        compiler_params=params(8),
        cost_estimate=cost(1 << 20, 1 << 20),
        name=name,
    )(*args)


def chunk_at(i):
    return 16 * (i // 2), 256 * (i % 2)


def cut_kernel(keep_ref, got_ref, out_ref):
    for i in range(out_ref.shape[0]):
        r, c = chunk_at(i)
        at = (slice(r, r + 16), slice(c, c + 256))
        out_ref[i] = (keep_ref[at] + got_ref[at].astype(F32)).astype(BF16)


def total_kernel(in_ref, out_ref):
    total = in_ref[0].astype(F32)
    for i in range(1, in_ref.shape[0]):
        total = total + in_ref[i].astype(F32)
    total = total.astype(BF16)
    for i in range(out_ref.shape[0]):
        out_ref[i] = total


def exchange(chunks, copies):
    parts = lax.all_to_all(chunks, ("x", "z"), 0, 0, tiled=True)
    return small(total_kernel, jax.ShapeDtypeStruct((copies, 16, 256), BF16), "total", parts)


def sum_by_gather(keep, send):
    chunks = small(cut_kernel, jax.ShapeDtypeStruct((32, 16, 256), BF16), "cut", keep, to_core(send))
    mine = lax.all_gather(exchange(chunks, 1), ("x", "z"), axis=0, tiled=True)
    return mine, to_core(mine)


def sum_by_psum(keep, send):
    chunks = small(cut_kernel, jax.ShapeDtypeStruct((32, 16, 256), BF16), "cut", keep, to_core(send))
    mine = lax.psum(chunks, ("x", "z"))
    return mine, to_core(mine)


def spread(core_ref, mine_ref, other_ref, in_ref):
    core = core_ref[0]
    for side, ref in ((core, mine_ref), (1 - core, other_ref)):
        for i in range(32):
            r, c = chunk_at(i)
            in_ref[side, r : r + 16, c : c + 256] = ref[i]


def middle_kernel(core_ref, mine_ref, other_ref, b_ref, pooled_ref, cot_ref, u_ref, v_ref, *refs):
    x1_ref, a_ref, keep_ref, send_ref, sums, pooled, cot, u, v, sems = refs
    steps = u.shape[0]
    pairs = []
    for f in range(steps):
        pairs += [
            (u_ref.at[0, :, features(f)], u.at[f]),
            (v_ref.at[1, features(f), :], v.at[f]),
            (pooled_ref.at[:, features(f)], pooled.at[f]),
            (cot_ref.at[:, features(f)], cot.at[f]),
        ]
    copies = fetch(sems, pairs)
    spread(core_ref, mine_ref, other_ref, sums)
    z = g = None
    for f in range(steps):
        for copy in copies[4 * f : 4 * f + 4]:
            copy.wait()
        at = slice(f * WIDE, (f + 1) * WIDE)
        base = pooled[f].astype(F32)
        h0 = jnp.dot(sums[0], u[f], preferred_element_type=F32) + b_ref[0:1, at]
        x1 = (base * h0 + base).astype(BF16)
        x1_ref[:, at] = x1
        g1 = cot[f].astype(F32) + lax.dot_general(sums[1], v[f], NT, preferred_element_type=F32)
        a_ref[:, at] = (g1 * h0 + g1).astype(BF16)
        wide = (g1 * base).astype(BF16)
        more_z = jnp.dot(x1, v[f], preferred_element_type=F32)
        more_g = lax.dot_general(wide, u[f], NT, preferred_element_type=F32)
        z, g = (more_z, more_g) if f == 0 else (z + more_z, g + more_g)
    emit(core_ref, z, g, keep_ref, send_ref)


def middle(core, mine, other, bias, pooled, cot, u, v):
    samp, feats = pooled.shape
    rank = v.shape[-1]
    steps = feats // WIDE
    feat = jax.ShapeDtypeStruct((samp, feats), BF16)
    return pl.pallas_call(
        middle_kernel,
        in_specs=[smem()] + [vmem()] * 3 + [anyspace()] + [hbm()] * 3,
        out_specs=[vmem()] * 4,
        out_shape=[feat, feat, jax.ShapeDtypeStruct((samp, rank), F32), jax.ShapeDtypeStruct((samp, rank), BF16)],
        scratch_shapes=[
            pltpu.VMEM((2, samp, rank), BF16),
            pltpu.VMEM((steps, samp, WIDE), BF16),
            pltpu.VMEM((steps, samp, WIDE), BF16),
            pltpu.VMEM((steps, rank, WIDE), BF16),
            pltpu.VMEM((steps, WIDE, rank), BF16),
            pltpu.SemaphoreType.DMA((4 * steps,)),
        ],
        compiler_params=params(24),
        cost_estimate=cost(1 << 31, 8 << 20),
        name="middle",
    )(core, mine, other, bias, pooled, pinned(cot), pinned(u), pinned(v))


def last_kernel(core_ref, mine_ref, other_ref, b_ref, turned_ref, pooled_ref, cot_ref, x1_ref, a_ref, u_ref, v_ref, *refs, side):
    crossed_ref, p0, p1, p2, p3, sums, turned, pooled, cot, x1, a, u, v, crossed, sems = refs[-15:]
    steps = u.shape[0]
    pairs = []
    for f in range(steps):
        from_f = features(side * steps + f)
        pairs += [
            (u_ref.at[1, :, from_f], u.at[f]),
            (v_ref.at[0, from_f, :], v.at[f]),
            (pooled_ref.at[:, from_f], pooled.at[f]),
            (cot_ref.at[:, from_f], cot.at[f]),
            (x1_ref.at[:, from_f], x1.at[f]),
            (a_ref.at[:, from_f], a.at[f]),
            (turned_ref.at[pl.ds(2 * f, 2)], turned.at[f]),
        ]
    n = len(pairs) // steps
    copies = fetch(sems, pairs)
    spread(core_ref, mine_ref, other_ref, sums)
    outs = []
    rows, emb = p0.shape[1:]
    for f in range(steps):
        for copy in copies[n * f : n * f + n]:
            copy.wait()
        at = slice((side * steps + f) * WIDE, (side * steps + f + 1) * WIDE)
        h1 = jnp.dot(sums[0], u[f], preferred_element_type=F32) + b_ref[1:2, at]
        crossed[f] = (pooled[f].astype(F32) * h1 + x1[f].astype(F32)).astype(BF16)
        out = pltpu.make_async_copy(
            crossed.at[f], crossed_ref.at[:, features(side * steps + f)], sems.at[n * steps + f]
        )
        out.start()
        outs.append(out)
        grad = cot[f].astype(F32) * h1 + a[f].astype(F32)
        grad = (grad + lax.dot_general(sums[1], v[f], NT, preferred_element_type=F32)).astype(BF16)
        for i in range(2):
            part = jnp.dot(turned[f, i], grad[:, i * emb : (i + 1) * emb], preferred_element_type=F32)
            p0[2 * f + i] = part[:rows]
            for k, ref in enumerate((p1, p2, p3)):
                ref[2 * f + i] = part[(k + 1) * rows : (k + 2) * rows].astype(BF16)
    for out in outs:
        out.wait()


def last(side, before, core, mine, other, bias, turned, pooled, cot, x1, a, u, v):
    half, rows, samp = turned.shape
    rank = v.shape[-1]
    emb = pooled.shape[1] // (2 * half)
    steps = pooled.shape[1] // WIDE // 2
    block = (half, rows // 4, emb)
    feat = pltpu.VMEM((steps, samp, WIDE), BF16)
    args = (core, mine, other, bias, pinned(turned), pooled, pinned(cot), x1, a, pinned(u), pinned(v), *before)
    return pl.pallas_call(
        functools.partial(last_kernel, side=side),
        in_specs=[smem()] + [vmem()] * 3 + [hbm(), anyspace(), hbm(), anyspace(), anyspace(), hbm(), hbm()] + [anyspace()] * len(before),
        out_specs=[anyspace()] + [vmem()] * 4,
        out_shape=[jax.ShapeDtypeStruct(pooled.shape, BF16), jax.ShapeDtypeStruct(block, F32)]
        + [jax.ShapeDtypeStruct(block, BF16)] * 3,
        scratch_shapes=[
            pltpu.VMEM((2, samp, rank), BF16),
            pltpu.VMEM((steps, 2, rows, samp), BF16),
            feat,
            feat,
            feat,
            feat,
            pltpu.VMEM((steps, rank, WIDE), BF16),
            pltpu.VMEM((steps, WIDE, rank), BF16),
            feat,
            pltpu.SemaphoreType.DMA((8 * steps,)),
        ],
        input_output_aliases={11: 0} if before else {},
        compiler_params=params(24),
        cost_estimate=cost(3 << 28, 7 << 20),
        name="last",
    )(*args)


def right(arr):
    return lax.ppermute(arr, "row", [(i, (i + 1) & 3) for i in range(4)])


def left(arr):
    return lax.ppermute(arr, "row", [(i, (i + 3) & 3) for i in range(4)])


def add(a, b):
    return a.astype(F32) + b.astype(F32)


def scalar(axis):
    return lax.axis_index(axis).astype(jnp.int32).reshape(1)


def local(emb_rows, entry_ids, entry_sample, cross_v, cross_u, cross_bias, cotangent):
    samp = cotangent.shape[0]
    rows = emb_rows.shape[1] * lax.axis_size("row")
    mine, core = scalar("row"), scalar("c")
    own_a, own_b = cast_halves(emb_rows)
    left_a, right_b = right(own_a), left(own_b)
    left_b, right_a = right(own_b), left(own_a)
    counts_a, turned_a, edges = make_counts(mine, entry_ids, entry_sample, samp, rows, 0)
    left_a, right_b, edges = lax.optimization_barrier((left_a, right_b, edges))
    far_a, far_b = right(left_a), left(right_b)
    counts_b, turned_b = make_counts(mine, entry_ids, entry_sample, samp, rows, 1, edges)
    embs = (own_a, own_b, right_a, right_b, far_a, far_b, left_a, left_b)
    pooled, keep, send = first_sums(core, (counts_a, counts_b), embs, cotangent, cross_v, cross_u)
    sums = sum_by_gather(keep, send)
    x1, a, keep, send = middle(core, *sums, cross_bias, pooled, cotangent, cross_u, cross_v)
    sums = sum_by_psum(keep, send)
    front = (core, *sums, cross_bias)
    rest = (pooled, cotangent, x1, a, cross_u, cross_v)
    crossed, p0a, p1a, p2a, p3a = last(0, (), *front, turned_a, *rest)
    from_left, sum_a = lax.optimization_barrier((right(p2a), left(p3a)))
    crossed, p0b, p1b, p2b, p3b = last(1, (crossed,), *front, turned_b, *rest)
    from_right, sum_b = lax.optimization_barrier((left(p2b), right(p1b)))
    far_a = right(add(p1a, from_left).astype(BF16))
    far_b = left(add(p3b, from_right).astype(BF16))
    grads = jnp.concatenate([p0a + add(sum_a, far_a), p0b + add(sum_b, far_b)], axis=0)
    return crossed, grads


def solution(mesh):
    fine = jax.sharding.Mesh(mesh.devices.reshape(4, 8, 2, 4), ("x", "z", "c", "row"))
    table = ("x", "z", "c")
    placed = (
        P(table, "row", None),
        P(table, None),
        P(table, None),
        P(None, table, None),
        P(None, None, table),
        P(None, table),
        P("row", table),
    )
    return jax.shard_map(
        local,
        mesh=fine,
        in_specs=placed,
        out_specs=(P("row", table), P(table, "row", None)),
        check_vma=False,
    )
```

time: 726 us -> 294 us (0.40)
  blocking collectives: 511 us -> 56.1 us
  matrix products: 81.4 us -> 0 us
  waiting for transfers between devices: 101 us -> 151 us
  starting transfers between devices: 0.08 us -> 39.6 us
  Pallas kernels: 0 us -> 29.3 us
  local copies, waits for them, and re-layouts: 16.6 us -> 0.96 us
    psum x2 -> x0, blocking collectives: 511 us -> none  [widen(): narrow = lax.psum(part, 'table').astype(jnp.bfloat16)]
    psum x0 -> x1, waiting for transfers between devices: none -> 136 us  [sum_by_psum(): mine = lax.psum(chunks, ('x', 'z'))]
    dot_general x18 -> x0, matrix products: 81.4 us -> none  [the longest x8 51.7 us: step(): jnp.einsum('tes,ter->tsr', sample_hot, row_hot, preferred_element_type=jn...]
    reduce_scatter x1 -> x0, waiting for transfers between devices: 52.7 us -> none  [local(): lax.psum_scatter(term.reshape(samp_dev * lax.axis_size('row'), feat_dev)....]
    all_gather x1 -> x0, waiting for transfers between devices: 48.1 us -> none  [local(): piece = lax.all_gather(grad_pooled, 'row', axis=0, tiled=True)]
    ppermute x0 -> x16, starting transfers between devices: none -> 39.5 us  [the longest x4 24.4 us: to_core(): return lax.ppermute(arr, 'c', [(0, 1), (1, 0)])]
    all_gather x0 -> x1, blocking collectives: none -> 37.3 us  [sum_by_gather(): mine = lax.all_gather(exchange(chunks, 1), ('x', 'z'), axis=0, tiled=True)]
    pallas_call x0 -> x10, Pallas kernels: none -> 29.3 us  [the longest x2 12.1 us: make_counts(): pl.pallas_call(functools.partial(counts_kernel, first_table=half * side),...]
  transfers between devices with their start and end apart: 2 -> 17, of which waited for: 2 -> 10; matrix products, arithmetic and copies ran while one was open for 0% -> 0% of each run, Pallas kernels for 0% -> 5%
where the time goes in v2:
time: 294 us; the launch traced here: 292 us
  waiting for transfers between devices  151 us (51%)
  blocking collectives  56.1 us (19%)
  starting transfers between devices  39.6 us (13%)
  Pallas kernels  29.3 us (10%)
  between operations  14.2 us (5%)
    psum x1, waiting for transfers between devices, sum_by_psum(): mine = lax.psum(chunks, ('x', 'z'))  136 us
    all_gather x1, blocking collectives, sum_by_gather(): mine = lax.all_gather(exchange(chunks, 1), ('x', 'z'), axis=0, tiled=True)  37.3 us
    ppermute x4, starting transfers between devices, to_core(): return lax.ppermute(arr, 'c', [(0, 1), (1, 0)])  24.4 us
    all_to_all x1, blocking collectives, exchange(): parts = lax.all_to_all(chunks, ('x', 'z'), 0, 0, tiled=True)  18.8 us
    pallas_call x2, Pallas kernels, make_counts(): pl.pallas_call(functools.partial(counts_kernel, first_table=half * side),...  12.1 us
    ppermute x6, starting transfers between devices, left(): return lax.ppermute(arr, 'row', [(i, i + 3 & 3) for i in range(4)])  9.92 us
    pallas_call x2, Pallas kernels, last(): pl.pallas_call(functools.partial(last_kernel, side=side), in_specs=[smem(...  6.71 us
  transfers between devices with their start and end apart: 17, of which 10 were waited for; matrix products, arithmetic and copies ran while one was open for 0% of the time, Pallas kernels for 5%

profile of v2, /device:TPU:1, one launch (start us, length us, event | category | flops | bytes accessed | tf_op | source)
XLA Modules:
  0.0 292.1 jit_solution(15388285634857978613)
XLA Ops:
  7.2 1.2 cast.1
  8.5 2.2 collective-permute-start
  10.7 1.5 collective-permute-start.1
  12.2 1.4 collective-permute-start.2
  13.7 6.0 %counts.2 = (bf16[4,256,512]{2,1,0:T(8,128)(2,1)}, bf16[4,512,256]{2,1,0:T(8,128)(2,1)}, s32[16]{0:T(128)S(1)}) custom-call(s32[1]{0:T(128)} %bitcast.1.mine_ref, s32[8,4096]{1,0:T(8,128)} %ids_ref.3, s32[8,4096]{1,0:T(8,128)} %own_ref.3), custom_call_target="tpu_custom_call" | custom-call | flops 1610612736 | bytes 3145728 | tf_op jit(solution)/shard_map/counts/pallas_call | solution.py:129
  20.1 2.3 collective-permute-start.4
  22.4 6.1 %counts.3 = (bf16[4,256,512]{2,1,0:T(8,128)(2,1)}, bf16[4,512,256]{2,1,0:T(8,128)(2,1)}) custom-call(s32[1]{0:T(128)} %bitcast.1.mine_ref, s32[8,4096]{1,0:T(8,128)} %ids_ref.3, s32[8,4096]{1,0:T(8,128)} %own_ref.3, s32[16]{0:T(128)S(1)} %get-tuple-element.37.refs_0_), custom_call_target="tpu_custom_call" | custom-call | flops 1610612736 | bytes 3145728 | tf_op jit(solution)/shard_map/counts/pallas_call | solution.py:129
  28.6 4.2 %first_sums.1 = (bf16[256,2048]{1,0:T(8,128)(2,1)S(1)}, f32[256,512]{1,0:T(8,128)S(1)}, bf16[256,512]{1,0:T(8,128)(2,1)S(1)}) custom-call(s32[1]{0:T(128)} %bitcast.core_ref, bf16[4,256,512]{2,1,0:T(8,128)(2,1)} %get-tuple-element.33.counts_a, bf16[4,256,512]{2,1,0:T(8,128)(2,1)} %get-tuple-element.38.counts_b, ...), custom_call_target="tpu_custom_call" | custom-call | flops 1610612736 | bytes 10485760 | tf_op jit(solution)/shard_map/first_sums/pallas_call | solution.py:209
  32.7 4.7 %collective-permute-start.6 = (bf16[256,512]{1,0:T(8,128)(2,1)S(1)}, bf16[256,512]{1,0:T(8,128)(2,1)S(1)}, u32[]{:S(2)}, u32[]{:S(2)}) collective-permute-start(bf16[256,512]{1,0:T(8,128)(2,1)S(1)} %get-tuple-element.42), channel_id=1, source_target_pairs={{0,4},{4,0},{1,5},{5,1},{2,6},{6,2},{3,7},{7,3},{8,12},{12,8},{9,1... | collective-permute-start | bytes 786440 | tf_op jit(solution)/shard_map/ppermute | solution.py:232
  37.5 1.2 collective-permute-done.6.got_ref
  38.7 18.8 %all_to_all.5.in_ref = bf16[32,16,256]{2,1,0:T(8,128)(2,1)S(1)} all-to-all(bf16[32,16,256]{2,1,0:T(8,128)(2,1)S(1)} %cut.2), channel_id=1, replica_groups=mesh['x'=4,'z'=8,'c'=2,'row'=4] {'x','z'}, dimensions={0} | all-to-all | bytes 524288 | tf_op jit(solution)/shard_map/all_to_all | solution.py:268
  57.6 37.3 %all_gather.3.mine_ref = bf16[32,16,256]{2,1,0:T(8,128)(2,1)S(1)} all-gather(bf16[1,16,256]{2,1,0:T(8,128)(2,1)S(1)} %total.1), channel_id=1, replica_groups=mesh['x'=4,'z'=8,'c'=2,'row'=4] {'x','z'}, dimensions={0}, use_global_device_ids=true | all-gather | bytes 270336 | tf_op jit(solution)/shard_map/all_gather | solution.py:274
  94.8 14.1 %collective-permute-start.7 = (bf16[32,16,256]{2,1,0:T(8,128)(2,1)S(1)}, bf16[32,16,256]{2,1,0:T(8,128)(2,1)S(1)}, u32[]{:S(2)}, u32[]{:S(2)}) collective-permute-start(bf16[32,16,256]{2,1,0:T(8,128)(2,1)S(1)} %all_gather.3.mine_ref), channel_id=1, source_target_pairs={{0,4},{4,0},{1,5},{5,1},{2,6},{6,2},{3,7},{7,3},{8,12},{12,8},{9,1... | collective-permute-start | bytes 786440 | tf_op jit(solution)/shard_map/ppermute | solution.py:232
  109.0 1.2 collective-permute-done.7.other_ref
  110.1 4.3 %middle.1 = (bf16[256,2048]{1,0:T(8,128)(2,1)S(1)}, bf16[256,2048]{1,0:T(8,128)(2,1)S(1)}, f32[256,512]{1,0:T(8,128)S(1)}, bf16[256,512]{1,0:T(8,128)(2,1)S(1)}) custom-call(s32[1]{0:T(128)} %bitcast.core_ref, bf16[32,16,256]{2,1,0:T(8,128)(2,1)S(1)} %all_gather.3.mine_ref, bf16[32,16,256]{2,1,0:T(8,128)(2,1)S(1)} %collective-permute-done.7.other_ref, ...), custom_call_target="tpu_custom_call" | custom-call | flops 2147483648 | bytes 8388608 | tf_op jit(solution)/shard_map/middle/pallas_call | solution.py:328
  114.9 1.2 collective-permute-done.8.got_ref
  116.8 135.5 %all-reduce.2.cloned.1.call-done.mine_ref = bf16[32,16,256]{2,1,0:T(8,128)(2,1)} async-done(((bf16[32,16,256]{2,1,0:T(8,128)(2,1)}), bf16[32,16,256]{2,1,0:T(8,128)(2,1)}) %all-reduce.2.cloned.1.call-update) | async-done | bytes 262160 | tf_op jit(solution)/shard_map/psum | solution.py:280
  252.3 5.1 %collective-permute-start.9 = (bf16[32,16,256]{2,1,0:T(8,128)(2,1)}, bf16[32,16,256]{2,1,0:T(8,128)(2,1)S(1)}, u32[]{:S(2)}, u32[]{:S(2)}) collective-permute-start(bf16[32,16,256]{2,1,0:T(8,128)(2,1)} %all-reduce.2.cloned.1.call-done.mine_ref), channel_id=1, source_target_pairs={{0,4},{4,0},{1,5},{5,1},{2,6},{6,2},{3,7},{7,3},{8,12},{12,8},{9,1... | collective-permute-start | bytes 786440 | tf_op jit(solution)/shard_map/ppermute | solution.py:232
  257.4 1.4 collective-permute-done.9.other_ref
  258.8 0.9 copy-done
  259.8 3.4 %last.2 = (bf16[256,2048]{1,0:T(8,128)(2,1)}, f32[4,128,256]{2,1,0:T(8,128)S(1)}, bf16[4,128,256]{2,1,0:T(8,128)(2,1)S(1)}, bf16[4,128,256]{2,1,0:T(8,128)(2,1)S(1)}, bf16[4,128,256]{2,1,0:T(8,128)(2,1)S(1)}) custom-call(s32[1]{0:T(128)} %bitcast.core_ref, bf16[32,16,256]{2,1,0:T(8,128)(2,1)S(1)} %copy-done, ...), custom_call_target="tpu_custom_call" | custom-call | flops 805306368 | bytes 7340032 | tf_op jit(solution)/shard_map/last/pallas_call | solution.py:397
  263.1 1.3 collective-permute-start.10
  264.4 1.5 collective-permute-start.11
  265.9 3.4 %last.3 = (bf16[256,2048]{1,0:T(8,128)(2,1)}, f32[4,128,256]{2,1,0:T(8,128)S(1)}, bf16[4,128,256]{2,1,0:T(8,128)(2,1)S(1)}, bf16[4,128,256]{2,1,0:T(8,128)(2,1)S(1)}, bf16[4,128,256]{2,1,0:T(8,128)(2,1)S(1)}) custom-call(s32[1]{0:T(128)} %bitcast.core_ref, bf16[32,16,256]{2,1,0:T(8,128)(2,1)S(1)} %copy-done, ...), custom_call_target="tpu_custom_call", output_to_operand_aliasing={{0}: (11, {})} | custom-call | flops 805306368 | bytes 7340032 | tf_op jit(solution)/shard_map/last/pallas_call | solution.py:397
  269.2 1.3 collective-permute-start.13
  270.8 1.1 collective-permute-done.10
  272.0 1.0 collective-permute-start.12
  273.0 4.6 %collective-permute-done.13 = bf16[4,128,256]{2,1,0:T(8,128)(2,1)S(1)} collective-permute-done((bf16[4,128,256]{2,1,0:T(8,128)(2,1)S(1)}, bf16[4,128,256]{2,1,0:T(8,128)(2,1)S(1)}, u32[]{:S(2)}, u32[]{:S(2)}) %collective-permute-start.13) | collective-permute-done | bytes 262176 | tf_op jit(solution)/shard_map/ppermute | solution.py:427
  277.6 0.8 collective-permute-done.14
  278.4 1.9 collective-permute-start.15
  280.3 3.7 %collective-permute-done.12 = bf16[4,128,256]{2,1,0:T(8,128)(2,1)S(1)} collective-permute-done((bf16[4,128,256]{2,1,0:T(8,128)(2,1)S(1)}, bf16[4,128,256]{2,1,0:T(8,128)(2,1)S(1)}, u32[]{:S(2)}, u32[]{:S(2)}) %collective-permute-start.12) | collective-permute-done | bytes 262176 | tf_op jit(solution)/shard_map/ppermute | solution.py:423
  284.2 1.1 pad_maximum_fusion
  (24 shorter events, 2.5 us)
Async XLA Ops:
  7.2 245.2 %all-reduce.2.cloned.1.call-start = ((), (), s32[]{:S(2)}) async-start(), calls=%async_computation.1 | async-start | bytes 524288 | tf_op jit(solution)/shard_map/psum | solution.py:280
  8.5 11.2 %collective-permute-start = (bf16[4,128,256]{2,1,0:T(8,128)(2,1)S(1)}, bf16[4,128,256]{2,1,0:T(8,128)(2,1)S(1)}, u32[]{:S(2)}, u32[]{:S(2)}) collective-permute-start(bf16[4,128,256]{2,1,0:T(8,128)(2,1)S(1)} %get-tuple-element.34.refs_0_), channel_id=1, source_target_pairs={{0,1},{1,2},{2,3},{3,0},{4,5},{5,6},{6,7},{7,4},{8,9},{9,10},{10,1... | collective-permute-start | bytes 786440 | tf_op jit(solution)/shard_map/ppermute | solution.py:423
  10.7 9.0 %collective-permute-start.1 = (bf16[4,128,256]{2,1,0:T(8,128)(2,1)S(1)}, bf16[4,128,256]{2,1,0:T(8,128)(2,1)S(1)}, u32[]{:S(2)}, u32[]{:S(2)}) collective-permute-start(bf16[4,128,256]{2,1,0:T(8,128)(2,1)S(1)} %get-tuple-element.35.refs_1_), channel_id=1, source_target_pairs={{0,3},{1,0},{2,1},{3,2},{4,7},{5,4},{6,5},{7,6},{8,11},{9,8},{10,9... | collective-permute-start | bytes 786440 | tf_op jit(solution)/shard_map/ppermute | solution.py:427
  12.2 16.3 %collective-permute-start.2 = (bf16[4,128,256]{2,1,0:T(8,128)(2,1)S(1)}, bf16[4,128,256]{2,1,0:T(8,128)(2,1)S(1)}, u32[]{:S(2)}, u32[]{:S(2)}) collective-permute-start(bf16[4,128,256]{2,1,0:T(8,128)(2,1)S(1)} %get-tuple-element.34.refs_0_), channel_id=1, source_target_pairs={{0,3},{1,0},{2,1},{3,2},{4,7},{5,4},{6,5},{7,6},{8,11},{9,8},{10,9... | collective-permute-start | bytes 786440 | tf_op jit(solution)/shard_map/ppermute | solution.py:427
  13.6 15.0 %collective-permute-start.5 = (bf16[4,128,256]{2,1,0:T(8,128)(2,1)S(1)}, bf16[4,128,256]{2,1,0:T(8,128)(2,1)S(1)}, u32[]{:S(2)}, u32[]{:S(2)}) collective-permute-start(bf16[4,128,256]{2,1,0:T(8,128)(2,1)S(1)} %get-tuple-element.35.refs_1_), channel_id=1, source_target_pairs={{0,1},{1,2},{2,3},{3,0},{4,5},{5,6},{6,7},{7,4},{8,9},{9,10},{10,1... | collective-permute-start | bytes 786440 | tf_op jit(solution)/shard_map/ppermute | solution.py:423
  19.7 8.9 %collective-permute-start.3 = (bf16[4,128,256]{2,1,0:T(8,128)(2,1)S(1)}, bf16[4,128,256]{2,1,0:T(8,128)(2,1)S(1)}, u32[]{:S(2)}, u32[]{:S(2)}) collective-permute-start(bf16[4,128,256]{2,1,0:T(8,128)(2,1)S(1)} %collective-permute-done.refs_6_), channel_id=1, source_target_pairs={{0,1},{1,2},{2,3},{3,0},{4,5},{5,6},{6,7},{7,4},{8,9},{9,10},{10,1... | collective-permute-start | bytes 786440 | tf_op jit(solution)/shard_map/ppermute | solution.py:423
  20.1 8.4 %collective-permute-start.4 = (bf16[4,128,256]{2,1,0:T(8,128)(2,1)S(1)}, bf16[4,128,256]{2,1,0:T(8,128)(2,1)S(1)}, u32[]{:S(2)}, u32[]{:S(2)}) collective-permute-start(bf16[4,128,256]{2,1,0:T(8,128)(2,1)S(1)} %collective-permute-done.1.refs_3_), channel_id=1, source_target_pairs={{0,3},{1,0},{2,1},{3,2},{4,7},{5,4},{6,5},{7,6},{8,11},{9,8},{10,9... | collective-permute-start | bytes 786440 | tf_op jit(solution)/shard_map/ppermute | solution.py:427
  28.6 81.6 %copy-start.1 = (f32[2,2048]{1,0:T(2,128)S(1)}, f32[2,2048]{1,0:T(2,128)}, u32[]{:S(2)}) copy-start(f32[2,2048]{1,0:T(2,128)} %b_ref.5) | copy-start | bytes 49156
  32.7 5.9 %collective-permute-start.6 = (bf16[256,512]{1,0:T(8,128)(2,1)S(1)}, bf16[256,512]{1,0:T(8,128)(2,1)S(1)}, u32[]{:S(2)}, u32[]{:S(2)}) collective-permute-start(bf16[256,512]{1,0:T(8,128)(2,1)S(1)} %get-tuple-element.42), channel_id=1, source_target_pairs={{0,4},{4,0},{1,5},{5,1},{2,6},{6,2},{3,7},{7,3},{8,12},{12,8},{9,1... | collective-permute-start | bytes 786440 | tf_op jit(solution)/shard_map/ppermute | solution.py:232
  94.8 15.3 %collective-permute-start.7 = (bf16[32,16,256]{2,1,0:T(8,128)(2,1)S(1)}, bf16[32,16,256]{2,1,0:T(8,128)(2,1)S(1)}, u32[]{:S(2)}, u32[]{:S(2)}) collective-permute-start(bf16[32,16,256]{2,1,0:T(8,128)(2,1)S(1)} %all_gather.3.mine_ref), channel_id=1, source_target_pairs={{0,4},{4,0},{1,5},{5,1},{2,6},{6,2},{3,7},{7,3},{8,12},{12,8},{9,1... | collective-permute-start | bytes 786440 | tf_op jit(solution)/shard_map/ppermute | solution.py:232
  114.4 1.6 collective-permute-start.8
  252.3 6.5 %collective-permute-start.9 = (bf16[32,16,256]{2,1,0:T(8,128)(2,1)}, bf16[32,16,256]{2,1,0:T(8,128)(2,1)S(1)}, u32[]{:S(2)}, u32[]{:S(2)}) collective-permute-start(bf16[32,16,256]{2,1,0:T(8,128)(2,1)} %all-reduce.2.cloned.1.call-done.mine_ref), channel_id=1, source_target_pairs={{0,4},{4,0},{1,5},{5,1},{2,6},{6,2},{3,7},{7,3},{8,12},{12,8},{9,1... | collective-permute-start | bytes 786440 | tf_op jit(solution)/shard_map/ppermute | solution.py:232
  258.8 0.9 copy-start
  263.1 8.8 %collective-permute-start.10 = (bf16[4,128,256]{2,1,0:T(8,128)(2,1)S(1)}, bf16[4,128,256]{2,1,0:T(8,128)(2,1)S(1)}, u32[]{:S(2)}, u32[]{:S(2)}) collective-permute-start(bf16[4,128,256]{2,1,0:T(8,128)(2,1)S(1)} %get-tuple-element.53), channel_id=1, source_target_pairs={{0,1},{1,2},{2,3},{3,0},{4,5},{5,6},{6,7},{7,4},{8,9},{9,10},{10,1... | collective-permute-start | bytes 786440 | tf_op jit(solution)/shard_map/ppermute | solution.py:423
  264.4 7.5 %collective-permute-start.11 = (bf16[4,128,256]{2,1,0:T(8,128)(2,1)S(1)}, bf16[4,128,256]{2,1,0:T(8,128)(2,1)S(1)}, u32[]{:S(2)}, u32[]{:S(2)}) collective-permute-start(bf16[4,128,256]{2,1,0:T(8,128)(2,1)S(1)} %get-tuple-element.54), channel_id=1, source_target_pairs={{0,3},{1,0},{2,1},{3,2},{4,7},{5,4},{6,5},{7,6},{8,11},{9,8},{10,9... | collective-permute-start | bytes 786440 | tf_op jit(solution)/shard_map/ppermute | solution.py:427
  269.2 8.4 %collective-permute-start.13 = (bf16[4,128,256]{2,1,0:T(8,128)(2,1)S(1)}, bf16[4,128,256]{2,1,0:T(8,128)(2,1)S(1)}, u32[]{:S(2)}, u32[]{:S(2)}) collective-permute-start(bf16[4,128,256]{2,1,0:T(8,128)(2,1)S(1)} %get-tuple-element.59), channel_id=1, source_target_pairs={{0,3},{1,0},{2,1},{3,2},{4,7},{5,4},{6,5},{7,6},{8,11},{9,8},{10,9... | collective-permute-start | bytes 786440 | tf_op jit(solution)/shard_map/ppermute | solution.py:427
  270.6 7.8 %collective-permute-start.14 = (bf16[4,128,256]{2,1,0:T(8,128)(2,1)S(1)}, bf16[4,128,256]{2,1,0:T(8,128)(2,1)S(1)}, u32[]{:S(2)}, u32[]{:S(2)}) collective-permute-start(bf16[4,128,256]{2,1,0:T(8,128)(2,1)S(1)} %get-tuple-element.60), channel_id=1, source_target_pairs={{0,1},{1,2},{2,3},{3,0},{4,5},{5,6},{6,7},{7,4},{8,9},{9,10},{10,1... | collective-permute-start | bytes 786440 | tf_op jit(solution)/shard_map/ppermute | solution.py:423
  272.0 12.0 %collective-permute-start.12 = (bf16[4,128,256]{2,1,0:T(8,128)(2,1)S(1)}, bf16[4,128,256]{2,1,0:T(8,128)(2,1)S(1)}, u32[]{:S(2)}, u32[]{:S(2)}) collective-permute-start(bf16[4,128,256]{2,1,0:T(8,128)(2,1)S(1)} %add_convert_fusion.1), channel_id=1, source_target_pairs={{0,1},{1,2},{2,3},{3,0},{4,5},{5,6},{6,7},{7,4},{8,9},{9,10},{10,1... | collective-permute-start | bytes 786440 | tf_op jit(solution)/shard_map/ppermute | solution.py:423
  278.4 5.7 %collective-permute-start.15 = (bf16[4,128,256]{2,1,0:T(8,128)(2,1)S(1)}, bf16[4,128,256]{2,1,0:T(8,128)(2,1)S(1)}, u32[]{:S(2)}, u32[]{:S(2)}) collective-permute-start(bf16[4,128,256]{2,1,0:T(8,128)(2,1)S(1)} %add_convert_fusion), channel_id=1, source_target_pairs={{0,3},{1,0},{2,1},{3,2},{4,7},{5,4},{6,5},{7,6},{8,11},{9,8},{10,9... | collective-permute-start | bytes 786440 | tf_op jit(solution)/shard_map/ppermute | solution.py:427
Sparse Core Ops, SparseCore 0:
  116.9 135.3 all-reduce.1

commit v3 on v2

v3 whole, which is shorter than its diff:
```python
import functools

import jax
import jax.numpy as jnp
from jax import lax
from jax.experimental import pallas as pl
from jax.experimental.pallas import tpu as pltpu
from jax.sharding import PartitionSpec as P

F32 = jnp.float32
BF16 = jnp.bfloat16
EB = 512
NT = (((1,), (1,)), ((), ()))
TN = (((0,), (0,)), ((), ()))


def vmem():
    return pl.BlockSpec(memory_space=pltpu.VMEM)


def smem():
    return pl.BlockSpec(memory_space=pltpu.SMEM)


def params(mib):
    return pltpu.CompilerParams(vmem_limit_bytes=mib * 2**20)


def cost(flops, moved):
    return pl.CostEstimate(flops=flops, bytes_accessed=moved, transcendentals=0)


def pinned(arr):
    return pltpu.with_memory_space_constraint(arr, pltpu.HBM)


def kept(*arrs):
    return [pltpu.with_memory_space_constraint(arr, pltpu.VMEM) for arr in arrs]


def hbm():
    return pl.BlockSpec(memory_space=pltpu.HBM)


def cast_kernel(in_ref, a_ref, b_ref, held, sems):
    half = a_ref.shape[0]
    outs = (a_ref, b_ref)
    copies = fetch(sems, [(in_ref.at[pl.ds(i * half, half)], held.at[i]) for i in range(2)])
    for i in range(2):
        copies[i].wait()
        outs[i][...] = held[i].astype(BF16)


def cast_halves(emb_rows):
    tabs, rows, emb = emb_rows.shape
    half = (tabs // 2, rows, emb)
    return pl.pallas_call(
        cast_kernel,
        in_specs=[hbm()],
        out_specs=[vmem()] * 2,
        out_shape=[pltpu.VMEM(half, BF16)] * 2,
        scratch_shapes=[pltpu.VMEM((2,) + half, F32), pltpu.SemaphoreType.DMA((2,))],
        compiler_params=params(16),
        cost_estimate=cost(1 << 18, 3 << 19),
        name="cast",
    )(pinned(emb_rows))


def counts_kernel(mine_ref, ids_ref, own_ref, *refs, first_table):
    if first_table:
        edges_ref, *loads, out_ref, turned_ref = refs[: (len(refs) - 1) // 2]
        loaded, (acc_ref, ids, own, sems) = refs[len(loads) + 3 : -4], refs[-4:]
    else:
        out_ref, turned_ref, edges_ref, acc_ref, ids, own, sems = refs
        loads = loaded = ()
    samp, rows = acc_ref.shape
    tabs, entries = own.shape
    mine = mine_ref[0]
    low = mine * samp
    turn = mine * (rows // 4)
    copies = fetch(sems, [(own_ref, own), (ids_ref, ids), *zip(loads, loaded)])
    copies[0].wait()
    if not first_table:
        owners = own[...]
        first = jnp.sum((owners < low).astype(jnp.int32), axis=1, keepdims=True)
        last = jnp.sum((owners < low + samp).astype(jnp.int32), axis=1, keepdims=True)
        for i in range(tabs):
            edges_ref[i] = first[i, 0]
            edges_ref[tabs + i] = last[i, 0]
    copies[1].wait()
    grid = lax.broadcasted_iota(jnp.int32, (samp, EB), 0).astype(F32).astype(BF16)
    one, zero = jnp.ones((), BF16), jnp.zeros((), BF16)

    @pl.loop(0, out_ref.shape[0])
    def _(i):
        t = i + first_table
        start = edges_ref[t] // 128
        steps = (edges_ref[tabs + t] - start * 128 + EB - 1) // EB
        start = jnp.minimum(start, (entries - steps * EB) // 128)
        acc_ref[...] = jnp.zeros_like(acc_ref)

        def body(block, carry):
            at = pl.ds(pl.multiple_of(start * 128 + block * EB, 128), EB)
            who = own[pl.ds(t, 1), at] - low
            row = (ids[pl.ds(t, 1), at] - turn) & (rows - 1)
            hot = [
                jnp.where(grid == values.astype(F32).astype(BF16), one, zero) for values in (who, row, row - samp)
            ]
            acc_ref[...] += lax.dot_general(
                hot[0], jnp.concatenate(hot[1:], axis=0), NT, preferred_element_type=F32
            )
            return carry

        lax.fori_loop(0, steps, body, 0)
        total = acc_ref[...].astype(BF16)
        out_ref[i] = total
        turned_ref[i] = total.T

    for copy in copies[2:]:
        copy.wait()


def make_counts(mine, ids, owners, samp, rows, edges=None, loads=()):
    tabs, entries = ids.shape
    assert rows == 2 * samp and samp <= 256
    half = tabs // 2
    first = edges is None
    out_shape = [pltpu.VMEM((half, samp, rows), BF16), pltpu.VMEM((half, rows, samp), BF16)]
    if first:
        out_specs = [vmem(), vmem(), smem()]
        out_shape.append(jax.ShapeDtypeStruct((2 * tabs,), jnp.int32))
    else:
        out_specs = [vmem()] * (2 + len(loads))
        out_shape += [pltpu.VMEM(arr.shape, arr.dtype) for arr in loads]
    return pl.pallas_call(
        functools.partial(counts_kernel, first_table=0 if first else half),
        in_specs=[smem(), hbm(), hbm()] + ([] if first else [smem()] + [hbm()] * len(loads)),
        out_specs=out_specs,
        out_shape=out_shape,
        scratch_shapes=[
            pltpu.VMEM((samp, rows), F32),
            pltpu.VMEM((tabs, entries), jnp.int32),
            pltpu.VMEM((tabs, entries), jnp.int32),
            pltpu.SemaphoreType.DMA((2 + len(loads),)),
        ],
        compiler_params=params(16),
        cost_estimate=cost(half * samp * rows * 3072, 3 << 20),
        name="counts",
    )(mine, pinned(ids), pinned(owners), *([] if first else [edges, *map(pinned, loads)]))


WIDE = 512


def fetch(sems, pairs):
    copies = [pltpu.make_async_copy(src, dst, sems.at[i]) for i, (src, dst) in enumerate(pairs)]
    for copy in copies:
        copy.start()
    return copies


def emit(core_ref, z, g, keep_ref, send_ref):
    even = core_ref[0] == 0
    keep_ref[...] = jnp.where(even, z, g)
    send_ref[...] = jnp.where(even, g, z).astype(BF16)


def anyspace():
    return pl.BlockSpec(memory_space=pl.ANY)


def first_kernel(core_ref, counts_a, counts_b, *refs):
    embs, (cot, v, u, pooled_ref, keep_ref, send_ref) = refs[:8], refs[8:]
    half = counts_a.shape[0]
    z = g = None
    for f in range(half):
        parts = []
        for t in (2 * f, 2 * f + 1):
            side, at = divmod(t, half)
            rows = jnp.concatenate([embs[2 * k + side][at] for k in range(4)], axis=0)
            parts.append(jnp.dot((counts_a, counts_b)[side][at], rows, preferred_element_type=F32).astype(BF16))
        pooled = jnp.concatenate(parts, axis=1)
        at = slice(f * WIDE, (f + 1) * WIDE)
        pooled_ref[:, at] = pooled
        wide = (cot[:, at].astype(F32) * pooled.astype(F32)).astype(BF16)
        more_z = jnp.dot(pooled, v[0, at, :], preferred_element_type=F32)
        more_g = lax.dot_general(wide, u[1, :, at], NT, preferred_element_type=F32)
        z, g = (more_z, more_g) if f == 0 else (z + more_z, g + more_g)
    emit(core_ref, z, g, keep_ref, send_ref)


def first_sums(core, counts, embs, cot, v, u):
    half, samp, rows = counts[0].shape
    emb = embs[0].shape[-1]
    rank = v.shape[-1]
    assert 2 * emb == WIDE
    return pl.pallas_call(
        first_kernel,
        in_specs=[smem()] + [vmem()] * 13,
        out_specs=[vmem()] * 3,
        out_shape=[
            pltpu.VMEM((samp, 2 * half * emb), BF16),
            pltpu.VMEM((samp, rank), F32),
            pltpu.VMEM((samp, rank), BF16),
        ],
        compiler_params=params(16),
        cost_estimate=cost(3 << 29, 10 << 20),
        name="first_sums",
    )(core, *kept(*counts), *embs, *kept(cot, v, u))


def swap(arr, axis):
    return lax.ppermute(arr, axis, [(0, 1), (1, 0)])


def small(kernel, out_shape, name, *args):
    return pl.pallas_call(
        kernel,
        in_specs=[vmem()] * len(args),
        out_specs=jax.tree.map(lambda _: vmem(), out_shape),
        out_shape=out_shape,
        compiler_params=params(8),
        cost_estimate=cost(1 << 20, 1 << 20),
        name=name,
    )(*args)


CHUNKS = 16
CHUNK = (32, 256)


def chunk_at(i):
    r, c = CHUNK[0] * (i // 2), CHUNK[1] * (i % 2)
    return slice(r, r + CHUNK[0]), slice(c, c + CHUNK[1])


def cut_kernel(keep_ref, got_ref, out_ref):
    for i in range(CHUNKS):
        at = chunk_at(i)
        out_ref[i] = (keep_ref[at] + got_ref[at].astype(F32)).astype(BF16)


def total_kernel(in_ref, keep_ref, send_ref):
    total = in_ref[0].astype(F32)
    for i in range(1, CHUNKS):
        total = total + in_ref[i].astype(F32)
    keep_ref[...] = total
    send_ref[...] = total.astype(BF16)


def copies_kernel(keep_ref, got_ref, out_ref):
    total = (keep_ref[...] + got_ref[...].astype(F32)).astype(BF16)
    for i in range(CHUNKS):
        out_ref[i] = total


def sum_all(keep, send):
    among = ("x", "zh")
    shape = pltpu.VMEM((CHUNKS,) + CHUNK, BF16)
    chunks = small(cut_kernel, shape, "cut", keep, swap(send, "c"))
    parts = lax.all_to_all(chunks, among, 0, 0, tiled=True)
    keep, send = small(total_kernel, [pltpu.VMEM(CHUNK, F32), pltpu.VMEM(CHUNK, BF16)], "total", parts)
    copies = small(copies_kernel, shape, "copies", keep, swap(send, "zl"))
    mine = lax.all_to_all(copies, among, 0, 0, tiled=True)
    return mine, swap(mine, "c")


def spread(core_ref, mine_ref, other_ref, in_ref):
    core = core_ref[0]
    for side, ref in ((core, mine_ref), (1 - core, other_ref)):
        for i in range(CHUNKS):
            in_ref[(side, *chunk_at(i))] = ref[i]


def middle_kernel(core_ref, mine_ref, other_ref, b_ref, pooled, cot, u_ref, v_ref, x1_ref, a_ref, keep_ref, send_ref, sums):
    spread(core_ref, mine_ref, other_ref, sums)
    z = g = None
    for f in range(pooled.shape[1] // WIDE):
        at = slice(f * WIDE, (f + 1) * WIDE)
        u, v = u_ref[0, :, at], v_ref[1, at, :]
        base = pooled[:, at].astype(F32)
        h0 = jnp.dot(sums[0], u, preferred_element_type=F32) + b_ref[0:1, at]
        x1 = (base * h0 + base).astype(BF16)
        x1_ref[:, at] = x1
        g1 = cot[:, at].astype(F32) + lax.dot_general(sums[1], v, NT, preferred_element_type=F32)
        a_ref[:, at] = (g1 * h0 + g1).astype(BF16)
        wide = (g1 * base).astype(BF16)
        more_z = jnp.dot(x1, v, preferred_element_type=F32)
        more_g = lax.dot_general(wide, u, NT, preferred_element_type=F32)
        z, g = (more_z, more_g) if f == 0 else (z + more_z, g + more_g)
    emit(core_ref, z, g, keep_ref, send_ref)


def middle(core, mine, other, bias, pooled, cot, u, v):
    samp, feats = pooled.shape
    rank = v.shape[-1]
    feat = pltpu.VMEM((samp, feats), BF16)
    return pl.pallas_call(
        middle_kernel,
        in_specs=[smem()] + [vmem()] * 7,
        out_specs=[vmem()] * 4,
        out_shape=[feat, feat, pltpu.VMEM((samp, rank), F32), pltpu.VMEM((samp, rank), BF16)],
        scratch_shapes=[pltpu.VMEM((2, samp, rank), BF16)],
        compiler_params=params(16),
        cost_estimate=cost(1 << 31, 8 << 20),
        name="middle",
    )(core, mine, other, bias, *kept(pooled, cot, u, v))


def last_kernel(core_ref, mine_ref, other_ref, b_ref, turned, pooled, cot, x1, a, u_ref, v_ref, *refs, side):
    crossed_ref, p0, p1, p2, p3, sums, crossed, sems = refs[-8:]
    steps = crossed.shape[0]
    spread(core_ref, mine_ref, other_ref, sums)
    outs = []
    rows, emb = p0.shape[1:]
    for f in range(steps):
        at = slice((side * steps + f) * WIDE, (side * steps + f + 1) * WIDE)
        h1 = jnp.dot(sums[0], u_ref[1, :, at], preferred_element_type=F32) + b_ref[1:2, at]
        crossed[f] = (pooled[:, at].astype(F32) * h1 + x1[:, at].astype(F32)).astype(BF16)
        out = pltpu.make_async_copy(crossed.at[f], crossed_ref.at[:, at], sems.at[f])
        out.start()
        outs.append(out)
        grad = cot[:, at].astype(F32) * h1 + a[:, at].astype(F32)
        grad = (grad + lax.dot_general(sums[1], v_ref[0, at, :], NT, preferred_element_type=F32)).astype(BF16)
        for i in range(2):
            part = jnp.dot(turned[2 * f + i], grad[:, i * emb : (i + 1) * emb], preferred_element_type=F32)
            p0[2 * f + i] = part[:rows]
            for k, ref in enumerate((p1, p2, p3)):
                ref[2 * f + i] = part[(k + 1) * rows : (k + 2) * rows].astype(BF16)
    for out in outs:
        out.wait()


def last(side, before, core, mine, other, bias, turned, pooled, cot, x1, a, u, v):
    half, rows, samp = turned.shape
    rank = v.shape[-1]
    emb = pooled.shape[1] // (2 * half)
    steps = pooled.shape[1] // WIDE // 2
    block = (half, rows // 4, emb)
    args = (core, mine, other, bias, *kept(turned, pooled, cot, x1, a, u, v), *before)
    return pl.pallas_call(
        functools.partial(last_kernel, side=side),
        in_specs=[smem()] + [vmem()] * 10 + [anyspace()] * len(before),
        out_specs=[anyspace()] + [vmem()] * 4,
        out_shape=[pltpu.HBM(pooled.shape, BF16), pltpu.VMEM(block, F32)] + [pltpu.VMEM(block, BF16)] * 3,
        scratch_shapes=[
            pltpu.VMEM((2, samp, rank), BF16),
            pltpu.VMEM((steps, samp, WIDE), BF16),
            pltpu.SemaphoreType.DMA((steps,)),
        ],
        input_output_aliases={11: 0} if before else {},
        compiler_params=params(16),
        cost_estimate=cost(3 << 28, 7 << 20),
        name="last",
    )(*args)


def right(arr):
    return lax.ppermute(arr, "row", [(i, (i + 1) & 3) for i in range(4)])


def left(arr):
    return lax.ppermute(arr, "row", [(i, (i + 3) & 3) for i in range(4)])


def add(a, b):
    return a.astype(F32) + b.astype(F32)


def scalar(axis):
    return lax.axis_index(axis).astype(jnp.int32).reshape(1)


def local(emb_rows, entry_ids, entry_sample, cross_v, cross_u, cross_bias, cotangent):
    samp = cotangent.shape[0]
    rows = emb_rows.shape[1] * lax.axis_size("row")
    mine, core = scalar("row"), scalar("c")
    own_a, own_b = cast_halves(emb_rows)
    left_a, right_b = right(own_a), left(own_b)
    left_b, right_a = right(own_b), left(own_a)
    counts_a, turned_a, edges = make_counts(mine, entry_ids, entry_sample, samp, rows)
    left_a, right_b, edges = lax.optimization_barrier((left_a, right_b, edges))
    far_a, far_b = right(left_a), left(right_b)
    loads = (cotangent, cross_v, cross_u)
    counts_b, turned_b, cot, v, u = make_counts(mine, entry_ids, entry_sample, samp, rows, edges, loads)
    embs = (own_a, own_b, right_a, right_b, far_a, far_b, left_a, left_b)
    pooled, keep, send = first_sums(core, (counts_a, counts_b), embs, cot, v, u)
    sums = sum_all(keep, send)
    x1, a, keep, send = middle(core, *sums, cross_bias, pooled, cot, u, v)
    sums = sum_all(keep, send)
    front = (core, *sums, cross_bias)
    rest = (pooled, cot, x1, a, u, v)
    crossed, p0a, p1a, p2a, p3a = last(0, (), *front, turned_a, *rest)
    from_left, sum_a = lax.optimization_barrier((right(p2a), left(p3a)))
    crossed, p0b, p1b, p2b, p3b = last(1, (crossed,), *front, turned_b, *rest)
    from_right, sum_b = lax.optimization_barrier((left(p2b), right(p1b)))
    far_a = right(add(p1a, from_left).astype(BF16))
    far_b = left(add(p3b, from_right).astype(BF16))
    grads = jnp.concatenate([p0a + add(sum_a, far_a), p0b + add(sum_b, far_b)], axis=0)
    return crossed, grads


def solution(mesh):
    fine = jax.sharding.Mesh(mesh.devices.reshape(4, 4, 2, 2, 4), ("x", "zh", "zl", "c", "row"))
    table = ("x", "zh", "zl", "c")
    placed = (
        P(table, "row", None),
        P(table, None),
        P(table, None),
        P(None, table, None),
        P(None, None, table),
        P(None, table),
        P("row", table),
    )
    return jax.shard_map(
        local,
        mesh=fine,
        in_specs=placed,
        out_specs=(P("row", table), P(table, "row", None)),
        check_vma=False,
    )
```

time: 294 us -> 141 us (0.48)
  waiting for transfers between devices: 151 us -> 20.6 us
  between operations: 14.2 us -> 0.78 us
  starting transfers between devices: 39.6 us -> 27.8 us
  blocking collectives: 56.1 us -> 66.4 us
  Pallas kernels: 29.3 us -> 21.9 us
    psum x1 -> x0, waiting for transfers between devices: 136 us -> none  [sum_by_psum(): mine = lax.psum(chunks, ('x', 'z'))]
    all_to_all x1 -> x4, blocking collectives: 18.8 us -> 66.4 us  [the longest x2 37.9 us: sum_all(): parts = lax.all_to_all(chunks, among, 0, 0, tiled=True)]
    all_gather x1 -> x0, blocking collectives: 37.3 us -> none  [sum_by_gather(): mine = lax.all_gather(exchange(chunks, 1), ('x', 'z'), axis=0, tiled=True)]
    ppermute x4 -> x6, starting transfers between devices: 24.4 us -> 11.3 us  [swap(): return lax.ppermute(arr, axis, [(0, 1), (1, 0)])]
    ppermute x4 -> x6, waiting for transfers between devices: 4.86 us -> 9.39 us  [swap(): return lax.ppermute(arr, axis, [(0, 1), (1, 0)])]
    pallas_call x7 -> x10, Pallas kernels: 21.3 us -> 17.1 us  [the longest x2 11 us: make_counts(): pl.pallas_call(functools.partial(counts_kernel, first_table=0 if first el...]
    pallas_call x2, Pallas kernels: 6.71 us -> 3.56 us  [last(): pl.pallas_call(functools.partial(last_kernel, side=side), in_specs=[smem(...]
  transfers between devices with their start and end apart: 17 -> 18, of which waited for: 10 -> 10; matrix products, arithmetic and copies ran while one was open for 0% -> 0% of each run, Pallas kernels for 5% -> 9%
where the time goes in v3:
time: 141 us; the launch traced here: 139 us
  blocking collectives  66.4 us (47%)
  starting transfers between devices  27.8 us (20%)
  Pallas kernels  21.9 us (16%)
  waiting for transfers between devices  20.6 us (15%)
    all_to_all x2, blocking collectives, sum_all(): parts = lax.all_to_all(chunks, among, 0, 0, tiled=True)  37.9 us
    all_to_all x2, blocking collectives, sum_all(): mine = lax.all_to_all(copies, among, 0, 0, tiled=True)  28.6 us
    ppermute x6, starting transfers between devices, swap(): return lax.ppermute(arr, axis, [(0, 1), (1, 0)])  11.3 us
    pallas_call x2, Pallas kernels, make_counts(): pl.pallas_call(functools.partial(counts_kernel, first_table=0 if first el...  11 us
    ppermute x6, starting transfers between devices, left(): return lax.ppermute(arr, 'row', [(i, i + 3 & 3) for i in range(4)])  10.8 us
    ppermute x6, waiting for transfers between devices, swap(): return lax.ppermute(arr, axis, [(0, 1), (1, 0)])  9.39 us
    ppermute x6, waiting for transfers between devices, left(): return lax.ppermute(arr, 'row', [(i, i + 3 & 3) for i in range(4)])  6.12 us
    ppermute x6, starting transfers between devices, right(): return lax.ppermute(arr, 'row', [(i, i + 1 & 3) for i in range(4)])  5.69 us
  transfers between devices with their start and end apart: 18, of which 10 were waited for; matrix products, arithmetic and copies ran while one was open for 0% of the time, Pallas kernels for 9%

profile of v3, /device:TPU:1, one launch (start us, length us, event | category | flops | bytes accessed | tf_op | source)
XLA Modules:
  0.0 139.0 jit_solution(8488652503907621920)
XLA Ops:
  0.6 1.2 cast.1
  1.9 2.2 %collective-permute-start = (bf16[4,128,256]{2,1,0:T(8,128)(2,1)S(1)}, bf16[4,128,256]{2,1,0:T(8,128)(2,1)S(1)}, u32[]{:S(2)}, u32[]{:S(2)}) collective-permute-start(bf16[4,128,256]{2,1,0:T(8,128)(2,1)S(1)} %get-tuple-element.41.refs_0_), channel_id=1, source_target_pairs={{0,1},{1,2},{2,3},{3,0},{4,5},{5,6},{6,7},{7,4},{8,9},{9,10},{10,1... | collective-permute-start | bytes 786440 | tf_op jit(solution)/shard_map/ppermute | solution.py:359
  4.1 1.5 %collective-permute-start.1 = (bf16[4,128,256]{2,1,0:T(8,128)(2,1)S(1)}, bf16[4,128,256]{2,1,0:T(8,128)(2,1)S(1)}, u32[]{:S(2)}, u32[]{:S(2)}) collective-permute-start(bf16[4,128,256]{2,1,0:T(8,128)(2,1)S(1)} %get-tuple-element.42.refs_1_), channel_id=1, source_target_pairs={{0,3},{1,0},{2,1},{3,2},{4,7},{5,4},{6,5},{7,6},{8,11},{9,8},{10,9... | collective-permute-start | bytes 786440 | tf_op jit(solution)/shard_map/ppermute | solution.py:363
  5.6 1.4 collective-permute-start.2
  7.1 5.3 %counts.2 = (bf16[4,256,512]{2,1,0:T(8,128)(2,1)S(1)}, bf16[4,512,256]{2,1,0:T(8,128)(2,1)S(1)}, s32[16]{0:T(128)S(1)}) custom-call(s32[1]{0:T(128)} %bitcast.1.mine_ref, s32[8,4096]{1,0:T(8,128)} %ids_ref.3, s32[8,4096]{1,0:T(8,128)} %own_ref.3), custom_call_target="tpu_custom_call" | custom-call | flops 1610612736 | bytes 3145728 | tf_op jit(solution)/shard_map/counts/pallas_call | solution.py:135
  13.6 2.3 %collective-permute-start.4 = (bf16[4,128,256]{2,1,0:T(8,128)(2,1)S(1)}, bf16[4,128,256]{2,1,0:T(8,128)(2,1)}, u32[]{:S(2)}, u32[]{:S(2)}) collective-permute-start(bf16[4,128,256]{2,1,0:T(8,128)(2,1)S(1)} %collective-permute-done.1.refs_3_), channel_id=1, source_target_pairs={{0,3},{1,0},{2,1},{3,2},{4,7},{5,4},{6,5},{7,6},{8,11},{9,8},{10,9... | collective-permute-start | bytes 786440 | tf_op jit(solution)/shard_map/ppermute | solution.py:363
  15.9 5.7 %counts.3 = (bf16[4,256,512]{2,1,0:T(8,128)(2,1)S(1)}, bf16[4,512,256]{2,1,0:T(8,128)(2,1)S(1)}, bf16[256,2048]{1,0:T(8,128)(2,1)S(1)}, bf16[2,2048,512]{2,1,0:T(8,128)(2,1)S(1)}, bf16[2,512,2048]{2,1,0:T(8,128)(2,1)S(1)}) custom-call(s32[1]{0:T(128)} %bitcast.1.mine_ref, s32[8,4096]{1,0:T(8,128)} %ids_ref.3, s32[8,4096]{1,0:T(8,128)} %own_ref.3, ...), custom_call_target="tpu_custom_call" | custom-call | flops 1610612736 | bytes 3145728 | tf_op jit(solution)/shard_map/counts/pallas_call | solution.py:135
  21.6 3.2 %first_sums.1 = (bf16[256,2048]{1,0:T(8,128)(2,1)S(1)}, f32[256,512]{1,0:T(8,128)S(1)}, bf16[256,512]{1,0:T(8,128)(2,1)S(1)}) custom-call(s32[1]{0:T(128)} %bitcast.core_ref, bf16[4,256,512]{2,1,0:T(8,128)(2,1)S(1)} %get-tuple-element.40.counts_a, bf16[4,256,512]{2,1,0:T(8,128)(2,1)S(1)} %get-tuple-element.45.counts_b, ...), custom_call_target="tpu_custom_call" | custom-call | flops 1610612736 | bytes 10485760 | tf_op jit(solution)/shard_map/first_sums/pallas_call | solution.py:197
  24.8 3.3 %collective-permute-start.6 = (bf16[256,512]{1,0:T(8,128)(2,1)S(1)}, bf16[256,512]{1,0:T(8,128)(2,1)S(1)}, u32[]{:S(2)}, u32[]{:S(2)}) collective-permute-start(bf16[256,512]{1,0:T(8,128)(2,1)S(1)} %get-tuple-element.52), channel_id=1, source_target_pairs={{0,4},{4,0},{1,5},{5,1},{2,6},{6,2},{3,7},{7,3},{8,12},{12,8},{9,1... | collective-permute-start | bytes 786440 | tf_op jit(solution)/shard_map/ppermute | solution.py:213
  28.1 1.2 collective-permute-done.6.got_ref
  29.4 22.7 %all_to_all.20.in_ref = bf16[16,32,256]{2,1,0:T(8,128)(2,1)S(1)} all-to-all(bf16[16,32,256]{2,1,0:T(8,128)(2,1)S(1)} %cut.2), channel_id=1, replica_groups=mesh['x'=4,'zh'=4,'zl'=2,'c'=2,'row'=4] {'x','zh'}, dimensions={0} | all-to-all | bytes 524288 | tf_op jit(solution)/shard_map/all_to_all | solution.py:261
  52.5 2.3 %collective-permute-done.7.got_ref = bf16[32,256]{1,0:T(8,128)(2,1)S(1)} collective-permute-done((bf16[32,256]{1,0:T(8,128)(2,1)S(1)}, bf16[32,256]{1,0:T(8,128)(2,1)S(1)}, u32[]{:S(2)}, u32[]{:S(2)}) %collective-permute-start.7) | collective-permute-done | bytes 16416 | tf_op jit(solution)/shard_map/ppermute | solution.py:213
  54.9 14.6 %all_to_all.21.mine_ref = bf16[16,32,256]{2,1,0:T(8,128)(2,1)S(1)} all-to-all(bf16[16,32,256]{2,1,0:T(8,128)(2,1)S(1)} %copies.2), channel_id=1, replica_groups=mesh['x'=4,'zh'=4,'zl'=2,'c'=2,'row'=4] {'x','zh'}, dimensions={0} | all-to-all | bytes 524288 | tf_op jit(solution)/shard_map/all_to_all | solution.py:264
  69.5 3.1 %collective-permute-start.8 = (bf16[16,32,256]{2,1,0:T(8,128)(2,1)S(1)}, bf16[16,32,256]{2,1,0:T(8,128)(2,1)S(1)}, u32[]{:S(2)}, u32[]{:S(2)}) collective-permute-start(bf16[16,32,256]{2,1,0:T(8,128)(2,1)S(1)} %all_to_all.21.mine_ref), channel_id=1, source_target_pairs={{0,4},{4,0},{1,5},{5,1},{2,6},{6,2},{3,7},{7,3},{8,12},{12,8},{9,1... | collective-permute-start | bytes 786440 | tf_op jit(solution)/shard_map/ppermute | solution.py:213
  72.5 1.2 collective-permute-done.8.other_ref
  73.7 2.7 %middle.1 = (bf16[256,2048]{1,0:T(8,128)(2,1)S(1)}, bf16[256,2048]{1,0:T(8,128)(2,1)S(1)}, f32[256,512]{1,0:T(8,128)S(1)}, bf16[256,512]{1,0:T(8,128)(2,1)S(1)}) custom-call(s32[1]{0:T(128)} %bitcast.core_ref, bf16[16,32,256]{2,1,0:T(8,128)(2,1)S(1)} %all_to_all.21.mine_ref, bf16[16,32,256]{2,1,0:T(8,128)(2,1)S(1)} %collective-permute-done.8.other_ref, ...), custom_call_target="tpu_custom_call" | custom-call | flops 2147483648 | bytes 8388608 | tf_op jit(solution)/shard_map/middle/pallas_call | solution.py:298
  77.0 1.2 collective-permute-done.9.got_ref
  78.3 15.1 %all_to_all.22.in_ref = bf16[16,32,256]{2,1,0:T(8,128)(2,1)S(1)} all-to-all(bf16[16,32,256]{2,1,0:T(8,128)(2,1)S(1)} %cut.3), channel_id=1, replica_groups=mesh['x'=4,'zh'=4,'zl'=2,'c'=2,'row'=4] {'x','zh'}, dimensions={0} | all-to-all | bytes 524288 | tf_op jit(solution)/shard_map/all_to_all | solution.py:261
  93.7 2.4 %collective-permute-done.10.got_ref = bf16[32,256]{1,0:T(8,128)(2,1)S(1)} collective-permute-done((bf16[32,256]{1,0:T(8,128)(2,1)S(1)}, bf16[32,256]{1,0:T(8,128)(2,1)S(1)}, u32[]{:S(2)}, u32[]{:S(2)}) %collective-permute-start.10) | collective-permute-done | bytes 16416 | tf_op jit(solution)/shard_map/ppermute | solution.py:213
  96.1 14.0 %all_to_all.23.mine_ref = bf16[16,32,256]{2,1,0:T(8,128)(2,1)S(1)} all-to-all(bf16[16,32,256]{2,1,0:T(8,128)(2,1)S(1)} %copies.3), channel_id=1, replica_groups=mesh['x'=4,'zh'=4,'zl'=2,'c'=2,'row'=4] {'x','zh'}, dimensions={0} | all-to-all | bytes 524288 | tf_op jit(solution)/shard_map/all_to_all | solution.py:264
  110.1 3.7 %collective-permute-start.11 = (bf16[16,32,256]{2,1,0:T(8,128)(2,1)S(1)}, bf16[16,32,256]{2,1,0:T(8,128)(2,1)S(1)}, u32[]{:S(2)}, u32[]{:S(2)}) collective-permute-start(bf16[16,32,256]{2,1,0:T(8,128)(2,1)S(1)} %all_to_all.23.mine_ref), channel_id=1, source_target_pairs={{0,4},{4,0},{1,5},{5,1},{2,6},{6,2},{3,7},{7,3},{8,12},{12,8},{9,1... | collective-permute-start | bytes 786440 | tf_op jit(solution)/shard_map/ppermute | solution.py:213
  113.8 1.2 collective-permute-done.11.other_ref
  115.0 1.8 %last.2 = (bf16[256,2048]{1,0:T(8,128)(2,1)}, f32[4,128,256]{2,1,0:T(8,128)S(1)}, bf16[4,128,256]{2,1,0:T(8,128)(2,1)S(1)}, bf16[4,128,256]{2,1,0:T(8,128)(2,1)S(1)}, bf16[4,128,256]{2,1,0:T(8,128)(2,1)S(1)}) custom-call(s32[1]{0:T(128)} %bitcast.core_ref, bf16[16,32,256]{2,1,0:T(8,128)(2,1)S(1)} %all_to_all.23.mine_ref, ...), custom_call_target="tpu_custom_call" | custom-call | flops 805306368 | bytes 7340032 | tf_op jit(solution)/shard_map/last/pallas_call | solution.py:341
  116.7 1.4 collective-permute-start.12
  118.1 1.4 %collective-permute-start.13 = (bf16[4,128,256]{2,1,0:T(8,128)(2,1)S(1)}, bf16[4,128,256]{2,1,0:T(8,128)(2,1)S(1)}, u32[]{:S(2)}, u32[]{:S(2)}) collective-permute-start(bf16[4,128,256]{2,1,0:T(8,128)(2,1)S(1)} %get-tuple-element.68), channel_id=1, source_target_pairs={{0,3},{1,0},{2,1},{3,2},{4,7},{5,4},{6,5},{7,6},{8,11},{9,8},{10,9... | collective-permute-start | bytes 786440 | tf_op jit(solution)/shard_map/ppermute | solution.py:363
  119.5 1.8 %last.3 = (bf16[256,2048]{1,0:T(8,128)(2,1)}, f32[4,128,256]{2,1,0:T(8,128)S(1)}, bf16[4,128,256]{2,1,0:T(8,128)(2,1)S(1)}, bf16[4,128,256]{2,1,0:T(8,128)(2,1)S(1)}, bf16[4,128,256]{2,1,0:T(8,128)(2,1)S(1)}) custom-call(s32[1]{0:T(128)} %bitcast.core_ref, bf16[16,32,256]{2,1,0:T(8,128)(2,1)S(1)} %all_to_all.23.mine_ref, ...), custom_call_target="tpu_custom_call", output_to_operand_aliasing={{0}: (11, {})} | custom-call | flops 805306368 | bytes 7340032 | tf_op jit(solution)/shard_map/last/pallas_call | solution.py:341
  121.3 1.4 %collective-permute-start.15 = (bf16[4,128,256]{2,1,0:T(8,128)(2,1)S(1)}, bf16[4,128,256]{2,1,0:T(8,128)(2,1)S(1)}, u32[]{:S(2)}, u32[]{:S(2)}) collective-permute-start(bf16[4,128,256]{2,1,0:T(8,128)(2,1)S(1)} %get-tuple-element.73), channel_id=1, source_target_pairs={{0,3},{1,0},{2,1},{3,2},{4,7},{5,4},{6,5},{7,6},{8,11},{9,8},{10,9... | collective-permute-start | bytes 786440 | tf_op jit(solution)/shard_map/ppermute | solution.py:363
  122.9 2.7 %collective-permute-done.12 = bf16[4,128,256]{2,1,0:T(8,128)(2,1)S(1)} collective-permute-done((bf16[4,128,256]{2,1,0:T(8,128)(2,1)S(1)}, bf16[4,128,256]{2,1,0:T(8,128)(2,1)S(1)}, u32[]{:S(2)}, u32[]{:S(2)}) %collective-permute-start.12) | collective-permute-done | bytes 262176 | tf_op jit(solution)/shard_map/ppermute | solution.py:359
  126.5 4.5 %collective-permute-done.15 = bf16[4,128,256]{2,1,0:T(8,128)(2,1)S(1)} collective-permute-done((bf16[4,128,256]{2,1,0:T(8,128)(2,1)S(1)}, bf16[4,128,256]{2,1,0:T(8,128)(2,1)S(1)}, u32[]{:S(2)}, u32[]{:S(2)}) %collective-permute-start.15) | collective-permute-done | bytes 262176 | tf_op jit(solution)/shard_map/ppermute | solution.py:363
  131.0 2.7 %collective-permute-start.17 = (bf16[4,128,256]{2,1,0:T(8,128)(2,1)S(1)}, bf16[4,128,256]{2,1,0:T(8,128)(2,1)S(1)}, u32[]{:S(2)}, u32[]{:S(2)}) collective-permute-start(bf16[4,128,256]{2,1,0:T(8,128)(2,1)S(1)} %add_convert_fusion), channel_id=1, source_target_pairs={{0,3},{1,0},{2,1},{3,2},{4,7},{5,4},{6,5},{7,6},{8,11},{9,8},{10,9... | collective-permute-start | bytes 786440 | tf_op jit(solution)/shard_map/ppermute | solution.py:363
  133.7 2.4 %collective-permute-done.14 = bf16[4,128,256]{2,1,0:T(8,128)(2,1)S(1)} collective-permute-done((bf16[4,128,256]{2,1,0:T(8,128)(2,1)S(1)}, bf16[4,128,256]{2,1,0:T(8,128)(2,1)S(1)}, u32[]{:S(2)}, u32[]{:S(2)}) %collective-permute-start.14) | collective-permute-done | bytes 262176 | tf_op jit(solution)/shard_map/ppermute | solution.py:359
  136.3 1.6 %collective-permute-done.17 = bf16[4,128,256]{2,1,0:T(8,128)(2,1)S(1)} collective-permute-done((bf16[4,128,256]{2,1,0:T(8,128)(2,1)S(1)}, bf16[4,128,256]{2,1,0:T(8,128)(2,1)S(1)}, u32[]{:S(2)}, u32[]{:S(2)}) %collective-permute-start.17) | collective-permute-done | bytes 262176 | tf_op jit(solution)/shard_map/ppermute | solution.py:363
  (28 shorter events, 5.0 us)
Async XLA Ops:
  1.9 10.5 %collective-permute-start = (bf16[4,128,256]{2,1,0:T(8,128)(2,1)S(1)}, bf16[4,128,256]{2,1,0:T(8,128)(2,1)S(1)}, u32[]{:S(2)}, u32[]{:S(2)}) collective-permute-start(bf16[4,128,256]{2,1,0:T(8,128)(2,1)S(1)} %get-tuple-element.41.refs_0_), channel_id=1, source_target_pairs={{0,1},{1,2},{2,3},{3,0},{4,5},{5,6},{6,7},{7,4},{8,9},{9,10},{10,1... | collective-permute-start | bytes 786440 | tf_op jit(solution)/shard_map/ppermute | solution.py:359
  4.1 8.3 %collective-permute-start.1 = (bf16[4,128,256]{2,1,0:T(8,128)(2,1)S(1)}, bf16[4,128,256]{2,1,0:T(8,128)(2,1)S(1)}, u32[]{:S(2)}, u32[]{:S(2)}) collective-permute-start(bf16[4,128,256]{2,1,0:T(8,128)(2,1)S(1)} %get-tuple-element.42.refs_1_), channel_id=1, source_target_pairs={{0,3},{1,0},{2,1},{3,2},{4,7},{5,4},{6,5},{7,6},{8,11},{9,8},{10,9... | collective-permute-start | bytes 786440 | tf_op jit(solution)/shard_map/ppermute | solution.py:363
  5.6 15.9 %collective-permute-start.2 = (bf16[4,128,256]{2,1,0:T(8,128)(2,1)S(1)}, bf16[4,128,256]{2,1,0:T(8,128)(2,1)S(1)}, u32[]{:S(2)}, u32[]{:S(2)}) collective-permute-start(bf16[4,128,256]{2,1,0:T(8,128)(2,1)S(1)} %get-tuple-element.41.refs_0_), channel_id=1, source_target_pairs={{0,3},{1,0},{2,1},{3,2},{4,7},{5,4},{6,5},{7,6},{8,11},{9,8},{10,9... | collective-permute-start | bytes 786440 | tf_op jit(solution)/shard_map/ppermute | solution.py:363
  7.0 14.6 %collective-permute-start.5 = (bf16[4,128,256]{2,1,0:T(8,128)(2,1)S(1)}, bf16[4,128,256]{2,1,0:T(8,128)(2,1)}, u32[]{:S(2)}, u32[]{:S(2)}) collective-permute-start(bf16[4,128,256]{2,1,0:T(8,128)(2,1)S(1)} %get-tuple-element.42.refs_1_), channel_id=1, source_target_pairs={{0,1},{1,2},{2,3},{3,0},{4,5},{5,6},{6,7},{7,4},{8,9},{9,10},{10,1... | collective-permute-start | bytes 786440 | tf_op jit(solution)/shard_map/ppermute | solution.py:359
  12.4 9.1 %collective-permute-start.3 = (bf16[4,128,256]{2,1,0:T(8,128)(2,1)S(1)}, bf16[4,128,256]{2,1,0:T(8,128)(2,1)}, u32[]{:S(2)}, u32[]{:S(2)}) collective-permute-start(bf16[4,128,256]{2,1,0:T(8,128)(2,1)S(1)} %collective-permute-done.refs_6_), channel_id=1, source_target_pairs={{0,1},{1,2},{2,3},{3,0},{4,5},{5,6},{6,7},{7,4},{8,9},{9,10},{10,1... | collective-permute-start | bytes 786440 | tf_op jit(solution)/shard_map/ppermute | solution.py:359
  13.6 8.1 %collective-permute-start.4 = (bf16[4,128,256]{2,1,0:T(8,128)(2,1)S(1)}, bf16[4,128,256]{2,1,0:T(8,128)(2,1)}, u32[]{:S(2)}, u32[]{:S(2)}) collective-permute-start(bf16[4,128,256]{2,1,0:T(8,128)(2,1)S(1)} %collective-permute-done.1.refs_3_), channel_id=1, source_target_pairs={{0,3},{1,0},{2,1},{3,2},{4,7},{5,4},{6,5},{7,6},{8,11},{9,8},{10,9... | collective-permute-start | bytes 786440 | tf_op jit(solution)/shard_map/ppermute | solution.py:363
  21.6 52.1 %copy-start = (f32[2,2048]{1,0:T(2,128)S(1)}, f32[2,2048]{1,0:T(2,128)}, u32[]{:S(2)}) copy-start(f32[2,2048]{1,0:T(2,128)} %b_ref.5) | copy-start | bytes 49156
  24.8 4.5 %collective-permute-start.6 = (bf16[256,512]{1,0:T(8,128)(2,1)S(1)}, bf16[256,512]{1,0:T(8,128)(2,1)S(1)}, u32[]{:S(2)}, u32[]{:S(2)}) collective-permute-start(bf16[256,512]{1,0:T(8,128)(2,1)S(1)} %get-tuple-element.52), channel_id=1, source_target_pairs={{0,4},{4,0},{1,5},{5,1},{2,6},{6,2},{3,7},{7,3},{8,12},{12,8},{9,1... | collective-permute-start | bytes 786440 | tf_op jit(solution)/shard_map/ppermute | solution.py:213
  52.2 2.7 %collective-permute-start.7 = (bf16[32,256]{1,0:T(8,128)(2,1)S(1)}, bf16[32,256]{1,0:T(8,128)(2,1)S(1)}, u32[]{:S(2)}, u32[]{:S(2)}) collective-permute-start(bf16[32,256]{1,0:T(8,128)(2,1)S(1)} %get-tuple-element.54), channel_id=1, source_target_pairs={{0,8},{8,0},{1,9},{9,1},{2,10},{10,2},{3,11},{11,3},{4,12},{12,4},... | collective-permute-start | bytes 49160 | tf_op jit(solution)/shard_map/ppermute | solution.py:213
  69.5 4.2 %collective-permute-start.8 = (bf16[16,32,256]{2,1,0:T(8,128)(2,1)S(1)}, bf16[16,32,256]{2,1,0:T(8,128)(2,1)S(1)}, u32[]{:S(2)}, u32[]{:S(2)}) collective-permute-start(bf16[16,32,256]{2,1,0:T(8,128)(2,1)S(1)} %all_to_all.21.mine_ref), channel_id=1, source_target_pairs={{0,4},{4,0},{1,5},{5,1},{2,6},{6,2},{3,7},{7,3},{8,12},{12,8},{9,1... | collective-permute-start | bytes 786440 | tf_op jit(solution)/shard_map/ppermute | solution.py:213
  76.4 1.8 %collective-permute-start.9 = (bf16[256,512]{1,0:T(8,128)(2,1)S(1)}, bf16[256,512]{1,0:T(8,128)(2,1)S(1)}, u32[]{:S(2)}, u32[]{:S(2)}) collective-permute-start(bf16[256,512]{1,0:T(8,128)(2,1)S(1)} %get-tuple-element.57), channel_id=1, source_target_pairs={{0,4},{4,0},{1,5},{5,1},{2,6},{6,2},{3,7},{7,3},{8,12},{12,8},{9,1... | collective-permute-start | bytes 786440 | tf_op jit(solution)/shard_map/ppermute | solution.py:213
  93.4 2.7 %collective-permute-start.10 = (bf16[32,256]{1,0:T(8,128)(2,1)S(1)}, bf16[32,256]{1,0:T(8,128)(2,1)S(1)}, u32[]{:S(2)}, u32[]{:S(2)}) collective-permute-start(bf16[32,256]{1,0:T(8,128)(2,1)S(1)} %get-tuple-element.59), channel_id=1, source_target_pairs={{0,8},{8,0},{1,9},{9,1},{2,10},{10,2},{3,11},{11,3},{4,12},{12,4},... | collective-permute-start | bytes 49160 | tf_op jit(solution)/shard_map/ppermute | solution.py:213
  110.1 4.8 %collective-permute-start.11 = (bf16[16,32,256]{2,1,0:T(8,128)(2,1)S(1)}, bf16[16,32,256]{2,1,0:T(8,128)(2,1)S(1)}, u32[]{:S(2)}, u32[]{:S(2)}) collective-permute-start(bf16[16,32,256]{2,1,0:T(8,128)(2,1)S(1)} %all_to_all.23.mine_ref), channel_id=1, source_target_pairs={{0,4},{4,0},{1,5},{5,1},{2,6},{6,2},{3,7},{7,3},{8,12},{12,8},{9,1... | collective-permute-start | bytes 786440 | tf_op jit(solution)/shard_map/ppermute | solution.py:213
  116.7 8.8 %collective-permute-start.12 = (bf16[4,128,256]{2,1,0:T(8,128)(2,1)S(1)}, bf16[4,128,256]{2,1,0:T(8,128)(2,1)S(1)}, u32[]{:S(2)}, u32[]{:S(2)}) collective-permute-start(bf16[4,128,256]{2,1,0:T(8,128)(2,1)S(1)} %get-tuple-element.67), channel_id=1, source_target_pairs={{0,1},{1,2},{2,3},{3,0},{4,5},{5,6},{6,7},{7,4},{8,9},{9,10},{10,1... | collective-permute-start | bytes 786440 | tf_op jit(solution)/shard_map/ppermute | solution.py:359
  118.1 7.5 %collective-permute-start.13 = (bf16[4,128,256]{2,1,0:T(8,128)(2,1)S(1)}, bf16[4,128,256]{2,1,0:T(8,128)(2,1)S(1)}, u32[]{:S(2)}, u32[]{:S(2)}) collective-permute-start(bf16[4,128,256]{2,1,0:T(8,128)(2,1)S(1)} %get-tuple-element.68), channel_id=1, source_target_pairs={{0,3},{1,0},{2,1},{3,2},{4,7},{5,4},{6,5},{7,6},{8,11},{9,8},{10,9... | collective-permute-start | bytes 786440 | tf_op jit(solution)/shard_map/ppermute | solution.py:363
  121.3 9.6 %collective-permute-start.15 = (bf16[4,128,256]{2,1,0:T(8,128)(2,1)S(1)}, bf16[4,128,256]{2,1,0:T(8,128)(2,1)S(1)}, u32[]{:S(2)}, u32[]{:S(2)}) collective-permute-start(bf16[4,128,256]{2,1,0:T(8,128)(2,1)S(1)} %get-tuple-element.73), channel_id=1, source_target_pairs={{0,3},{1,0},{2,1},{3,2},{4,7},{5,4},{6,5},{7,6},{8,11},{9,8},{10,9... | collective-permute-start | bytes 786440 | tf_op jit(solution)/shard_map/ppermute | solution.py:363
  122.8 8.2 %collective-permute-start.16 = (bf16[4,128,256]{2,1,0:T(8,128)(2,1)S(1)}, bf16[4,128,256]{2,1,0:T(8,128)(2,1)S(1)}, u32[]{:S(2)}, u32[]{:S(2)}) collective-permute-start(bf16[4,128,256]{2,1,0:T(8,128)(2,1)S(1)} %get-tuple-element.74), channel_id=1, source_target_pairs={{0,1},{1,2},{2,3},{3,0},{4,5},{5,6},{6,7},{7,4},{8,9},{9,10},{10,1... | collective-permute-start | bytes 786440 | tf_op jit(solution)/shard_map/ppermute | solution.py:359
  125.6 10.6 %collective-permute-start.14 = (bf16[4,128,256]{2,1,0:T(8,128)(2,1)S(1)}, bf16[4,128,256]{2,1,0:T(8,128)(2,1)S(1)}, u32[]{:S(2)}, u32[]{:S(2)}) collective-permute-start(bf16[4,128,256]{2,1,0:T(8,128)(2,1)S(1)} %add_convert_fusion.1), channel_id=1, source_target_pairs={{0,1},{1,2},{2,3},{3,0},{4,5},{5,6},{6,7},{7,4},{8,9},{9,10},{10,1... | collective-permute-start | bytes 786440 | tf_op jit(solution)/shard_map/ppermute | solution.py:359
  131.0 6.9 %collective-permute-start.17 = (bf16[4,128,256]{2,1,0:T(8,128)(2,1)S(1)}, bf16[4,128,256]{2,1,0:T(8,128)(2,1)S(1)}, u32[]{:S(2)}, u32[]{:S(2)}) collective-permute-start(bf16[4,128,256]{2,1,0:T(8,128)(2,1)S(1)} %add_convert_fusion), channel_id=1, source_target_pairs={{0,3},{1,0},{2,1},{3,2},{4,7},{5,4},{6,5},{7,6},{8,11},{9,8},{10,9... | collective-permute-start | bytes 786440 | tf_op jit(solution)/shard_map/ppermute | solution.py:363

commit v4 on v3

--- a/solution.py
+++ b/solution.py
@@ -225,13 +225,12 @@
     )(*args)
 
 
-CHUNKS = 16
-CHUNK = (32, 256)
+CHUNKS = 8
+CHUNK = (32, 512)
 
 
 def chunk_at(i):
-    r, c = CHUNK[0] * (i // 2), CHUNK[1] * (i % 2)
-    return slice(r, r + CHUNK[0]), slice(c, c + CHUNK[1])
+    return slice(CHUNK[0] * i, CHUNK[0] * (i + 1)), slice(None)
 
 
 def cut_kernel(keep_ref, got_ref, out_ref):
@@ -240,28 +239,34 @@
         out_ref[i] = (keep_ref[at] + got_ref[at].astype(F32)).astype(BF16)
 
 
-def total_kernel(in_ref, keep_ref, send_ref):
-    total = in_ref[0].astype(F32)
-    for i in range(1, CHUNKS):
-        total = total + in_ref[i].astype(F32)
-    keep_ref[...] = total
-    send_ref[...] = total.astype(BF16)
-
-
-def copies_kernel(keep_ref, got_ref, out_ref):
-    total = (keep_ref[...] + got_ref[...].astype(F32)).astype(BF16)
-    for i in range(CHUNKS):
+def total_kernel(*refs):
+    *ins, out_ref = refs
+    total = sum(ref[i].astype(F32) for ref in ins for i in range(ref.shape[0])).astype(BF16)
+    for i in range(out_ref.shape[0]):
         out_ref[i] = total
 
 
-def sum_all(keep, send):
-    among = ("x", "zh")
+def total(copies, *arrays):
+    return small(total_kernel, pltpu.VMEM((copies,) + CHUNK, BF16), "total", *arrays)
+
+
+def swap_all(arr):
+    return lax.all_to_all(arr, ("x", "zl"), 0, 0, tiled=True)
+
+
+def turn(arr, k):
+    return lax.ppermute(arr, "zh", [(i, (i + k) & 3) for i in range(4)])
+
+
+def sum_all(keep, send, by_turns):
     shape = pltpu.VMEM((CHUNKS,) + CHUNK, BF16)
-    chunks = small(cut_kernel, shape, "cut", keep, swap(send, "c"))
-    parts = lax.all_to_all(chunks, among, 0, 0, tiled=True)
-    keep, send = small(total_kernel, [pltpu.VMEM(CHUNK, F32), pltpu.VMEM(CHUNK, BF16)], "total", parts)
-    copies = small(copies_kernel, shape, "copies", keep, swap(send, "zl"))
-    mine = lax.all_to_all(copies, among, 0, 0, tiled=True)
+    parts = swap_all(small(cut_kernel, shape, "cut", keep, swap(send, "c")))
+    if by_turns:
+        own = total(1, parts)
+        near = (own, turn(own, 1), turn(own, 3), turn(own, 2))
+    else:
+        near = (lax.all_to_all(total(4, parts), "zh", 0, 0, tiled=True),)
+    mine = swap_all(total(CHUNKS, *near))
     return mine, swap(mine, "c")
 
 
@@ -307,52 +312,96 @@
     )(core, mine, other, bias, *kept(pooled, cot, u, v))
 
 
-def last_kernel(core_ref, mine_ref, other_ref, b_ref, turned, pooled, cot, x1, a, u_ref, v_ref, *refs, side):
-    crossed_ref, p0, p1, p2, p3, sums, crossed, sems = refs[-8:]
-    steps = crossed.shape[0]
+def row_grads(turned_ref, table, first, count, grad):
+    return jnp.dot(turned_ref[table, first : first + count, :], grad, preferred_element_type=F32)
+
+
+def far_kernel(core_ref, mine_ref, other_ref, b_ref, turned_a, turned_b, pooled, cot, x1, a, u_ref, v_ref, *refs):
+    crossed_ref, grad_ref, far_a, far_b, sums = refs
+    half, rows, emb = far_a.shape
     spread(core_ref, mine_ref, other_ref, sums)
-    outs = []
-    rows, emb = p0.shape[1:]
-    for f in range(steps):
-        at = slice((side * steps + f) * WIDE, (side * steps + f + 1) * WIDE)
+    for f in range(pooled.shape[1] // WIDE):
+        at = slice(f * WIDE, (f + 1) * WIDE)
         h1 = jnp.dot(sums[0], u_ref[1, :, at], preferred_element_type=F32) + b_ref[1:2, at]
-        crossed[f] = (pooled[:, at].astype(F32) * h1 + x1[:, at].astype(F32)).astype(BF16)
-        out = pltpu.make_async_copy(crossed.at[f], crossed_ref.at[:, at], sems.at[f])
-        out.start()
-        outs.append(out)
+        crossed_ref[:, at] = (pooled[:, at].astype(F32) * h1 + x1[:, at].astype(F32)).astype(BF16)
         grad = cot[:, at].astype(F32) * h1 + a[:, at].astype(F32)
         grad = (grad + lax.dot_general(sums[1], v_ref[0, at, :], NT, preferred_element_type=F32)).astype(BF16)
+        grad_ref[:, at] = grad
         for i in range(2):
-            part = jnp.dot(turned[2 * f + i], grad[:, i * emb : (i + 1) * emb], preferred_element_type=F32)
-            p0[2 * f + i] = part[:rows]
-            for k, ref in enumerate((p1, p2, p3)):
-                ref[2 * f + i] = part[(k + 1) * rows : (k + 2) * rows].astype(BF16)
-    for out in outs:
-        out.wait()
-
-
-def last(side, before, core, mine, other, bias, turned, pooled, cot, x1, a, u, v):
-    half, rows, samp = turned.shape
+            side, t = divmod(2 * f + i, half)
+            part = row_grads((turned_a, turned_b)[side], t, 2 * rows, rows, grad[:, i * emb : (i + 1) * emb])
+            (far_a, far_b)[side][t] = part.astype(BF16)
+
+
+def far_rows(core, mine, other, bias, turned, pooled, cot, x1, a, u, v):
+    half, rows, samp = turned[0].shape
     rank = v.shape[-1]
-    emb = pooled.shape[1] // (2 * half)
-    steps = pooled.shape[1] // WIDE // 2
-    block = (half, rows // 4, emb)
-    args = (core, mine, other, bias, *kept(turned, pooled, cot, x1, a, u, v), *before)
-    return pl.pallas_call(
-        functools.partial(last_kernel, side=side),
-        in_specs=[smem()] + [vmem()] * 10 + [anyspace()] * len(before),
-        out_specs=[anyspace()] + [vmem()] * 4,
-        out_shape=[pltpu.HBM(pooled.shape, BF16), pltpu.VMEM(block, F32)] + [pltpu.VMEM(block, BF16)] * 3,
-        scratch_shapes=[
-            pltpu.VMEM((2, samp, rank), BF16),
-            pltpu.VMEM((steps, samp, WIDE), BF16),
-            pltpu.SemaphoreType.DMA((steps,)),
-        ],
-        input_output_aliases={11: 0} if before else {},
+    feats = pooled.shape[1]
+    piece = pltpu.VMEM((half, rows // 4, feats // (2 * half)), BF16)
+    return pl.pallas_call(
+        far_kernel,
+        in_specs=[smem()] + [vmem()] * 11,
+        out_specs=[vmem()] * 4,
+        out_shape=[pltpu.VMEM(pooled.shape, BF16)] * 2 + [piece, piece],
+        scratch_shapes=[pltpu.VMEM((2, samp, rank), BF16)],
+        compiler_params=params(16),
+        cost_estimate=cost(5 << 28, 7 << 20),
+        name="far_rows",
+    )(core, mine, other, bias, *kept(*turned, pooled, cot, x1, a, u, v))
+
+
+def near_kernel(turned_a, turned_b, grad, made_ref, crossed_ref, p0_ref, p1_a, p1_b, p3_a, p3_b, sem):
+    copy = pltpu.make_async_copy(made_ref, crossed_ref, sem)
+    copy.start()
+    half, rows, emb = p1_a.shape
+    for t in range(2 * half):
+        side, at = divmod(t, half)
+        part = grad[:, t * emb : (t + 1) * emb]
+        turned = (turned_a, turned_b)[side]
+        first = row_grads(turned, at, 0, 2 * rows, part)
+        p0_ref[t] = first[:rows]
+        (p1_a, p1_b)[side][at] = first[rows:].astype(BF16)
+        (p3_a, p3_b)[side][at] = row_grads(turned, at, 3 * rows, rows, part).astype(BF16)
+    copy.wait()
+
+
+def near_rows(turned, grad, crossed):
+    half, rows, samp = turned[0].shape
+    block = (half, rows // 4, grad.shape[1] // (2 * half))
+    return pl.pallas_call(
+        near_kernel,
+        in_specs=[vmem()] * 4,
+        out_specs=[anyspace()] + [vmem()] * 5,
+        out_shape=[pltpu.HBM(crossed.shape, BF16), pltpu.VMEM((2 * half,) + block[1:], F32)]
+        + [pltpu.VMEM(block, BF16)] * 4,
+        scratch_shapes=[pltpu.SemaphoreType.DMA],
         compiler_params=params(16),
         cost_estimate=cost(3 << 28, 7 << 20),
-        name="last",
-    )(*args)
+        name="near_rows",
+    )(*kept(*turned, grad, crossed))
+
+
+def finish_kernel(p0, sum_ref, far_ref, *refs, side):
+    out_ref, held, sem = refs[-3:]
+    half = held.shape[0]
+    held[...] = p0[side * half : (side + 1) * half] + (sum_ref[...].astype(F32) + far_ref[...].astype(F32))
+    copy = pltpu.make_async_copy(held, out_ref.at[pl.ds(side * half, half)], sem)
+    copy.start()
+    copy.wait()
+
+
+def finish(side, before, p0, near, far):
+    return pl.pallas_call(
+        functools.partial(finish_kernel, side=side),
+        in_specs=[vmem()] * 3 + [anyspace()] * len(before),
+        out_specs=anyspace(),
+        out_shape=pltpu.HBM(p0.shape, F32),
+        scratch_shapes=[pltpu.VMEM(near.shape, F32), pltpu.SemaphoreType.DMA],
+        input_output_aliases={3: 0} if before else {},
+        compiler_params=params(8),
+        cost_estimate=cost(1 << 20, 1 << 20),
+        name="finish",
+    )(*kept(p0), near, far, *before)
 
 
 def right(arr):
@@ -385,19 +434,18 @@
     counts_b, turned_b, cot, v, u = make_counts(mine, entry_ids, entry_sample, samp, rows, edges, loads)
     embs = (own_a, own_b, right_a, right_b, far_a, far_b, left_a, left_b)
     pooled, keep, send = first_sums(core, (counts_a, counts_b), embs, cot, v, u)
-    sums = sum_all(keep, send)
+    sums = sum_all(keep, send, False)
     x1, a, keep, send = middle(core, *sums, cross_bias, pooled, cot, u, v)
-    sums = sum_all(keep, send)
-    front = (core, *sums, cross_bias)
-    rest = (pooled, cot, x1, a, u, v)
-    crossed, p0a, p1a, p2a, p3a = last(0, (), *front, turned_a, *rest)
-    from_left, sum_a = lax.optimization_barrier((right(p2a), left(p3a)))
-    crossed, p0b, p1b, p2b, p3b = last(1, (crossed,), *front, turned_b, *rest)
-    from_right, sum_b = lax.optimization_barrier((left(p2b), right(p1b)))
+    sums = sum_all(keep, send, True)
+    turned = (turned_a, turned_b)
+    crossed, grad, p2a, p2b = far_rows(core, *sums, cross_bias, turned, pooled, cot, x1, a, u, v)
+    from_left, from_right = right(p2a), left(p2b)
+    crossed, p0, p1a, p1b, p3a, p3b = near_rows(turned, grad, crossed)
+    sum_b, sum_a = right(p1b), left(p3a)
     far_a = right(add(p1a, from_left).astype(BF16))
     far_b = left(add(p3b, from_right).astype(BF16))
-    grads = jnp.concatenate([p0a + add(sum_a, far_a), p0b + add(sum_b, far_b)], axis=0)
-    return crossed, grads
+    grads = finish(0, (), p0, sum_a, far_a)
+    return crossed, finish(1, (grads,), p0, sum_b, far_b)
 
 
 def solution(mesh):

time: 141 us -> 131 us (0.929); the launches traced: 139 us -> 131 us
  blocking collectives: 66.4 us -> 52.1 us
  starting transfers between devices: 27.8 us -> 32.2 us
  Pallas kernels: 21.9 us -> 24.5 us
    all_to_all x4 -> x5, blocking collectives: 66.4 us -> 52.1 us  [the longest x4 38.1 us: swap_all(): return lax.all_to_all(arr, ('x', 'zl'), 0, 0, tiled=True)]
    ppermute x0 -> x3, waiting for transfers between devices: none -> 5.47 us  [turn(): return lax.ppermute(arr, 'zh', [(i, i + k & 3) for i in range(4)])]
    ppermute x6 -> x4, waiting for transfers between devices: 9.39 us -> 4.65 us  [swap(): return lax.ppermute(arr, axis, [(0, 1), (1, 0)])]
    ppermute x6, waiting for transfers between devices: 6.12 us -> 2.14 us  [left(): return lax.ppermute(arr, 'row', [(i, i + 3 & 3) for i in range(4)])]
    ppermute x6, waiting for transfers between devices: 5.13 us -> 8.99 us  [right(): return lax.ppermute(arr, 'row', [(i, i + 1 & 3) for i in range(4)])]
    ppermute x0 -> x3, starting transfers between devices: none -> 3.69 us  [turn(): return lax.ppermute(arr, 'zh', [(i, i + k & 3) for i in range(4)])]
    ppermute x6, starting transfers between devices: 5.69 us -> 2.55 us  [right(): return lax.ppermute(arr, 'row', [(i, i + 1 & 3) for i in range(4)])]
    ppermute x6, starting transfers between devices: 10.8 us -> 12.9 us  [left(): return lax.ppermute(arr, 'row', [(i, i + 3 & 3) for i in range(4)])]
  transfers between devices with their start and end apart: 18 -> 19, of which waited for: 10 -> 10; matrix products, arithmetic and copies ran while one was open for 0% -> 0% of each run, Pallas kernels for 9% -> 11%
where the time goes in v4:
time: 131 us
  blocking collectives  52.1 us (40%)
  starting transfers between devices  32.2 us (25%)
  Pallas kernels  24.5 us (19%)
  waiting for transfers between devices  21.2 us (16%)
    all_to_all x4, blocking collectives, swap_all(): return lax.all_to_all(arr, ('x', 'zl'), 0, 0, tiled=True)  38.1 us
    all_to_all x1, blocking collectives, sum_all(): near = (lax.all_to_all(total(4, parts), 'zh', 0, 0, tiled=True),)  14 us
    ppermute x4, starting transfers between devices, swap(): return lax.ppermute(arr, axis, [(0, 1), (1, 0)])  13.1 us
    ppermute x6, starting transfers between devices, left(): return lax.ppermute(arr, 'row', [(i, i + 3 & 3) for i in range(4)])  12.9 us
    pallas_call x2, Pallas kernels, make_counts(): pl.pallas_call(functools.partial(counts_kernel, first_table=0 if first el...  12.4 us
    ppermute x6, waiting for transfers between devices, right(): return lax.ppermute(arr, 'row', [(i, i + 1 & 3) for i in range(4)])  8.99 us
    ppermute x3, waiting for transfers between devices, turn(): return lax.ppermute(arr, 'zh', [(i, i + k & 3) for i in range(4)])  5.47 us
    ppermute x4, waiting for transfers between devices, swap(): return lax.ppermute(arr, axis, [(0, 1), (1, 0)])  4.65 us
  transfers between devices with their start and end apart: 19, of which 10 were waited for; matrix products, arithmetic and copies ran while one was open for 0% of the time, Pallas kernels for 11%

profile of v4, /device:TPU:1, one launch (start us, length us, event | category | flops | bytes accessed | tf_op | source)
XLA Modules:
  0.0 131.2 jit_solution(17719601006637167344)
XLA Ops:
  0.6 1.2 cast.1
  1.9 2.2 %collective-permute-start = (bf16[4,128,256]{2,1,0:T(8,128)(2,1)S(1)}, bf16[4,128,256]{2,1,0:T(8,128)(2,1)S(1)}, u32[]{:S(2)}, u32[]{:S(2)}) collective-permute-start(bf16[4,128,256]{2,1,0:T(8,128)(2,1)S(1)} %get-tuple-element.33.refs_0_), channel_id=1, source_target_pairs={{0,1},{1,2},{2,3},{3,0},{4,5},{5,6},{6,7},{7,4},{8,9},{9,10},{10,1... | collective-permute-start | bytes 786440 | tf_op jit(solution)/shard_map/ppermute | solution.py:408
  4.1 1.5 %collective-permute-start.1 = (bf16[4,128,256]{2,1,0:T(8,128)(2,1)S(1)}, bf16[4,128,256]{2,1,0:T(8,128)(2,1)S(1)}, u32[]{:S(2)}, u32[]{:S(2)}) collective-permute-start(bf16[4,128,256]{2,1,0:T(8,128)(2,1)S(1)} %get-tuple-element.34.refs_1_), channel_id=1, source_target_pairs={{0,3},{1,0},{2,1},{3,2},{4,7},{5,4},{6,5},{7,6},{8,11},{9,8},{10,9... | collective-permute-start | bytes 786440 | tf_op jit(solution)/shard_map/ppermute | solution.py:412
  5.6 1.4 %collective-permute-start.2 = (bf16[4,128,256]{2,1,0:T(8,128)(2,1)S(1)}, bf16[4,128,256]{2,1,0:T(8,128)(2,1)S(1)}, u32[]{:S(2)}, u32[]{:S(2)}) collective-permute-start(bf16[4,128,256]{2,1,0:T(8,128)(2,1)S(1)} %get-tuple-element.33.refs_0_), channel_id=1, source_target_pairs={{0,3},{1,0},{2,1},{3,2},{4,7},{5,4},{6,5},{7,6},{8,11},{9,8},{10,9... | collective-permute-start | bytes 786440 | tf_op jit(solution)/shard_map/ppermute | solution.py:412
  7.1 6.0 %counts.2 = (bf16[4,256,512]{2,1,0:T(8,128)(2,1)S(1)}, bf16[4,512,256]{2,1,0:T(8,128)(2,1)S(1)}, s32[16]{0:T(128)S(1)}) custom-call(s32[1]{0:T(128)} %bitcast.mine_ref, s32[8,4096]{1,0:T(8,128)} %ids_ref.3, s32[8,4096]{1,0:T(8,128)} %own_ref.3), custom_call_target="tpu_custom_call" | custom-call | flops 1610612736 | bytes 3145728 | tf_op jit(solution)/shard_map/counts/pallas_call | solution.py:135
  13.1 2.0 %collective-permute-start.4 = (bf16[4,128,256]{2,1,0:T(8,128)(2,1)S(1)}, bf16[4,128,256]{2,1,0:T(8,128)(2,1)}, u32[]{:S(2)}, u32[]{:S(2)}) collective-permute-start(bf16[4,128,256]{2,1,0:T(8,128)(2,1)S(1)} %collective-permute-done.1.refs_3_), channel_id=1, source_target_pairs={{0,3},{1,0},{2,1},{3,2},{4,7},{5,4},{6,5},{7,6},{8,11},{9,8},{10,9... | collective-permute-start | bytes 786440 | tf_op jit(solution)/shard_map/ppermute | solution.py:412
  15.1 6.4 %counts.3 = (bf16[4,256,512]{2,1,0:T(8,128)(2,1)S(1)}, bf16[4,512,256]{2,1,0:T(8,128)(2,1)S(1)}, bf16[256,2048]{1,0:T(8,128)(2,1)S(1)}, bf16[2,2048,512]{2,1,0:T(8,128)(2,1)S(1)}, bf16[2,512,2048]{2,1,0:T(8,128)(2,1)S(1)}) custom-call(s32[1]{0:T(128)} %bitcast.mine_ref, s32[8,4096]{1,0:T(8,128)} %ids_ref.3, s32[8,4096]{1,0:T(8,128)} %own_ref.3, ...), custom_call_target="tpu_custom_call" | custom-call | flops 1610612736 | bytes 3145728 | tf_op jit(solution)/shard_map/counts/pallas_call | solution.py:135
  22.0 3.2 %first_sums.1 = (bf16[256,2048]{1,0:T(8,128)(2,1)S(1)}, f32[256,512]{1,0:T(8,128)S(1)}, bf16[256,512]{1,0:T(8,128)(2,1)S(1)}) custom-call(s32[1]{0:T(128)} %bitcast.1.core_ref, bf16[4,256,512]{2,1,0:T(8,128)(2,1)S(1)} %get-tuple-element.38.counts_a, bf16[4,256,512]{2,1,0:T(8,128)(2,1)S(1)} %get-tuple-element.39.counts_b, ...), custom_call_target="tpu_custom_call" | custom-call | flops 1610612736 | bytes 10485760 | tf_op jit(solution)/shard_map/first_sums/pallas_call | solution.py:197
  25.2 4.4 %collective-permute-start.6 = (bf16[256,512]{1,0:T(8,128)(2,1)S(1)}, bf16[256,512]{1,0:T(8,128)(2,1)S(1)}, u32[]{:S(2)}, u32[]{:S(2)}) collective-permute-start(bf16[256,512]{1,0:T(8,128)(2,1)S(1)} %get-tuple-element.46), channel_id=1, source_target_pairs={{0,4},{4,0},{1,5},{5,1},{2,6},{6,2},{3,7},{7,3},{8,12},{12,8},{9,1... | collective-permute-start | bytes 786440 | tf_op jit(solution)/shard_map/ppermute | solution.py:213
  29.6 1.2 collective-permute-done.6.got_ref
  30.8 11.4 %all_to_all.25.refs_0_ = bf16[8,32,512]{2,1,0:T(8,128)(2,1)S(1)} all-to-all(bf16[8,32,512]{2,1,0:T(8,128)(2,1)S(1)} %cut.2), channel_id=1, replica_groups=mesh['x'=4,'zh'=4,'zl'=2,'c'=2,'row'=4] {'x','zl'}, dimensions={0} | all-to-all | bytes 524288 | tf_op jit(solution)/shard_map/all_to_all | solution.py:254
  42.2 14.0 %all_to_all.26.refs_0_ = bf16[4,32,512]{2,1,0:T(8,128)(2,1)S(1)} all-to-all(bf16[4,32,512]{2,1,0:T(8,128)(2,1)S(1)} %total.4), channel_id=1, replica_groups=mesh['x'=4,'zh'=4,'zl'=2,'c'=2,'row'=4] {'zh'}, dimensions={0} | all-to-all | bytes 262144 | tf_op jit(solution)/shard_map/all_to_all | solution.py:268
  56.2 8.7 %all_to_all.27.mine_ref = bf16[8,32,512]{2,1,0:T(8,128)(2,1)S(1)} all-to-all(bf16[8,32,512]{2,1,0:T(8,128)(2,1)S(1)} %total.5), channel_id=1, replica_groups=mesh['x'=4,'zh'=4,'zl'=2,'c'=2,'row'=4] {'x','zl'}, dimensions={0} | all-to-all | bytes 524288 | tf_op jit(solution)/shard_map/all_to_all | solution.py:254
  64.9 4.4 %collective-permute-start.7 = (bf16[8,32,512]{2,1,0:T(8,128)(2,1)S(1)}, bf16[8,32,512]{2,1,0:T(8,128)(2,1)S(1)}, u32[]{:S(2)}, u32[]{:S(2)}) collective-permute-start(bf16[8,32,512]{2,1,0:T(8,128)(2,1)S(1)} %all_to_all.27.mine_ref), channel_id=1, source_target_pairs={{0,4},{4,0},{1,5},{5,1},{2,6},{6,2},{3,7},{7,3},{8,12},{12,8},{9,1... | collective-permute-start | bytes 786440 | tf_op jit(solution)/shard_map/ppermute | solution.py:213
  69.4 1.2 collective-permute-done.7.other_ref
  70.5 2.7 %middle.1 = (bf16[256,2048]{1,0:T(8,128)(2,1)S(1)}, bf16[256,2048]{1,0:T(8,128)(2,1)S(1)}, f32[256,512]{1,0:T(8,128)S(1)}, bf16[256,512]{1,0:T(8,128)(2,1)S(1)}) custom-call(s32[1]{0:T(128)} %bitcast.1.core_ref, bf16[8,32,512]{2,1,0:T(8,128)(2,1)S(1)} %all_to_all.27.mine_ref, bf16[8,32,512]{2,1,0:T(8,128)(2,1)S(1)} %collective-permute-done.7.other_ref, ...), custom_call_target="tpu_custom_call" | custom-call | flops 2147483648 | bytes 8388608 | tf_op jit(solution)/shard_map/middle/pallas_call | solution.py:303
  73.7 1.2 collective-permute-done.8.got_ref
  74.9 9.0 %all_to_all.28.refs_0_ = bf16[8,32,512]{2,1,0:T(8,128)(2,1)S(1)} all-to-all(bf16[8,32,512]{2,1,0:T(8,128)(2,1)S(1)} %cut.3), channel_id=1, replica_groups=mesh['x'=4,'zh'=4,'zl'=2,'c'=2,'row'=4] {'x','zl'}, dimensions={0} | all-to-all | bytes 524288 | tf_op jit(solution)/shard_map/all_to_all | solution.py:254
  84.9 2.7 %collective-permute-start.10 = (bf16[1,32,512]{2,1,0:T(8,128)(2,1)S(1)}, bf16[1,32,512]{2,1,0:T(8,128)(2,1)S(1)}, u32[]{:S(2)}, u32[]{:S(2)}) collective-permute-start(bf16[1,32,512]{2,1,0:T(8,128)(2,1)S(1)} %total.6.refs_0_), channel_id=1, source_target_pairs={{0,48},{16,0},{32,16},{48,32},{1,49},{17,1},{33,17},{49,33},{2,50}... | collective-permute-start | bytes 98312 | tf_op jit(solution)/shard_map/ppermute | solution.py:258
  87.6 3.7 %collective-permute-done.11.refs_3_ = bf16[1,32,512]{2,1,0:T(8,128)(2,1)S(1)} collective-permute-done((bf16[1,32,512]{2,1,0:T(8,128)(2,1)S(1)}, bf16[1,32,512]{2,1,0:T(8,128)(2,1)S(1)}, u32[]{:S(2)}, u32[]{:S(2)}) %collective-permute-start.11) | collective-permute-done | bytes 32800 | tf_op jit(solution)/shard_map/ppermute | solution.py:258
  91.3 1.8 %collective-permute-done.9.refs_1_ = bf16[1,32,512]{2,1,0:T(8,128)(2,1)S(1)} collective-permute-done((bf16[1,32,512]{2,1,0:T(8,128)(2,1)S(1)}, bf16[1,32,512]{2,1,0:T(8,128)(2,1)S(1)}, u32[]{:S(2)}, u32[]{:S(2)}) %collective-permute-start.9) | collective-permute-done | bytes 32800 | tf_op jit(solution)/shard_map/ppermute | solution.py:258
  93.1 9.0 %all_to_all.29.mine_ref = bf16[8,32,512]{2,1,0:T(8,128)(2,1)S(1)} all-to-all(bf16[8,32,512]{2,1,0:T(8,128)(2,1)S(1)} %total.7), channel_id=1, replica_groups=mesh['x'=4,'zh'=4,'zl'=2,'c'=2,'row'=4] {'x','zl'}, dimensions={0} | all-to-all | bytes 524288 | tf_op jit(solution)/shard_map/all_to_all | solution.py:254
  102.2 3.8 %collective-permute-start.12 = (bf16[8,32,512]{2,1,0:T(8,128)(2,1)S(1)}, bf16[8,32,512]{2,1,0:T(8,128)(2,1)S(1)}, u32[]{:S(2)}, u32[]{:S(2)}) collective-permute-start(bf16[8,32,512]{2,1,0:T(8,128)(2,1)S(1)} %all_to_all.29.mine_ref), channel_id=1, source_target_pairs={{0,4},{4,0},{1,5},{5,1},{2,6},{6,2},{3,7},{7,3},{8,12},{12,8},{9,1... | collective-permute-start | bytes 786440 | tf_op jit(solution)/shard_map/ppermute | solution.py:213
  105.9 1.2 collective-permute-done.12.other_ref
  107.1 2.1 %far_rows.1 = (bf16[256,2048]{1,0:T(8,128)(2,1)S(1)}, bf16[256,2048]{1,0:T(8,128)(2,1)S(1)}, bf16[4,128,256]{2,1,0:T(8,128)(2,1)S(1)}, bf16[4,128,256]{2,1,0:T(8,128)(2,1)S(1)}) custom-call(s32[1]{0:T(128)} %bitcast.1.core_ref, bf16[8,32,512]{2,1,0:T(8,128)(2,1)S(1)} %all_to_all.29.mine_ref, bf16[8,32,512]{2,1,0:T(8,128)(2,1)S(1)} %collective-permute-done.12.other_ref, ...), custom_call_target="tpu_custom_call" | custom-call | flops 1342177280 | bytes 7340032 | tf_op jit(solution)/shard_map/far_rows/pallas_call | solution.py:341
  109.3 2.7 %collective-permute-start.14 = (bf16[4,128,256]{2,1,0:T(8,128)(2,1)S(1)}, bf16[4,128,256]{2,1,0:T(8,128)(2,1)S(1)}, u32[]{:S(2)}, u32[]{:S(2)}) collective-permute-start(bf16[4,128,256]{2,1,0:T(8,128)(2,1)S(1)} %get-tuple-element.58), channel_id=1, source_target_pairs={{0,3},{1,0},{2,1},{3,2},{4,7},{5,4},{6,5},{7,6},{8,11},{9,8},{10,9... | collective-permute-start | bytes 786440 | tf_op jit(solution)/shard_map/ppermute | solution.py:412
  112.0 1.0 near_rows.1
  113.0 2.7 %collective-permute-start.16 = (bf16[4,128,256]{2,1,0:T(8,128)(2,1)S(1)}, bf16[4,128,256]{2,1,0:T(8,128)(2,1)S(1)}, u32[]{:S(2)}, u32[]{:S(2)}) collective-permute-start(bf16[4,128,256]{2,1,0:T(8,128)(2,1)S(1)} %get-tuple-element.59), channel_id=1, source_target_pairs={{0,3},{1,0},{2,1},{3,2},{4,7},{5,4},{6,5},{7,6},{8,11},{9,8},{10,9... | collective-permute-start | bytes 786440 | tf_op jit(solution)/shard_map/ppermute | solution.py:412
  115.7 2.3 %collective-permute-done.17 = bf16[4,128,256]{2,1,0:T(8,128)(2,1)S(1)} collective-permute-done((bf16[4,128,256]{2,1,0:T(8,128)(2,1)S(1)}, bf16[4,128,256]{2,1,0:T(8,128)(2,1)S(1)}, u32[]{:S(2)}, u32[]{:S(2)}) %collective-permute-start.17) | collective-permute-done | bytes 262176 | tf_op jit(solution)/shard_map/ppermute | solution.py:408
  118.2 2.7 %collective-permute-start.15 = (bf16[4,128,256]{2,1,0:T(8,128)(2,1)S(1)}, bf16[4,128,256]{2,1,0:T(8,128)(2,1)S(1)}, u32[]{:S(2)}, u32[]{:S(2)}) collective-permute-start(bf16[4,128,256]{2,1,0:T(8,128)(2,1)S(1)} %add_convert_fusion.1), channel_id=1, source_target_pairs={{0,3},{1,0},{2,1},{3,2},{4,7},{5,4},{6,5},{7,6},{8,11},{9,8},{10,9... | collective-permute-start | bytes 786440 | tf_op jit(solution)/shard_map/ppermute | solution.py:412
  121.0 1.6 %collective-permute-done.16.sum_ref = bf16[4,128,256]{2,1,0:T(8,128)(2,1)S(1)} collective-permute-done((bf16[4,128,256]{2,1,0:T(8,128)(2,1)S(1)}, bf16[4,128,256]{2,1,0:T(8,128)(2,1)S(1)}, u32[]{:S(2)}, u32[]{:S(2)}) %collective-permute-start.16) | collective-permute-done | bytes 262176 | tf_op jit(solution)/shard_map/ppermute | solution.py:412
  122.6 6.7 %collective-permute-done.18.far_ref = bf16[4,128,256]{2,1,0:T(8,128)(2,1)S(1)} collective-permute-done((bf16[4,128,256]{2,1,0:T(8,128)(2,1)S(1)}, bf16[4,128,256]{2,1,0:T(8,128)(2,1)S(1)}, u32[]{:S(2)}, u32[]{:S(2)}) %collective-permute-start.18) | collective-permute-done | bytes 262176 | tf_op jit(solution)/shard_map/ppermute | solution.py:408
  (30 shorter events, 4.4 us)
Async XLA Ops:
  1.9 11.2 %collective-permute-start = (bf16[4,128,256]{2,1,0:T(8,128)(2,1)S(1)}, bf16[4,128,256]{2,1,0:T(8,128)(2,1)S(1)}, u32[]{:S(2)}, u32[]{:S(2)}) collective-permute-start(bf16[4,128,256]{2,1,0:T(8,128)(2,1)S(1)} %get-tuple-element.33.refs_0_), channel_id=1, source_target_pairs={{0,1},{1,2},{2,3},{3,0},{4,5},{5,6},{6,7},{7,4},{8,9},{9,10},{10,1... | collective-permute-start | bytes 786440 | tf_op jit(solution)/shard_map/ppermute | solution.py:408
  4.1 9.0 %collective-permute-start.1 = (bf16[4,128,256]{2,1,0:T(8,128)(2,1)S(1)}, bf16[4,128,256]{2,1,0:T(8,128)(2,1)S(1)}, u32[]{:S(2)}, u32[]{:S(2)}) collective-permute-start(bf16[4,128,256]{2,1,0:T(8,128)(2,1)S(1)} %get-tuple-element.34.refs_1_), channel_id=1, source_target_pairs={{0,3},{1,0},{2,1},{3,2},{4,7},{5,4},{6,5},{7,6},{8,11},{9,8},{10,9... | collective-permute-start | bytes 786440 | tf_op jit(solution)/shard_map/ppermute | solution.py:412
  5.6 15.9 %collective-permute-start.2 = (bf16[4,128,256]{2,1,0:T(8,128)(2,1)S(1)}, bf16[4,128,256]{2,1,0:T(8,128)(2,1)S(1)}, u32[]{:S(2)}, u32[]{:S(2)}) collective-permute-start(bf16[4,128,256]{2,1,0:T(8,128)(2,1)S(1)} %get-tuple-element.33.refs_0_), channel_id=1, source_target_pairs={{0,3},{1,0},{2,1},{3,2},{4,7},{5,4},{6,5},{7,6},{8,11},{9,8},{10,9... | collective-permute-start | bytes 786440 | tf_op jit(solution)/shard_map/ppermute | solution.py:412
  7.0 14.5 %collective-permute-start.5 = (bf16[4,128,256]{2,1,0:T(8,128)(2,1)S(1)}, bf16[4,128,256]{2,1,0:T(8,128)(2,1)}, u32[]{:S(2)}, u32[]{:S(2)}) collective-permute-start(bf16[4,128,256]{2,1,0:T(8,128)(2,1)S(1)} %get-tuple-element.34.refs_1_), channel_id=1, source_target_pairs={{0,1},{1,2},{2,3},{3,0},{4,5},{5,6},{6,7},{7,4},{8,9},{9,10},{10,1... | collective-permute-start | bytes 786440 | tf_op jit(solution)/shard_map/ppermute | solution.py:408
  13.1 8.9 %collective-permute-start.4 = (bf16[4,128,256]{2,1,0:T(8,128)(2,1)S(1)}, bf16[4,128,256]{2,1,0:T(8,128)(2,1)}, u32[]{:S(2)}, u32[]{:S(2)}) collective-permute-start(bf16[4,128,256]{2,1,0:T(8,128)(2,1)S(1)} %collective-permute-done.1.refs_3_), channel_id=1, source_target_pairs={{0,3},{1,0},{2,1},{3,2},{4,7},{5,4},{6,5},{7,6},{8,11},{9,8},{10,9... | collective-permute-start | bytes 786440 | tf_op jit(solution)/shard_map/ppermute | solution.py:412
  15.1 6.9 %collective-permute-start.3 = (bf16[4,128,256]{2,1,0:T(8,128)(2,1)S(1)}, bf16[4,128,256]{2,1,0:T(8,128)(2,1)}, u32[]{:S(2)}, u32[]{:S(2)}) collective-permute-start(bf16[4,128,256]{2,1,0:T(8,128)(2,1)S(1)} %collective-permute-done.refs_6_), channel_id=1, source_target_pairs={{0,1},{1,2},{2,3},{3,0},{4,5},{5,6},{6,7},{7,4},{8,9},{9,10},{10,1... | collective-permute-start | bytes 786440 | tf_op jit(solution)/shard_map/ppermute | solution.py:408
  22.0 48.5 %copy-start = (f32[2,2048]{1,0:T(2,128)S(1)}, f32[2,2048]{1,0:T(2,128)}, u32[]{:S(2)}) copy-start(f32[2,2048]{1,0:T(2,128)} %b_ref.3) | copy-start | bytes 49156
  25.2 5.6 %collective-permute-start.6 = (bf16[256,512]{1,0:T(8,128)(2,1)S(1)}, bf16[256,512]{1,0:T(8,128)(2,1)S(1)}, u32[]{:S(2)}, u32[]{:S(2)}) collective-permute-start(bf16[256,512]{1,0:T(8,128)(2,1)S(1)} %get-tuple-element.46), channel_id=1, source_target_pairs={{0,4},{4,0},{1,5},{5,1},{2,6},{6,2},{3,7},{7,3},{8,12},{12,8},{9,1... | collective-permute-start | bytes 786440 | tf_op jit(solution)/shard_map/ppermute | solution.py:213
  64.9 5.6 %collective-permute-start.7 = (bf16[8,32,512]{2,1,0:T(8,128)(2,1)S(1)}, bf16[8,32,512]{2,1,0:T(8,128)(2,1)S(1)}, u32[]{:S(2)}, u32[]{:S(2)}) collective-permute-start(bf16[8,32,512]{2,1,0:T(8,128)(2,1)S(1)} %all_to_all.27.mine_ref), channel_id=1, source_target_pairs={{0,4},{4,0},{1,5},{5,1},{2,6},{6,2},{3,7},{7,3},{8,12},{12,8},{9,1... | collective-permute-start | bytes 786440 | tf_op jit(solution)/shard_map/ppermute | solution.py:213
  73.2 1.6 %collective-permute-start.8 = (bf16[256,512]{1,0:T(8,128)(2,1)S(1)}, bf16[256,512]{1,0:T(8,128)(2,1)S(1)}, u32[]{:S(2)}, u32[]{:S(2)}) collective-permute-start(bf16[256,512]{1,0:T(8,128)(2,1)S(1)} %get-tuple-element.49), channel_id=1, source_target_pairs={{0,4},{4,0},{1,5},{5,1},{2,6},{6,2},{3,7},{7,3},{8,12},{12,8},{9,1... | collective-permute-start | bytes 786440 | tf_op jit(solution)/shard_map/ppermute | solution.py:213
  83.9 7.3 %collective-permute-start.11 = (bf16[1,32,512]{2,1,0:T(8,128)(2,1)S(1)}, bf16[1,32,512]{2,1,0:T(8,128)(2,1)S(1)}, u32[]{:S(2)}, u32[]{:S(2)}) collective-permute-start(bf16[1,32,512]{2,1,0:T(8,128)(2,1)S(1)} %total.6.refs_0_), channel_id=1, source_target_pairs={{0,32},{16,48},{32,0},{48,16},{1,33},{17,49},{33,1},{49,17},{2,34}... | collective-permute-start | bytes 98312 | tf_op jit(solution)/shard_map/ppermute | solution.py:258
  84.9 6.4 %collective-permute-start.10 = (bf16[1,32,512]{2,1,0:T(8,128)(2,1)S(1)}, bf16[1,32,512]{2,1,0:T(8,128)(2,1)S(1)}, u32[]{:S(2)}, u32[]{:S(2)}) collective-permute-start(bf16[1,32,512]{2,1,0:T(8,128)(2,1)S(1)} %total.6.refs_0_), channel_id=1, source_target_pairs={{0,48},{16,0},{32,16},{48,32},{1,49},{17,1},{33,17},{49,33},{2,50}... | collective-permute-start | bytes 98312 | tf_op jit(solution)/shard_map/ppermute | solution.py:258
  87.6 5.5 %collective-permute-start.9 = (bf16[1,32,512]{2,1,0:T(8,128)(2,1)S(1)}, bf16[1,32,512]{2,1,0:T(8,128)(2,1)S(1)}, u32[]{:S(2)}, u32[]{:S(2)}) collective-permute-start(bf16[1,32,512]{2,1,0:T(8,128)(2,1)S(1)} %total.6.refs_0_), channel_id=1, source_target_pairs={{0,16},{16,32},{32,48},{48,0},{1,17},{17,33},{33,49},{49,1},{2,18}... | collective-permute-start | bytes 98312 | tf_op jit(solution)/shard_map/ppermute | solution.py:258
  102.2 4.9 %collective-permute-start.12 = (bf16[8,32,512]{2,1,0:T(8,128)(2,1)S(1)}, bf16[8,32,512]{2,1,0:T(8,128)(2,1)S(1)}, u32[]{:S(2)}, u32[]{:S(2)}) collective-permute-start(bf16[8,32,512]{2,1,0:T(8,128)(2,1)S(1)} %all_to_all.29.mine_ref), channel_id=1, source_target_pairs={{0,4},{4,0},{1,5},{5,1},{2,6},{6,2},{3,7},{7,3},{8,12},{12,8},{9,1... | collective-permute-start | bytes 786440 | tf_op jit(solution)/shard_map/ppermute | solution.py:213
  109.2 8.8 %collective-permute-start.17 = (bf16[4,128,256]{2,1,0:T(8,128)(2,1)S(1)}, bf16[4,128,256]{2,1,0:T(8,128)(2,1)S(1)}, u32[]{:S(2)}, u32[]{:S(2)}) collective-permute-start(bf16[4,128,256]{2,1,0:T(8,128)(2,1)S(1)} %get-tuple-element.61), channel_id=1, source_target_pairs={{0,1},{1,2},{2,3},{3,0},{4,5},{5,6},{6,7},{7,4},{8,9},{9,10},{10,1... | collective-permute-start | bytes 786440 | tf_op jit(solution)/shard_map/ppermute | solution.py:408
  109.3 8.9 %collective-permute-start.14 = (bf16[4,128,256]{2,1,0:T(8,128)(2,1)S(1)}, bf16[4,128,256]{2,1,0:T(8,128)(2,1)S(1)}, u32[]{:S(2)}, u32[]{:S(2)}) collective-permute-start(bf16[4,128,256]{2,1,0:T(8,128)(2,1)S(1)} %get-tuple-element.58), channel_id=1, source_target_pairs={{0,3},{1,0},{2,1},{3,2},{4,7},{5,4},{6,5},{7,6},{8,11},{9,8},{10,9... | collective-permute-start | bytes 786440 | tf_op jit(solution)/shard_map/ppermute | solution.py:412
  112.9 17.2 %collective-permute-start.13 = (bf16[4,128,256]{2,1,0:T(8,128)(2,1)S(1)}, bf16[4,128,256]{2,1,0:T(8,128)(2,1)S(1)}, u32[]{:S(2)}, u32[]{:S(2)}) collective-permute-start(bf16[4,128,256]{2,1,0:T(8,128)(2,1)S(1)} %get-tuple-element.56), channel_id=1, source_target_pairs={{0,1},{1,2},{2,3},{3,0},{4,5},{5,6},{6,7},{7,4},{8,9},{9,10},{10,1... | collective-permute-start | bytes 786440 | tf_op jit(solution)/shard_map/ppermute | solution.py:408
  113.0 9.5 %collective-permute-start.16 = (bf16[4,128,256]{2,1,0:T(8,128)(2,1)S(1)}, bf16[4,128,256]{2,1,0:T(8,128)(2,1)S(1)}, u32[]{:S(2)}, u32[]{:S(2)}) collective-permute-start(bf16[4,128,256]{2,1,0:T(8,128)(2,1)S(1)} %get-tuple-element.59), channel_id=1, source_target_pairs={{0,3},{1,0},{2,1},{3,2},{4,7},{5,4},{6,5},{7,6},{8,11},{9,8},{10,9... | collective-permute-start | bytes 786440 | tf_op jit(solution)/shard_map/ppermute | solution.py:412
  118.1 11.2 %collective-permute-start.18 = (bf16[4,128,256]{2,1,0:T(8,128)(2,1)S(1)}, bf16[4,128,256]{2,1,0:T(8,128)(2,1)S(1)}, u32[]{:S(2)}, u32[]{:S(2)}) collective-permute-start(bf16[4,128,256]{2,1,0:T(8,128)(2,1)S(1)} %add_convert_fusion), channel_id=1, source_target_pairs={{0,1},{1,2},{2,3},{3,0},{4,5},{5,6},{6,7},{7,4},{8,9},{9,10},{10,1... | collective-permute-start | bytes 786440 | tf_op jit(solution)/shard_map/ppermute | solution.py:408
  118.2 11.9 %collective-permute-start.15 = (bf16[4,128,256]{2,1,0:T(8,128)(2,1)S(1)}, bf16[4,128,256]{2,1,0:T(8,128)(2,1)S(1)}, u32[]{:S(2)}, u32[]{:S(2)}) collective-permute-start(bf16[4,128,256]{2,1,0:T(8,128)(2,1)S(1)} %add_convert_fusion.1), channel_id=1, source_target_pairs={{0,3},{1,0},{2,1},{3,2},{4,7},{5,4},{6,5},{7,6},{8,11},{9,8},{10,9... | collective-permute-start | bytes 786440 | tf_op jit(solution)/shard_map/ppermute | solution.py:412

commit v5 on v4

--- a/solution.py
+++ b/solution.py
@@ -68,10 +68,10 @@
 
 def counts_kernel(mine_ref, ids_ref, own_ref, *refs, first_table):
     if first_table:
-        edges_ref, *loads, out_ref, turned_ref = refs[: (len(refs) - 1) // 2]
-        loaded, (acc_ref, ids, own, sems) = refs[len(loads) + 3 : -4], refs[-4:]
+        edges_ref, *loads, out_ref = refs[: (len(refs) - 2) // 2]
+        loaded, (acc_ref, ids, own, sems) = refs[len(loads) + 2 : -4], refs[-4:]
     else:
-        out_ref, turned_ref, edges_ref, acc_ref, ids, own, sems = refs
+        out_ref, edges_ref, acc_ref, ids, own, sems = refs
         loads = loaded = ()
     samp, rows = acc_ref.shape
     tabs, entries = own.shape
@@ -112,9 +112,7 @@
             return carry
 
         lax.fori_loop(0, steps, body, 0)
-        total = acc_ref[...].astype(BF16)
-        out_ref[i] = total
-        turned_ref[i] = total.T
+        out_ref[i] = acc_ref[...].astype(BF16)
 
     for copy in copies[2:]:
         copy.wait()
@@ -125,12 +123,12 @@
     assert rows == 2 * samp and samp <= 256
     half = tabs // 2
     first = edges is None
-    out_shape = [pltpu.VMEM((half, samp, rows), BF16), pltpu.VMEM((half, rows, samp), BF16)]
+    out_shape = [pltpu.VMEM((half, samp, rows), BF16)]
     if first:
-        out_specs = [vmem(), vmem(), smem()]
+        out_specs = [vmem(), smem()]
         out_shape.append(jax.ShapeDtypeStruct((2 * tabs,), jnp.int32))
     else:
-        out_specs = [vmem()] * (2 + len(loads))
+        out_specs = [vmem()] * (1 + len(loads))
         out_shape += [pltpu.VMEM(arr.shape, arr.dtype) for arr in loads]
     return pl.pallas_call(
         functools.partial(counts_kernel, first_table=0 if first else half),
@@ -147,6 +145,24 @@
         cost_estimate=cost(half * samp * rows * 3072, 3 << 20),
         name="counts",
     )(mine, pinned(ids), pinned(owners), *([] if first else [edges, *map(pinned, loads)]))
+
+
+def turned_kernel(in_ref, out_ref, *, first):
+    for i in range(out_ref.shape[0]):
+        out_ref[i] = in_ref[first + i].T
+
+
+def turned_pair(counts, first):
+    half, samp, rows = counts.shape
+    return pl.pallas_call(
+        functools.partial(turned_kernel, first=first),
+        in_specs=[vmem()],
+        out_specs=vmem(),
+        out_shape=pltpu.VMEM((2, rows, samp), BF16),
+        compiler_params=params(8),
+        cost_estimate=cost(1 << 30, 1 << 20),
+        name="turned",
+    )(*kept(counts))
 
 
 WIDE = 512
@@ -258,16 +274,20 @@
     return lax.ppermute(arr, "zh", [(i, (i + k) & 3) for i in range(4)])
 
 
-def sum_all(keep, send, by_turns):
+def beside(arr, counts, first):
+    arr, counts = lax.optimization_barrier((arr, counts))
+    return lax.optimization_barrier((swap(arr, "c"), turned_pair(counts, first)))
+
+
+def sum_all(keep, send, counts, by_neighbours):
+    got, turned_front = beside(send, counts, 0)
     shape = pltpu.VMEM((CHUNKS,) + CHUNK, BF16)
-    parts = swap_all(small(cut_kernel, shape, "cut", keep, swap(send, "c")))
-    if by_turns:
-        own = total(1, parts)
-        near = (own, turn(own, 1), turn(own, 3), turn(own, 2))
-    else:
-        near = (lax.all_to_all(total(4, parts), "zh", 0, 0, tiled=True),)
-    mine = swap_all(total(CHUNKS, *near))
-    return mine, swap(mine, "c")
+    own = total(1, swap_all(small(cut_kernel, shape, "cut", keep, got)))
+    up, down = turn(own, 1), turn(own, 3)
+    far = turn(up, 1) if by_neighbours else turn(own, 2)
+    mine = swap_all(total(CHUNKS, own, up, down, far))
+    other, turned_back = beside(mine, counts, 2)
+    return mine, other, (turned_front, turned_back)
 
 
 def spread(core_ref, mine_ref, other_ref, in_ref):
@@ -316,8 +336,9 @@
     return jnp.dot(turned_ref[table, first : first + count, :], grad, preferred_element_type=F32)
 
 
-def far_kernel(core_ref, mine_ref, other_ref, b_ref, turned_a, turned_b, pooled, cot, x1, a, u_ref, v_ref, *refs):
-    crossed_ref, grad_ref, far_a, far_b, sums = refs
+def far_kernel(core_ref, mine_ref, other_ref, b_ref, *refs):
+    turned, refs = refs[:4], refs[4:]
+    pooled, cot, x1, a, u_ref, v_ref, crossed_ref, grad_ref, far_a, far_b, sums = refs
     half, rows, emb = far_a.shape
     spread(core_ref, mine_ref, other_ref, sums)
     for f in range(pooled.shape[1] // WIDE):
@@ -329,18 +350,19 @@
         grad_ref[:, at] = grad
         for i in range(2):
             side, t = divmod(2 * f + i, half)
-            part = row_grads((turned_a, turned_b)[side], t, 2 * rows, rows, grad[:, i * emb : (i + 1) * emb])
+            part = row_grads(turned[f], i, 2 * rows, rows, grad[:, i * emb : (i + 1) * emb])
             (far_a, far_b)[side][t] = part.astype(BF16)
 
 
 def far_rows(core, mine, other, bias, turned, pooled, cot, x1, a, u, v):
-    half, rows, samp = turned[0].shape
+    _, rows, samp = turned[0].shape
+    half = 2 * len(turned) // 2
     rank = v.shape[-1]
     feats = pooled.shape[1]
     piece = pltpu.VMEM((half, rows // 4, feats // (2 * half)), BF16)
     return pl.pallas_call(
         far_kernel,
-        in_specs=[smem()] + [vmem()] * 11,
+        in_specs=[smem()] + [vmem()] * 13,
         out_specs=[vmem()] * 4,
         out_shape=[pltpu.VMEM(pooled.shape, BF16)] * 2 + [piece, piece],
         scratch_shapes=[pltpu.VMEM((2, samp, rank), BF16)],
@@ -350,27 +372,29 @@
     )(core, mine, other, bias, *kept(*turned, pooled, cot, x1, a, u, v))
 
 
-def near_kernel(turned_a, turned_b, grad, made_ref, crossed_ref, p0_ref, p1_a, p1_b, p3_a, p3_b, sem):
+def near_kernel(*refs):
+    turned, refs = refs[:4], refs[4:]
+    grad, made_ref, crossed_ref, p0_ref, p1_a, p1_b, p3_a, p3_b, sem = refs
     copy = pltpu.make_async_copy(made_ref, crossed_ref, sem)
     copy.start()
     half, rows, emb = p1_a.shape
     for t in range(2 * half):
         side, at = divmod(t, half)
         part = grad[:, t * emb : (t + 1) * emb]
-        turned = (turned_a, turned_b)[side]
-        first = row_grads(turned, at, 0, 2 * rows, part)
+        first = row_grads(turned[t // 2], t % 2, 0, 2 * rows, part)
         p0_ref[t] = first[:rows]
         (p1_a, p1_b)[side][at] = first[rows:].astype(BF16)
-        (p3_a, p3_b)[side][at] = row_grads(turned, at, 3 * rows, rows, part).astype(BF16)
+        (p3_a, p3_b)[side][at] = row_grads(turned[t // 2], t % 2, 3 * rows, rows, part).astype(BF16)
     copy.wait()
 
 
 def near_rows(turned, grad, crossed):
-    half, rows, samp = turned[0].shape
+    _, rows, samp = turned[0].shape
+    half = 2 * len(turned) // 2
     block = (half, rows // 4, grad.shape[1] // (2 * half))
     return pl.pallas_call(
         near_kernel,
-        in_specs=[vmem()] * 4,
+        in_specs=[vmem()] * 6,
         out_specs=[anyspace()] + [vmem()] * 5,
         out_shape=[pltpu.HBM(crossed.shape, BF16), pltpu.VMEM((2 * half,) + block[1:], F32)]
         + [pltpu.VMEM(block, BF16)] * 4,
@@ -427,17 +451,17 @@
     own_a, own_b = cast_halves(emb_rows)
     left_a, right_b = right(own_a), left(own_b)
     left_b, right_a = right(own_b), left(own_a)
-    counts_a, turned_a, edges = make_counts(mine, entry_ids, entry_sample, samp, rows)
+    counts_a, edges = make_counts(mine, entry_ids, entry_sample, samp, rows)
     left_a, right_b, edges = lax.optimization_barrier((left_a, right_b, edges))
     far_a, far_b = right(left_a), left(right_b)
     loads = (cotangent, cross_v, cross_u)
-    counts_b, turned_b, cot, v, u = make_counts(mine, entry_ids, entry_sample, samp, rows, edges, loads)
+    counts_b, cot, v, u = make_counts(mine, entry_ids, entry_sample, samp, rows, edges, loads)
     embs = (own_a, own_b, right_a, right_b, far_a, far_b, left_a, left_b)
     pooled, keep, send = first_sums(core, (counts_a, counts_b), embs, cot, v, u)
-    sums = sum_all(keep, send, False)
+    *sums, turned_a = sum_all(keep, send, counts_a, True)
     x1, a, keep, send = middle(core, *sums, cross_bias, pooled, cot, u, v)
-    sums = sum_all(keep, send, True)
-    turned = (turned_a, turned_b)
+    *sums, turned_b = sum_all(keep, send, counts_b, False)
+    turned = (*turned_a, *turned_b)
     crossed, grad, p2a, p2b = far_rows(core, *sums, cross_bias, turned, pooled, cot, x1, a, u, v)
     from_left, from_right = right(p2a), left(p2b)
     crossed, p0, p1a, p1b, p3a, p3b = near_rows(turned, grad, crossed)

time: 131 us -> 128 us (0.977)
  blocking collectives: 52.1 us -> 37.5 us
  starting transfers between devices: 32.2 us -> 42.2 us
  waiting for transfers between devices: 21.2 us -> 24.3 us
  Pallas kernels: 24.5 us -> 22.4 us
    all_to_all x1 -> x0, blocking collectives: 14 us -> none  [sum_all(): near = (lax.all_to_all(total(4, parts), 'zh', 0, 0, tiled=True),)]
    ppermute x3 -> x6, starting transfers between devices: 3.69 us -> 13 us  [turn(): return lax.ppermute(arr, 'zh', [(i, i + k & 3) for i in range(4)])]
    ppermute x3 -> x6, waiting for transfers between devices: 5.47 us -> 8.66 us  [turn(): return lax.ppermute(arr, 'zh', [(i, i + k & 3) for i in range(4)])]
    pallas_call x2, Pallas kernels: 12.4 us -> 10.6 us  [make_counts(): pl.pallas_call(functools.partial(counts_kernel, first_table=0 if first el...]
    pallas_call x2 -> x6, Pallas kernels: 3.07 us -> 3.81 us  [the longest x1 2.1 us: far_rows(): pl.pallas_call(far_kernel, in_specs=[smem()] + [vmem()] * 13, out_specs=[...]
  transfers between devices with their start and end apart: 19 -> 22, of which waited for: 10 -> 15; matrix products, arithmetic and copies ran while one was open for 0% -> 0% of each run, Pallas kernels for 11% -> 10%
where the time goes in v5:
time: 128 us; the launch traced here: 127 us
  starting transfers between devices  42.2 us (33%)
  blocking collectives  37.5 us (29%)
  waiting for transfers between devices  24.3 us (19%)
  Pallas kernels  22.4 us (18%)
    all_to_all x4, blocking collectives, swap_all(): return lax.all_to_all(arr, ('x', 'zl'), 0, 0, tiled=True)  37.5 us
    ppermute x6, starting transfers between devices, left(): return lax.ppermute(arr, 'row', [(i, i + 3 & 3) for i in range(4)])  13.8 us
    ppermute x6, starting transfers between devices, turn(): return lax.ppermute(arr, 'zh', [(i, i + k & 3) for i in range(4)])  13 us
    ppermute x4, starting transfers between devices, swap(): return lax.ppermute(arr, axis, [(0, 1), (1, 0)])  12.3 us
    pallas_call x2, Pallas kernels, make_counts(): pl.pallas_call(functools.partial(counts_kernel, first_table=0 if first el...  10.6 us
    ppermute x6, waiting for transfers between devices, right(): return lax.ppermute(arr, 'row', [(i, i + 1 & 3) for i in range(4)])  9.31 us
    ppermute x6, waiting for transfers between devices, turn(): return lax.ppermute(arr, 'zh', [(i, i + k & 3) for i in range(4)])  8.66 us
    ppermute x4, waiting for transfers between devices, swap(): return lax.ppermute(arr, axis, [(0, 1), (1, 0)])  3.88 us
  transfers between devices with their start and end apart: 22, of which 15 were waited for; matrix products, arithmetic and copies ran while one was open for 0% of the time, Pallas kernels for 10%

profile of v5, /device:TPU:1, one launch (start us, length us, event | category | flops | bytes accessed | tf_op | source)
XLA Modules:
  0.0 127.4 jit_solution(18328789139863775826)
XLA Ops:
  0.6 1.2 cast.1
  1.9 2.2 %collective-permute-start = (bf16[4,128,256]{2,1,0:T(8,128)(2,1)S(1)}, bf16[4,128,256]{2,1,0:T(8,128)(2,1)S(1)}, u32[]{:S(2)}, u32[]{:S(2)}) collective-permute-start(bf16[4,128,256]{2,1,0:T(8,128)(2,1)S(1)} %get-tuple-element.47.refs_0_), channel_id=1, source_target_pairs={{0,1},{1,2},{2,3},{3,0},{4,5},{5,6},{6,7},{7,4},{8,9},{9,10},{10,1... | collective-permute-start | bytes 786440 | tf_op jit(solution)/shard_map/ppermute | solution.py:432
  4.1 1.5 %collective-permute-start.1 = (bf16[4,128,256]{2,1,0:T(8,128)(2,1)S(1)}, bf16[4,128,256]{2,1,0:T(8,128)(2,1)S(1)}, u32[]{:S(2)}, u32[]{:S(2)}) collective-permute-start(bf16[4,128,256]{2,1,0:T(8,128)(2,1)S(1)} %get-tuple-element.48.refs_1_), channel_id=1, source_target_pairs={{0,3},{1,0},{2,1},{3,2},{4,7},{5,4},{6,5},{7,6},{8,11},{9,8},{10,9... | collective-permute-start | bytes 786440 | tf_op jit(solution)/shard_map/ppermute | solution.py:436
  5.6 1.4 %collective-permute-start.2 = (bf16[4,128,256]{2,1,0:T(8,128)(2,1)S(1)}, bf16[4,128,256]{2,1,0:T(8,128)(2,1)S(1)}, u32[]{:S(2)}, u32[]{:S(2)}) collective-permute-start(bf16[4,128,256]{2,1,0:T(8,128)(2,1)S(1)} %get-tuple-element.47.refs_0_), channel_id=1, source_target_pairs={{0,3},{1,0},{2,1},{3,2},{4,7},{5,4},{6,5},{7,6},{8,11},{9,8},{10,9... | collective-permute-start | bytes 786440 | tf_op jit(solution)/shard_map/ppermute | solution.py:436
  7.1 5.3 %counts.2 = (bf16[4,256,512]{2,1,0:T(8,128)(2,1)S(1)}, s32[16]{0:T(128)S(1)}) custom-call(s32[1]{0:T(128)} %bitcast.1.mine_ref, s32[8,4096]{1,0:T(8,128)} %ids_ref.3, s32[8,4096]{1,0:T(8,128)} %own_ref.3), custom_call_target="tpu_custom_call" | custom-call | flops 1610612736 | bytes 3145728 | tf_op jit(solution)/shard_map/counts/pallas_call | solution.py:133
  12.5 3.4 %collective-permute-start.4 = (bf16[4,128,256]{2,1,0:T(8,128)(2,1)S(1)}, bf16[4,128,256]{2,1,0:T(8,128)(2,1)S(1)}, u32[]{:S(2)}, u32[]{:S(2)}) collective-permute-start(bf16[4,128,256]{2,1,0:T(8,128)(2,1)S(1)} %collective-permute-done.1.refs_3_), channel_id=1, source_target_pairs={{0,3},{1,0},{2,1},{3,2},{4,7},{5,4},{6,5},{7,6},{8,11},{9,8},{10,9... | collective-permute-start | bytes 786440 | tf_op jit(solution)/shard_map/ppermute | solution.py:436
  15.8 5.3 %counts.3 = (bf16[4,256,512]{2,1,0:T(8,128)(2,1)S(1)}, bf16[256,2048]{1,0:T(8,128)(2,1)S(1)}, bf16[2,2048,512]{2,1,0:T(8,128)(2,1)S(1)}, bf16[2,512,2048]{2,1,0:T(8,128)(2,1)S(1)}) custom-call(s32[1]{0:T(128)} %bitcast.1.mine_ref, s32[8,4096]{1,0:T(8,128)} %ids_ref.3, s32[8,4096]{1,0:T(8,128)} %own_ref.3, s32[16]{0:T(128)S(1)} %get-tuple-element.50.refs_0_, ...), custom_call_target="tpu_custom_call" | custom-call | flops 1610612736 | bytes 3145728 | tf_op jit(solution)/shard_map/counts/pallas_call | solution.py:133
  22.2 2.0 %first_sums.1 = (bf16[256,2048]{1,0:T(8,128)(2,1)S(1)}, f32[256,512]{1,0:T(8,128)S(1)}, bf16[256,512]{1,0:T(8,128)(2,1)S(1)}) custom-call(s32[1]{0:T(128)} %bitcast.core_ref, bf16[4,256,512]{2,1,0:T(8,128)(2,1)S(1)} %get-tuple-element.64.counts_a.in_ref, bf16[4,256,512]{2,1,0:T(8,128)(2,1)S(1)} %get-tuple-element.75.counts_b.in_ref, ...), custom_call_target="tpu_custom_call" | custom-call | flops 1610612736 | bytes 10485760 | tf_op jit(solution)/shard_map/first_sums/pallas_call | solution.py:213
  24.3 4.1 %collective-permute-start.6 = (bf16[256,512]{1,0:T(8,128)(2,1)S(1)}, bf16[256,512]{1,0:T(8,128)(2,1)S(1)}, u32[]{:S(2)}, u32[]{:S(2)}) collective-permute-start(bf16[256,512]{1,0:T(8,128)(2,1)S(1)} %get-tuple-element.58), channel_id=1, source_target_pairs={{0,4},{4,0},{1,5},{5,1},{2,6},{6,2},{3,7},{7,3},{8,12},{12,8},{9,1... | collective-permute-start | bytes 786440 | tf_op jit(solution)/shard_map/ppermute | solution.py:229
  29.6 10.4 %all_to_all.20.refs_0_ = bf16[8,32,512]{2,1,0:T(8,128)(2,1)S(1)} all-to-all(bf16[8,32,512]{2,1,0:T(8,128)(2,1)S(1)} %cut.2), channel_id=1, replica_groups=mesh['x'=4,'zh'=4,'zl'=2,'c'=2,'row'=4] {'x','zl'}, dimensions={0} | all-to-all | bytes 524288 | tf_op jit(solution)/shard_map/all_to_all | solution.py:270
  40.1 3.7 %collective-permute-start.7 = (bf16[1,32,512]{2,1,0:T(8,128)(2,1)S(1)}, bf16[1,32,512]{2,1,0:T(8,128)(2,1)S(1)}, u32[]{:S(2)}, u32[]{:S(2)}) collective-permute-start(bf16[1,32,512]{2,1,0:T(8,128)(2,1)S(1)} %total.4.refs_0_), channel_id=1, source_target_pairs={{0,16},{16,32},{32,48},{48,0},{1,17},{17,33},{33,49},{49,1},{2,18}... | collective-permute-start | bytes 98312 | tf_op jit(solution)/shard_map/ppermute | solution.py:274
  43.7 2.2 %collective-permute-start.8 = (bf16[1,32,512]{2,1,0:T(8,128)(2,1)S(1)}, bf16[1,32,512]{2,1,0:T(8,128)(2,1)S(1)}, u32[]{:S(2)}, u32[]{:S(2)}) collective-permute-start(bf16[1,32,512]{2,1,0:T(8,128)(2,1)S(1)} %total.4.refs_0_), channel_id=1, source_target_pairs={{0,48},{16,0},{32,16},{48,32},{1,49},{17,1},{33,17},{49,33},{2,50}... | collective-permute-start | bytes 98312 | tf_op jit(solution)/shard_map/ppermute | solution.py:274
  46.0 1.2 collective-permute-done.7.refs_1_
  48.0 4.4 %collective-permute-done.9.refs_3_ = bf16[1,32,512]{2,1,0:T(8,128)(2,1)S(1)} collective-permute-done((bf16[1,32,512]{2,1,0:T(8,128)(2,1)S(1)}, bf16[1,32,512]{2,1,0:T(8,128)(2,1)S(1)}, u32[]{:S(2)}, u32[]{:S(2)}) %collective-permute-start.9) | collective-permute-done | bytes 32800 | tf_op jit(solution)/shard_map/ppermute | solution.py:274
  52.4 8.9 %all_to_all.21.mine_ref = bf16[8,32,512]{2,1,0:T(8,128)(2,1)S(1)} all-to-all(bf16[8,32,512]{2,1,0:T(8,128)(2,1)S(1)} %total.5), channel_id=1, replica_groups=mesh['x'=4,'zh'=4,'zl'=2,'c'=2,'row'=4] {'x','zl'}, dimensions={0} | all-to-all | bytes 524288 | tf_op jit(solution)/shard_map/all_to_all | solution.py:270
  61.3 4.2 %collective-permute-start.10 = (bf16[8,32,512]{2,1,0:T(8,128)(2,1)S(1)}, bf16[8,32,512]{2,1,0:T(8,128)(2,1)S(1)}, u32[]{:S(2)}, u32[]{:S(2)}) collective-permute-start(bf16[8,32,512]{2,1,0:T(8,128)(2,1)S(1)} %all_to_all.21.mine_ref), channel_id=1, source_target_pairs={{0,4},{4,0},{1,5},{5,1},{2,6},{6,2},{3,7},{7,3},{8,12},{12,8},{9,1... | collective-permute-start | bytes 786440 | tf_op jit(solution)/shard_map/ppermute | solution.py:229
  66.7 2.7 %middle.1 = (bf16[256,2048]{1,0:T(8,128)(2,1)S(1)}, bf16[256,2048]{1,0:T(8,128)(2,1)S(1)}, f32[256,512]{1,0:T(8,128)S(1)}, bf16[256,512]{1,0:T(8,128)(2,1)S(1)}) custom-call(s32[1]{0:T(128)} %bitcast.core_ref, bf16[8,32,512]{2,1,0:T(8,128)(2,1)S(1)} %all_to_all.21.mine_ref, bf16[8,32,512]{2,1,0:T(8,128)(2,1)S(1)} %collective-permute-done.10.other_ref, ...), custom_call_target="tpu_custom_call" | custom-call | flops 2147483648 | bytes 8388608 | tf_op jit(solution)/shard_map/middle/pallas_call | solution.py:323
  71.1 9.0 %all_to_all.22.refs_0_ = bf16[8,32,512]{2,1,0:T(8,128)(2,1)S(1)} all-to-all(bf16[8,32,512]{2,1,0:T(8,128)(2,1)S(1)} %cut.3), channel_id=1, replica_groups=mesh['x'=4,'zh'=4,'zl'=2,'c'=2,'row'=4] {'x','zl'}, dimensions={0} | all-to-all | bytes 524288 | tf_op jit(solution)/shard_map/all_to_all | solution.py:270
  80.1 4.3 %collective-permute-start.14 = (bf16[1,32,512]{2,1,0:T(8,128)(2,1)S(1)}, bf16[1,32,512]{2,1,0:T(8,128)(2,1)S(1)}, u32[]{:S(2)}, u32[]{:S(2)}) collective-permute-start(bf16[1,32,512]{2,1,0:T(8,128)(2,1)S(1)} %total.6.refs_0_), channel_id=1, source_target_pairs={{0,32},{16,48},{32,0},{48,16},{1,33},{17,49},{33,1},{49,17},{2,34}... | collective-permute-start | bytes 98312 | tf_op jit(solution)/shard_map/ppermute | solution.py:274
  84.4 2.4 %collective-permute-start.12 = (bf16[1,32,512]{2,1,0:T(8,128)(2,1)S(1)}, bf16[1,32,512]{2,1,0:T(8,128)(2,1)S(1)}, u32[]{:S(2)}, u32[]{:S(2)}) collective-permute-start(bf16[1,32,512]{2,1,0:T(8,128)(2,1)S(1)} %total.6.refs_0_), channel_id=1, source_target_pairs={{0,16},{16,32},{32,48},{48,0},{1,17},{17,33},{33,49},{49,1},{2,18}... | collective-permute-start | bytes 98312 | tf_op jit(solution)/shard_map/ppermute | solution.py:274
  86.9 1.5 %collective-permute-done.13.refs_2_ = bf16[1,32,512]{2,1,0:T(8,128)(2,1)S(1)} collective-permute-done((bf16[1,32,512]{2,1,0:T(8,128)(2,1)S(1)}, bf16[1,32,512]{2,1,0:T(8,128)(2,1)S(1)}, u32[]{:S(2)}, u32[]{:S(2)}) %collective-permute-start.13) | collective-permute-done | bytes 32800 | tf_op jit(solution)/shard_map/ppermute | solution.py:274
  88.3 1.1 collective-permute-done.12.refs_1_
  89.4 9.1 %all_to_all.23.mine_ref = bf16[8,32,512]{2,1,0:T(8,128)(2,1)S(1)} all-to-all(bf16[8,32,512]{2,1,0:T(8,128)(2,1)S(1)} %total.7), channel_id=1, replica_groups=mesh['x'=4,'zh'=4,'zl'=2,'c'=2,'row'=4] {'x','zl'}, dimensions={0} | all-to-all | bytes 524288 | tf_op jit(solution)/shard_map/all_to_all | solution.py:270
  98.6 3.6 %collective-permute-start.15 = (bf16[8,32,512]{2,1,0:T(8,128)(2,1)S(1)}, bf16[8,32,512]{2,1,0:T(8,128)(2,1)S(1)}, u32[]{:S(2)}, u32[]{:S(2)}) collective-permute-start(bf16[8,32,512]{2,1,0:T(8,128)(2,1)S(1)} %all_to_all.23.mine_ref), channel_id=1, source_target_pairs={{0,4},{4,0},{1,5},{5,1},{2,6},{6,2},{3,7},{7,3},{8,12},{12,8},{9,1... | collective-permute-start | bytes 786440 | tf_op jit(solution)/shard_map/ppermute | solution.py:229
  103.3 2.1 %far_rows.1 = (bf16[256,2048]{1,0:T(8,128)(2,1)S(1)}, bf16[256,2048]{1,0:T(8,128)(2,1)S(1)}, bf16[4,128,256]{2,1,0:T(8,128)(2,1)S(1)}, bf16[4,128,256]{2,1,0:T(8,128)(2,1)S(1)}) custom-call(s32[1]{0:T(128)} %bitcast.core_ref, bf16[8,32,512]{2,1,0:T(8,128)(2,1)S(1)} %all_to_all.23.mine_ref, bf16[8,32,512]{2,1,0:T(8,128)(2,1)S(1)} %collective-permute-done.15.other_ref, ...), custom_call_target="tpu_custom_call" | custom-call | flops 1342177280 | bytes 7340032 | tf_op jit(solution)/shard_map/far_rows/pallas_call | solution.py:363
  106.0 2.2 %collective-permute-start.17 = (bf16[4,128,256]{2,1,0:T(8,128)(2,1)S(1)}, bf16[4,128,256]{2,1,0:T(8,128)(2,1)S(1)}, u32[]{:S(2)}, u32[]{:S(2)}) collective-permute-start(bf16[4,128,256]{2,1,0:T(8,128)(2,1)S(1)} %get-tuple-element.86), channel_id=1, source_target_pairs={{0,3},{1,0},{2,1},{3,2},{4,7},{5,4},{6,5},{7,6},{8,11},{9,8},{10,9... | collective-permute-start | bytes 786440 | tf_op jit(solution)/shard_map/ppermute | solution.py:436
  108.2 1.0 near_rows.1
  109.3 2.7 %collective-permute-start.19 = (bf16[4,128,256]{2,1,0:T(8,128)(2,1)S(1)}, bf16[4,128,256]{2,1,0:T(8,128)(2,1)S(1)}, u32[]{:S(2)}, u32[]{:S(2)}) collective-permute-start(bf16[4,128,256]{2,1,0:T(8,128)(2,1)S(1)} %get-tuple-element.87), channel_id=1, source_target_pairs={{0,3},{1,0},{2,1},{3,2},{4,7},{5,4},{6,5},{7,6},{8,11},{9,8},{10,9... | collective-permute-start | bytes 786440 | tf_op jit(solution)/shard_map/ppermute | solution.py:436
  111.9 2.3 %collective-permute-done.20 = bf16[4,128,256]{2,1,0:T(8,128)(2,1)S(1)} collective-permute-done((bf16[4,128,256]{2,1,0:T(8,128)(2,1)S(1)}, bf16[4,128,256]{2,1,0:T(8,128)(2,1)S(1)}, u32[]{:S(2)}, u32[]{:S(2)}) %collective-permute-start.20) | collective-permute-done | bytes 262176 | tf_op jit(solution)/shard_map/ppermute | solution.py:432
  114.5 2.7 %collective-permute-start.18 = (bf16[4,128,256]{2,1,0:T(8,128)(2,1)S(1)}, bf16[4,128,256]{2,1,0:T(8,128)(2,1)S(1)}, u32[]{:S(2)}, u32[]{:S(2)}) collective-permute-start(bf16[4,128,256]{2,1,0:T(8,128)(2,1)S(1)} %add_convert_fusion.1), channel_id=1, source_target_pairs={{0,3},{1,0},{2,1},{3,2},{4,7},{5,4},{6,5},{7,6},{8,11},{9,8},{10,9... | collective-permute-start | bytes 786440 | tf_op jit(solution)/shard_map/ppermute | solution.py:436
  117.2 1.6 %collective-permute-done.19.sum_ref = bf16[4,128,256]{2,1,0:T(8,128)(2,1)S(1)} collective-permute-done((bf16[4,128,256]{2,1,0:T(8,128)(2,1)S(1)}, bf16[4,128,256]{2,1,0:T(8,128)(2,1)S(1)}, u32[]{:S(2)}, u32[]{:S(2)}) %collective-permute-start.19) | collective-permute-done | bytes 262176 | tf_op jit(solution)/shard_map/ppermute | solution.py:436
  118.8 6.7 %collective-permute-done.21.far_ref = bf16[4,128,256]{2,1,0:T(8,128)(2,1)S(1)} collective-permute-done((bf16[4,128,256]{2,1,0:T(8,128)(2,1)S(1)}, bf16[4,128,256]{2,1,0:T(8,128)(2,1)S(1)}, u32[]{:S(2)}, u32[]{:S(2)}) %collective-permute-start.21) | collective-permute-done | bytes 262176 | tf_op jit(solution)/shard_map/ppermute | solution.py:432
  (39 shorter events, 10.1 us)
Async XLA Ops:
  1.9 10.6 %collective-permute-start = (bf16[4,128,256]{2,1,0:T(8,128)(2,1)S(1)}, bf16[4,128,256]{2,1,0:T(8,128)(2,1)S(1)}, u32[]{:S(2)}, u32[]{:S(2)}) collective-permute-start(bf16[4,128,256]{2,1,0:T(8,128)(2,1)S(1)} %get-tuple-element.47.refs_0_), channel_id=1, source_target_pairs={{0,1},{1,2},{2,3},{3,0},{4,5},{5,6},{6,7},{7,4},{8,9},{9,10},{10,1... | collective-permute-start | bytes 786440 | tf_op jit(solution)/shard_map/ppermute | solution.py:432
  4.1 8.4 %collective-permute-start.1 = (bf16[4,128,256]{2,1,0:T(8,128)(2,1)S(1)}, bf16[4,128,256]{2,1,0:T(8,128)(2,1)S(1)}, u32[]{:S(2)}, u32[]{:S(2)}) collective-permute-start(bf16[4,128,256]{2,1,0:T(8,128)(2,1)S(1)} %get-tuple-element.48.refs_1_), channel_id=1, source_target_pairs={{0,3},{1,0},{2,1},{3,2},{4,7},{5,4},{6,5},{7,6},{8,11},{9,8},{10,9... | collective-permute-start | bytes 786440 | tf_op jit(solution)/shard_map/ppermute | solution.py:436
  5.6 15.5 %collective-permute-start.2 = (bf16[4,128,256]{2,1,0:T(8,128)(2,1)S(1)}, bf16[4,128,256]{2,1,0:T(8,128)(2,1)S(1)}, u32[]{:S(2)}, u32[]{:S(2)}) collective-permute-start(bf16[4,128,256]{2,1,0:T(8,128)(2,1)S(1)} %get-tuple-element.47.refs_0_), channel_id=1, source_target_pairs={{0,3},{1,0},{2,1},{3,2},{4,7},{5,4},{6,5},{7,6},{8,11},{9,8},{10,9... | collective-permute-start | bytes 786440 | tf_op jit(solution)/shard_map/ppermute | solution.py:436
  7.0 14.1 %collective-permute-start.5 = (bf16[4,128,256]{2,1,0:T(8,128)(2,1)S(1)}, bf16[4,128,256]{2,1,0:T(8,128)(2,1)S(1)}, u32[]{:S(2)}, u32[]{:S(2)}) collective-permute-start(bf16[4,128,256]{2,1,0:T(8,128)(2,1)S(1)} %get-tuple-element.48.refs_1_), channel_id=1, source_target_pairs={{0,1},{1,2},{2,3},{3,0},{4,5},{5,6},{6,7},{7,4},{8,9},{9,10},{10,1... | collective-permute-start | bytes 786440 | tf_op jit(solution)/shard_map/ppermute | solution.py:432
  12.5 9.5 %collective-permute-start.4 = (bf16[4,128,256]{2,1,0:T(8,128)(2,1)S(1)}, bf16[4,128,256]{2,1,0:T(8,128)(2,1)S(1)}, u32[]{:S(2)}, u32[]{:S(2)}) collective-permute-start(bf16[4,128,256]{2,1,0:T(8,128)(2,1)S(1)} %collective-permute-done.1.refs_3_), channel_id=1, source_target_pairs={{0,3},{1,0},{2,1},{3,2},{4,7},{5,4},{6,5},{7,6},{8,11},{9,8},{10,9... | collective-permute-start | bytes 786440 | tf_op jit(solution)/shard_map/ppermute | solution.py:436
  15.8 6.4 %collective-permute-start.3 = (bf16[4,128,256]{2,1,0:T(8,128)(2,1)S(1)}, bf16[4,128,256]{2,1,0:T(8,128)(2,1)S(1)}, u32[]{:S(2)}, u32[]{:S(2)}) collective-permute-start(bf16[4,128,256]{2,1,0:T(8,128)(2,1)S(1)} %collective-permute-done.refs_6_), channel_id=1, source_target_pairs={{0,1},{1,2},{2,3},{3,0},{4,5},{5,6},{6,7},{7,4},{8,9},{9,10},{10,1... | collective-permute-start | bytes 786440 | tf_op jit(solution)/shard_map/ppermute | solution.py:432
  24.3 5.2 %collective-permute-start.6 = (bf16[256,512]{1,0:T(8,128)(2,1)S(1)}, bf16[256,512]{1,0:T(8,128)(2,1)S(1)}, u32[]{:S(2)}, u32[]{:S(2)}) collective-permute-start(bf16[256,512]{1,0:T(8,128)(2,1)S(1)} %get-tuple-element.58), channel_id=1, source_target_pairs={{0,4},{4,0},{1,5},{5,1},{2,6},{6,2},{3,7},{7,3},{8,12},{12,8},{9,1... | collective-permute-start | bytes 786440 | tf_op jit(solution)/shard_map/ppermute | solution.py:229
  28.5 38.2 %copy-start = (f32[2,2048]{1,0:T(2,128)S(1)}, f32[2,2048]{1,0:T(2,128)}, u32[]{:S(2)}) copy-start(f32[2,2048]{1,0:T(2,128)} %b_ref.3) | copy-start | bytes 49156
  40.1 7.1 %collective-permute-start.7 = (bf16[1,32,512]{2,1,0:T(8,128)(2,1)S(1)}, bf16[1,32,512]{2,1,0:T(8,128)(2,1)S(1)}, u32[]{:S(2)}, u32[]{:S(2)}) collective-permute-start(bf16[1,32,512]{2,1,0:T(8,128)(2,1)S(1)} %total.4.refs_0_), channel_id=1, source_target_pairs={{0,16},{16,32},{32,48},{48,0},{1,17},{17,33},{33,49},{49,1},{2,18}... | collective-permute-start | bytes 98312 | tf_op jit(solution)/shard_map/ppermute | solution.py:274
  43.7 4.2 %collective-permute-start.8 = (bf16[1,32,512]{2,1,0:T(8,128)(2,1)S(1)}, bf16[1,32,512]{2,1,0:T(8,128)(2,1)S(1)}, u32[]{:S(2)}, u32[]{:S(2)}) collective-permute-start(bf16[1,32,512]{2,1,0:T(8,128)(2,1)S(1)} %total.4.refs_0_), channel_id=1, source_target_pairs={{0,48},{16,0},{32,16},{48,32},{1,49},{17,1},{33,17},{49,33},{2,50}... | collective-permute-start | bytes 98312 | tf_op jit(solution)/shard_map/ppermute | solution.py:274
  47.2 5.2 %collective-permute-start.9 = (bf16[1,32,512]{2,1,0:T(8,128)(2,1)S(1)}, bf16[1,32,512]{2,1,0:T(8,128)(2,1)S(1)}, u32[]{:S(2)}, u32[]{:S(2)}) collective-permute-start(bf16[1,32,512]{2,1,0:T(8,128)(2,1)S(1)} %collective-permute-done.7.refs_1_), channel_id=1, source_target_pairs={{0,16},{16,32},{32,48},{48,0},{1,17},{17,33},{33,49},{49,1},{2,18}... | collective-permute-start | bytes 98312 | tf_op jit(solution)/shard_map/ppermute | solution.py:274
  61.3 5.4 %collective-permute-start.10 = (bf16[8,32,512]{2,1,0:T(8,128)(2,1)S(1)}, bf16[8,32,512]{2,1,0:T(8,128)(2,1)S(1)}, u32[]{:S(2)}, u32[]{:S(2)}) collective-permute-start(bf16[8,32,512]{2,1,0:T(8,128)(2,1)S(1)} %all_to_all.21.mine_ref), channel_id=1, source_target_pairs={{0,4},{4,0},{1,5},{5,1},{2,6},{6,2},{3,7},{7,3},{8,12},{12,8},{9,1... | collective-permute-start | bytes 786440 | tf_op jit(solution)/shard_map/ppermute | solution.py:229
  69.4 1.6 %collective-permute-start.11 = (bf16[256,512]{1,0:T(8,128)(2,1)S(1)}, bf16[256,512]{1,0:T(8,128)(2,1)S(1)}, u32[]{:S(2)}, u32[]{:S(2)}) collective-permute-start(bf16[256,512]{1,0:T(8,128)(2,1)S(1)} %get-tuple-element.69), channel_id=1, source_target_pairs={{0,4},{4,0},{1,5},{5,1},{2,6},{6,2},{3,7},{7,3},{8,12},{12,8},{9,1... | collective-permute-start | bytes 786440 | tf_op jit(solution)/shard_map/ppermute | solution.py:229
  80.1 6.8 %collective-permute-start.14 = (bf16[1,32,512]{2,1,0:T(8,128)(2,1)S(1)}, bf16[1,32,512]{2,1,0:T(8,128)(2,1)S(1)}, u32[]{:S(2)}, u32[]{:S(2)}) collective-permute-start(bf16[1,32,512]{2,1,0:T(8,128)(2,1)S(1)} %total.6.refs_0_), channel_id=1, source_target_pairs={{0,32},{16,48},{32,0},{48,16},{1,33},{17,49},{33,1},{49,17},{2,34}... | collective-permute-start | bytes 98312 | tf_op jit(solution)/shard_map/ppermute | solution.py:274
  84.4 4.0 %collective-permute-start.13 = (bf16[1,32,512]{2,1,0:T(8,128)(2,1)S(1)}, bf16[1,32,512]{2,1,0:T(8,128)(2,1)S(1)}, u32[]{:S(2)}, u32[]{:S(2)}) collective-permute-start(bf16[1,32,512]{2,1,0:T(8,128)(2,1)S(1)} %total.6.refs_0_), channel_id=1, source_target_pairs={{0,48},{16,0},{32,16},{48,32},{1,49},{17,1},{33,17},{49,33},{2,50}... | collective-permute-start | bytes 98312 | tf_op jit(solution)/shard_map/ppermute | solution.py:274
  84.4 5.0 %collective-permute-start.12 = (bf16[1,32,512]{2,1,0:T(8,128)(2,1)S(1)}, bf16[1,32,512]{2,1,0:T(8,128)(2,1)S(1)}, u32[]{:S(2)}, u32[]{:S(2)}) collective-permute-start(bf16[1,32,512]{2,1,0:T(8,128)(2,1)S(1)} %total.6.refs_0_), channel_id=1, source_target_pairs={{0,16},{16,32},{32,48},{48,0},{1,17},{17,33},{33,49},{49,1},{2,18}... | collective-permute-start | bytes 98312 | tf_op jit(solution)/shard_map/ppermute | solution.py:274
  98.6 4.8 %collective-permute-start.15 = (bf16[8,32,512]{2,1,0:T(8,128)(2,1)S(1)}, bf16[8,32,512]{2,1,0:T(8,128)(2,1)S(1)}, u32[]{:S(2)}, u32[]{:S(2)}) collective-permute-start(bf16[8,32,512]{2,1,0:T(8,128)(2,1)S(1)} %all_to_all.23.mine_ref), channel_id=1, source_target_pairs={{0,4},{4,0},{1,5},{5,1},{2,6},{6,2},{3,7},{7,3},{8,12},{12,8},{9,1... | collective-permute-start | bytes 786440 | tf_op jit(solution)/shard_map/ppermute | solution.py:229
  105.4 8.8 %collective-permute-start.20 = (bf16[4,128,256]{2,1,0:T(8,128)(2,1)S(1)}, bf16[4,128,256]{2,1,0:T(8,128)(2,1)S(1)}, u32[]{:S(2)}, u32[]{:S(2)}) collective-permute-start(bf16[4,128,256]{2,1,0:T(8,128)(2,1)S(1)} %get-tuple-element.89), channel_id=1, source_target_pairs={{0,1},{1,2},{2,3},{3,0},{4,5},{5,6},{6,7},{7,4},{8,9},{9,10},{10,1... | collective-permute-start | bytes 786440 | tf_op jit(solution)/shard_map/ppermute | solution.py:432
  106.0 8.4 %collective-permute-start.17 = (bf16[4,128,256]{2,1,0:T(8,128)(2,1)S(1)}, bf16[4,128,256]{2,1,0:T(8,128)(2,1)S(1)}, u32[]{:S(2)}, u32[]{:S(2)}) collective-permute-start(bf16[4,128,256]{2,1,0:T(8,128)(2,1)S(1)} %get-tuple-element.86), channel_id=1, source_target_pairs={{0,3},{1,0},{2,1},{3,2},{4,7},{5,4},{6,5},{7,6},{8,11},{9,8},{10,9... | collective-permute-start | bytes 786440 | tf_op jit(solution)/shard_map/ppermute | solution.py:436
  109.2 17.2 %collective-permute-start.16 = (bf16[4,128,256]{2,1,0:T(8,128)(2,1)S(1)}, bf16[4,128,256]{2,1,0:T(8,128)(2,1)S(1)}, u32[]{:S(2)}, u32[]{:S(2)}) collective-permute-start(bf16[4,128,256]{2,1,0:T(8,128)(2,1)S(1)} %get-tuple-element.84), channel_id=1, source_target_pairs={{0,1},{1,2},{2,3},{3,0},{4,5},{5,6},{6,7},{7,4},{8,9},{9,10},{10,1... | collective-permute-start | bytes 786440 | tf_op jit(solution)/shard_map/ppermute | solution.py:432
  109.3 9.6 %collective-permute-start.19 = (bf16[4,128,256]{2,1,0:T(8,128)(2,1)S(1)}, bf16[4,128,256]{2,1,0:T(8,128)(2,1)S(1)}, u32[]{:S(2)}, u32[]{:S(2)}) collective-permute-start(bf16[4,128,256]{2,1,0:T(8,128)(2,1)S(1)} %get-tuple-element.87), channel_id=1, source_target_pairs={{0,3},{1,0},{2,1},{3,2},{4,7},{5,4},{6,5},{7,6},{8,11},{9,8},{10,9... | collective-permute-start | bytes 786440 | tf_op jit(solution)/shard_map/ppermute | solution.py:436
  114.3 11.2 %collective-permute-start.21 = (bf16[4,128,256]{2,1,0:T(8,128)(2,1)S(1)}, bf16[4,128,256]{2,1,0:T(8,128)(2,1)S(1)}, u32[]{:S(2)}, u32[]{:S(2)}) collective-permute-start(bf16[4,128,256]{2,1,0:T(8,128)(2,1)S(1)} %add_convert_fusion), channel_id=1, source_target_pairs={{0,1},{1,2},{2,3},{3,0},{4,5},{5,6},{6,7},{7,4},{8,9},{9,10},{10,1... | collective-permute-start | bytes 786440 | tf_op jit(solution)/shard_map/ppermute | solution.py:432
  114.5 11.9 %collective-permute-start.18 = (bf16[4,128,256]{2,1,0:T(8,128)(2,1)S(1)}, bf16[4,128,256]{2,1,0:T(8,128)(2,1)S(1)}, u32[]{:S(2)}, u32[]{:S(2)}) collective-permute-start(bf16[4,128,256]{2,1,0:T(8,128)(2,1)S(1)} %add_convert_fusion.1), channel_id=1, source_target_pairs={{0,3},{1,0},{2,1},{3,2},{4,7},{5,4},{6,5},{7,6},{8,11},{9,8},{10,9... | collective-permute-start | bytes 786440 | tf_op jit(solution)/shard_map/ppermute | solution.py:436

commit v6 on v4

--- a/solution.py
+++ b/solution.py
@@ -67,86 +67,91 @@
 
 
 def counts_kernel(mine_ref, ids_ref, own_ref, *refs, first_table):
+    refs, (acc_ref, sems) = refs[:-2], refs[-2:]
     if first_table:
-        edges_ref, *loads, out_ref, turned_ref = refs[: (len(refs) - 1) // 2]
-        loaded, (acc_ref, ids, own, sems) = refs[len(loads) + 3 : -4], refs[-4:]
+        ids, own = ids_ref, own_ref
+        edges_ref, *loads = refs[: len(refs) // 2]
+        out_ref, turned_ref, *loaded = refs[len(refs) // 2 :]
+        copies = fetch(sems, zip(loads, loaded))
     else:
-        out_ref, turned_ref, edges_ref, acc_ref, ids, own, sems = refs
-        loads = loaded = ()
-    samp, rows = acc_ref.shape
+        out_ref, turned_ref, edges_ref, ids, own = refs
+        copies = fetch(sems, [(own_ref, own), (ids_ref, ids)])
+    _, rows, samp = acc_ref.shape
     tabs, entries = own.shape
     mine = mine_ref[0]
     low = mine * samp
     turn = mine * (rows // 4)
-    copies = fetch(sems, [(own_ref, own), (ids_ref, ids), *zip(loads, loaded)])
-    copies[0].wait()
     if not first_table:
+        copies[0].wait()
         owners = own[...]
         first = jnp.sum((owners < low).astype(jnp.int32), axis=1, keepdims=True)
         last = jnp.sum((owners < low + samp).astype(jnp.int32), axis=1, keepdims=True)
         for i in range(tabs):
             edges_ref[i] = first[i, 0]
             edges_ref[tabs + i] = last[i, 0]
-    copies[1].wait()
+        copies[1].wait()
     grid = lax.broadcasted_iota(jnp.int32, (samp, EB), 0).astype(F32).astype(BF16)
     one, zero = jnp.ones((), BF16), jnp.zeros((), BF16)
 
-    @pl.loop(0, out_ref.shape[0])
-    def _(i):
-        t = i + first_table
-        start = edges_ref[t] // 128
-        steps = (edges_ref[tabs + t] - start * 128 + EB - 1) // EB
-        start = jnp.minimum(start, (entries - steps * EB) // 128)
+    @pl.loop(0, out_ref.shape[0] // 2)
+    def _(pair):
+        tables = [first_table + 2 * pair + j for j in range(2)]
+        starts = [edges_ref[t] // 128 for t in tables]
+        spans = [edges_ref[tabs + t] - start * 128 for t, start in zip(tables, starts)]
+        steps = (jnp.maximum(*spans) + EB - 1) // EB
+        starts = [jnp.minimum(start, (entries - steps * EB) // 128) * 128 for start in starts]
         acc_ref[...] = jnp.zeros_like(acc_ref)
 
         def body(block, carry):
-            at = pl.ds(pl.multiple_of(start * 128 + block * EB, 128), EB)
-            who = own[pl.ds(t, 1), at] - low
-            row = (ids[pl.ds(t, 1), at] - turn) & (rows - 1)
-            hot = [
-                jnp.where(grid == values.astype(F32).astype(BF16), one, zero) for values in (who, row, row - samp)
-            ]
-            acc_ref[...] += lax.dot_general(
-                hot[0], jnp.concatenate(hot[1:], axis=0), NT, preferred_element_type=F32
-            )
+            for j, t in enumerate(tables):
+                at = pl.ds(pl.multiple_of(starts[j] + block * EB, 128), EB)
+                who = own[pl.ds(t, 1), at] - low
+                row = (ids[pl.ds(t, 1), at] - turn) & (rows - 1)
+                hot = [
+                    jnp.where(grid == values.astype(F32).astype(BF16), one, zero) for values in (who, row, row - samp)
+                ]
+                acc_ref[j] += lax.dot_general(
+                    jnp.concatenate(hot[1:], axis=0), hot[0], NT, preferred_element_type=F32
+                )
             return carry
 
         lax.fori_loop(0, steps, body, 0)
-        total = acc_ref[...].astype(BF16)
-        out_ref[i] = total
-        turned_ref[i] = total.T
-
-    for copy in copies[2:]:
-        copy.wait()
+        for j in range(2):
+            total = acc_ref[j].astype(BF16)
+            turned_ref[2 * pair + j] = total
+            out_ref[2 * pair + j] = total.T
+
+    if first_table:
+        for copy in copies:
+            copy.wait()
 
 
 def make_counts(mine, ids, owners, samp, rows, edges=None, loads=()):
     tabs, entries = ids.shape
     assert rows == 2 * samp and samp <= 256
     half = tabs // 2
-    first = edges is None
     out_shape = [pltpu.VMEM((half, samp, rows), BF16), pltpu.VMEM((half, rows, samp), BF16)]
-    if first:
-        out_specs = [vmem(), vmem(), smem()]
+    if edges is None:
+        args = (mine, pinned(ids), pinned(owners))
+        in_specs = [smem(), hbm(), hbm()]
+        out_specs = [vmem(), vmem(), smem(), vmem(), vmem()]
         out_shape.append(jax.ShapeDtypeStruct((2 * tabs,), jnp.int32))
+        out_shape += [pltpu.VMEM(ids.shape, jnp.int32)] * 2
     else:
+        args = (mine, *kept(ids, owners), edges, *map(pinned, loads))
+        in_specs = [smem(), vmem(), vmem(), smem()] + [hbm()] * len(loads)
         out_specs = [vmem()] * (2 + len(loads))
         out_shape += [pltpu.VMEM(arr.shape, arr.dtype) for arr in loads]
     return pl.pallas_call(
-        functools.partial(counts_kernel, first_table=0 if first else half),
-        in_specs=[smem(), hbm(), hbm()] + ([] if first else [smem()] + [hbm()] * len(loads)),
+        functools.partial(counts_kernel, first_table=0 if edges is None else half),
+        in_specs=in_specs,
         out_specs=out_specs,
         out_shape=out_shape,
-        scratch_shapes=[
-            pltpu.VMEM((samp, rows), F32),
-            pltpu.VMEM((tabs, entries), jnp.int32),
-            pltpu.VMEM((tabs, entries), jnp.int32),
-            pltpu.SemaphoreType.DMA((2 + len(loads),)),
-        ],
+        scratch_shapes=[pltpu.VMEM((2, rows, samp), F32), pltpu.SemaphoreType.DMA((max(2, len(loads)),))],
         compiler_params=params(16),
         cost_estimate=cost(half * samp * rows * 3072, 3 << 20),
         name="counts",
-    )(mine, pinned(ids), pinned(owners), *([] if first else [edges, *map(pinned, loads)]))
+    )(*args)
 
 
 WIDE = 512
@@ -258,14 +263,15 @@
     return lax.ppermute(arr, "zh", [(i, (i + k) & 3) for i in range(4)])
 
 
-def sum_all(keep, send, by_turns):
+def sum_all(keep, send, by_pairs):
     shape = pltpu.VMEM((CHUNKS,) + CHUNK, BF16)
     parts = swap_all(small(cut_kernel, shape, "cut", keep, swap(send, "c")))
-    if by_turns:
-        own = total(1, parts)
+    own = total(1, parts)
+    if by_pairs:
+        two = total(1, own, lax.ppermute(own, "zh", [(0, 1), (1, 0), (2, 3), (3, 2)]))
+        near = (two, lax.ppermute(two, "zh", [(0, 3), (3, 0), (1, 2), (2, 1)]))
+    else:
         near = (own, turn(own, 1), turn(own, 3), turn(own, 2))
-    else:
-        near = (lax.all_to_all(total(4, parts), "zh", 0, 0, tiled=True),)
     mine = swap_all(total(CHUNKS, *near))
     return mine, swap(mine, "c")
 
@@ -316,8 +322,9 @@
     return jnp.dot(turned_ref[table, first : first + count, :], grad, preferred_element_type=F32)
 
 
-def far_kernel(core_ref, mine_ref, other_ref, b_ref, turned_a, turned_b, pooled, cot, x1, a, u_ref, v_ref, *refs):
-    crossed_ref, grad_ref, far_a, far_b, sums = refs
+def far_kernel(core_ref, mine_ref, other_ref, b_ref, *refs):
+    turned, refs = refs[:2], refs[2:]
+    pooled, cot, x1, a, u_ref, v_ref, crossed_ref, grad_ref, far_a, far_b, sums = refs
     half, rows, emb = far_a.shape
     spread(core_ref, mine_ref, other_ref, sums)
     for f in range(pooled.shape[1] // WIDE):
@@ -329,7 +336,7 @@
         grad_ref[:, at] = grad
         for i in range(2):
             side, t = divmod(2 * f + i, half)
-            part = row_grads((turned_a, turned_b)[side], t, 2 * rows, rows, grad[:, i * emb : (i + 1) * emb])
+            part = row_grads(turned[side], t, 2 * rows, rows, grad[:, i * emb : (i + 1) * emb])
             (far_a, far_b)[side][t] = part.astype(BF16)
 
 
@@ -350,18 +357,19 @@
     )(core, mine, other, bias, *kept(*turned, pooled, cot, x1, a, u, v))
 
 
-def near_kernel(turned_a, turned_b, grad, made_ref, crossed_ref, p0_ref, p1_a, p1_b, p3_a, p3_b, sem):
+def near_kernel(*refs):
+    turned, refs = refs[:2], refs[2:]
+    grad, made_ref, crossed_ref, p0_ref, p1_a, p1_b, p3_a, p3_b, sem = refs
     copy = pltpu.make_async_copy(made_ref, crossed_ref, sem)
     copy.start()
     half, rows, emb = p1_a.shape
     for t in range(2 * half):
         side, at = divmod(t, half)
         part = grad[:, t * emb : (t + 1) * emb]
-        turned = (turned_a, turned_b)[side]
-        first = row_grads(turned, at, 0, 2 * rows, part)
+        first = row_grads(turned[side], at, 0, 2 * rows, part)
         p0_ref[t] = first[:rows]
         (p1_a, p1_b)[side][at] = first[rows:].astype(BF16)
-        (p3_a, p3_b)[side][at] = row_grads(turned, at, 3 * rows, rows, part).astype(BF16)
+        (p3_a, p3_b)[side][at] = row_grads(turned[side], at, 3 * rows, rows, part).astype(BF16)
     copy.wait()
 
 
@@ -427,11 +435,11 @@
     own_a, own_b = cast_halves(emb_rows)
     left_a, right_b = right(own_a), left(own_b)
     left_b, right_a = right(own_b), left(own_a)
-    counts_a, turned_a, edges = make_counts(mine, entry_ids, entry_sample, samp, rows)
+    counts_a, turned_a, edges, ids, owners = make_counts(mine, entry_ids, entry_sample, samp, rows)
     left_a, right_b, edges = lax.optimization_barrier((left_a, right_b, edges))
     far_a, far_b = right(left_a), left(right_b)
     loads = (cotangent, cross_v, cross_u)
-    counts_b, turned_b, cot, v, u = make_counts(mine, entry_ids, entry_sample, samp, rows, edges, loads)
+    counts_b, turned_b, cot, v, u = make_counts(mine, ids, owners, samp, rows, edges, loads)
     embs = (own_a, own_b, right_a, right_b, far_a, far_b, left_a, left_b)
     pooled, keep, send = first_sums(core, (counts_a, counts_b), embs, cot, v, u)
     sums = sum_all(keep, send, False)

time: 131 us -> 129 us (0.985)
  blocking collectives: 52.1 us -> 37.9 us
  starting transfers between devices: 32.2 us -> 41.8 us
  Pallas kernels: 24.5 us -> 21.4 us
  waiting for transfers between devices: 21.2 us -> 24.3 us
  local copies, waits for them, and re-layouts: 0.01 us -> 1.56 us
    all_to_all x1 -> x0, blocking collectives: 14 us -> none  [sum_all(): near = (lax.all_to_all(total(4, parts), 'zh', 0, 0, tiled=True),)]
    ppermute x0 -> x2, waiting for transfers between devices: none -> 5.05 us  [the longest x1 2.56 us: sum_all(): lax.ppermute(own, 'zh', [(0, 1), (1, 0), (2, 3), (3, 2)])]
    ppermute x3, starting transfers between devices: 3.69 us -> 8.73 us  [turn(): return lax.ppermute(arr, 'zh', [(i, i + k & 3) for i in range(4)])]
    ppermute x0 -> x2, starting transfers between devices: none -> 3.66 us  [the longest x1 2.46 us: sum_all(): near = (two, lax.ppermute(two, 'zh', [(0, 3), (3, 0), (1, 2), (2, 1)]))]
    pallas_call x2, Pallas kernels: 12.4 us -> 9.24 us  [make_counts(): pl.pallas_call(functools.partial(counts_kernel, first_table=0 if edges is...]
    ppermute x3, waiting for transfers between devices: 5.47 us -> 2.53 us  [turn(): return lax.ppermute(arr, 'zh', [(i, i + k & 3) for i in range(4)])]
    unnamed x2 -> x6, local copies, waits for them, and re-layouts: 0.01 us -> 1.56 us
  transfers between devices with their start and end apart: 19 -> 21, of which waited for: 10 -> 12; matrix products, arithmetic and copies ran while one was open for 0% -> 0% of each run, Pallas kernels for 11% -> 9%
where the time goes in v6:
time: 129 us; the launch traced here: 128 us
  starting transfers between devices  41.8 us (32%)
  blocking collectives  37.9 us (29%)
  waiting for transfers between devices  24.3 us (19%)
  Pallas kernels  21.4 us (17%)
  local copies, waits for them, and re-layouts  1.56 us (1%)
    all_to_all x4, blocking collectives, swap_all(): return lax.all_to_all(arr, ('x', 'zl'), 0, 0, tiled=True)  37.9 us
    ppermute x4, starting transfers between devices, swap(): return lax.ppermute(arr, axis, [(0, 1), (1, 0)])  13.4 us
    ppermute x6, starting transfers between devices, left(): return lax.ppermute(arr, 'row', [(i, i + 3 & 3) for i in range(4)])  13.2 us
    pallas_call x2, Pallas kernels, make_counts(): pl.pallas_call(functools.partial(counts_kernel, first_table=0 if edges is...  9.24 us
    ppermute x6, waiting for transfers between devices, right(): return lax.ppermute(arr, 'row', [(i, i + 1 & 3) for i in range(4)])  9 us
    ppermute x3, starting transfers between devices, turn(): return lax.ppermute(arr, 'zh', [(i, i + k & 3) for i in range(4)])  8.73 us
    ppermute x4, waiting for transfers between devices, swap(): return lax.ppermute(arr, axis, [(0, 1), (1, 0)])  4.65 us
    pallas_call x1, Pallas kernels, first_sums(): pl.pallas_call(first_kernel, in_specs=[smem()] + [vmem()] * 13, out_specs...  3.15 us
  transfers between devices with their start and end apart: 21, of which 12 were waited for; matrix products, arithmetic and copies ran while one was open for 0% of the time, Pallas kernels for 9%

profile of v6, /device:TPU:1, one launch (start us, length us, event | category | flops | bytes accessed | tf_op | source)
XLA Modules:
  0.0 128.1 jit_solution(2585554539880293847)
XLA Ops:
  0.6 1.2 cast.1
  1.9 2.2 %collective-permute-start = (bf16[4,128,256]{2,1,0:T(8,128)(2,1)S(1)}, bf16[4,128,256]{2,1,0:T(8,128)(2,1)S(1)}, u32[]{:S(2)}, u32[]{:S(2)}) collective-permute-start(bf16[4,128,256]{2,1,0:T(8,128)(2,1)S(1)} %get-tuple-element.37.refs_0_), channel_id=1, source_target_pairs={{0,1},{1,2},{2,3},{3,0},{4,5},{5,6},{6,7},{7,4},{8,9},{9,10},{10,1... | collective-permute-start | bytes 786440 | tf_op jit(solution)/shard_map/ppermute | solution.py:416
  4.1 1.5 %collective-permute-start.1 = (bf16[4,128,256]{2,1,0:T(8,128)(2,1)S(1)}, bf16[4,128,256]{2,1,0:T(8,128)(2,1)S(1)}, u32[]{:S(2)}, u32[]{:S(2)}) collective-permute-start(bf16[4,128,256]{2,1,0:T(8,128)(2,1)S(1)} %get-tuple-element.38.refs_1_), channel_id=1, source_target_pairs={{0,3},{1,0},{2,1},{3,2},{4,7},{5,4},{6,5},{7,6},{8,11},{9,8},{10,9... | collective-permute-start | bytes 786440 | tf_op jit(solution)/shard_map/ppermute | solution.py:420
  5.6 1.4 %collective-permute-start.2 = (bf16[4,128,256]{2,1,0:T(8,128)(2,1)S(1)}, bf16[4,128,256]{2,1,0:T(8,128)(2,1)S(1)}, u32[]{:S(2)}, u32[]{:S(2)}) collective-permute-start(bf16[4,128,256]{2,1,0:T(8,128)(2,1)S(1)} %get-tuple-element.37.refs_0_), channel_id=1, source_target_pairs={{0,3},{1,0},{2,1},{3,2},{4,7},{5,4},{6,5},{7,6},{8,11},{9,8},{10,9... | collective-permute-start | bytes 786440 | tf_op jit(solution)/shard_map/ppermute | solution.py:420
  7.1 4.9 %counts.2 = (bf16[4,256,512]{2,1,0:T(8,128)(2,1)S(1)}, bf16[4,512,256]{2,1,0:T(8,128)(2,1)S(1)}, s32[16]{0:T(128)S(1)}, s32[8,4096]{1,0:T(8,128)S(1)}, s32[8,4096]{1,0:T(8,128)S(1)}) custom-call(s32[1]{0:T(128)} %bitcast.mine_ref, s32[8,4096]{1,0:T(8,128)} %ids_ref.1, s32[8,4096]{1,0:T(8,128)} %own_ref.1), custom_call_target="tpu_custom_call" | custom-call | flops 1610612736 | bytes 3145728 | tf_op jit(solution)/shard_map/counts/pallas_call | solution.py:145
  12.7 2.6 %collective-permute-start.4 = (bf16[4,128,256]{2,1,0:T(8,128)(2,1)S(1)}, bf16[4,128,256]{2,1,0:T(8,128)(2,1)}, u32[]{:S(2)}, u32[]{:S(2)}) collective-permute-start(bf16[4,128,256]{2,1,0:T(8,128)(2,1)S(1)} %collective-permute-done.1.refs_3_), channel_id=1, source_target_pairs={{0,3},{1,0},{2,1},{3,2},{4,7},{5,4},{6,5},{7,6},{8,11},{9,8},{10,9... | collective-permute-start | bytes 786440 | tf_op jit(solution)/shard_map/ppermute | solution.py:420
  16.2 4.3 %counts.3 = (bf16[4,256,512]{2,1,0:T(8,128)(2,1)S(1)}, bf16[4,512,256]{2,1,0:T(8,128)(2,1)S(1)}, bf16[256,2048]{1,0:T(8,128)(2,1)S(1)}, bf16[2,2048,512]{2,1,0:T(8,128)(2,1)S(1)}, bf16[2,512,2048]{2,1,0:T(8,128)(2,1)S(1)}) custom-call(s32[1]{0:T(128)} %bitcast.mine_ref, s32[8,4096]{1,0:T(8,128)S(1)} %get-tuple-element.35.ids_ref, s32[8,4096]{1,0:T(8,128)S(1)} %copy-done.1, ...), custom_call_target="tpu_custom_call" | custom-call | flops 1610612736 | bytes 3145728 | tf_op jit(solution)/shard_map/counts/pallas_call | solution.py:145
  20.5 1.5 %collective-permute-done.4.refs_5_ = bf16[4,128,256]{2,1,0:T(8,128)(2,1)} collective-permute-done((bf16[4,128,256]{2,1,0:T(8,128)(2,1)S(1)}, bf16[4,128,256]{2,1,0:T(8,128)(2,1)}, u32[]{:S(2)}, u32[]{:S(2)}) %collective-permute-start.4) | collective-permute-done | bytes 262176 | tf_op jit(solution)/shard_map/ppermute | solution.py:420
  22.0 3.2 %first_sums.1 = (bf16[256,2048]{1,0:T(8,128)(2,1)S(1)}, f32[256,512]{1,0:T(8,128)S(1)}, bf16[256,512]{1,0:T(8,128)(2,1)S(1)}) custom-call(s32[1]{0:T(128)} %bitcast.1.core_ref, bf16[4,256,512]{2,1,0:T(8,128)(2,1)S(1)} %get-tuple-element.42.counts_a, bf16[4,256,512]{2,1,0:T(8,128)(2,1)S(1)} %get-tuple-element.43.counts_b, ...), custom_call_target="tpu_custom_call" | custom-call | flops 1610612736 | bytes 10485760 | tf_op jit(solution)/shard_map/first_sums/pallas_call | solution.py:202
  25.2 4.4 %collective-permute-start.6 = (bf16[256,512]{1,0:T(8,128)(2,1)S(1)}, bf16[256,512]{1,0:T(8,128)(2,1)S(1)}, u32[]{:S(2)}, u32[]{:S(2)}) collective-permute-start(bf16[256,512]{1,0:T(8,128)(2,1)S(1)} %get-tuple-element.50), channel_id=1, source_target_pairs={{0,4},{4,0},{1,5},{5,1},{2,6},{6,2},{3,7},{7,3},{8,12},{12,8},{9,1... | collective-permute-start | bytes 786440 | tf_op jit(solution)/shard_map/ppermute | solution.py:218
  29.6 1.2 collective-permute-done.6.got_ref
  30.8 10.6 %all_to_all.20.refs_0_ = bf16[8,32,512]{2,1,0:T(8,128)(2,1)S(1)} all-to-all(bf16[8,32,512]{2,1,0:T(8,128)(2,1)S(1)} %cut.2), channel_id=1, replica_groups=mesh['x'=4,'zh'=4,'zl'=2,'c'=2,'row'=4] {'x','zl'}, dimensions={0} | all-to-all | bytes 524288 | tf_op jit(solution)/shard_map/all_to_all | solution.py:259
  41.4 6.4 %collective-permute-start.9 = (bf16[1,32,512]{2,1,0:T(8,128)(2,1)S(1)}, bf16[1,32,512]{2,1,0:T(8,128)(2,1)S(1)}, u32[]{:S(2)}, u32[]{:S(2)}) collective-permute-start(bf16[1,32,512]{2,1,0:T(8,128)(2,1)S(1)} %total.5.refs_0_), channel_id=1, source_target_pairs={{0,32},{16,48},{32,0},{48,16},{1,33},{17,49},{33,1},{49,17},{2,34}... | collective-permute-start | bytes 98312 | tf_op jit(solution)/shard_map/ppermute | solution.py:263
  47.8 2.4 %collective-permute-start.7 = (bf16[1,32,512]{2,1,0:T(8,128)(2,1)S(1)}, bf16[1,32,512]{2,1,0:T(8,128)(2,1)S(1)}, u32[]{:S(2)}, u32[]{:S(2)}) collective-permute-start(bf16[1,32,512]{2,1,0:T(8,128)(2,1)S(1)} %total.5.refs_0_), channel_id=1, source_target_pairs={{0,16},{16,32},{32,48},{48,0},{1,17},{17,33},{33,49},{49,1},{2,18}... | collective-permute-start | bytes 98312 | tf_op jit(solution)/shard_map/ppermute | solution.py:263
  50.1 1.8 %collective-permute-done.8.refs_2_ = bf16[1,32,512]{2,1,0:T(8,128)(2,1)S(1)} collective-permute-done((bf16[1,32,512]{2,1,0:T(8,128)(2,1)S(1)}, bf16[1,32,512]{2,1,0:T(8,128)(2,1)S(1)}, u32[]{:S(2)}, u32[]{:S(2)}) %collective-permute-start.8) | collective-permute-done | bytes 32800 | tf_op jit(solution)/shard_map/ppermute | solution.py:263
  52.7 9.0 %all_to_all.21.mine_ref = bf16[8,32,512]{2,1,0:T(8,128)(2,1)S(1)} all-to-all(bf16[8,32,512]{2,1,0:T(8,128)(2,1)S(1)} %total.6), channel_id=1, replica_groups=mesh['x'=4,'zh'=4,'zl'=2,'c'=2,'row'=4] {'x','zl'}, dimensions={0} | all-to-all | bytes 524288 | tf_op jit(solution)/shard_map/all_to_all | solution.py:259
  61.7 4.0 %collective-permute-start.10 = (bf16[8,32,512]{2,1,0:T(8,128)(2,1)S(1)}, bf16[8,32,512]{2,1,0:T(8,128)(2,1)S(1)}, u32[]{:S(2)}, u32[]{:S(2)}) collective-permute-start(bf16[8,32,512]{2,1,0:T(8,128)(2,1)S(1)} %all_to_all.21.mine_ref), channel_id=1, source_target_pairs={{0,4},{4,0},{1,5},{5,1},{2,6},{6,2},{3,7},{7,3},{8,12},{12,8},{9,1... | collective-permute-start | bytes 786440 | tf_op jit(solution)/shard_map/ppermute | solution.py:218
  66.9 2.7 %middle.1 = (bf16[256,2048]{1,0:T(8,128)(2,1)S(1)}, bf16[256,2048]{1,0:T(8,128)(2,1)S(1)}, f32[256,512]{1,0:T(8,128)S(1)}, bf16[256,512]{1,0:T(8,128)(2,1)S(1)}) custom-call(s32[1]{0:T(128)} %bitcast.1.core_ref, bf16[8,32,512]{2,1,0:T(8,128)(2,1)S(1)} %all_to_all.21.mine_ref, bf16[8,32,512]{2,1,0:T(8,128)(2,1)S(1)} %collective-permute-done.10.other_ref, ...), custom_call_target="tpu_custom_call" | custom-call | flops 2147483648 | bytes 8388608 | tf_op jit(solution)/shard_map/middle/pallas_call | solution.py:309
  71.3 9.0 %all_to_all.22.refs_0_ = bf16[8,32,512]{2,1,0:T(8,128)(2,1)S(1)} all-to-all(bf16[8,32,512]{2,1,0:T(8,128)(2,1)S(1)} %cut.3), channel_id=1, replica_groups=mesh['x'=4,'zh'=4,'zl'=2,'c'=2,'row'=4] {'x','zl'}, dimensions={0} | all-to-all | bytes 524288 | tf_op jit(solution)/shard_map/all_to_all | solution.py:259
  80.3 1.2 collective-permute-start.12
  81.5 2.6 %collective-permute-done.12.refs_1_ = bf16[1,32,512]{2,1,0:T(8,128)(2,1)S(1)} collective-permute-done((bf16[1,32,512]{2,1,0:T(8,128)(2,1)S(1)}, bf16[1,32,512]{2,1,0:T(8,128)(2,1)S(1)}, u32[]{:S(2)}, u32[]{:S(2)}) %collective-permute-start.12) | collective-permute-done | bytes 32800 | tf_op jit(solution)/shard_map/ppermute | solution.py:271
  84.1 2.5 %collective-permute-start.13 = (bf16[1,32,512]{2,1,0:T(8,128)(2,1)S(1)}, bf16[1,32,512]{2,1,0:T(8,128)(2,1)S(1)}, u32[]{:S(2)}, u32[]{:S(2)}) collective-permute-start(bf16[1,32,512]{2,1,0:T(8,128)(2,1)S(1)} %total.8.refs_0_), channel_id=1, source_target_pairs={{0,48},{48,0},{16,32},{32,16},{1,49},{49,1},{17,33},{33,17},{2,50}... | collective-permute-start | bytes 98312 | tf_op jit(solution)/shard_map/ppermute | solution.py:272
  86.6 2.5 %collective-permute-done.13.refs_1_ = bf16[1,32,512]{2,1,0:T(8,128)(2,1)S(1)} collective-permute-done((bf16[1,32,512]{2,1,0:T(8,128)(2,1)S(1)}, bf16[1,32,512]{2,1,0:T(8,128)(2,1)S(1)}, u32[]{:S(2)}, u32[]{:S(2)}) %collective-permute-start.13) | collective-permute-done | bytes 32800 | tf_op jit(solution)/shard_map/ppermute | solution.py:272
  89.1 9.3 %all_to_all.23.mine_ref = bf16[8,32,512]{2,1,0:T(8,128)(2,1)S(1)} all-to-all(bf16[8,32,512]{2,1,0:T(8,128)(2,1)S(1)} %total.9), channel_id=1, replica_groups=mesh['x'=4,'zh'=4,'zl'=2,'c'=2,'row'=4] {'x','zl'}, dimensions={0} | all-to-all | bytes 524288 | tf_op jit(solution)/shard_map/all_to_all | solution.py:259
  98.4 4.5 %collective-permute-start.14 = (bf16[8,32,512]{2,1,0:T(8,128)(2,1)S(1)}, bf16[8,32,512]{2,1,0:T(8,128)(2,1)S(1)}, u32[]{:S(2)}, u32[]{:S(2)}) collective-permute-start(bf16[8,32,512]{2,1,0:T(8,128)(2,1)S(1)} %all_to_all.23.mine_ref), channel_id=1, source_target_pairs={{0,4},{4,0},{1,5},{5,1},{2,6},{6,2},{3,7},{7,3},{8,12},{12,8},{9,1... | collective-permute-start | bytes 786440 | tf_op jit(solution)/shard_map/ppermute | solution.py:218
  104.0 2.1 %far_rows.1 = (bf16[256,2048]{1,0:T(8,128)(2,1)S(1)}, bf16[256,2048]{1,0:T(8,128)(2,1)S(1)}, bf16[4,128,256]{2,1,0:T(8,128)(2,1)S(1)}, bf16[4,128,256]{2,1,0:T(8,128)(2,1)S(1)}) custom-call(s32[1]{0:T(128)} %bitcast.1.core_ref, bf16[8,32,512]{2,1,0:T(8,128)(2,1)S(1)} %all_to_all.23.mine_ref, bf16[8,32,512]{2,1,0:T(8,128)(2,1)S(1)} %collective-permute-done.14.other_ref, ...), custom_call_target="tpu_custom_call" | custom-call | flops 1342177280 | bytes 7340032 | tf_op jit(solution)/shard_map/far_rows/pallas_call | solution.py:348
  106.6 2.3 %collective-permute-start.16 = (bf16[4,128,256]{2,1,0:T(8,128)(2,1)S(1)}, bf16[4,128,256]{2,1,0:T(8,128)(2,1)S(1)}, u32[]{:S(2)}, u32[]{:S(2)}) collective-permute-start(bf16[4,128,256]{2,1,0:T(8,128)(2,1)S(1)} %get-tuple-element.62), channel_id=1, source_target_pairs={{0,3},{1,0},{2,1},{3,2},{4,7},{5,4},{6,5},{7,6},{8,11},{9,8},{10,9... | collective-permute-start | bytes 786440 | tf_op jit(solution)/shard_map/ppermute | solution.py:420
  109.9 2.7 %collective-permute-start.18 = (bf16[4,128,256]{2,1,0:T(8,128)(2,1)S(1)}, bf16[4,128,256]{2,1,0:T(8,128)(2,1)S(1)}, u32[]{:S(2)}, u32[]{:S(2)}) collective-permute-start(bf16[4,128,256]{2,1,0:T(8,128)(2,1)S(1)} %get-tuple-element.63), channel_id=1, source_target_pairs={{0,3},{1,0},{2,1},{3,2},{4,7},{5,4},{6,5},{7,6},{8,11},{9,8},{10,9... | collective-permute-start | bytes 786440 | tf_op jit(solution)/shard_map/ppermute | solution.py:420
  112.6 2.3 %collective-permute-done.19 = bf16[4,128,256]{2,1,0:T(8,128)(2,1)S(1)} collective-permute-done((bf16[4,128,256]{2,1,0:T(8,128)(2,1)S(1)}, bf16[4,128,256]{2,1,0:T(8,128)(2,1)S(1)}, u32[]{:S(2)}, u32[]{:S(2)}) %collective-permute-start.19) | collective-permute-done | bytes 262176 | tf_op jit(solution)/shard_map/ppermute | solution.py:416
  115.1 2.7 %collective-permute-start.17 = (bf16[4,128,256]{2,1,0:T(8,128)(2,1)S(1)}, bf16[4,128,256]{2,1,0:T(8,128)(2,1)S(1)}, u32[]{:S(2)}, u32[]{:S(2)}) collective-permute-start(bf16[4,128,256]{2,1,0:T(8,128)(2,1)S(1)} %add_convert_fusion.1), channel_id=1, source_target_pairs={{0,3},{1,0},{2,1},{3,2},{4,7},{5,4},{6,5},{7,6},{8,11},{9,8},{10,9... | collective-permute-start | bytes 786440 | tf_op jit(solution)/shard_map/ppermute | solution.py:420
  117.9 1.6 %collective-permute-done.18.sum_ref = bf16[4,128,256]{2,1,0:T(8,128)(2,1)S(1)} collective-permute-done((bf16[4,128,256]{2,1,0:T(8,128)(2,1)S(1)}, bf16[4,128,256]{2,1,0:T(8,128)(2,1)S(1)}, u32[]{:S(2)}, u32[]{:S(2)}) %collective-permute-start.18) | collective-permute-done | bytes 262176 | tf_op jit(solution)/shard_map/ppermute | solution.py:420
  119.5 6.7 %collective-permute-done.20.far_ref = bf16[4,128,256]{2,1,0:T(8,128)(2,1)S(1)} collective-permute-done((bf16[4,128,256]{2,1,0:T(8,128)(2,1)S(1)}, bf16[4,128,256]{2,1,0:T(8,128)(2,1)S(1)}, u32[]{:S(2)}, u32[]{:S(2)}) %collective-permute-start.20) | collective-permute-done | bytes 262176 | tf_op jit(solution)/shard_map/ppermute | solution.py:416
  (38 shorter events, 10.1 us)
Async XLA Ops:
  1.9 10.8 %collective-permute-start = (bf16[4,128,256]{2,1,0:T(8,128)(2,1)S(1)}, bf16[4,128,256]{2,1,0:T(8,128)(2,1)S(1)}, u32[]{:S(2)}, u32[]{:S(2)}) collective-permute-start(bf16[4,128,256]{2,1,0:T(8,128)(2,1)S(1)} %get-tuple-element.37.refs_0_), channel_id=1, source_target_pairs={{0,1},{1,2},{2,3},{3,0},{4,5},{5,6},{6,7},{7,4},{8,9},{9,10},{10,1... | collective-permute-start | bytes 786440 | tf_op jit(solution)/shard_map/ppermute | solution.py:416
  4.1 8.6 %collective-permute-start.1 = (bf16[4,128,256]{2,1,0:T(8,128)(2,1)S(1)}, bf16[4,128,256]{2,1,0:T(8,128)(2,1)S(1)}, u32[]{:S(2)}, u32[]{:S(2)}) collective-permute-start(bf16[4,128,256]{2,1,0:T(8,128)(2,1)S(1)} %get-tuple-element.38.refs_1_), channel_id=1, source_target_pairs={{0,3},{1,0},{2,1},{3,2},{4,7},{5,4},{6,5},{7,6},{8,11},{9,8},{10,9... | collective-permute-start | bytes 786440 | tf_op jit(solution)/shard_map/ppermute | solution.py:420
  5.6 14.9 %collective-permute-start.2 = (bf16[4,128,256]{2,1,0:T(8,128)(2,1)S(1)}, bf16[4,128,256]{2,1,0:T(8,128)(2,1)S(1)}, u32[]{:S(2)}, u32[]{:S(2)}) collective-permute-start(bf16[4,128,256]{2,1,0:T(8,128)(2,1)S(1)} %get-tuple-element.37.refs_0_), channel_id=1, source_target_pairs={{0,3},{1,0},{2,1},{3,2},{4,7},{5,4},{6,5},{7,6},{8,11},{9,8},{10,9... | collective-permute-start | bytes 786440 | tf_op jit(solution)/shard_map/ppermute | solution.py:420
  7.0 13.5 %collective-permute-start.5 = (bf16[4,128,256]{2,1,0:T(8,128)(2,1)S(1)}, bf16[4,128,256]{2,1,0:T(8,128)(2,1)}, u32[]{:S(2)}, u32[]{:S(2)}) collective-permute-start(bf16[4,128,256]{2,1,0:T(8,128)(2,1)S(1)} %get-tuple-element.38.refs_1_), channel_id=1, source_target_pairs={{0,1},{1,2},{2,3},{3,0},{4,5},{5,6},{6,7},{7,4},{8,9},{9,10},{10,1... | collective-permute-start | bytes 786440 | tf_op jit(solution)/shard_map/ppermute | solution.py:416
  12.0 0.7 copy-start
  12.7 9.4 %collective-permute-start.4 = (bf16[4,128,256]{2,1,0:T(8,128)(2,1)S(1)}, bf16[4,128,256]{2,1,0:T(8,128)(2,1)}, u32[]{:S(2)}, u32[]{:S(2)}) collective-permute-start(bf16[4,128,256]{2,1,0:T(8,128)(2,1)S(1)} %collective-permute-done.1.refs_3_), channel_id=1, source_target_pairs={{0,3},{1,0},{2,1},{3,2},{4,7},{5,4},{6,5},{7,6},{8,11},{9,8},{10,9... | collective-permute-start | bytes 786440 | tf_op jit(solution)/shard_map/ppermute | solution.py:420
  15.3 6.8 %collective-permute-start.3 = (bf16[4,128,256]{2,1,0:T(8,128)(2,1)S(1)}, bf16[4,128,256]{2,1,0:T(8,128)(2,1)}, u32[]{:S(2)}, u32[]{:S(2)}) collective-permute-start(bf16[4,128,256]{2,1,0:T(8,128)(2,1)S(1)} %collective-permute-done.refs_6_), channel_id=1, source_target_pairs={{0,1},{1,2},{2,3},{3,0},{4,5},{5,6},{6,7},{7,4},{8,9},{9,10},{10,1... | collective-permute-start | bytes 786440 | tf_op jit(solution)/shard_map/ppermute | solution.py:416
  15.3 0.9 copy-start.1
  22.0 44.9 %copy-start.2 = (f32[2,2048]{1,0:T(2,128)S(1)}, f32[2,2048]{1,0:T(2,128)}, u32[]{:S(2)}) copy-start(f32[2,2048]{1,0:T(2,128)} %b_ref.3) | copy-start | bytes 49156
  25.2 5.6 %collective-permute-start.6 = (bf16[256,512]{1,0:T(8,128)(2,1)S(1)}, bf16[256,512]{1,0:T(8,128)(2,1)S(1)}, u32[]{:S(2)}, u32[]{:S(2)}) collective-permute-start(bf16[256,512]{1,0:T(8,128)(2,1)S(1)} %get-tuple-element.50), channel_id=1, source_target_pairs={{0,4},{4,0},{1,5},{5,1},{2,6},{6,2},{3,7},{7,3},{8,12},{12,8},{9,1... | collective-permute-start | bytes 786440 | tf_op jit(solution)/shard_map/ppermute | solution.py:218
  41.4 8.7 %collective-permute-start.9 = (bf16[1,32,512]{2,1,0:T(8,128)(2,1)S(1)}, bf16[1,32,512]{2,1,0:T(8,128)(2,1)S(1)}, u32[]{:S(2)}, u32[]{:S(2)}) collective-permute-start(bf16[1,32,512]{2,1,0:T(8,128)(2,1)S(1)} %total.5.refs_0_), channel_id=1, source_target_pairs={{0,32},{16,48},{32,0},{48,16},{1,33},{17,49},{33,1},{49,17},{2,34}... | collective-permute-start | bytes 98312 | tf_op jit(solution)/shard_map/ppermute | solution.py:263
  47.8 4.2 %collective-permute-start.8 = (bf16[1,32,512]{2,1,0:T(8,128)(2,1)S(1)}, bf16[1,32,512]{2,1,0:T(8,128)(2,1)S(1)}, u32[]{:S(2)}, u32[]{:S(2)}) collective-permute-start(bf16[1,32,512]{2,1,0:T(8,128)(2,1)S(1)} %total.5.refs_0_), channel_id=1, source_target_pairs={{0,48},{16,0},{32,16},{48,32},{1,49},{17,1},{33,17},{49,33},{2,50}... | collective-permute-start | bytes 98312 | tf_op jit(solution)/shard_map/ppermute | solution.py:263
  47.8 4.9 %collective-permute-start.7 = (bf16[1,32,512]{2,1,0:T(8,128)(2,1)S(1)}, bf16[1,32,512]{2,1,0:T(8,128)(2,1)S(1)}, u32[]{:S(2)}, u32[]{:S(2)}) collective-permute-start(bf16[1,32,512]{2,1,0:T(8,128)(2,1)S(1)} %total.5.refs_0_), channel_id=1, source_target_pairs={{0,16},{16,32},{32,48},{48,0},{1,17},{17,33},{33,49},{49,1},{2,18}... | collective-permute-start | bytes 98312 | tf_op jit(solution)/shard_map/ppermute | solution.py:263
  61.7 5.2 %collective-permute-start.10 = (bf16[8,32,512]{2,1,0:T(8,128)(2,1)S(1)}, bf16[8,32,512]{2,1,0:T(8,128)(2,1)S(1)}, u32[]{:S(2)}, u32[]{:S(2)}) collective-permute-start(bf16[8,32,512]{2,1,0:T(8,128)(2,1)S(1)} %all_to_all.21.mine_ref), channel_id=1, source_target_pairs={{0,4},{4,0},{1,5},{5,1},{2,6},{6,2},{3,7},{7,3},{8,12},{12,8},{9,1... | collective-permute-start | bytes 786440 | tf_op jit(solution)/shard_map/ppermute | solution.py:218
  69.6 1.6 %collective-permute-start.11 = (bf16[256,512]{1,0:T(8,128)(2,1)S(1)}, bf16[256,512]{1,0:T(8,128)(2,1)S(1)}, u32[]{:S(2)}, u32[]{:S(2)}) collective-permute-start(bf16[256,512]{1,0:T(8,128)(2,1)S(1)} %get-tuple-element.53), channel_id=1, source_target_pairs={{0,4},{4,0},{1,5},{5,1},{2,6},{6,2},{3,7},{7,3},{8,12},{12,8},{9,1... | collective-permute-start | bytes 786440 | tf_op jit(solution)/shard_map/ppermute | solution.py:218
  80.3 3.8 %collective-permute-start.12 = (bf16[1,32,512]{2,1,0:T(8,128)(2,1)S(1)}, bf16[1,32,512]{2,1,0:T(8,128)(2,1)S(1)}, u32[]{:S(2)}, u32[]{:S(2)}) collective-permute-start(bf16[1,32,512]{2,1,0:T(8,128)(2,1)S(1)} %total.7.refs_0_), channel_id=1, source_target_pairs={{0,16},{16,0},{32,48},{48,32},{1,17},{17,1},{33,49},{49,33},{2,18}... | collective-permute-start | bytes 98312 | tf_op jit(solution)/shard_map/ppermute | solution.py:271
  84.1 5.0 %collective-permute-start.13 = (bf16[1,32,512]{2,1,0:T(8,128)(2,1)S(1)}, bf16[1,32,512]{2,1,0:T(8,128)(2,1)S(1)}, u32[]{:S(2)}, u32[]{:S(2)}) collective-permute-start(bf16[1,32,512]{2,1,0:T(8,128)(2,1)S(1)} %total.8.refs_0_), channel_id=1, source_target_pairs={{0,48},{48,0},{16,32},{32,16},{1,49},{49,1},{17,33},{33,17},{2,50}... | collective-permute-start | bytes 98312 | tf_op jit(solution)/shard_map/ppermute | solution.py:272
  98.4 5.6 %collective-permute-start.14 = (bf16[8,32,512]{2,1,0:T(8,128)(2,1)S(1)}, bf16[8,32,512]{2,1,0:T(8,128)(2,1)S(1)}, u32[]{:S(2)}, u32[]{:S(2)}) collective-permute-start(bf16[8,32,512]{2,1,0:T(8,128)(2,1)S(1)} %all_to_all.23.mine_ref), channel_id=1, source_target_pairs={{0,4},{4,0},{1,5},{5,1},{2,6},{6,2},{3,7},{7,3},{8,12},{12,8},{9,1... | collective-permute-start | bytes 786440 | tf_op jit(solution)/shard_map/ppermute | solution.py:218
  106.1 8.8 %collective-permute-start.19 = (bf16[4,128,256]{2,1,0:T(8,128)(2,1)S(1)}, bf16[4,128,256]{2,1,0:T(8,128)(2,1)S(1)}, u32[]{:S(2)}, u32[]{:S(2)}) collective-permute-start(bf16[4,128,256]{2,1,0:T(8,128)(2,1)S(1)} %get-tuple-element.65), channel_id=1, source_target_pairs={{0,1},{1,2},{2,3},{3,0},{4,5},{5,6},{6,7},{7,4},{8,9},{9,10},{10,1... | collective-permute-start | bytes 786440 | tf_op jit(solution)/shard_map/ppermute | solution.py:416
  106.6 8.5 %collective-permute-start.16 = (bf16[4,128,256]{2,1,0:T(8,128)(2,1)S(1)}, bf16[4,128,256]{2,1,0:T(8,128)(2,1)S(1)}, u32[]{:S(2)}, u32[]{:S(2)}) collective-permute-start(bf16[4,128,256]{2,1,0:T(8,128)(2,1)S(1)} %get-tuple-element.62), channel_id=1, source_target_pairs={{0,3},{1,0},{2,1},{3,2},{4,7},{5,4},{6,5},{7,6},{8,11},{9,8},{10,9... | collective-permute-start | bytes 786440 | tf_op jit(solution)/shard_map/ppermute | solution.py:420
  109.8 17.2 %collective-permute-start.15 = (bf16[4,128,256]{2,1,0:T(8,128)(2,1)S(1)}, bf16[4,128,256]{2,1,0:T(8,128)(2,1)S(1)}, u32[]{:S(2)}, u32[]{:S(2)}) collective-permute-start(bf16[4,128,256]{2,1,0:T(8,128)(2,1)S(1)} %get-tuple-element.60), channel_id=1, source_target_pairs={{0,1},{1,2},{2,3},{3,0},{4,5},{5,6},{6,7},{7,4},{8,9},{9,10},{10,1... | collective-permute-start | bytes 786440 | tf_op jit(solution)/shard_map/ppermute | solution.py:416
  109.9 9.5 %collective-permute-start.18 = (bf16[4,128,256]{2,1,0:T(8,128)(2,1)S(1)}, bf16[4,128,256]{2,1,0:T(8,128)(2,1)S(1)}, u32[]{:S(2)}, u32[]{:S(2)}) collective-permute-start(bf16[4,128,256]{2,1,0:T(8,128)(2,1)S(1)} %get-tuple-element.63), channel_id=1, source_target_pairs={{0,3},{1,0},{2,1},{3,2},{4,7},{5,4},{6,5},{7,6},{8,11},{9,8},{10,9... | collective-permute-start | bytes 786440 | tf_op jit(solution)/shard_map/ppermute | solution.py:420
  115.0 11.2 %collective-permute-start.20 = (bf16[4,128,256]{2,1,0:T(8,128)(2,1)S(1)}, bf16[4,128,256]{2,1,0:T(8,128)(2,1)S(1)}, u32[]{:S(2)}, u32[]{:S(2)}) collective-permute-start(bf16[4,128,256]{2,1,0:T(8,128)(2,1)S(1)} %add_convert_fusion), channel_id=1, source_target_pairs={{0,1},{1,2},{2,3},{3,0},{4,5},{5,6},{6,7},{7,4},{8,9},{9,10},{10,1... | collective-permute-start | bytes 786440 | tf_op jit(solution)/shard_map/ppermute | solution.py:416
  115.1 11.9 %collective-permute-start.17 = (bf16[4,128,256]{2,1,0:T(8,128)(2,1)S(1)}, bf16[4,128,256]{2,1,0:T(8,128)(2,1)S(1)}, u32[]{:S(2)}, u32[]{:S(2)}) collective-permute-start(bf16[4,128,256]{2,1,0:T(8,128)(2,1)S(1)} %add_convert_fusion.1), channel_id=1, source_target_pairs={{0,3},{1,0},{2,1},{3,2},{4,7},{5,4},{6,5},{7,6},{8,11},{9,8},{10,9... | collective-permute-start | bytes 786440 | tf_op jit(solution)/shard_map/ppermute | solution.py:420

commit v7 on v6

--- a/solution.py
+++ b/solution.py
@@ -44,11 +44,10 @@
 
 def cast_kernel(in_ref, a_ref, b_ref, held, sems):
     half = a_ref.shape[0]
-    outs = (a_ref, b_ref)
-    copies = fetch(sems, [(in_ref.at[pl.ds(i * half, half)], held.at[i]) for i in range(2)])
-    for i in range(2):
-        copies[i].wait()
-        outs[i][...] = held[i].astype(BF16)
+    copies = fetch(sems, [(in_ref.at[i], held.at[i]) for i in range(2 * half)])
+    for i, copy in enumerate(copies):
+        copy.wait()
+        (a_ref, b_ref)[i // half][i % half] = held[i].astype(BF16)
 
 
 def cast_halves(emb_rows):
@@ -59,37 +58,36 @@
         in_specs=[hbm()],
         out_specs=[vmem()] * 2,
         out_shape=[pltpu.VMEM(half, BF16)] * 2,
-        scratch_shapes=[pltpu.VMEM((2,) + half, F32), pltpu.SemaphoreType.DMA((2,))],
-        compiler_params=params(16),
+        scratch_shapes=[pltpu.VMEM(emb_rows.shape, F32), pltpu.SemaphoreType.DMA((tabs,))],
+        compiler_params=params(4),
         cost_estimate=cost(1 << 18, 3 << 19),
         name="cast",
     )(pinned(emb_rows))
 
 
 def counts_kernel(mine_ref, ids_ref, own_ref, *refs, first_table):
-    refs, (acc_ref, sems) = refs[:-2], refs[-2:]
+    refs, (acc_ref, ids, own, sems) = refs[:-4], refs[-4:]
     if first_table:
-        ids, own = ids_ref, own_ref
         edges_ref, *loads = refs[: len(refs) // 2]
         out_ref, turned_ref, *loaded = refs[len(refs) // 2 :]
-        copies = fetch(sems, zip(loads, loaded))
     else:
-        out_ref, turned_ref, edges_ref, ids, own = refs
-        copies = fetch(sems, [(own_ref, own), (ids_ref, ids)])
+        out_ref, turned_ref, edges_ref = refs
+        loads = loaded = ()
+    copies = fetch(sems, [(own_ref, own), (ids_ref, ids), *zip(loads, loaded)])
     _, rows, samp = acc_ref.shape
     tabs, entries = own.shape
     mine = mine_ref[0]
     low = mine * samp
     turn = mine * (rows // 4)
+    copies[0].wait()
     if not first_table:
-        copies[0].wait()
         owners = own[...]
         first = jnp.sum((owners < low).astype(jnp.int32), axis=1, keepdims=True)
         last = jnp.sum((owners < low + samp).astype(jnp.int32), axis=1, keepdims=True)
         for i in range(tabs):
             edges_ref[i] = first[i, 0]
             edges_ref[tabs + i] = last[i, 0]
-        copies[1].wait()
+    copies[1].wait()
     grid = lax.broadcasted_iota(jnp.int32, (samp, EB), 0).astype(F32).astype(BF16)
     one, zero = jnp.ones((), BF16), jnp.zeros((), BF16)
 
@@ -121,9 +119,8 @@
             turned_ref[2 * pair + j] = total
             out_ref[2 * pair + j] = total.T
 
-    if first_table:
-        for copy in copies:
-            copy.wait()
+    for copy in copies[2:]:
+        copy.wait()
 
 
 def make_counts(mine, ids, owners, samp, rows, edges=None, loads=()):
@@ -131,24 +128,28 @@
     assert rows == 2 * samp and samp <= 256
     half = tabs // 2
     out_shape = [pltpu.VMEM((half, samp, rows), BF16), pltpu.VMEM((half, rows, samp), BF16)]
+    args = (mine, pinned(ids), pinned(owners))
+    in_specs, out_specs = [smem(), hbm(), hbm()], [vmem(), vmem()]
     if edges is None:
-        args = (mine, pinned(ids), pinned(owners))
-        in_specs = [smem(), hbm(), hbm()]
-        out_specs = [vmem(), vmem(), smem(), vmem(), vmem()]
+        out_specs.append(smem())
         out_shape.append(jax.ShapeDtypeStruct((2 * tabs,), jnp.int32))
-        out_shape += [pltpu.VMEM(ids.shape, jnp.int32)] * 2
     else:
-        args = (mine, *kept(ids, owners), edges, *map(pinned, loads))
-        in_specs = [smem(), vmem(), vmem(), smem()] + [hbm()] * len(loads)
-        out_specs = [vmem()] * (2 + len(loads))
+        args += (edges, *map(pinned, loads))
+        in_specs += [smem()] + [hbm()] * len(loads)
+        out_specs += [vmem()] * len(loads)
         out_shape += [pltpu.VMEM(arr.shape, arr.dtype) for arr in loads]
     return pl.pallas_call(
         functools.partial(counts_kernel, first_table=0 if edges is None else half),
         in_specs=in_specs,
         out_specs=out_specs,
         out_shape=out_shape,
-        scratch_shapes=[pltpu.VMEM((2, rows, samp), F32), pltpu.SemaphoreType.DMA((max(2, len(loads)),))],
-        compiler_params=params(16),
+        scratch_shapes=[
+            pltpu.VMEM((2, rows, samp), F32),
+            pltpu.VMEM((tabs, entries), jnp.int32),
+            pltpu.VMEM((tabs, entries), jnp.int32),
+            pltpu.SemaphoreType.DMA((2 + len(loads),)),
+        ],
+        compiler_params=params(6),
         cost_estimate=cost(half * samp * rows * 3072, 3 << 20),
         name="counts",
     )(*args)
@@ -164,10 +165,38 @@
     return copies
 
 
-def emit(core_ref, z, g, keep_ref, send_ref):
-    even = core_ref[0] == 0
-    keep_ref[...] = jnp.where(even, z, g)
-    send_ref[...] = jnp.where(even, g, z).astype(BF16)
+def sum_z(x, v_ref, layer):
+    return jnp.dot(x[...], v_ref[layer], preferred_element_type=F32)
+
+
+def sum_g(wide, u_ref, layer):
+    return lax.dot_general(wide[...], u_ref[layer], NT, preferred_element_type=F32)
+
+
+def one_sum(even, x, wide, v_ref, u_ref, layer, out_ref):
+    @pl.when(even)
+    def _():
+        out_ref[...] = sum_z(x, v_ref, layer).astype(out_ref.dtype)
+
+    @pl.when(jnp.logical_not(even))
+    def _():
+        out_ref[...] = sum_g(wide, u_ref, 1 - layer).astype(out_ref.dtype)
+
+
+def keep_kernel(core_ref, x, wide, v_ref, u_ref, out_ref, *, layer):
+    one_sum(core_ref[0] == 0, x, wide, v_ref, u_ref, layer, out_ref)
+
+
+def keep_sum(core, x, wide, v, u, layer):
+    return pl.pallas_call(
+        functools.partial(keep_kernel, layer=layer),
+        in_specs=[smem()] + [vmem()] * 4,
+        out_specs=vmem(),
+        out_shape=pltpu.VMEM((x.shape[0], v.shape[-1]), F32),
+        compiler_params=params(8),
+        cost_estimate=cost(1 << 29, 4 << 20),
+        name="keep_sum",
+    )(core, *kept(x, wide, v, u))
 
 
 def anyspace():
@@ -175,40 +204,32 @@
 
 
 def first_kernel(core_ref, counts_a, counts_b, *refs):
-    embs, (cot, v, u, pooled_ref, keep_ref, send_ref) = refs[:8], refs[8:]
-    half = counts_a.shape[0]
-    z = g = None
-    for f in range(half):
-        parts = []
-        for t in (2 * f, 2 * f + 1):
-            side, at = divmod(t, half)
-            rows = jnp.concatenate([embs[2 * k + side][at] for k in range(4)], axis=0)
-            parts.append(jnp.dot((counts_a, counts_b)[side][at], rows, preferred_element_type=F32).astype(BF16))
-        pooled = jnp.concatenate(parts, axis=1)
-        at = slice(f * WIDE, (f + 1) * WIDE)
+    embs, (cot, v_ref, u_ref, pooled_ref, wide_ref, send_ref) = refs[:8], refs[8:]
+    half, _, emb = embs[0].shape
+    for t in range(2 * half):
+        side, i = divmod(t, half)
+        rows = jnp.concatenate([embs[2 * k + side][i] for k in range(4)], axis=0)
+        pooled = jnp.dot((counts_a, counts_b)[side][i], rows, preferred_element_type=F32).astype(BF16)
+        at = slice(t * emb, (t + 1) * emb)
         pooled_ref[:, at] = pooled
-        wide = (cot[:, at].astype(F32) * pooled.astype(F32)).astype(BF16)
-        more_z = jnp.dot(pooled, v[0, at, :], preferred_element_type=F32)
-        more_g = lax.dot_general(wide, u[1, :, at], NT, preferred_element_type=F32)
-        z, g = (more_z, more_g) if f == 0 else (z + more_z, g + more_g)
-    emit(core_ref, z, g, keep_ref, send_ref)
+        wide_ref[:, at] = (cot[:, at].astype(F32) * pooled.astype(F32)).astype(BF16)
+    one_sum(core_ref[0] != 0, pooled_ref, wide_ref, v_ref, u_ref, 0, send_ref)
 
 
 def first_sums(core, counts, embs, cot, v, u):
     half, samp, rows = counts[0].shape
     emb = embs[0].shape[-1]
     rank = v.shape[-1]
-    assert 2 * emb == WIDE
     return pl.pallas_call(
         first_kernel,
         in_specs=[smem()] + [vmem()] * 13,
         out_specs=[vmem()] * 3,
         out_shape=[
             pltpu.VMEM((samp, 2 * half * emb), BF16),
-            pltpu.VMEM((samp, rank), F32),
+            pltpu.VMEM((samp, 2 * half * emb), BF16),
             pltpu.VMEM((samp, rank), BF16),
         ],
-        compiler_params=params(16),
+        compiler_params=params(8),
         cost_estimate=cost(3 << 29, 10 << 20),
         name="first_sums",
     )(core, *kept(*counts), *embs, *kept(cot, v, u))
@@ -263,16 +284,13 @@
     return lax.ppermute(arr, "zh", [(i, (i + k) & 3) for i in range(4)])
 
 
-def sum_all(keep, send, by_pairs):
+def sum_all(core, send, x, wide, v, u, layer):
+    send, x = lax.optimization_barrier((send, x))
+    got, keep = lax.optimization_barrier((swap(send, "c"), keep_sum(core, x, wide, v, u, layer)))
     shape = pltpu.VMEM((CHUNKS,) + CHUNK, BF16)
-    parts = swap_all(small(cut_kernel, shape, "cut", keep, swap(send, "c")))
+    parts = swap_all(small(cut_kernel, shape, "cut", keep, got))
     own = total(1, parts)
-    if by_pairs:
-        two = total(1, own, lax.ppermute(own, "zh", [(0, 1), (1, 0), (2, 3), (3, 2)]))
-        near = (two, lax.ppermute(two, "zh", [(0, 3), (3, 0), (1, 2), (2, 1)]))
-    else:
-        near = (own, turn(own, 1), turn(own, 3), turn(own, 2))
-    mine = swap_all(total(CHUNKS, *near))
+    mine = swap_all(total(CHUNKS, own, turn(own, 1), turn(own, 3), turn(own, 2)))
     return mine, swap(mine, "c")
 
 
@@ -283,23 +301,18 @@
             in_ref[(side, *chunk_at(i))] = ref[i]
 
 
-def middle_kernel(core_ref, mine_ref, other_ref, b_ref, pooled, cot, u_ref, v_ref, x1_ref, a_ref, keep_ref, send_ref, sums):
+def middle_kernel(core_ref, mine_ref, other_ref, b_ref, pooled, cot, u_ref, v_ref, x1_ref, a_ref, wide_ref, send_ref, sums):
     spread(core_ref, mine_ref, other_ref, sums)
-    z = g = None
     for f in range(pooled.shape[1] // WIDE):
         at = slice(f * WIDE, (f + 1) * WIDE)
-        u, v = u_ref[0, :, at], v_ref[1, at, :]
         base = pooled[:, at].astype(F32)
-        h0 = jnp.dot(sums[0], u, preferred_element_type=F32) + b_ref[0:1, at]
-        x1 = (base * h0 + base).astype(BF16)
-        x1_ref[:, at] = x1
-        g1 = cot[:, at].astype(F32) + lax.dot_general(sums[1], v, NT, preferred_element_type=F32)
+        h0 = jnp.dot(sums[0], u_ref[0, :, at], preferred_element_type=F32) + b_ref[0:1, at]
+        x1_ref[:, at] = (base * h0 + base).astype(BF16)
+        g1 = lax.dot_general(sums[1], v_ref[1, at, :], NT, preferred_element_type=F32)
+        g1 = cot[:, at].astype(F32) + g1
         a_ref[:, at] = (g1 * h0 + g1).astype(BF16)
-        wide = (g1 * base).astype(BF16)
-        more_z = jnp.dot(x1, v, preferred_element_type=F32)
-        more_g = lax.dot_general(wide, u, NT, preferred_element_type=F32)
-        z, g = (more_z, more_g) if f == 0 else (z + more_z, g + more_g)
-    emit(core_ref, z, g, keep_ref, send_ref)
+        wide_ref[:, at] = (g1 * base).astype(BF16)
+    one_sum(core_ref[0] != 0, x1_ref, wide_ref, v_ref, u_ref, 1, send_ref)
 
 
 def middle(core, mine, other, bias, pooled, cot, u, v):
@@ -310,9 +323,9 @@
         middle_kernel,
         in_specs=[smem()] + [vmem()] * 7,
         out_specs=[vmem()] * 4,
-        out_shape=[feat, feat, pltpu.VMEM((samp, rank), F32), pltpu.VMEM((samp, rank), BF16)],
+        out_shape=[feat, feat, feat, pltpu.VMEM((samp, rank), BF16)],
         scratch_shapes=[pltpu.VMEM((2, samp, rank), BF16)],
-        compiler_params=params(16),
+        compiler_params=params(10),
         cost_estimate=cost(1 << 31, 8 << 20),
         name="middle",
     )(core, mine, other, bias, *kept(pooled, cot, u, v))
@@ -351,7 +364,7 @@
         out_specs=[vmem()] * 4,
         out_shape=[pltpu.VMEM(pooled.shape, BF16)] * 2 + [piece, piece],
         scratch_shapes=[pltpu.VMEM((2, samp, rank), BF16)],
-        compiler_params=params(16),
+        compiler_params=params(8),
         cost_estimate=cost(5 << 28, 7 << 20),
         name="far_rows",
     )(core, mine, other, bias, *kept(*turned, pooled, cot, x1, a, u, v))
@@ -383,7 +396,7 @@
         out_shape=[pltpu.HBM(crossed.shape, BF16), pltpu.VMEM((2 * half,) + block[1:], F32)]
         + [pltpu.VMEM(block, BF16)] * 4,
         scratch_shapes=[pltpu.SemaphoreType.DMA],
-        compiler_params=params(16),
+        compiler_params=params(8),
         cost_estimate=cost(3 << 28, 7 << 20),
         name="near_rows",
     )(*kept(*turned, grad, crossed))
@@ -406,7 +419,7 @@
         out_shape=pltpu.HBM(p0.shape, F32),
         scratch_shapes=[pltpu.VMEM(near.shape, F32), pltpu.SemaphoreType.DMA],
         input_output_aliases={3: 0} if before else {},
-        compiler_params=params(8),
+        compiler_params=params(4),
         cost_estimate=cost(1 << 20, 1 << 20),
         name="finish",
     )(*kept(p0), near, far, *before)
@@ -435,16 +448,16 @@
     own_a, own_b = cast_halves(emb_rows)
     left_a, right_b = right(own_a), left(own_b)
     left_b, right_a = right(own_b), left(own_a)
-    counts_a, turned_a, edges, ids, owners = make_counts(mine, entry_ids, entry_sample, samp, rows)
+    counts_a, turned_a, edges = make_counts(mine, entry_ids, entry_sample, samp, rows)
     left_a, right_b, edges = lax.optimization_barrier((left_a, right_b, edges))
     far_a, far_b = right(left_a), left(right_b)
     loads = (cotangent, cross_v, cross_u)
-    counts_b, turned_b, cot, v, u = make_counts(mine, ids, owners, samp, rows, edges, loads)
+    counts_b, turned_b, cot, v, u = make_counts(mine, entry_ids, entry_sample, samp, rows, edges, loads)
     embs = (own_a, own_b, right_a, right_b, far_a, far_b, left_a, left_b)
-    pooled, keep, send = first_sums(core, (counts_a, counts_b), embs, cot, v, u)
-    sums = sum_all(keep, send, False)
-    x1, a, keep, send = middle(core, *sums, cross_bias, pooled, cot, u, v)
-    sums = sum_all(keep, send, True)
+    pooled, wide, send = first_sums(core, (counts_a, counts_b), embs, cot, v, u)
+    sums = sum_all(core, send, pooled, wide, v, u, 0)
+    x1, a, wide, send = middle(core, *sums, cross_bias, pooled, cot, u, v)
+    sums = sum_all(core, send, x1, wide, v, u, 1)
     turned = (turned_a, turned_b)
     crossed, grad, p2a, p2b = far_rows(core, *sums, cross_bias, turned, pooled, cot, x1, a, u, v)
     from_left, from_right = right(p2a), left(p2b)

time: 129 us -> 127 us (0.984)
  starting transfers between devices: 41.8 us -> 43.8 us
  local copies, waits for them, and re-layouts: 1.56 us -> 0.01 us
  waiting for transfers between devices: 24.3 us -> 22.8 us
    ppermute x3 -> x6, starting transfers between devices: 8.73 us -> 15.1 us  [turn(): return lax.ppermute(arr, 'zh', [(i, i + k & 3) for i in range(4)])]
    ppermute x2 -> x0, waiting for transfers between devices: 5.05 us -> none  [the longest x1 2.56 us: sum_all(): lax.ppermute(own, 'zh', [(0, 1), (1, 0), (2, 3), (3, 2)])]
    ppermute x2 -> x0, starting transfers between devices: 3.66 us -> none  [the longest x1 2.46 us: sum_all(): near = (two, lax.ppermute(two, 'zh', [(0, 3), (3, 0), (1, 2), (2, 1)]))]
    ppermute x3 -> x6, waiting for transfers between devices: 2.53 us -> 5.78 us  [turn(): return lax.ppermute(arr, 'zh', [(i, i + k & 3) for i in range(4)])]
    ppermute x6, waiting for transfers between devices: 3.1 us -> 4.99 us  [left(): return lax.ppermute(arr, 'row', [(i, i + 3 & 3) for i in range(4)])]
    unnamed x6 -> x2, local copies, waits for them, and re-layouts: 1.56 us -> 0.01 us
    ppermute x4, waiting for transfers between devices: 4.65 us -> 3.16 us  [swap(): return lax.ppermute(arr, axis, [(0, 1), (1, 0)])]
    pallas_call x0 -> x2, Pallas kernels: none -> 1.47 us  [keep_sum(): pl.pallas_call(functools.partial(keep_kernel, layer=layer), in_specs=[sme...]
  transfers between devices with their start and end apart: 21 -> 22, of which waited for: 12 -> 13; matrix products, arithmetic and copies ran while one was open for 0% -> 0% of each run, Pallas kernels for 9% -> 10%
where the time goes in v7:
time: 127 us
  starting transfers between devices  43.8 us (34%)
  blocking collectives  36.9 us (29%)
  waiting for transfers between devices  22.8 us (18%)
  Pallas kernels  22.2 us (17%)
    all_to_all x4, blocking collectives, swap_all(): return lax.all_to_all(arr, ('x', 'zl'), 0, 0, tiled=True)  36.9 us
    ppermute x6, starting transfers between devices, turn(): return lax.ppermute(arr, 'zh', [(i, i + k & 3) for i in range(4)])  15.1 us
    ppermute x4, starting transfers between devices, swap(): return lax.ppermute(arr, axis, [(0, 1), (1, 0)])  13 us
    ppermute x6, starting transfers between devices, left(): return lax.ppermute(arr, 'row', [(i, i + 3 & 3) for i in range(4)])  12.5 us
    pallas_call x2, Pallas kernels, make_counts(): pl.pallas_call(functools.partial(counts_kernel, first_table=0 if edges is...  9.43 us
    ppermute x6, waiting for transfers between devices, right(): return lax.ppermute(arr, 'row', [(i, i + 1 & 3) for i in range(4)])  8.85 us
    ppermute x6, waiting for transfers between devices, turn(): return lax.ppermute(arr, 'zh', [(i, i + k & 3) for i in range(4)])  5.78 us
    ppermute x6, waiting for transfers between devices, left(): return lax.ppermute(arr, 'row', [(i, i + 3 & 3) for i in range(4)])  4.99 us
  transfers between devices with their start and end apart: 22, of which 13 were waited for; matrix products, arithmetic and copies ran while one was open for 0% of the time, Pallas kernels for 10%

profile of v7, /device:TPU:1, one launch (start us, length us, event | category | flops | bytes accessed | tf_op | source)
XLA Modules:
  0.0 126.9 jit_solution(10958819842270334692)
XLA Ops:
  0.6 1.4 %cast.1 = (bf16[4,128,256]{2,1,0:T(8,128)(2,1)S(1)}, bf16[4,128,256]{2,1,0:T(8,128)(2,1)S(1)}) custom-call(f32[8,128,256]{2,1,0:T(8,128)} %in_ref.1), custom_call_target="tpu_custom_call" | custom-call | flops 262144 | bytes 1572864 | tf_op jit(solution)/shard_map/cast/pallas_call | solution.py:56
  2.0 2.2 %collective-permute-start = (bf16[4,128,256]{2,1,0:T(8,128)(2,1)S(1)}, bf16[4,128,256]{2,1,0:T(8,128)(2,1)S(1)}, u32[]{:S(2)}, u32[]{:S(2)}) collective-permute-start(bf16[4,128,256]{2,1,0:T(8,128)(2,1)S(1)} %get-tuple-element.41.refs_0_), channel_id=1, source_target_pairs={{0,1},{1,2},{2,3},{3,0},{4,5},{5,6},{6,7},{7,4},{8,9},{9,10},{10,1... | collective-permute-start | bytes 786440 | tf_op jit(solution)/shard_map/ppermute | solution.py:429
  4.2 1.5 %collective-permute-start.1 = (bf16[4,128,256]{2,1,0:T(8,128)(2,1)S(1)}, bf16[4,128,256]{2,1,0:T(8,128)(2,1)S(1)}, u32[]{:S(2)}, u32[]{:S(2)}) collective-permute-start(bf16[4,128,256]{2,1,0:T(8,128)(2,1)S(1)} %get-tuple-element.42.refs_1_), channel_id=1, source_target_pairs={{0,3},{1,0},{2,1},{3,2},{4,7},{5,4},{6,5},{7,6},{8,11},{9,8},{10,9... | collective-permute-start | bytes 786440 | tf_op jit(solution)/shard_map/ppermute | solution.py:433
  5.7 1.4 %collective-permute-start.2 = (bf16[4,128,256]{2,1,0:T(8,128)(2,1)S(1)}, bf16[4,128,256]{2,1,0:T(8,128)(2,1)S(1)}, u32[]{:S(2)}, u32[]{:S(2)}) collective-permute-start(bf16[4,128,256]{2,1,0:T(8,128)(2,1)S(1)} %get-tuple-element.41.refs_0_), channel_id=1, source_target_pairs={{0,3},{1,0},{2,1},{3,2},{4,7},{5,4},{6,5},{7,6},{8,11},{9,8},{10,9... | collective-permute-start | bytes 786440 | tf_op jit(solution)/shard_map/ppermute | solution.py:433
  7.2 4.4 %counts.2 = (bf16[4,256,512]{2,1,0:T(8,128)(2,1)S(1)}, bf16[4,512,256]{2,1,0:T(8,128)(2,1)S(1)}, s32[16]{0:T(128)S(1)}) custom-call(s32[1]{0:T(128)} %bitcast.mine_ref, s32[8,4096]{1,0:T(8,128)} %ids_ref.3, s32[8,4096]{1,0:T(8,128)} %own_ref.3), custom_call_target="tpu_custom_call" | custom-call | flops 1610612736 | bytes 3145728 | tf_op jit(solution)/shard_map/counts/pallas_call | solution.py:141
  11.7 2.2 %collective-permute-start.4 = (bf16[4,128,256]{2,1,0:T(8,128)(2,1)S(1)}, bf16[4,128,256]{2,1,0:T(8,128)(2,1)}, u32[]{:S(2)}, u32[]{:S(2)}) collective-permute-start(bf16[4,128,256]{2,1,0:T(8,128)(2,1)S(1)} %collective-permute-done.1.refs_3_), channel_id=1, source_target_pairs={{0,3},{1,0},{2,1},{3,2},{4,7},{5,4},{6,5},{7,6},{8,11},{9,8},{10,9... | collective-permute-start | bytes 786440 | tf_op jit(solution)/shard_map/ppermute | solution.py:433
  13.9 5.0 %counts.3 = (bf16[4,256,512]{2,1,0:T(8,128)(2,1)S(1)}, bf16[4,512,256]{2,1,0:T(8,128)(2,1)S(1)}, bf16[256,2048]{1,0:T(8,128)(2,1)S(1)}, bf16[2,2048,512]{2,1,0:T(8,128)(2,1)S(1)}, bf16[2,512,2048]{2,1,0:T(8,128)(2,1)S(1)}) custom-call(s32[1]{0:T(128)} %bitcast.mine_ref, s32[8,4096]{1,0:T(8,128)} %ids_ref.3, s32[8,4096]{1,0:T(8,128)} %own_ref.3, ...), custom_call_target="tpu_custom_call" | custom-call | flops 1610612736 | bytes 3145728 | tf_op jit(solution)/shard_map/counts/pallas_call | solution.py:141
  18.9 3.3 %collective-permute-done.4.refs_5_ = bf16[4,128,256]{2,1,0:T(8,128)(2,1)} collective-permute-done((bf16[4,128,256]{2,1,0:T(8,128)(2,1)S(1)}, bf16[4,128,256]{2,1,0:T(8,128)(2,1)}, u32[]{:S(2)}, u32[]{:S(2)}) %collective-permute-start.4) | collective-permute-done | bytes 262176 | tf_op jit(solution)/shard_map/ppermute | solution.py:433
  22.1 2.6 %first_sums.1 = (bf16[256,2048]{1,0:T(8,128)(2,1)S(1)}, bf16[256,2048]{1,0:T(8,128)(2,1)S(1)}, bf16[256,512]{1,0:T(8,128)(2,1)S(1)}) custom-call(s32[1]{0:T(128)} %bitcast.1.core_ref, bf16[4,256,512]{2,1,0:T(8,128)(2,1)S(1)} %get-tuple-element.46.counts_a, bf16[4,256,512]{2,1,0:T(8,128)(2,1)S(1)} %get-tuple-element.47.counts_b, ...), custom_call_target="tpu_custom_call" | custom-call | flops 1610612736 | bytes 10485760 | tf_op jit(solution)/shard_map/first_sums/pallas_call | solution.py:223
  24.7 4.7 %collective-permute-start.6 = (bf16[256,512]{1,0:T(8,128)(2,1)S(1)}, bf16[256,512]{1,0:T(8,128)(2,1)S(1)}, u32[]{:S(2)}, u32[]{:S(2)}) collective-permute-start(bf16[256,512]{1,0:T(8,128)(2,1)S(1)} %get-tuple-element.55), channel_id=1, source_target_pairs={{0,4},{4,0},{1,5},{5,1},{2,6},{6,2},{3,7},{7,3},{8,12},{12,8},{9,1... | collective-permute-start | bytes 786440 | tf_op jit(solution)/shard_map/ppermute | solution.py:239
  30.6 10.1 %all_to_all.20.refs_0_ = bf16[8,32,512]{2,1,0:T(8,128)(2,1)S(1)} all-to-all(bf16[8,32,512]{2,1,0:T(8,128)(2,1)S(1)} %cut.2), channel_id=1, replica_groups=mesh['x'=4,'zh'=4,'zl'=2,'c'=2,'row'=4] {'x','zl'}, dimensions={0} | all-to-all | bytes 524288 | tf_op jit(solution)/shard_map/all_to_all | solution.py:280
  40.7 6.1 %collective-permute-start.9 = (bf16[1,32,512]{2,1,0:T(8,128)(2,1)S(1)}, bf16[1,32,512]{2,1,0:T(8,128)(2,1)S(1)}, u32[]{:S(2)}, u32[]{:S(2)}) collective-permute-start(bf16[1,32,512]{2,1,0:T(8,128)(2,1)S(1)} %total.4.refs_0_), channel_id=1, source_target_pairs={{0,32},{16,48},{32,0},{48,16},{1,33},{17,49},{33,1},{49,17},{2,34}... | collective-permute-start | bytes 98312 | tf_op jit(solution)/shard_map/ppermute | solution.py:284
  47.1 2.1 %collective-permute-start.7 = (bf16[1,32,512]{2,1,0:T(8,128)(2,1)S(1)}, bf16[1,32,512]{2,1,0:T(8,128)(2,1)S(1)}, u32[]{:S(2)}, u32[]{:S(2)}) collective-permute-start(bf16[1,32,512]{2,1,0:T(8,128)(2,1)S(1)} %total.4.refs_0_), channel_id=1, source_target_pairs={{0,16},{16,32},{32,48},{48,0},{1,17},{17,33},{33,49},{49,1},{2,18}... | collective-permute-start | bytes 98312 | tf_op jit(solution)/shard_map/ppermute | solution.py:284
  49.2 1.3 %collective-permute-done.8.refs_2_ = bf16[1,32,512]{2,1,0:T(8,128)(2,1)S(1)} collective-permute-done((bf16[1,32,512]{2,1,0:T(8,128)(2,1)S(1)}, bf16[1,32,512]{2,1,0:T(8,128)(2,1)S(1)}, u32[]{:S(2)}, u32[]{:S(2)}) %collective-permute-start.8) | collective-permute-done | bytes 32800 | tf_op jit(solution)/shard_map/ppermute | solution.py:284
  50.5 1.8 %collective-permute-done.7.refs_1_ = bf16[1,32,512]{2,1,0:T(8,128)(2,1)S(1)} collective-permute-done((bf16[1,32,512]{2,1,0:T(8,128)(2,1)S(1)}, bf16[1,32,512]{2,1,0:T(8,128)(2,1)S(1)}, u32[]{:S(2)}, u32[]{:S(2)}) %collective-permute-start.7) | collective-permute-done | bytes 32800 | tf_op jit(solution)/shard_map/ppermute | solution.py:284
  52.4 8.7 %all_to_all.21.mine_ref = bf16[8,32,512]{2,1,0:T(8,128)(2,1)S(1)} all-to-all(bf16[8,32,512]{2,1,0:T(8,128)(2,1)S(1)} %total.5), channel_id=1, replica_groups=mesh['x'=4,'zh'=4,'zl'=2,'c'=2,'row'=4] {'x','zl'}, dimensions={0} | all-to-all | bytes 524288 | tf_op jit(solution)/shard_map/all_to_all | solution.py:280
  61.0 4.0 %collective-permute-start.10 = (bf16[8,32,512]{2,1,0:T(8,128)(2,1)S(1)}, bf16[8,32,512]{2,1,0:T(8,128)(2,1)S(1)}, u32[]{:S(2)}, u32[]{:S(2)}) collective-permute-start(bf16[8,32,512]{2,1,0:T(8,128)(2,1)S(1)} %all_to_all.21.mine_ref), channel_id=1, source_target_pairs={{0,4},{4,0},{1,5},{5,1},{2,6},{6,2},{3,7},{7,3},{8,12},{12,8},{9,1... | collective-permute-start | bytes 786440 | tf_op jit(solution)/shard_map/ppermute | solution.py:239
  65.1 1.2 collective-permute-done.10.other_ref
  66.2 2.3 %middle.1 = (bf16[256,2048]{1,0:T(8,128)(2,1)S(1)}, bf16[256,2048]{1,0:T(8,128)(2,1)S(1)}, bf16[256,2048]{1,0:T(8,128)(2,1)S(1)}, bf16[256,512]{1,0:T(8,128)(2,1)S(1)}) custom-call(s32[1]{0:T(128)} %bitcast.1.core_ref, bf16[8,32,512]{2,1,0:T(8,128)(2,1)S(1)} %all_to_all.21.mine_ref, bf16[8,32,512]{2,1,0:T(8,128)(2,1)S(1)} %collective-permute-done.10.other_ref, ...), custom_call_target="tpu_custom_call" | custom-call | flops 2147483648 | bytes 8388608 | tf_op jit(solution)/shard_map/middle/pallas_call | solution.py:322
  70.2 9.0 %all_to_all.22.refs_0_ = bf16[8,32,512]{2,1,0:T(8,128)(2,1)S(1)} all-to-all(bf16[8,32,512]{2,1,0:T(8,128)(2,1)S(1)} %cut.3), channel_id=1, replica_groups=mesh['x'=4,'zh'=4,'zl'=2,'c'=2,'row'=4] {'x','zl'}, dimensions={0} | all-to-all | bytes 524288 | tf_op jit(solution)/shard_map/all_to_all | solution.py:280
  79.3 4.3 %collective-permute-start.14 = (bf16[1,32,512]{2,1,0:T(8,128)(2,1)S(1)}, bf16[1,32,512]{2,1,0:T(8,128)(2,1)S(1)}, u32[]{:S(2)}, u32[]{:S(2)}) collective-permute-start(bf16[1,32,512]{2,1,0:T(8,128)(2,1)S(1)} %total.6.refs_0_), channel_id=1, source_target_pairs={{0,32},{16,48},{32,0},{48,16},{1,33},{17,49},{33,1},{49,17},{2,34}... | collective-permute-start | bytes 98312 | tf_op jit(solution)/shard_map/ppermute | solution.py:284
  83.6 2.4 %collective-permute-start.12 = (bf16[1,32,512]{2,1,0:T(8,128)(2,1)S(1)}, bf16[1,32,512]{2,1,0:T(8,128)(2,1)S(1)}, u32[]{:S(2)}, u32[]{:S(2)}) collective-permute-start(bf16[1,32,512]{2,1,0:T(8,128)(2,1)S(1)} %total.6.refs_0_), channel_id=1, source_target_pairs={{0,16},{16,32},{32,48},{48,0},{1,17},{17,33},{33,49},{49,1},{2,18}... | collective-permute-start | bytes 98312 | tf_op jit(solution)/shard_map/ppermute | solution.py:284
  86.0 1.5 %collective-permute-done.13.refs_2_ = bf16[1,32,512]{2,1,0:T(8,128)(2,1)S(1)} collective-permute-done((bf16[1,32,512]{2,1,0:T(8,128)(2,1)S(1)}, bf16[1,32,512]{2,1,0:T(8,128)(2,1)S(1)}, u32[]{:S(2)}, u32[]{:S(2)}) %collective-permute-start.13) | collective-permute-done | bytes 32800 | tf_op jit(solution)/shard_map/ppermute | solution.py:284
  88.6 9.1 %all_to_all.23.mine_ref = bf16[8,32,512]{2,1,0:T(8,128)(2,1)S(1)} all-to-all(bf16[8,32,512]{2,1,0:T(8,128)(2,1)S(1)} %total.7), channel_id=1, replica_groups=mesh['x'=4,'zh'=4,'zl'=2,'c'=2,'row'=4] {'x','zl'}, dimensions={0} | all-to-all | bytes 524288 | tf_op jit(solution)/shard_map/all_to_all | solution.py:280
  97.7 3.8 %collective-permute-start.15 = (bf16[8,32,512]{2,1,0:T(8,128)(2,1)S(1)}, bf16[8,32,512]{2,1,0:T(8,128)(2,1)S(1)}, u32[]{:S(2)}, u32[]{:S(2)}) collective-permute-start(bf16[8,32,512]{2,1,0:T(8,128)(2,1)S(1)} %all_to_all.23.mine_ref), channel_id=1, source_target_pairs={{0,4},{4,0},{1,5},{5,1},{2,6},{6,2},{3,7},{7,3},{8,12},{12,8},{9,1... | collective-permute-start | bytes 786440 | tf_op jit(solution)/shard_map/ppermute | solution.py:239
  102.7 2.1 %far_rows.1 = (bf16[256,2048]{1,0:T(8,128)(2,1)S(1)}, bf16[256,2048]{1,0:T(8,128)(2,1)S(1)}, bf16[4,128,256]{2,1,0:T(8,128)(2,1)S(1)}, bf16[4,128,256]{2,1,0:T(8,128)(2,1)S(1)}) custom-call(s32[1]{0:T(128)} %bitcast.1.core_ref, bf16[8,32,512]{2,1,0:T(8,128)(2,1)S(1)} %all_to_all.23.mine_ref, bf16[8,32,512]{2,1,0:T(8,128)(2,1)S(1)} %collective-permute-done.15.other_ref, ...), custom_call_target="tpu_custom_call" | custom-call | flops 1342177280 | bytes 7340032 | tf_op jit(solution)/shard_map/far_rows/pallas_call | solution.py:361
  105.6 2.0 %collective-permute-start.17 = (bf16[4,128,256]{2,1,0:T(8,128)(2,1)S(1)}, bf16[4,128,256]{2,1,0:T(8,128)(2,1)S(1)}, u32[]{:S(2)}, u32[]{:S(2)}) collective-permute-start(bf16[4,128,256]{2,1,0:T(8,128)(2,1)S(1)} %get-tuple-element.74), channel_id=1, source_target_pairs={{0,3},{1,0},{2,1},{3,2},{4,7},{5,4},{6,5},{7,6},{8,11},{9,8},{10,9... | collective-permute-start | bytes 786440 | tf_op jit(solution)/shard_map/ppermute | solution.py:433
  108.7 2.7 %collective-permute-start.19 = (bf16[4,128,256]{2,1,0:T(8,128)(2,1)S(1)}, bf16[4,128,256]{2,1,0:T(8,128)(2,1)S(1)}, u32[]{:S(2)}, u32[]{:S(2)}) collective-permute-start(bf16[4,128,256]{2,1,0:T(8,128)(2,1)S(1)} %get-tuple-element.75), channel_id=1, source_target_pairs={{0,3},{1,0},{2,1},{3,2},{4,7},{5,4},{6,5},{7,6},{8,11},{9,8},{10,9... | collective-permute-start | bytes 786440 | tf_op jit(solution)/shard_map/ppermute | solution.py:433
  111.3 2.3 %collective-permute-done.20 = bf16[4,128,256]{2,1,0:T(8,128)(2,1)S(1)} collective-permute-done((bf16[4,128,256]{2,1,0:T(8,128)(2,1)S(1)}, bf16[4,128,256]{2,1,0:T(8,128)(2,1)S(1)}, u32[]{:S(2)}, u32[]{:S(2)}) %collective-permute-start.20) | collective-permute-done | bytes 262176 | tf_op jit(solution)/shard_map/ppermute | solution.py:429
  113.9 2.7 %collective-permute-start.18 = (bf16[4,128,256]{2,1,0:T(8,128)(2,1)S(1)}, bf16[4,128,256]{2,1,0:T(8,128)(2,1)S(1)}, u32[]{:S(2)}, u32[]{:S(2)}) collective-permute-start(bf16[4,128,256]{2,1,0:T(8,128)(2,1)S(1)} %add_convert_fusion.1), channel_id=1, source_target_pairs={{0,3},{1,0},{2,1},{3,2},{4,7},{5,4},{6,5},{7,6},{8,11},{9,8},{10,9... | collective-permute-start | bytes 786440 | tf_op jit(solution)/shard_map/ppermute | solution.py:433
  116.6 1.7 %collective-permute-done.19.sum_ref = bf16[4,128,256]{2,1,0:T(8,128)(2,1)S(1)} collective-permute-done((bf16[4,128,256]{2,1,0:T(8,128)(2,1)S(1)}, bf16[4,128,256]{2,1,0:T(8,128)(2,1)S(1)}, u32[]{:S(2)}, u32[]{:S(2)}) %collective-permute-start.19) | collective-permute-done | bytes 262176 | tf_op jit(solution)/shard_map/ppermute | solution.py:433
  118.4 6.5 %collective-permute-done.21.far_ref = bf16[4,128,256]{2,1,0:T(8,128)(2,1)S(1)} collective-permute-done((bf16[4,128,256]{2,1,0:T(8,128)(2,1)S(1)}, bf16[4,128,256]{2,1,0:T(8,128)(2,1)S(1)}, u32[]{:S(2)}, u32[]{:S(2)}) %collective-permute-start.21) | collective-permute-done | bytes 262176 | tf_op jit(solution)/shard_map/ppermute | solution.py:429
  (37 shorter events, 9.5 us)
Async XLA Ops:
  2.0 9.6 %collective-permute-start = (bf16[4,128,256]{2,1,0:T(8,128)(2,1)S(1)}, bf16[4,128,256]{2,1,0:T(8,128)(2,1)S(1)}, u32[]{:S(2)}, u32[]{:S(2)}) collective-permute-start(bf16[4,128,256]{2,1,0:T(8,128)(2,1)S(1)} %get-tuple-element.41.refs_0_), channel_id=1, source_target_pairs={{0,1},{1,2},{2,3},{3,0},{4,5},{5,6},{6,7},{7,4},{8,9},{9,10},{10,1... | collective-permute-start | bytes 786440 | tf_op jit(solution)/shard_map/ppermute | solution.py:429
  4.2 7.5 %collective-permute-start.1 = (bf16[4,128,256]{2,1,0:T(8,128)(2,1)S(1)}, bf16[4,128,256]{2,1,0:T(8,128)(2,1)S(1)}, u32[]{:S(2)}, u32[]{:S(2)}) collective-permute-start(bf16[4,128,256]{2,1,0:T(8,128)(2,1)S(1)} %get-tuple-element.42.refs_1_), channel_id=1, source_target_pairs={{0,3},{1,0},{2,1},{3,2},{4,7},{5,4},{6,5},{7,6},{8,11},{9,8},{10,9... | collective-permute-start | bytes 786440 | tf_op jit(solution)/shard_map/ppermute | solution.py:433
  5.7 13.1 %collective-permute-start.2 = (bf16[4,128,256]{2,1,0:T(8,128)(2,1)S(1)}, bf16[4,128,256]{2,1,0:T(8,128)(2,1)S(1)}, u32[]{:S(2)}, u32[]{:S(2)}) collective-permute-start(bf16[4,128,256]{2,1,0:T(8,128)(2,1)S(1)} %get-tuple-element.41.refs_0_), channel_id=1, source_target_pairs={{0,3},{1,0},{2,1},{3,2},{4,7},{5,4},{6,5},{7,6},{8,11},{9,8},{10,9... | collective-permute-start | bytes 786440 | tf_op jit(solution)/shard_map/ppermute | solution.py:433
  7.1 11.8 %collective-permute-start.5 = (bf16[4,128,256]{2,1,0:T(8,128)(2,1)S(1)}, bf16[4,128,256]{2,1,0:T(8,128)(2,1)}, u32[]{:S(2)}, u32[]{:S(2)}) collective-permute-start(bf16[4,128,256]{2,1,0:T(8,128)(2,1)S(1)} %get-tuple-element.42.refs_1_), channel_id=1, source_target_pairs={{0,1},{1,2},{2,3},{3,0},{4,5},{5,6},{6,7},{7,4},{8,9},{9,10},{10,1... | collective-permute-start | bytes 786440 | tf_op jit(solution)/shard_map/ppermute | solution.py:429
  11.7 10.5 %collective-permute-start.4 = (bf16[4,128,256]{2,1,0:T(8,128)(2,1)S(1)}, bf16[4,128,256]{2,1,0:T(8,128)(2,1)}, u32[]{:S(2)}, u32[]{:S(2)}) collective-permute-start(bf16[4,128,256]{2,1,0:T(8,128)(2,1)S(1)} %collective-permute-done.1.refs_3_), channel_id=1, source_target_pairs={{0,3},{1,0},{2,1},{3,2},{4,7},{5,4},{6,5},{7,6},{8,11},{9,8},{10,9... | collective-permute-start | bytes 786440 | tf_op jit(solution)/shard_map/ppermute | solution.py:433
  13.9 8.3 %collective-permute-start.3 = (bf16[4,128,256]{2,1,0:T(8,128)(2,1)S(1)}, bf16[4,128,256]{2,1,0:T(8,128)(2,1)}, u32[]{:S(2)}, u32[]{:S(2)}) collective-permute-start(bf16[4,128,256]{2,1,0:T(8,128)(2,1)S(1)} %collective-permute-done.refs_6_), channel_id=1, source_target_pairs={{0,1},{1,2},{2,3},{3,0},{4,5},{5,6},{6,7},{7,4},{8,9},{9,10},{10,1... | collective-permute-start | bytes 786440 | tf_op jit(solution)/shard_map/ppermute | solution.py:429
  24.7 5.8 %collective-permute-start.6 = (bf16[256,512]{1,0:T(8,128)(2,1)S(1)}, bf16[256,512]{1,0:T(8,128)(2,1)S(1)}, u32[]{:S(2)}, u32[]{:S(2)}) collective-permute-start(bf16[256,512]{1,0:T(8,128)(2,1)S(1)} %get-tuple-element.55), channel_id=1, source_target_pairs={{0,4},{4,0},{1,5},{5,1},{2,6},{6,2},{3,7},{7,3},{8,12},{12,8},{9,1... | collective-permute-start | bytes 786440 | tf_op jit(solution)/shard_map/ppermute | solution.py:239
  29.4 36.8 %copy-start = (f32[2,2048]{1,0:T(2,128)S(1)}, f32[2,2048]{1,0:T(2,128)}, u32[]{:S(2)}) copy-start(f32[2,2048]{1,0:T(2,128)} %b_ref.3) | copy-start | bytes 49156
  40.7 8.5 %collective-permute-start.9 = (bf16[1,32,512]{2,1,0:T(8,128)(2,1)S(1)}, bf16[1,32,512]{2,1,0:T(8,128)(2,1)S(1)}, u32[]{:S(2)}, u32[]{:S(2)}) collective-permute-start(bf16[1,32,512]{2,1,0:T(8,128)(2,1)S(1)} %total.4.refs_0_), channel_id=1, source_target_pairs={{0,32},{16,48},{32,0},{48,16},{1,33},{17,49},{33,1},{49,17},{2,34}... | collective-permute-start | bytes 98312 | tf_op jit(solution)/shard_map/ppermute | solution.py:284
  46.8 3.7 %collective-permute-start.8 = (bf16[1,32,512]{2,1,0:T(8,128)(2,1)S(1)}, bf16[1,32,512]{2,1,0:T(8,128)(2,1)S(1)}, u32[]{:S(2)}, u32[]{:S(2)}) collective-permute-start(bf16[1,32,512]{2,1,0:T(8,128)(2,1)S(1)} %total.4.refs_0_), channel_id=1, source_target_pairs={{0,48},{16,0},{32,16},{48,32},{1,49},{17,1},{33,17},{49,33},{2,50}... | collective-permute-start | bytes 98312 | tf_op jit(solution)/shard_map/ppermute | solution.py:284
  47.1 5.2 %collective-permute-start.7 = (bf16[1,32,512]{2,1,0:T(8,128)(2,1)S(1)}, bf16[1,32,512]{2,1,0:T(8,128)(2,1)S(1)}, u32[]{:S(2)}, u32[]{:S(2)}) collective-permute-start(bf16[1,32,512]{2,1,0:T(8,128)(2,1)S(1)} %total.4.refs_0_), channel_id=1, source_target_pairs={{0,16},{16,32},{32,48},{48,0},{1,17},{17,33},{33,49},{49,1},{2,18}... | collective-permute-start | bytes 98312 | tf_op jit(solution)/shard_map/ppermute | solution.py:284
  61.0 5.2 %collective-permute-start.10 = (bf16[8,32,512]{2,1,0:T(8,128)(2,1)S(1)}, bf16[8,32,512]{2,1,0:T(8,128)(2,1)S(1)}, u32[]{:S(2)}, u32[]{:S(2)}) collective-permute-start(bf16[8,32,512]{2,1,0:T(8,128)(2,1)S(1)} %all_to_all.21.mine_ref), channel_id=1, source_target_pairs={{0,4},{4,0},{1,5},{5,1},{2,6},{6,2},{3,7},{7,3},{8,12},{12,8},{9,1... | collective-permute-start | bytes 786440 | tf_op jit(solution)/shard_map/ppermute | solution.py:239
  68.5 1.7 %collective-permute-start.11 = (bf16[256,512]{1,0:T(8,128)(2,1)S(1)}, bf16[256,512]{1,0:T(8,128)(2,1)S(1)}, u32[]{:S(2)}, u32[]{:S(2)}) collective-permute-start(bf16[256,512]{1,0:T(8,128)(2,1)S(1)} %get-tuple-element.62), channel_id=1, source_target_pairs={{0,4},{4,0},{1,5},{5,1},{2,6},{6,2},{3,7},{7,3},{8,12},{12,8},{9,1... | collective-permute-start | bytes 786440 | tf_op jit(solution)/shard_map/ppermute | solution.py:239
  79.3 6.8 %collective-permute-start.14 = (bf16[1,32,512]{2,1,0:T(8,128)(2,1)S(1)}, bf16[1,32,512]{2,1,0:T(8,128)(2,1)S(1)}, u32[]{:S(2)}, u32[]{:S(2)}) collective-permute-start(bf16[1,32,512]{2,1,0:T(8,128)(2,1)S(1)} %total.6.refs_0_), channel_id=1, source_target_pairs={{0,32},{16,48},{32,0},{48,16},{1,33},{17,49},{33,1},{49,17},{2,34}... | collective-permute-start | bytes 98312 | tf_op jit(solution)/shard_map/ppermute | solution.py:284
  83.6 4.0 %collective-permute-start.13 = (bf16[1,32,512]{2,1,0:T(8,128)(2,1)S(1)}, bf16[1,32,512]{2,1,0:T(8,128)(2,1)S(1)}, u32[]{:S(2)}, u32[]{:S(2)}) collective-permute-start(bf16[1,32,512]{2,1,0:T(8,128)(2,1)S(1)} %total.6.refs_0_), channel_id=1, source_target_pairs={{0,48},{16,0},{32,16},{48,32},{1,49},{17,1},{33,17},{49,33},{2,50}... | collective-permute-start | bytes 98312 | tf_op jit(solution)/shard_map/ppermute | solution.py:284
  83.6 5.0 %collective-permute-start.12 = (bf16[1,32,512]{2,1,0:T(8,128)(2,1)S(1)}, bf16[1,32,512]{2,1,0:T(8,128)(2,1)S(1)}, u32[]{:S(2)}, u32[]{:S(2)}) collective-permute-start(bf16[1,32,512]{2,1,0:T(8,128)(2,1)S(1)} %total.6.refs_0_), channel_id=1, source_target_pairs={{0,16},{16,32},{32,48},{48,0},{1,17},{17,33},{33,49},{49,1},{2,18}... | collective-permute-start | bytes 98312 | tf_op jit(solution)/shard_map/ppermute | solution.py:284
  97.7 5.0 %collective-permute-start.15 = (bf16[8,32,512]{2,1,0:T(8,128)(2,1)S(1)}, bf16[8,32,512]{2,1,0:T(8,128)(2,1)S(1)}, u32[]{:S(2)}, u32[]{:S(2)}) collective-permute-start(bf16[8,32,512]{2,1,0:T(8,128)(2,1)S(1)} %all_to_all.23.mine_ref), channel_id=1, source_target_pairs={{0,4},{4,0},{1,5},{5,1},{2,6},{6,2},{3,7},{7,3},{8,12},{12,8},{9,1... | collective-permute-start | bytes 786440 | tf_op jit(solution)/shard_map/ppermute | solution.py:239
  104.8 8.8 %collective-permute-start.20 = (bf16[4,128,256]{2,1,0:T(8,128)(2,1)S(1)}, bf16[4,128,256]{2,1,0:T(8,128)(2,1)S(1)}, u32[]{:S(2)}, u32[]{:S(2)}) collective-permute-start(bf16[4,128,256]{2,1,0:T(8,128)(2,1)S(1)} %get-tuple-element.77), channel_id=1, source_target_pairs={{0,1},{1,2},{2,3},{3,0},{4,5},{5,6},{6,7},{7,4},{8,9},{9,10},{10,1... | collective-permute-start | bytes 786440 | tf_op jit(solution)/shard_map/ppermute | solution.py:429
  105.6 8.3 %collective-permute-start.17 = (bf16[4,128,256]{2,1,0:T(8,128)(2,1)S(1)}, bf16[4,128,256]{2,1,0:T(8,128)(2,1)S(1)}, u32[]{:S(2)}, u32[]{:S(2)}) collective-permute-start(bf16[4,128,256]{2,1,0:T(8,128)(2,1)S(1)} %get-tuple-element.74), channel_id=1, source_target_pairs={{0,3},{1,0},{2,1},{3,2},{4,7},{5,4},{6,5},{7,6},{8,11},{9,8},{10,9... | collective-permute-start | bytes 786440 | tf_op jit(solution)/shard_map/ppermute | solution.py:433
  108.6 17.2 %collective-permute-start.16 = (bf16[4,128,256]{2,1,0:T(8,128)(2,1)S(1)}, bf16[4,128,256]{2,1,0:T(8,128)(2,1)S(1)}, u32[]{:S(2)}, u32[]{:S(2)}) collective-permute-start(bf16[4,128,256]{2,1,0:T(8,128)(2,1)S(1)} %get-tuple-element.72), channel_id=1, source_target_pairs={{0,1},{1,2},{2,3},{3,0},{4,5},{5,6},{6,7},{7,4},{8,9},{9,10},{10,1... | collective-permute-start | bytes 786440 | tf_op jit(solution)/shard_map/ppermute | solution.py:429
  108.7 9.7 %collective-permute-start.19 = (bf16[4,128,256]{2,1,0:T(8,128)(2,1)S(1)}, bf16[4,128,256]{2,1,0:T(8,128)(2,1)S(1)}, u32[]{:S(2)}, u32[]{:S(2)}) collective-permute-start(bf16[4,128,256]{2,1,0:T(8,128)(2,1)S(1)} %get-tuple-element.75), channel_id=1, source_target_pairs={{0,3},{1,0},{2,1},{3,2},{4,7},{5,4},{6,5},{7,6},{8,11},{9,8},{10,9... | collective-permute-start | bytes 786440 | tf_op jit(solution)/shard_map/ppermute | solution.py:433
  113.7 11.2 %collective-permute-start.21 = (bf16[4,128,256]{2,1,0:T(8,128)(2,1)S(1)}, bf16[4,128,256]{2,1,0:T(8,128)(2,1)S(1)}, u32[]{:S(2)}, u32[]{:S(2)}) collective-permute-start(bf16[4,128,256]{2,1,0:T(8,128)(2,1)S(1)} %add_convert_fusion), channel_id=1, source_target_pairs={{0,1},{1,2},{2,3},{3,0},{4,5},{5,6},{6,7},{7,4},{8,9},{9,10},{10,1... | collective-permute-start | bytes 786440 | tf_op jit(solution)/shard_map/ppermute | solution.py:429
  113.9 11.9 %collective-permute-start.18 = (bf16[4,128,256]{2,1,0:T(8,128)(2,1)S(1)}, bf16[4,128,256]{2,1,0:T(8,128)(2,1)S(1)}, u32[]{:S(2)}, u32[]{:S(2)}) collective-permute-start(bf16[4,128,256]{2,1,0:T(8,128)(2,1)S(1)} %add_convert_fusion.1), channel_id=1, source_target_pairs={{0,3},{1,0},{2,1},{3,2},{4,7},{5,4},{6,5},{7,6},{8,11},{9,8},{10,9... | collective-permute-start | bytes 786440 | tf_op jit(solution)/shard_map/ppermute | solution.py:433

commit v8 on v7

--- a/solution.py
+++ b/solution.py
@@ -44,10 +44,11 @@
 
 def cast_kernel(in_ref, a_ref, b_ref, held, sems):
     half = a_ref.shape[0]
-    copies = fetch(sems, [(in_ref.at[i], held.at[i]) for i in range(2 * half)])
-    for i, copy in enumerate(copies):
-        copy.wait()
-        (a_ref, b_ref)[i // half][i % half] = held[i].astype(BF16)
+    outs = (a_ref, b_ref)
+    copies = fetch(sems, [(in_ref.at[pl.ds(i * half, half)], held.at[i]) for i in range(2)])
+    for i in range(2):
+        copies[i].wait()
+        outs[i][...] = held[i].astype(BF16)
 
 
 def cast_halves(emb_rows):
@@ -58,7 +59,7 @@
         in_specs=[hbm()],
         out_specs=[vmem()] * 2,
         out_shape=[pltpu.VMEM(half, BF16)] * 2,
-        scratch_shapes=[pltpu.VMEM(emb_rows.shape, F32), pltpu.SemaphoreType.DMA((tabs,))],
+        scratch_shapes=[pltpu.VMEM((2,) + half, F32), pltpu.SemaphoreType.DMA((2,))],
         compiler_params=params(4),
         cost_estimate=cost(1 << 18, 3 << 19),
         name="cast",
@@ -69,9 +70,9 @@
     refs, (acc_ref, ids, own, sems) = refs[:-4], refs[-4:]
     if first_table:
         edges_ref, *loads = refs[: len(refs) // 2]
-        out_ref, turned_ref, *loaded = refs[len(refs) // 2 :]
+        out_ref, *loaded = refs[len(refs) // 2 :]
     else:
-        out_ref, turned_ref, edges_ref = refs
+        out_ref, edges_ref = refs
         loads = loaded = ()
     copies = fetch(sems, [(own_ref, own), (ids_ref, ids), *zip(loads, loaded)])
     _, rows, samp = acc_ref.shape
@@ -115,9 +116,7 @@
 
         lax.fori_loop(0, steps, body, 0)
         for j in range(2):
-            total = acc_ref[j].astype(BF16)
-            turned_ref[2 * pair + j] = total
-            out_ref[2 * pair + j] = total.T
+            out_ref[2 * pair + j] = acc_ref[j].astype(BF16).T
 
     for copy in copies[2:]:
         copy.wait()
@@ -127,9 +126,9 @@
     tabs, entries = ids.shape
     assert rows == 2 * samp and samp <= 256
     half = tabs // 2
-    out_shape = [pltpu.VMEM((half, samp, rows), BF16), pltpu.VMEM((half, rows, samp), BF16)]
+    out_shape = [pltpu.VMEM((half, samp, rows), BF16)]
     args = (mine, pinned(ids), pinned(owners))
-    in_specs, out_specs = [smem(), hbm(), hbm()], [vmem(), vmem()]
+    in_specs, out_specs = [smem(), hbm(), hbm()], [vmem()]
     if edges is None:
         out_specs.append(smem())
         out_shape.append(jax.ShapeDtypeStruct((2 * tabs,), jnp.int32))
@@ -155,6 +154,24 @@
     )(*args)
 
 
+def turned_kernel(in_ref, out_ref):
+    for i in range(out_ref.shape[0]):
+        out_ref[i] = in_ref[i].T
+
+
+def turned_counts(counts):
+    half, samp, rows = counts.shape
+    return pl.pallas_call(
+        turned_kernel,
+        in_specs=[vmem()],
+        out_specs=vmem(),
+        out_shape=pltpu.VMEM((half, rows, samp), BF16),
+        compiler_params=params(8),
+        cost_estimate=cost(1 << 29, 2 << 20),
+        name="turned",
+    )(*kept(counts))
+
+
 WIDE = 512
 
 
@@ -284,38 +301,91 @@
     return lax.ppermute(arr, "zh", [(i, (i + k) & 3) for i in range(4)])
 
 
-def sum_all(core, send, x, wide, v, u, layer):
+def layout(chunks_ref, sum_ref):
+    for i in range(CHUNKS):
+        sum_ref[chunk_at(i)] = chunks_ref[i]
+
+
+def z_u(total, u_ref, layer, at):
+    return jnp.dot(total, u_ref[layer, :, at], preferred_element_type=F32)
+
+
+def g_v(total, v_ref, layer, at):
+    return lax.dot_general(total, v_ref[layer, at, :], NT, preferred_element_type=F32)
+
+
+def steps_of(feats):
+    return [slice(f, f + WIDE) for f in range(0, feats, WIDE)]
+
+
+def product_kernel(core_ref, mine_ref, v_ref, u_ref, out_ref, sum_ref, *, layer):
+    layout(mine_ref, sum_ref)
+
+    @pl.when(core_ref[0] == 0)
+    def _():
+        for at in steps_of(out_ref.shape[1]):
+            out_ref[:, at] = z_u(sum_ref[...], u_ref, layer, at)
+
+    @pl.when(core_ref[0] != 0)
+    def _():
+        for at in steps_of(out_ref.shape[1]):
+            out_ref[:, at] = g_v(sum_ref[...], v_ref, 1 - layer, at)
+
+
+def product(core, mine, v, u, layer):
+    samp, rank = CHUNKS * CHUNK[0], CHUNK[1]
+    return pl.pallas_call(
+        functools.partial(product_kernel, layer=layer),
+        in_specs=[smem()] + [vmem()] * 3,
+        out_specs=vmem(),
+        out_shape=pltpu.VMEM((samp, u.shape[-1]), F32),
+        scratch_shapes=[pltpu.VMEM((samp, rank), BF16)],
+        compiler_params=params(8),
+        cost_estimate=cost(1 << 29, 4 << 20),
+        name="product",
+    )(core, mine, *kept(v, u))
+
+
+def by_core(core_ref, body, prod, sum_ref, v_ref, u_ref, layer):
+    @pl.when(core_ref[0] == 0)
+    def _():
+        body(lambda at: prod[:, at], lambda at: g_v(sum_ref[...], v_ref, 1 - layer, at))
+
+    @pl.when(core_ref[0] != 0)
+    def _():
+        body(lambda at: z_u(sum_ref[...], u_ref, layer, at), lambda at: prod[:, at])
+
+
+def sum_all(core, send, x, wide, v, u, layer, counts):
     send, x = lax.optimization_barrier((send, x))
     got, keep = lax.optimization_barrier((swap(send, "c"), keep_sum(core, x, wide, v, u, layer)))
     shape = pltpu.VMEM((CHUNKS,) + CHUNK, BF16)
     parts = swap_all(small(cut_kernel, shape, "cut", keep, got))
-    own = total(1, parts)
-    mine = swap_all(total(CHUNKS, own, turn(own, 1), turn(own, 3), turn(own, 2)))
-    return mine, swap(mine, "c")
-
-
-def spread(core_ref, mine_ref, other_ref, in_ref):
-    core = core_ref[0]
-    for side, ref in ((core, mine_ref), (1 - core, other_ref)):
-        for i in range(CHUNKS):
-            in_ref[(side, *chunk_at(i))] = ref[i]
-
-
-def middle_kernel(core_ref, mine_ref, other_ref, b_ref, pooled, cot, u_ref, v_ref, x1_ref, a_ref, wide_ref, send_ref, sums):
-    spread(core_ref, mine_ref, other_ref, sums)
-    for f in range(pooled.shape[1] // WIDE):
-        at = slice(f * WIDE, (f + 1) * WIDE)
-        base = pooled[:, at].astype(F32)
-        h0 = jnp.dot(sums[0], u_ref[0, :, at], preferred_element_type=F32) + b_ref[0:1, at]
-        x1_ref[:, at] = (base * h0 + base).astype(BF16)
-        g1 = lax.dot_general(sums[1], v_ref[1, at, :], NT, preferred_element_type=F32)
-        g1 = cot[:, at].astype(F32) + g1
-        a_ref[:, at] = (g1 * h0 + g1).astype(BF16)
-        wide_ref[:, at] = (g1 * base).astype(BF16)
+    own, counts = lax.optimization_barrier((total(1, parts), counts))
+    near = (turn(own, 1), turn(own, 3), turn(own, 2), turned_counts(counts))
+    *near, turned = lax.optimization_barrier(near)
+    mine = swap_all(total(CHUNKS, own, *near))
+    prod, other = lax.optimization_barrier((product(core, mine, v, u, layer), swap(mine, "c")))
+    return prod, other, turned
+
+
+def middle_kernel(core_ref, prod, other_ref, b_ref, pooled, cot, u_ref, v_ref, x1_ref, a_ref, wide_ref, send_ref, sum_ref):
+    layout(other_ref, sum_ref)
+
+    def body(h, g):
+        for at in steps_of(pooled.shape[1]):
+            base = pooled[:, at].astype(F32)
+            h0 = h(at) + b_ref[0:1, at]
+            x1_ref[:, at] = (base * h0 + base).astype(BF16)
+            g1 = cot[:, at].astype(F32) + g(at)
+            a_ref[:, at] = (g1 * h0 + g1).astype(BF16)
+            wide_ref[:, at] = (g1 * base).astype(BF16)
+
+    by_core(core_ref, body, prod, sum_ref, v_ref, u_ref, 0)
     one_sum(core_ref[0] != 0, x1_ref, wide_ref, v_ref, u_ref, 1, send_ref)
 
 
-def middle(core, mine, other, bias, pooled, cot, u, v):
+def middle(core, prod, other, bias, pooled, cot, u, v):
     samp, feats = pooled.shape
     rank = v.shape[-1]
     feat = pltpu.VMEM((samp, feats), BF16)
@@ -324,36 +394,36 @@
         in_specs=[smem()] + [vmem()] * 7,
         out_specs=[vmem()] * 4,
         out_shape=[feat, feat, feat, pltpu.VMEM((samp, rank), BF16)],
-        scratch_shapes=[pltpu.VMEM((2, samp, rank), BF16)],
+        scratch_shapes=[pltpu.VMEM((samp, rank), BF16)],
         compiler_params=params(10),
         cost_estimate=cost(1 << 31, 8 << 20),
         name="middle",
-    )(core, mine, other, bias, *kept(pooled, cot, u, v))
+    )(core, *kept(prod), other, bias, *kept(pooled, cot, u, v))
 
 
 def row_grads(turned_ref, table, first, count, grad):
     return jnp.dot(turned_ref[table, first : first + count, :], grad, preferred_element_type=F32)
 
 
-def far_kernel(core_ref, mine_ref, other_ref, b_ref, *refs):
-    turned, refs = refs[:2], refs[2:]
-    pooled, cot, x1, a, u_ref, v_ref, crossed_ref, grad_ref, far_a, far_b, sums = refs
+def far_kernel(core_ref, prod, other_ref, b_ref, turned_a, turned_b, pooled, cot, x1, a, u_ref, v_ref, *refs):
+    crossed_ref, grad_ref, far_a, far_b, sum_ref = refs
     half, rows, emb = far_a.shape
-    spread(core_ref, mine_ref, other_ref, sums)
-    for f in range(pooled.shape[1] // WIDE):
-        at = slice(f * WIDE, (f + 1) * WIDE)
-        h1 = jnp.dot(sums[0], u_ref[1, :, at], preferred_element_type=F32) + b_ref[1:2, at]
-        crossed_ref[:, at] = (pooled[:, at].astype(F32) * h1 + x1[:, at].astype(F32)).astype(BF16)
-        grad = cot[:, at].astype(F32) * h1 + a[:, at].astype(F32)
-        grad = (grad + lax.dot_general(sums[1], v_ref[0, at, :], NT, preferred_element_type=F32)).astype(BF16)
-        grad_ref[:, at] = grad
-        for i in range(2):
-            side, t = divmod(2 * f + i, half)
-            part = row_grads(turned[side], t, 2 * rows, rows, grad[:, i * emb : (i + 1) * emb])
-            (far_a, far_b)[side][t] = part.astype(BF16)
-
-
-def far_rows(core, mine, other, bias, turned, pooled, cot, x1, a, u, v):
+    layout(other_ref, sum_ref)
+
+    def body(h, g):
+        for at in steps_of(pooled.shape[1]):
+            h1 = h(at) + b_ref[1:2, at]
+            crossed_ref[:, at] = (pooled[:, at].astype(F32) * h1 + x1[:, at].astype(F32)).astype(BF16)
+            grad_ref[:, at] = (cot[:, at].astype(F32) * h1 + a[:, at].astype(F32) + g(at)).astype(BF16)
+
+    by_core(core_ref, body, prod, sum_ref, v_ref, u_ref, 1)
+    for t in range(2 * half):
+        side, i = divmod(t, half)
+        part = row_grads((turned_a, turned_b)[side], i, 2 * rows, rows, grad_ref[:, t * emb : (t + 1) * emb])
+        (far_a, far_b)[side][i] = part.astype(BF16)
+
+
+def far_rows(core, prod, other, bias, turned, pooled, cot, x1, a, u, v):
     half, rows, samp = turned[0].shape
     rank = v.shape[-1]
     feats = pooled.shape[1]
@@ -363,11 +433,11 @@
         in_specs=[smem()] + [vmem()] * 11,
         out_specs=[vmem()] * 4,
         out_shape=[pltpu.VMEM(pooled.shape, BF16)] * 2 + [piece, piece],
-        scratch_shapes=[pltpu.VMEM((2, samp, rank), BF16)],
+        scratch_shapes=[pltpu.VMEM((samp, rank), BF16)],
         compiler_params=params(8),
         cost_estimate=cost(5 << 28, 7 << 20),
         name="far_rows",
-    )(core, mine, other, bias, *kept(*turned, pooled, cot, x1, a, u, v))
+    )(core, *kept(prod), other, bias, *kept(*turned, pooled, cot, x1, a, u, v))
 
 
 def near_kernel(*refs):
@@ -402,27 +472,29 @@
     )(*kept(*turned, grad, crossed))
 
 
-def finish_kernel(p0, sum_ref, far_ref, *refs, side):
-    out_ref, held, sem = refs[-3:]
-    half = held.shape[0]
-    held[...] = p0[side * half : (side + 1) * half] + (sum_ref[...].astype(F32) + far_ref[...].astype(F32))
-    copy = pltpu.make_async_copy(held, out_ref.at[pl.ds(side * half, half)], sem)
-    copy.start()
-    copy.wait()
-
-
-def finish(side, before, p0, near, far):
-    return pl.pallas_call(
-        functools.partial(finish_kernel, side=side),
-        in_specs=[vmem()] * 3 + [anyspace()] * len(before),
+def finish_kernel(p0, near_a, far_a, near_b, far_b, out_ref, held, sems):
+    half = near_a.shape[0]
+    copies = []
+    for side, (near, far) in enumerate(((near_a, far_a), (near_b, far_b))):
+        at = pl.ds(side * half, half)
+        held[at] = p0[at] + (near[...].astype(F32) + far[...].astype(F32))
+        copies += [pltpu.make_async_copy(held.at[at], out_ref.at[at], sems.at[side])]
+        copies[-1].start()
+    for copy in copies:
+        copy.wait()
+
+
+def finish(p0, *others):
+    return pl.pallas_call(
+        finish_kernel,
+        in_specs=[vmem()] * 5,
         out_specs=anyspace(),
         out_shape=pltpu.HBM(p0.shape, F32),
-        scratch_shapes=[pltpu.VMEM(near.shape, F32), pltpu.SemaphoreType.DMA],
-        input_output_aliases={3: 0} if before else {},
+        scratch_shapes=[pltpu.VMEM(p0.shape, F32), pltpu.SemaphoreType.DMA((2,))],
         compiler_params=params(4),
         cost_estimate=cost(1 << 20, 1 << 20),
         name="finish",
-    )(*kept(p0), near, far, *before)
+    )(*kept(p0), *others)
 
 
 def right(arr):
@@ -448,25 +520,24 @@
     own_a, own_b = cast_halves(emb_rows)
     left_a, right_b = right(own_a), left(own_b)
     left_b, right_a = right(own_b), left(own_a)
-    counts_a, turned_a, edges = make_counts(mine, entry_ids, entry_sample, samp, rows)
+    counts_a, edges = make_counts(mine, entry_ids, entry_sample, samp, rows)
     left_a, right_b, edges = lax.optimization_barrier((left_a, right_b, edges))
     far_a, far_b = right(left_a), left(right_b)
     loads = (cotangent, cross_v, cross_u)
-    counts_b, turned_b, cot, v, u = make_counts(mine, entry_ids, entry_sample, samp, rows, edges, loads)
+    counts_b, cot, v, u = make_counts(mine, entry_ids, entry_sample, samp, rows, edges, loads)
     embs = (own_a, own_b, right_a, right_b, far_a, far_b, left_a, left_b)
     pooled, wide, send = first_sums(core, (counts_a, counts_b), embs, cot, v, u)
-    sums = sum_all(core, send, pooled, wide, v, u, 0)
-    x1, a, wide, send = middle(core, *sums, cross_bias, pooled, cot, u, v)
-    sums = sum_all(core, send, x1, wide, v, u, 1)
+    prod, other, turned_a = sum_all(core, send, pooled, wide, v, u, 0, counts_a)
+    x1, a, wide, send = middle(core, prod, other, cross_bias, pooled, cot, u, v)
+    prod, other, turned_b = sum_all(core, send, x1, wide, v, u, 1, counts_b)
     turned = (turned_a, turned_b)
-    crossed, grad, p2a, p2b = far_rows(core, *sums, cross_bias, turned, pooled, cot, x1, a, u, v)
+    crossed, grad, p2a, p2b = far_rows(core, prod, other, cross_bias, turned, pooled, cot, x1, a, u, v)
     from_left, from_right = right(p2a), left(p2b)
     crossed, p0, p1a, p1b, p3a, p3b = near_rows(turned, grad, crossed)
     sum_b, sum_a = right(p1b), left(p3a)
     far_a = right(add(p1a, from_left).astype(BF16))
     far_b = left(add(p3b, from_right).astype(BF16))
-    grads = finish(0, (), p0, sum_a, far_a)
-    return crossed, finish(1, (grads,), p0, sum_b, far_b)
+    return crossed, finish(p0, sum_a, far_a, sum_b, far_b)
 
 
 def solution(mesh):

time: 127 us -> 124 us (0.976)
  waiting for transfers between devices: 22.8 us -> 20.9 us
    ppermute x4, waiting for transfers between devices: 3.16 us -> 1.62 us  [swap(): return lax.ppermute(arr, axis, [(0, 1), (1, 0)])]
    pallas_call x2 -> x5, Pallas kernels: 1.77 us -> 3.23 us  [the longest x2 1.52 us: product(): pl.pallas_call(functools.partial(product_kernel, layer=layer), in_specs=[...]
    ppermute x6, waiting for transfers between devices: 8.85 us -> 10.1 us  [right(): return lax.ppermute(arr, 'row', [(i, i + 1 & 3) for i in range(4)])]
  transfers between devices with their start and end apart: 22 -> 22, of which waited for: 13 -> 13; matrix products, arithmetic and copies ran while one was open for 0% -> 0% of each run, Pallas kernels for 10% -> 12%
where the time goes in v8:
time: 124 us
  starting transfers between devices  42.8 us (35%)
  blocking collectives  37.2 us (30%)
  Pallas kernels  22 us (18%)
  waiting for transfers between devices  20.9 us (17%)
    all_to_all x4, blocking collectives, swap_all(): return lax.all_to_all(arr, ('x', 'zl'), 0, 0, tiled=True)  37.2 us
    ppermute x6, starting transfers between devices, turn(): return lax.ppermute(arr, 'zh', [(i, i + k & 3) for i in range(4)])  15.1 us
    ppermute x4, starting transfers between devices, swap(): return lax.ppermute(arr, axis, [(0, 1), (1, 0)])  12.7 us
    ppermute x6, starting transfers between devices, left(): return lax.ppermute(arr, 'row', [(i, i + 3 & 3) for i in range(4)])  11.3 us
    ppermute x6, waiting for transfers between devices, right(): return lax.ppermute(arr, 'row', [(i, i + 1 & 3) for i in range(4)])  10.1 us
    pallas_call x2, Pallas kernels, make_counts(): pl.pallas_call(functools.partial(counts_kernel, first_table=0 if edges is...  9.86 us
    ppermute x6, waiting for transfers between devices, turn(): return lax.ppermute(arr, 'zh', [(i, i + k & 3) for i in range(4)])  5.11 us
    ppermute x6, waiting for transfers between devices, left(): return lax.ppermute(arr, 'row', [(i, i + 3 & 3) for i in range(4)])  4 us
  transfers between devices with their start and end apart: 22, of which 13 were waited for; matrix products, arithmetic and copies ran while one was open for 0% of the time, Pallas kernels for 12%

profile of v8, /device:TPU:1, one launch (start us, length us, event | category | flops | bytes accessed | tf_op | source)
XLA Modules:
  0.0 124.1 jit_solution(11828309663542134007)
XLA Ops:
  0.6 1.2 %cast.1 = (bf16[4,128,256]{2,1,0:T(8,128)(2,1)S(1)}, bf16[4,128,256]{2,1,0:T(8,128)(2,1)S(1)}) custom-call(f32[8,128,256]{2,1,0:T(8,128)} %in_ref.1), custom_call_target="tpu_custom_call" | custom-call | flops 262144 | bytes 1572864 | tf_op jit(solution)/shard_map/cast/pallas_call | solution.py:57
  1.9 2.2 %collective-permute-start = (bf16[4,128,256]{2,1,0:T(8,128)(2,1)S(1)}, bf16[4,128,256]{2,1,0:T(8,128)(2,1)S(1)}, u32[]{:S(2)}, u32[]{:S(2)}) collective-permute-start(bf16[4,128,256]{2,1,0:T(8,128)(2,1)S(1)} %get-tuple-element.55.refs_0_), channel_id=1, source_target_pairs={{0,1},{1,2},{2,3},{3,0},{4,5},{5,6},{6,7},{7,4},{8,9},{9,10},{10,1... | collective-permute-start | bytes 786440 | tf_op jit(solution)/shard_map/ppermute | solution.py:501
  4.1 1.5 %collective-permute-start.1 = (bf16[4,128,256]{2,1,0:T(8,128)(2,1)S(1)}, bf16[4,128,256]{2,1,0:T(8,128)(2,1)S(1)}, u32[]{:S(2)}, u32[]{:S(2)}) collective-permute-start(bf16[4,128,256]{2,1,0:T(8,128)(2,1)S(1)} %get-tuple-element.56.refs_1_), channel_id=1, source_target_pairs={{0,3},{1,0},{2,1},{3,2},{4,7},{5,4},{6,5},{7,6},{8,11},{9,8},{10,9... | collective-permute-start | bytes 786440 | tf_op jit(solution)/shard_map/ppermute | solution.py:505
  5.6 1.4 %collective-permute-start.2 = (bf16[4,128,256]{2,1,0:T(8,128)(2,1)S(1)}, bf16[4,128,256]{2,1,0:T(8,128)(2,1)S(1)}, u32[]{:S(2)}, u32[]{:S(2)}) collective-permute-start(bf16[4,128,256]{2,1,0:T(8,128)(2,1)S(1)} %get-tuple-element.55.refs_0_), channel_id=1, source_target_pairs={{0,3},{1,0},{2,1},{3,2},{4,7},{5,4},{6,5},{7,6},{8,11},{9,8},{10,9... | collective-permute-start | bytes 786440 | tf_op jit(solution)/shard_map/ppermute | solution.py:505
  7.1 4.9 %counts.2 = (bf16[4,256,512]{2,1,0:T(8,128)(2,1)S(1)}, s32[16]{0:T(128)S(1)}) custom-call(s32[1]{0:T(128)} %bitcast.1.mine_ref, s32[8,4096]{1,0:T(8,128)} %ids_ref.3, s32[8,4096]{1,0:T(8,128)} %own_ref.3), custom_call_target="tpu_custom_call" | custom-call | flops 1610612736 | bytes 3145728 | tf_op jit(solution)/shard_map/counts/pallas_call | solution.py:140
  12.0 2.7 %collective-permute-start.4 = (bf16[4,128,256]{2,1,0:T(8,128)(2,1)S(1)}, bf16[4,128,256]{2,1,0:T(8,128)(2,1)S(1)}, u32[]{:S(2)}, u32[]{:S(2)}) collective-permute-start(bf16[4,128,256]{2,1,0:T(8,128)(2,1)S(1)} %collective-permute-done.1.refs_3_), channel_id=1, source_target_pairs={{0,3},{1,0},{2,1},{3,2},{4,7},{5,4},{6,5},{7,6},{8,11},{9,8},{10,9... | collective-permute-start | bytes 786440 | tf_op jit(solution)/shard_map/ppermute | solution.py:505
  14.7 5.0 %counts.3 = (bf16[4,256,512]{2,1,0:T(8,128)(2,1)S(1)}, bf16[256,2048]{1,0:T(8,128)(2,1)S(1)}, bf16[2,2048,512]{2,1,0:T(8,128)(2,1)S(1)}, bf16[2,512,2048]{2,1,0:T(8,128)(2,1)S(1)}) custom-call(s32[1]{0:T(128)} %bitcast.1.mine_ref, s32[8,4096]{1,0:T(8,128)} %ids_ref.3, s32[8,4096]{1,0:T(8,128)} %own_ref.3, s32[16]{0:T(128)S(1)} %get-tuple-element.58.refs_0_, ...), custom_call_target="tpu_custom_call" | custom-call | flops 1610612736 | bytes 3145728 | tf_op jit(solution)/shard_map/counts/pallas_call | solution.py:140
  19.7 2.2 %collective-permute-done.4.refs_5_ = bf16[4,128,256]{2,1,0:T(8,128)(2,1)S(1)} collective-permute-done((bf16[4,128,256]{2,1,0:T(8,128)(2,1)S(1)}, bf16[4,128,256]{2,1,0:T(8,128)(2,1)S(1)}, u32[]{:S(2)}, u32[]{:S(2)}) %collective-permute-start.4) | collective-permute-done | bytes 262176 | tf_op jit(solution)/shard_map/ppermute | solution.py:505
  21.9 1.5 %first_sums.1 = (bf16[256,2048]{1,0:T(8,128)(2,1)S(1)}, bf16[256,2048]{1,0:T(8,128)(2,1)S(1)}, bf16[256,512]{1,0:T(8,128)(2,1)S(1)}) custom-call(s32[1]{0:T(128)} %bitcast.core_ref, bf16[4,256,512]{2,1,0:T(8,128)(2,1)S(1)} %get-tuple-element.73.counts_a.in_ref, bf16[4,256,512]{2,1,0:T(8,128)(2,1)S(1)} %get-tuple-element.88.counts_b.in_ref, ...), custom_call_target="tpu_custom_call" | custom-call | flops 1610612736 | bytes 10485760 | tf_op jit(solution)/shard_map/first_sums/pallas_call | solution.py:240
  23.4 4.4 %collective-permute-start.6 = (bf16[256,512]{1,0:T(8,128)(2,1)S(1)}, bf16[256,512]{1,0:T(8,128)(2,1)S(1)}, u32[]{:S(2)}, u32[]{:S(2)}) collective-permute-start(bf16[256,512]{1,0:T(8,128)(2,1)S(1)} %get-tuple-element.67), channel_id=1, source_target_pairs={{0,4},{4,0},{1,5},{5,1},{2,6},{6,2},{3,7},{7,3},{8,12},{12,8},{9,1... | collective-permute-start | bytes 786440 | tf_op jit(solution)/shard_map/ppermute | solution.py:256
  29.0 10.4 %all_to_all.20.refs_0_ = bf16[8,32,512]{2,1,0:T(8,128)(2,1)S(1)} all-to-all(bf16[8,32,512]{2,1,0:T(8,128)(2,1)S(1)} %cut.2), channel_id=1, replica_groups=mesh['x'=4,'zh'=4,'zl'=2,'c'=2,'row'=4] {'x','zl'}, dimensions={0} | all-to-all | bytes 524288 | tf_op jit(solution)/shard_map/all_to_all | solution.py:297
  39.4 6.1 %collective-permute-start.9 = (bf16[1,32,512]{2,1,0:T(8,128)(2,1)S(1)}, bf16[1,32,512]{2,1,0:T(8,128)(2,1)S(1)}, u32[]{:S(2)}, u32[]{:S(2)}) collective-permute-start(bf16[1,32,512]{2,1,0:T(8,128)(2,1)S(1)} %total.4.refs_0_), channel_id=1, source_target_pairs={{0,32},{16,48},{32,0},{48,16},{1,33},{17,49},{33,1},{49,17},{2,34}... | collective-permute-start | bytes 98312 | tf_op jit(solution)/shard_map/ppermute | solution.py:301
  45.8 2.1 %collective-permute-start.7 = (bf16[1,32,512]{2,1,0:T(8,128)(2,1)S(1)}, bf16[1,32,512]{2,1,0:T(8,128)(2,1)S(1)}, u32[]{:S(2)}, u32[]{:S(2)}) collective-permute-start(bf16[1,32,512]{2,1,0:T(8,128)(2,1)S(1)} %total.4.refs_0_), channel_id=1, source_target_pairs={{0,16},{16,32},{32,48},{48,0},{1,17},{17,33},{33,49},{49,1},{2,18}... | collective-permute-start | bytes 98312 | tf_op jit(solution)/shard_map/ppermute | solution.py:301
  48.2 1.0 collective-permute-done.8.refs_2_
  49.2 1.8 %collective-permute-done.7.refs_1_ = bf16[1,32,512]{2,1,0:T(8,128)(2,1)S(1)} collective-permute-done((bf16[1,32,512]{2,1,0:T(8,128)(2,1)S(1)}, bf16[1,32,512]{2,1,0:T(8,128)(2,1)S(1)}, u32[]{:S(2)}, u32[]{:S(2)}) %collective-permute-start.7) | collective-permute-done | bytes 32800 | tf_op jit(solution)/shard_map/ppermute | solution.py:301
  51.0 8.7 %all_to_all.21.mine_ref = bf16[8,32,512]{2,1,0:T(8,128)(2,1)S(1)} all-to-all(bf16[8,32,512]{2,1,0:T(8,128)(2,1)S(1)} %total.5), channel_id=1, replica_groups=mesh['x'=4,'zh'=4,'zl'=2,'c'=2,'row'=4] {'x','zl'}, dimensions={0} | all-to-all | bytes 524288 | tf_op jit(solution)/shard_map/all_to_all | solution.py:297
  59.7 4.0 %collective-permute-start.10 = (bf16[8,32,512]{2,1,0:T(8,128)(2,1)S(1)}, bf16[8,32,512]{2,1,0:T(8,128)(2,1)S(1)}, u32[]{:S(2)}, u32[]{:S(2)}) collective-permute-start(bf16[8,32,512]{2,1,0:T(8,128)(2,1)S(1)} %all_to_all.21.mine_ref), channel_id=1, source_target_pairs={{0,4},{4,0},{1,5},{5,1},{2,6},{6,2},{3,7},{7,3},{8,12},{12,8},{9,1... | collective-permute-start | bytes 786440 | tf_op jit(solution)/shard_map/ppermute | solution.py:256
  64.9 1.8 %middle.1 = (bf16[256,2048]{1,0:T(8,128)(2,1)S(1)}, bf16[256,2048]{1,0:T(8,128)(2,1)S(1)}, bf16[256,2048]{1,0:T(8,128)(2,1)S(1)}, bf16[256,512]{1,0:T(8,128)(2,1)S(1)}) custom-call(s32[1]{0:T(128)} %bitcast.core_ref, f32[256,2048]{1,0:T(8,128)S(1)} %product.2.prod, bf16[8,32,512]{2,1,0:T(8,128)(2,1)S(1)} %collective-permute-done.10.other_ref, ...), custom_call_target="tpu_custom_call" | custom-call | flops 2147483648 | bytes 8388608 | tf_op jit(solution)/shard_map/middle/pallas_call | solution.py:392
  68.4 9.0 %all_to_all.22.refs_0_ = bf16[8,32,512]{2,1,0:T(8,128)(2,1)S(1)} all-to-all(bf16[8,32,512]{2,1,0:T(8,128)(2,1)S(1)} %cut.3), channel_id=1, replica_groups=mesh['x'=4,'zh'=4,'zl'=2,'c'=2,'row'=4] {'x','zl'}, dimensions={0} | all-to-all | bytes 524288 | tf_op jit(solution)/shard_map/all_to_all | solution.py:297
  77.5 4.3 %collective-permute-start.14 = (bf16[1,32,512]{2,1,0:T(8,128)(2,1)S(1)}, bf16[1,32,512]{2,1,0:T(8,128)(2,1)S(1)}, u32[]{:S(2)}, u32[]{:S(2)}) collective-permute-start(bf16[1,32,512]{2,1,0:T(8,128)(2,1)S(1)} %total.6.refs_0_), channel_id=1, source_target_pairs={{0,32},{16,48},{32,0},{48,16},{1,33},{17,49},{33,1},{49,17},{2,34}... | collective-permute-start | bytes 98312 | tf_op jit(solution)/shard_map/ppermute | solution.py:301
  81.8 2.4 %collective-permute-start.12 = (bf16[1,32,512]{2,1,0:T(8,128)(2,1)S(1)}, bf16[1,32,512]{2,1,0:T(8,128)(2,1)S(1)}, u32[]{:S(2)}, u32[]{:S(2)}) collective-permute-start(bf16[1,32,512]{2,1,0:T(8,128)(2,1)S(1)} %total.6.refs_0_), channel_id=1, source_target_pairs={{0,16},{16,32},{32,48},{48,0},{1,17},{17,33},{33,49},{49,1},{2,18}... | collective-permute-start | bytes 98312 | tf_op jit(solution)/shard_map/ppermute | solution.py:301
  84.5 1.3 %collective-permute-done.13.refs_2_ = bf16[1,32,512]{2,1,0:T(8,128)(2,1)S(1)} collective-permute-done((bf16[1,32,512]{2,1,0:T(8,128)(2,1)S(1)}, bf16[1,32,512]{2,1,0:T(8,128)(2,1)S(1)}, u32[]{:S(2)}, u32[]{:S(2)}) %collective-permute-start.13) | collective-permute-done | bytes 32800 | tf_op jit(solution)/shard_map/ppermute | solution.py:301
  85.7 1.1 collective-permute-done.12.refs_1_
  86.8 9.1 %all_to_all.23.mine_ref = bf16[8,32,512]{2,1,0:T(8,128)(2,1)S(1)} all-to-all(bf16[8,32,512]{2,1,0:T(8,128)(2,1)S(1)} %total.7), channel_id=1, replica_groups=mesh['x'=4,'zh'=4,'zl'=2,'c'=2,'row'=4] {'x','zl'}, dimensions={0} | all-to-all | bytes 524288 | tf_op jit(solution)/shard_map/all_to_all | solution.py:297
  95.9 3.8 %collective-permute-start.15 = (bf16[8,32,512]{2,1,0:T(8,128)(2,1)S(1)}, bf16[8,32,512]{2,1,0:T(8,128)(2,1)S(1)}, u32[]{:S(2)}, u32[]{:S(2)}) collective-permute-start(bf16[8,32,512]{2,1,0:T(8,128)(2,1)S(1)} %all_to_all.23.mine_ref), channel_id=1, source_target_pairs={{0,4},{4,0},{1,5},{5,1},{2,6},{6,2},{3,7},{7,3},{8,12},{12,8},{9,1... | collective-permute-start | bytes 786440 | tf_op jit(solution)/shard_map/ppermute | solution.py:256
  101.0 1.8 %far_rows.1 = (bf16[256,2048]{1,0:T(8,128)(2,1)S(1)}, bf16[256,2048]{1,0:T(8,128)(2,1)S(1)}, bf16[4,128,256]{2,1,0:T(8,128)(2,1)S(1)}, bf16[4,128,256]{2,1,0:T(8,128)(2,1)S(1)}) custom-call(s32[1]{0:T(128)} %bitcast.core_ref, f32[256,2048]{1,0:T(8,128)S(1)} %product.3.prod, bf16[8,32,512]{2,1,0:T(8,128)(2,1)S(1)} %collective-permute-done.15.other_ref, ...), custom_call_target="tpu_custom_call" | custom-call | flops 1342177280 | bytes 7340032 | tf_op jit(solution)/shard_map/far_rows/pallas_call | solution.py:431
  103.4 2.1 %collective-permute-start.20 = (bf16[4,128,256]{2,1,0:T(8,128)(2,1)S(1)}, bf16[4,128,256]{2,1,0:T(8,128)(2,1)S(1)}, u32[]{:S(2)}, u32[]{:S(2)}) collective-permute-start(bf16[4,128,256]{2,1,0:T(8,128)(2,1)S(1)} %get-tuple-element.105), channel_id=1, source_target_pairs={{0,3},{1,0},{2,1},{3,2},{4,7},{5,4},{6,5},{7,6},{8,11},{9,8},{10,9... | collective-permute-start | bytes 786440 | tf_op jit(solution)/shard_map/ppermute | solution.py:505
  108.0 3.6 %collective-permute-done.17 = bf16[4,128,256]{2,1,0:T(8,128)(2,1)S(1)} collective-permute-done((bf16[4,128,256]{2,1,0:T(8,128)(2,1)S(1)}, bf16[4,128,256]{2,1,0:T(8,128)(2,1)S(1)}, u32[]{:S(2)}, u32[]{:S(2)}) %collective-permute-start.17) | collective-permute-done | bytes 262176 | tf_op jit(solution)/shard_map/ppermute | solution.py:501
  111.9 2.7 %collective-permute-start.21 = (bf16[4,128,256]{2,1,0:T(8,128)(2,1)S(1)}, bf16[4,128,256]{2,1,0:T(8,128)(2,1)S(1)}, u32[]{:S(2)}, u32[]{:S(2)}) collective-permute-start(bf16[4,128,256]{2,1,0:T(8,128)(2,1)S(1)} %add_convert_fusion), channel_id=1, source_target_pairs={{0,3},{1,0},{2,1},{3,2},{4,7},{5,4},{6,5},{7,6},{8,11},{9,8},{10,9... | collective-permute-start | bytes 786440 | tf_op jit(solution)/shard_map/ppermute | solution.py:505
  114.6 1.7 %collective-permute-done.16.near_a = bf16[4,128,256]{2,1,0:T(8,128)(2,1)S(1)} collective-permute-done((bf16[4,128,256]{2,1,0:T(8,128)(2,1)S(1)}, bf16[4,128,256]{2,1,0:T(8,128)(2,1)S(1)}, u32[]{:S(2)}, u32[]{:S(2)}) %collective-permute-start.16) | collective-permute-done | bytes 262176 | tf_op jit(solution)/shard_map/ppermute | solution.py:505
  117.2 5.6 %collective-permute-done.18.far_a = bf16[4,128,256]{2,1,0:T(8,128)(2,1)S(1)} collective-permute-done((bf16[4,128,256]{2,1,0:T(8,128)(2,1)S(1)}, bf16[4,128,256]{2,1,0:T(8,128)(2,1)S(1)}, u32[]{:S(2)}, u32[]{:S(2)}) %collective-permute-start.18) | collective-permute-done | bytes 262176 | tf_op jit(solution)/shard_map/ppermute | solution.py:501
  122.9 1.1 finish.1
  (40 shorter events, 10.7 us)
Async XLA Ops:
  1.9 10.1 %collective-permute-start = (bf16[4,128,256]{2,1,0:T(8,128)(2,1)S(1)}, bf16[4,128,256]{2,1,0:T(8,128)(2,1)S(1)}, u32[]{:S(2)}, u32[]{:S(2)}) collective-permute-start(bf16[4,128,256]{2,1,0:T(8,128)(2,1)S(1)} %get-tuple-element.55.refs_0_), channel_id=1, source_target_pairs={{0,1},{1,2},{2,3},{3,0},{4,5},{5,6},{6,7},{7,4},{8,9},{9,10},{10,1... | collective-permute-start | bytes 786440 | tf_op jit(solution)/shard_map/ppermute | solution.py:501
  4.1 7.9 %collective-permute-start.1 = (bf16[4,128,256]{2,1,0:T(8,128)(2,1)S(1)}, bf16[4,128,256]{2,1,0:T(8,128)(2,1)S(1)}, u32[]{:S(2)}, u32[]{:S(2)}) collective-permute-start(bf16[4,128,256]{2,1,0:T(8,128)(2,1)S(1)} %get-tuple-element.56.refs_1_), channel_id=1, source_target_pairs={{0,3},{1,0},{2,1},{3,2},{4,7},{5,4},{6,5},{7,6},{8,11},{9,8},{10,9... | collective-permute-start | bytes 786440 | tf_op jit(solution)/shard_map/ppermute | solution.py:505
  5.6 14.0 %collective-permute-start.2 = (bf16[4,128,256]{2,1,0:T(8,128)(2,1)S(1)}, bf16[4,128,256]{2,1,0:T(8,128)(2,1)S(1)}, u32[]{:S(2)}, u32[]{:S(2)}) collective-permute-start(bf16[4,128,256]{2,1,0:T(8,128)(2,1)S(1)} %get-tuple-element.55.refs_0_), channel_id=1, source_target_pairs={{0,3},{1,0},{2,1},{3,2},{4,7},{5,4},{6,5},{7,6},{8,11},{9,8},{10,9... | collective-permute-start | bytes 786440 | tf_op jit(solution)/shard_map/ppermute | solution.py:505
  7.0 12.7 %collective-permute-start.5 = (bf16[4,128,256]{2,1,0:T(8,128)(2,1)S(1)}, bf16[4,128,256]{2,1,0:T(8,128)(2,1)S(1)}, u32[]{:S(2)}, u32[]{:S(2)}) collective-permute-start(bf16[4,128,256]{2,1,0:T(8,128)(2,1)S(1)} %get-tuple-element.56.refs_1_), channel_id=1, source_target_pairs={{0,1},{1,2},{2,3},{3,0},{4,5},{5,6},{6,7},{7,4},{8,9},{9,10},{10,1... | collective-permute-start | bytes 786440 | tf_op jit(solution)/shard_map/ppermute | solution.py:501
  12.0 9.9 %collective-permute-start.4 = (bf16[4,128,256]{2,1,0:T(8,128)(2,1)S(1)}, bf16[4,128,256]{2,1,0:T(8,128)(2,1)S(1)}, u32[]{:S(2)}, u32[]{:S(2)}) collective-permute-start(bf16[4,128,256]{2,1,0:T(8,128)(2,1)S(1)} %collective-permute-done.1.refs_3_), channel_id=1, source_target_pairs={{0,3},{1,0},{2,1},{3,2},{4,7},{5,4},{6,5},{7,6},{8,11},{9,8},{10,9... | collective-permute-start | bytes 786440 | tf_op jit(solution)/shard_map/ppermute | solution.py:505
  14.7 7.2 %collective-permute-start.3 = (bf16[4,128,256]{2,1,0:T(8,128)(2,1)S(1)}, bf16[4,128,256]{2,1,0:T(8,128)(2,1)S(1)}, u32[]{:S(2)}, u32[]{:S(2)}) collective-permute-start(bf16[4,128,256]{2,1,0:T(8,128)(2,1)S(1)} %collective-permute-done.refs_6_), channel_id=1, source_target_pairs={{0,1},{1,2},{2,3},{3,0},{4,5},{5,6},{6,7},{7,4},{8,9},{9,10},{10,1... | collective-permute-start | bytes 786440 | tf_op jit(solution)/shard_map/ppermute | solution.py:501
  23.4 5.6 %collective-permute-start.6 = (bf16[256,512]{1,0:T(8,128)(2,1)S(1)}, bf16[256,512]{1,0:T(8,128)(2,1)S(1)}, u32[]{:S(2)}, u32[]{:S(2)}) collective-permute-start(bf16[256,512]{1,0:T(8,128)(2,1)S(1)} %get-tuple-element.67), channel_id=1, source_target_pairs={{0,4},{4,0},{1,5},{5,1},{2,6},{6,2},{3,7},{7,3},{8,12},{12,8},{9,1... | collective-permute-start | bytes 786440 | tf_op jit(solution)/shard_map/ppermute | solution.py:256
  39.4 8.8 %collective-permute-start.9 = (bf16[1,32,512]{2,1,0:T(8,128)(2,1)S(1)}, bf16[1,32,512]{2,1,0:T(8,128)(2,1)S(1)}, u32[]{:S(2)}, u32[]{:S(2)}) collective-permute-start(bf16[1,32,512]{2,1,0:T(8,128)(2,1)S(1)} %total.4.refs_0_), channel_id=1, source_target_pairs={{0,32},{16,48},{32,0},{48,16},{1,33},{17,49},{33,1},{49,17},{2,34}... | collective-permute-start | bytes 98312 | tf_op jit(solution)/shard_map/ppermute | solution.py:301
  45.5 3.7 %collective-permute-start.8 = (bf16[1,32,512]{2,1,0:T(8,128)(2,1)S(1)}, bf16[1,32,512]{2,1,0:T(8,128)(2,1)S(1)}, u32[]{:S(2)}, u32[]{:S(2)}) collective-permute-start(bf16[1,32,512]{2,1,0:T(8,128)(2,1)S(1)} %total.4.refs_0_), channel_id=1, source_target_pairs={{0,48},{16,0},{32,16},{48,32},{1,49},{17,1},{33,17},{49,33},{2,50}... | collective-permute-start | bytes 98312 | tf_op jit(solution)/shard_map/ppermute | solution.py:301
  45.8 5.2 %collective-permute-start.7 = (bf16[1,32,512]{2,1,0:T(8,128)(2,1)S(1)}, bf16[1,32,512]{2,1,0:T(8,128)(2,1)S(1)}, u32[]{:S(2)}, u32[]{:S(2)}) collective-permute-start(bf16[1,32,512]{2,1,0:T(8,128)(2,1)S(1)} %total.4.refs_0_), channel_id=1, source_target_pairs={{0,16},{16,32},{32,48},{48,0},{1,17},{17,33},{33,49},{49,1},{2,18}... | collective-permute-start | bytes 98312 | tf_op jit(solution)/shard_map/ppermute | solution.py:301
  59.7 5.2 %copy-start = (f32[2,2048]{1,0:T(2,128)S(1)}, f32[2,2048]{1,0:T(2,128)}, u32[]{:S(2)}) copy-start(f32[2,2048]{1,0:T(2,128)} %b_ref.3) | copy-start | bytes 49156
  59.7 5.2 %collective-permute-start.10 = (bf16[8,32,512]{2,1,0:T(8,128)(2,1)S(1)}, bf16[8,32,512]{2,1,0:T(8,128)(2,1)S(1)}, u32[]{:S(2)}, u32[]{:S(2)}) collective-permute-start(bf16[8,32,512]{2,1,0:T(8,128)(2,1)S(1)} %all_to_all.21.mine_ref), channel_id=1, source_target_pairs={{0,4},{4,0},{1,5},{5,1},{2,6},{6,2},{3,7},{7,3},{8,12},{12,8},{9,1... | collective-permute-start | bytes 786440 | tf_op jit(solution)/shard_map/ppermute | solution.py:256
  66.7 1.6 %collective-permute-start.11 = (bf16[256,512]{1,0:T(8,128)(2,1)S(1)}, bf16[256,512]{1,0:T(8,128)(2,1)S(1)}, u32[]{:S(2)}, u32[]{:S(2)}) collective-permute-start(bf16[256,512]{1,0:T(8,128)(2,1)S(1)} %get-tuple-element.82), channel_id=1, source_target_pairs={{0,4},{4,0},{1,5},{5,1},{2,6},{6,2},{3,7},{7,3},{8,12},{12,8},{9,1... | collective-permute-start | bytes 786440 | tf_op jit(solution)/shard_map/ppermute | solution.py:256
  77.5 7.0 %collective-permute-start.14 = (bf16[1,32,512]{2,1,0:T(8,128)(2,1)S(1)}, bf16[1,32,512]{2,1,0:T(8,128)(2,1)S(1)}, u32[]{:S(2)}, u32[]{:S(2)}) collective-permute-start(bf16[1,32,512]{2,1,0:T(8,128)(2,1)S(1)} %total.6.refs_0_), channel_id=1, source_target_pairs={{0,32},{16,48},{32,0},{48,16},{1,33},{17,49},{33,1},{49,17},{2,34}... | collective-permute-start | bytes 98312 | tf_op jit(solution)/shard_map/ppermute | solution.py:301
  81.8 4.0 %collective-permute-start.13 = (bf16[1,32,512]{2,1,0:T(8,128)(2,1)S(1)}, bf16[1,32,512]{2,1,0:T(8,128)(2,1)S(1)}, u32[]{:S(2)}, u32[]{:S(2)}) collective-permute-start(bf16[1,32,512]{2,1,0:T(8,128)(2,1)S(1)} %total.6.refs_0_), channel_id=1, source_target_pairs={{0,48},{16,0},{32,16},{48,32},{1,49},{17,1},{33,17},{49,33},{2,50}... | collective-permute-start | bytes 98312 | tf_op jit(solution)/shard_map/ppermute | solution.py:301
  81.8 5.0 %collective-permute-start.12 = (bf16[1,32,512]{2,1,0:T(8,128)(2,1)S(1)}, bf16[1,32,512]{2,1,0:T(8,128)(2,1)S(1)}, u32[]{:S(2)}, u32[]{:S(2)}) collective-permute-start(bf16[1,32,512]{2,1,0:T(8,128)(2,1)S(1)} %total.6.refs_0_), channel_id=1, source_target_pairs={{0,16},{16,32},{32,48},{48,0},{1,17},{17,33},{33,49},{49,1},{2,18}... | collective-permute-start | bytes 98312 | tf_op jit(solution)/shard_map/ppermute | solution.py:301
  95.9 5.0 %collective-permute-start.15 = (bf16[8,32,512]{2,1,0:T(8,128)(2,1)S(1)}, bf16[8,32,512]{2,1,0:T(8,128)(2,1)S(1)}, u32[]{:S(2)}, u32[]{:S(2)}) collective-permute-start(bf16[8,32,512]{2,1,0:T(8,128)(2,1)S(1)} %all_to_all.23.mine_ref), channel_id=1, source_target_pairs={{0,4},{4,0},{1,5},{5,1},{2,6},{6,2},{3,7},{7,3},{8,12},{12,8},{9,1... | collective-permute-start | bytes 786440 | tf_op jit(solution)/shard_map/ppermute | solution.py:256
  102.7 8.9 %collective-permute-start.17 = (bf16[4,128,256]{2,1,0:T(8,128)(2,1)S(1)}, bf16[4,128,256]{2,1,0:T(8,128)(2,1)S(1)}, u32[]{:S(2)}, u32[]{:S(2)}) collective-permute-start(bf16[4,128,256]{2,1,0:T(8,128)(2,1)S(1)} %get-tuple-element.102), channel_id=1, source_target_pairs={{0,1},{1,2},{2,3},{3,0},{4,5},{5,6},{6,7},{7,4},{8,9},{9,10},{10,1... | collective-permute-start | bytes 786440 | tf_op jit(solution)/shard_map/ppermute | solution.py:501
  103.4 8.4 %collective-permute-start.20 = (bf16[4,128,256]{2,1,0:T(8,128)(2,1)S(1)}, bf16[4,128,256]{2,1,0:T(8,128)(2,1)S(1)}, u32[]{:S(2)}, u32[]{:S(2)}) collective-permute-start(bf16[4,128,256]{2,1,0:T(8,128)(2,1)S(1)} %get-tuple-element.105), channel_id=1, source_target_pairs={{0,3},{1,0},{2,1},{3,2},{4,7},{5,4},{6,5},{7,6},{8,11},{9,8},{10,9... | collective-permute-start | bytes 786440 | tf_op jit(solution)/shard_map/ppermute | solution.py:505
  106.5 9.9 %collective-permute-start.16 = (bf16[4,128,256]{2,1,0:T(8,128)(2,1)S(1)}, bf16[4,128,256]{2,1,0:T(8,128)(2,1)S(1)}, u32[]{:S(2)}, u32[]{:S(2)}) collective-permute-start(bf16[4,128,256]{2,1,0:T(8,128)(2,1)S(1)} %get-tuple-element.100), channel_id=1, source_target_pairs={{0,3},{1,0},{2,1},{3,2},{4,7},{5,4},{6,5},{7,6},{8,11},{9,8},{10,9... | collective-permute-start | bytes 786440 | tf_op jit(solution)/shard_map/ppermute | solution.py:505
  107.4 9.9 %collective-permute-start.19 = (bf16[4,128,256]{2,1,0:T(8,128)(2,1)S(1)}, bf16[4,128,256]{2,1,0:T(8,128)(2,1)S(1)}, u32[]{:S(2)}, u32[]{:S(2)}) collective-permute-start(bf16[4,128,256]{2,1,0:T(8,128)(2,1)S(1)} %get-tuple-element.103), channel_id=1, source_target_pairs={{0,1},{1,2},{2,3},{3,0},{4,5},{5,6},{6,7},{7,4},{8,9},{9,10},{10,1... | collective-permute-start | bytes 786440 | tf_op jit(solution)/shard_map/ppermute | solution.py:501
  111.7 11.2 %collective-permute-start.18 = (bf16[4,128,256]{2,1,0:T(8,128)(2,1)S(1)}, bf16[4,128,256]{2,1,0:T(8,128)(2,1)S(1)}, u32[]{:S(2)}, u32[]{:S(2)}) collective-permute-start(bf16[4,128,256]{2,1,0:T(8,128)(2,1)S(1)} %add_convert_fusion.1), channel_id=1, source_target_pairs={{0,1},{1,2},{2,3},{3,0},{4,5},{5,6},{6,7},{7,4},{8,9},{9,10},{10,1... | collective-permute-start | bytes 786440 | tf_op jit(solution)/shard_map/ppermute | solution.py:501
  111.9 11.0 %collective-permute-start.21 = (bf16[4,128,256]{2,1,0:T(8,128)(2,1)S(1)}, bf16[4,128,256]{2,1,0:T(8,128)(2,1)S(1)}, u32[]{:S(2)}, u32[]{:S(2)}) collective-permute-start(bf16[4,128,256]{2,1,0:T(8,128)(2,1)S(1)} %add_convert_fusion), channel_id=1, source_target_pairs={{0,3},{1,0},{2,1},{3,2},{4,7},{5,4},{6,5},{7,6},{8,11},{9,8},{10,9... | collective-permute-start | bytes 786440 | tf_op jit(solution)/shard_map/ppermute | solution.py:505

commit v9 on v8

--- a/solution.py
+++ b/solution.py
@@ -10,6 +10,7 @@
 F32 = jnp.float32
 BF16 = jnp.bfloat16
 EB = 512
+EARLY = 2
 NT = (((1,), (1,)), ((), ()))
 TN = (((0,), (0,)), ((), ()))
 
@@ -125,8 +126,8 @@
 def make_counts(mine, ids, owners, samp, rows, edges=None, loads=()):
     tabs, entries = ids.shape
     assert rows == 2 * samp and samp <= 256
-    half = tabs // 2
-    out_shape = [pltpu.VMEM((half, samp, rows), BF16)]
+    count = EARLY if edges is None else tabs - EARLY
+    out_shape = [pltpu.VMEM((count, samp, rows), BF16)]
     args = (mine, pinned(ids), pinned(owners))
     in_specs, out_specs = [smem(), hbm(), hbm()], [vmem()]
     if edges is None:
@@ -138,7 +139,7 @@
         out_specs += [vmem()] * len(loads)
         out_shape += [pltpu.VMEM(arr.shape, arr.dtype) for arr in loads]
     return pl.pallas_call(
-        functools.partial(counts_kernel, first_table=0 if edges is None else half),
+        functools.partial(counts_kernel, first_table=0 if edges is None else EARLY),
         in_specs=in_specs,
         out_specs=out_specs,
         out_shape=out_shape,
@@ -149,7 +150,7 @@
             pltpu.SemaphoreType.DMA((2 + len(loads),)),
         ],
         compiler_params=params(6),
-        cost_estimate=cost(half * samp * rows * 3072, 3 << 20),
+        cost_estimate=cost(count * samp * rows * 3072, 3 << 20),
         name="counts",
     )(*args)
 
@@ -160,16 +161,20 @@
 
 
 def turned_counts(counts):
-    half, samp, rows = counts.shape
+    count, samp, rows = counts.shape
     return pl.pallas_call(
         turned_kernel,
         in_specs=[vmem()],
         out_specs=vmem(),
-        out_shape=pltpu.VMEM((half, rows, samp), BF16),
+        out_shape=pltpu.VMEM((count, rows, samp), BF16),
         compiler_params=params(8),
         cost_estimate=cost(1 << 29, 2 << 20),
         name="turned",
     )(*kept(counts))
+
+
+def of_table(pair, t):
+    return pair[0][t] if t < EARLY else pair[1][t - EARLY]
 
 
 WIDE = 512
@@ -226,7 +231,7 @@
     for t in range(2 * half):
         side, i = divmod(t, half)
         rows = jnp.concatenate([embs[2 * k + side][i] for k in range(4)], axis=0)
-        pooled = jnp.dot((counts_a, counts_b)[side][i], rows, preferred_element_type=F32).astype(BF16)
+        pooled = jnp.dot(of_table((counts_a, counts_b), t), rows, preferred_element_type=F32).astype(BF16)
         at = slice(t * emb, (t + 1) * emb)
         pooled_ref[:, at] = pooled
         wide_ref[:, at] = (cot[:, at].astype(F32) * pooled.astype(F32)).astype(BF16)
@@ -234,8 +239,8 @@
 
 
 def first_sums(core, counts, embs, cot, v, u):
-    half, samp, rows = counts[0].shape
-    emb = embs[0].shape[-1]
+    _, samp, rows = counts[0].shape
+    half, _, emb = embs[0].shape
     rank = v.shape[-1]
     return pl.pallas_call(
         first_kernel,
@@ -401,8 +406,8 @@
     )(core, *kept(prod), other, bias, *kept(pooled, cot, u, v))
 
 
-def row_grads(turned_ref, table, first, count, grad):
-    return jnp.dot(turned_ref[table, first : first + count, :], grad, preferred_element_type=F32)
+def row_grads(turned, table, first, count, grad):
+    return jnp.dot(of_table(turned, table)[first : first + count, :], grad, preferred_element_type=F32)
 
 
 def far_kernel(core_ref, prod, other_ref, b_ref, turned_a, turned_b, pooled, cot, x1, a, u_ref, v_ref, *refs):
@@ -419,12 +424,13 @@
     by_core(core_ref, body, prod, sum_ref, v_ref, u_ref, 1)
     for t in range(2 * half):
         side, i = divmod(t, half)
-        part = row_grads((turned_a, turned_b)[side], i, 2 * rows, rows, grad_ref[:, t * emb : (t + 1) * emb])
+        part = row_grads((turned_a, turned_b), t, 2 * rows, rows, grad_ref[:, t * emb : (t + 1) * emb])
         (far_a, far_b)[side][i] = part.astype(BF16)
 
 
 def far_rows(core, prod, other, bias, turned, pooled, cot, x1, a, u, v):
-    half, rows, samp = turned[0].shape
+    _, rows, samp = turned[0].shape
+    half = (turned[0].shape[0] + turned[1].shape[0]) // 2
     rank = v.shape[-1]
     feats = pooled.shape[1]
     piece = pltpu.VMEM((half, rows // 4, feats // (2 * half)), BF16)
@@ -449,15 +455,16 @@
     for t in range(2 * half):
         side, at = divmod(t, half)
         part = grad[:, t * emb : (t + 1) * emb]
-        first = row_grads(turned[side], at, 0, 2 * rows, part)
+        first = row_grads(turned, t, 0, 2 * rows, part)
         p0_ref[t] = first[:rows]
         (p1_a, p1_b)[side][at] = first[rows:].astype(BF16)
-        (p3_a, p3_b)[side][at] = row_grads(turned[side], at, 3 * rows, rows, part).astype(BF16)
+        (p3_a, p3_b)[side][at] = row_grads(turned, t, 3 * rows, rows, part).astype(BF16)
     copy.wait()
 
 
 def near_rows(turned, grad, crossed):
-    half, rows, samp = turned[0].shape
+    _, rows, samp = turned[0].shape
+    half = (turned[0].shape[0] + turned[1].shape[0]) // 2
     block = (half, rows // 4, grad.shape[1] // (2 * half))
     return pl.pallas_call(
         near_kernel,

time: 124 us -> 124 us (level)
  transfers between devices with their start and end apart: 22 -> 22, of which waited for: 13 -> 14; matrix products, arithmetic and copies ran while one was open for 0% -> 0% of each run, Pallas kernels for 12% -> 11%
where the time goes in v9:
time: 124 us
  starting transfers between devices  42.9 us (35%)
  blocking collectives  37 us (30%)
  waiting for transfers between devices  21.8 us (18%)
  Pallas kernels  21.3 us (17%)
    all_to_all x4, blocking collectives, swap_all(): return lax.all_to_all(arr, ('x', 'zl'), 0, 0, tiled=True)  37 us
    ppermute x6, starting transfers between devices, turn(): return lax.ppermute(arr, 'zh', [(i, i + k & 3) for i in range(4)])  15.1 us
    ppermute x4, starting transfers between devices, swap(): return lax.ppermute(arr, axis, [(0, 1), (1, 0)])  13 us
    ppermute x6, starting transfers between devices, left(): return lax.ppermute(arr, 'row', [(i, i + 3 & 3) for i in range(4)])  10.9 us
    ppermute x6, waiting for transfers between devices, right(): return lax.ppermute(arr, 'row', [(i, i + 1 & 3) for i in range(4)])  10.2 us
    pallas_call x2, Pallas kernels, make_counts(): pl.pallas_call(functools.partial(counts_kernel, first_table=0 if edges is...  9.38 us
    ppermute x6, waiting for transfers between devices, turn(): return lax.ppermute(arr, 'zh', [(i, i + k & 3) for i in range(4)])  5.12 us
    ppermute x6, waiting for transfers between devices, left(): return lax.ppermute(arr, 'row', [(i, i + 3 & 3) for i in range(4)])  4.88 us
  transfers between devices with their start and end apart: 22, of which 14 were waited for; matrix products, arithmetic and copies ran while one was open for 0% of the time, Pallas kernels for 11%

profile of v9, /device:TPU:1, one launch (start us, length us, event | category | flops | bytes accessed | tf_op | source)
XLA Modules:
  0.0 124.1 jit_solution(15343100417438145561)
XLA Ops:
  0.6 1.2 %cast.1 = (bf16[4,128,256]{2,1,0:T(8,128)(2,1)S(1)}, bf16[4,128,256]{2,1,0:T(8,128)(2,1)S(1)}) custom-call(f32[8,128,256]{2,1,0:T(8,128)} %in_ref.1), custom_call_target="tpu_custom_call" | custom-call | flops 262144 | bytes 1572864 | tf_op jit(solution)/shard_map/cast/pallas_call | solution.py:58
  1.9 2.2 %collective-permute-start = (bf16[4,128,256]{2,1,0:T(8,128)(2,1)S(1)}, bf16[4,128,256]{2,1,0:T(8,128)(2,1)S(1)}, u32[]{:S(2)}, u32[]{:S(2)}) collective-permute-start(bf16[4,128,256]{2,1,0:T(8,128)(2,1)S(1)} %get-tuple-element.55.refs_0_), channel_id=1, source_target_pairs={{0,1},{1,2},{2,3},{3,0},{4,5},{5,6},{6,7},{7,4},{8,9},{9,10},{10,1... | collective-permute-start | bytes 786440 | tf_op jit(solution)/shard_map/ppermute | solution.py:508
  4.1 1.5 %collective-permute-start.1 = (bf16[4,128,256]{2,1,0:T(8,128)(2,1)S(1)}, bf16[4,128,256]{2,1,0:T(8,128)(2,1)S(1)}, u32[]{:S(2)}, u32[]{:S(2)}) collective-permute-start(bf16[4,128,256]{2,1,0:T(8,128)(2,1)S(1)} %get-tuple-element.56.refs_1_), channel_id=1, source_target_pairs={{0,3},{1,0},{2,1},{3,2},{4,7},{5,4},{6,5},{7,6},{8,11},{9,8},{10,9... | collective-permute-start | bytes 786440 | tf_op jit(solution)/shard_map/ppermute | solution.py:512
  5.6 1.4 %collective-permute-start.2 = (bf16[4,128,256]{2,1,0:T(8,128)(2,1)S(1)}, bf16[4,128,256]{2,1,0:T(8,128)(2,1)S(1)}, u32[]{:S(2)}, u32[]{:S(2)}) collective-permute-start(bf16[4,128,256]{2,1,0:T(8,128)(2,1)S(1)} %get-tuple-element.55.refs_0_), channel_id=1, source_target_pairs={{0,3},{1,0},{2,1},{3,2},{4,7},{5,4},{6,5},{7,6},{8,11},{9,8},{10,9... | collective-permute-start | bytes 786440 | tf_op jit(solution)/shard_map/ppermute | solution.py:512
  7.1 3.2 %counts.2 = (bf16[2,256,512]{2,1,0:T(8,128)(2,1)S(1)}, s32[16]{0:T(128)S(1)}) custom-call(s32[1]{0:T(128)} %bitcast.1.mine_ref, s32[8,4096]{1,0:T(8,128)} %ids_ref.3, s32[8,4096]{1,0:T(8,128)} %own_ref.3), custom_call_target="tpu_custom_call" | custom-call | flops 805306368 | bytes 3145728 | tf_op jit(solution)/shard_map/counts/pallas_call | solution.py:141
  10.7 2.3 %collective-permute-start.4 = (bf16[4,128,256]{2,1,0:T(8,128)(2,1)S(1)}, bf16[4,128,256]{2,1,0:T(8,128)(2,1)S(1)}, u32[]{:S(2)}, u32[]{:S(2)}) collective-permute-start(bf16[4,128,256]{2,1,0:T(8,128)(2,1)S(1)} %collective-permute-done.1.refs_3_), channel_id=1, source_target_pairs={{0,3},{1,0},{2,1},{3,2},{4,7},{5,4},{6,5},{7,6},{8,11},{9,8},{10,9... | collective-permute-start | bytes 786440 | tf_op jit(solution)/shard_map/ppermute | solution.py:512
  13.0 6.2 %counts.3 = (bf16[6,256,512]{2,1,0:T(8,128)(2,1)S(1)}, bf16[256,2048]{1,0:T(8,128)(2,1)S(1)}, bf16[2,2048,512]{2,1,0:T(8,128)(2,1)S(1)}, bf16[2,512,2048]{2,1,0:T(8,128)(2,1)S(1)}) custom-call(s32[1]{0:T(128)} %bitcast.1.mine_ref, s32[8,4096]{1,0:T(8,128)} %ids_ref.3, s32[8,4096]{1,0:T(8,128)} %own_ref.3, s32[16]{0:T(128)S(1)} %get-tuple-element.58.refs_0_, ...), custom_call_target="tpu_custom_call" | custom-call | flops 2415919104 | bytes 3145728 | tf_op jit(solution)/shard_map/counts/pallas_call | solution.py:141
  19.2 2.7 %collective-permute-done.4.refs_5_ = bf16[4,128,256]{2,1,0:T(8,128)(2,1)S(1)} collective-permute-done((bf16[4,128,256]{2,1,0:T(8,128)(2,1)S(1)}, bf16[4,128,256]{2,1,0:T(8,128)(2,1)S(1)}, u32[]{:S(2)}, u32[]{:S(2)}) %collective-permute-start.4) | collective-permute-done | bytes 262176 | tf_op jit(solution)/shard_map/ppermute | solution.py:512
  21.9 1.5 %first_sums.1 = (bf16[256,2048]{1,0:T(8,128)(2,1)S(1)}, bf16[256,2048]{1,0:T(8,128)(2,1)S(1)}, bf16[256,512]{1,0:T(8,128)(2,1)S(1)}) custom-call(s32[1]{0:T(128)} %bitcast.core_ref, bf16[2,256,512]{2,1,0:T(8,128)(2,1)S(1)} %get-tuple-element.73.counts_a.in_ref, bf16[6,256,512]{2,1,0:T(8,128)(2,1)S(1)} %get-tuple-element.88.counts_b.in_ref, ...), custom_call_target="tpu_custom_call" | custom-call | flops 1610612736 | bytes 10485760 | tf_op jit(solution)/shard_map/first_sums/pallas_call | solution.py:245
  23.4 4.7 %collective-permute-start.6 = (bf16[256,512]{1,0:T(8,128)(2,1)S(1)}, bf16[256,512]{1,0:T(8,128)(2,1)S(1)}, u32[]{:S(2)}, u32[]{:S(2)}) collective-permute-start(bf16[256,512]{1,0:T(8,128)(2,1)S(1)} %get-tuple-element.67), channel_id=1, source_target_pairs={{0,4},{4,0},{1,5},{5,1},{2,6},{6,2},{3,7},{7,3},{8,12},{12,8},{9,1... | collective-permute-start | bytes 786440 | tf_op jit(solution)/shard_map/ppermute | solution.py:261
  29.3 10.1 %all_to_all.20.refs_0_ = bf16[8,32,512]{2,1,0:T(8,128)(2,1)S(1)} all-to-all(bf16[8,32,512]{2,1,0:T(8,128)(2,1)S(1)} %cut.2), channel_id=1, replica_groups=mesh['x'=4,'zh'=4,'zl'=2,'c'=2,'row'=4] {'x','zl'}, dimensions={0} | all-to-all | bytes 524288 | tf_op jit(solution)/shard_map/all_to_all | solution.py:302
  39.4 6.1 %collective-permute-start.9 = (bf16[1,32,512]{2,1,0:T(8,128)(2,1)S(1)}, bf16[1,32,512]{2,1,0:T(8,128)(2,1)S(1)}, u32[]{:S(2)}, u32[]{:S(2)}) collective-permute-start(bf16[1,32,512]{2,1,0:T(8,128)(2,1)S(1)} %total.4.refs_0_), channel_id=1, source_target_pairs={{0,32},{16,48},{32,0},{48,16},{1,33},{17,49},{33,1},{49,17},{2,34}... | collective-permute-start | bytes 98312 | tf_op jit(solution)/shard_map/ppermute | solution.py:306
  45.8 2.1 %collective-permute-start.7 = (bf16[1,32,512]{2,1,0:T(8,128)(2,1)S(1)}, bf16[1,32,512]{2,1,0:T(8,128)(2,1)S(1)}, u32[]{:S(2)}, u32[]{:S(2)}) collective-permute-start(bf16[1,32,512]{2,1,0:T(8,128)(2,1)S(1)} %total.4.refs_0_), channel_id=1, source_target_pairs={{0,16},{16,32},{32,48},{48,0},{1,17},{17,33},{33,49},{49,1},{2,18}... | collective-permute-start | bytes 98312 | tf_op jit(solution)/shard_map/ppermute | solution.py:306
  48.1 1.1 collective-permute-done.8.refs_2_
  49.2 1.8 %collective-permute-done.7.refs_1_ = bf16[1,32,512]{2,1,0:T(8,128)(2,1)S(1)} collective-permute-done((bf16[1,32,512]{2,1,0:T(8,128)(2,1)S(1)}, bf16[1,32,512]{2,1,0:T(8,128)(2,1)S(1)}, u32[]{:S(2)}, u32[]{:S(2)}) %collective-permute-start.7) | collective-permute-done | bytes 32800 | tf_op jit(solution)/shard_map/ppermute | solution.py:306
  51.0 8.7 %all_to_all.21.mine_ref = bf16[8,32,512]{2,1,0:T(8,128)(2,1)S(1)} all-to-all(bf16[8,32,512]{2,1,0:T(8,128)(2,1)S(1)} %total.5), channel_id=1, replica_groups=mesh['x'=4,'zh'=4,'zl'=2,'c'=2,'row'=4] {'x','zl'}, dimensions={0} | all-to-all | bytes 524288 | tf_op jit(solution)/shard_map/all_to_all | solution.py:302
  59.7 4.0 %collective-permute-start.10 = (bf16[8,32,512]{2,1,0:T(8,128)(2,1)S(1)}, bf16[8,32,512]{2,1,0:T(8,128)(2,1)S(1)}, u32[]{:S(2)}, u32[]{:S(2)}) collective-permute-start(bf16[8,32,512]{2,1,0:T(8,128)(2,1)S(1)} %all_to_all.21.mine_ref), channel_id=1, source_target_pairs={{0,4},{4,0},{1,5},{5,1},{2,6},{6,2},{3,7},{7,3},{8,12},{12,8},{9,1... | collective-permute-start | bytes 786440 | tf_op jit(solution)/shard_map/ppermute | solution.py:261
  64.9 1.8 %middle.1 = (bf16[256,2048]{1,0:T(8,128)(2,1)S(1)}, bf16[256,2048]{1,0:T(8,128)(2,1)S(1)}, bf16[256,2048]{1,0:T(8,128)(2,1)S(1)}, bf16[256,512]{1,0:T(8,128)(2,1)S(1)}) custom-call(s32[1]{0:T(128)} %bitcast.core_ref, f32[256,2048]{1,0:T(8,128)S(1)} %product.2.prod, bf16[8,32,512]{2,1,0:T(8,128)(2,1)S(1)} %collective-permute-done.10.other_ref, ...), custom_call_target="tpu_custom_call" | custom-call | flops 2147483648 | bytes 8388608 | tf_op jit(solution)/shard_map/middle/pallas_call | solution.py:397
  68.4 9.0 %all_to_all.22.refs_0_ = bf16[8,32,512]{2,1,0:T(8,128)(2,1)S(1)} all-to-all(bf16[8,32,512]{2,1,0:T(8,128)(2,1)S(1)} %cut.3), channel_id=1, replica_groups=mesh['x'=4,'zh'=4,'zl'=2,'c'=2,'row'=4] {'x','zl'}, dimensions={0} | all-to-all | bytes 524288 | tf_op jit(solution)/shard_map/all_to_all | solution.py:302
  77.5 4.3 %collective-permute-start.14 = (bf16[1,32,512]{2,1,0:T(8,128)(2,1)S(1)}, bf16[1,32,512]{2,1,0:T(8,128)(2,1)S(1)}, u32[]{:S(2)}, u32[]{:S(2)}) collective-permute-start(bf16[1,32,512]{2,1,0:T(8,128)(2,1)S(1)} %total.6.refs_0_), channel_id=1, source_target_pairs={{0,32},{16,48},{32,0},{48,16},{1,33},{17,49},{33,1},{49,17},{2,34}... | collective-permute-start | bytes 98312 | tf_op jit(solution)/shard_map/ppermute | solution.py:306
  81.8 2.4 %collective-permute-start.12 = (bf16[1,32,512]{2,1,0:T(8,128)(2,1)S(1)}, bf16[1,32,512]{2,1,0:T(8,128)(2,1)S(1)}, u32[]{:S(2)}, u32[]{:S(2)}) collective-permute-start(bf16[1,32,512]{2,1,0:T(8,128)(2,1)S(1)} %total.6.refs_0_), channel_id=1, source_target_pairs={{0,16},{16,32},{32,48},{48,0},{1,17},{17,33},{33,49},{49,1},{2,18}... | collective-permute-start | bytes 98312 | tf_op jit(solution)/shard_map/ppermute | solution.py:306
  84.6 1.1 collective-permute-done.13.refs_2_
  85.7 1.1 collective-permute-done.12.refs_1_
  86.8 9.2 %all_to_all.23.mine_ref = bf16[8,32,512]{2,1,0:T(8,128)(2,1)S(1)} all-to-all(bf16[8,32,512]{2,1,0:T(8,128)(2,1)S(1)} %total.7), channel_id=1, replica_groups=mesh['x'=4,'zh'=4,'zl'=2,'c'=2,'row'=4] {'x','zl'}, dimensions={0} | all-to-all | bytes 524288 | tf_op jit(solution)/shard_map/all_to_all | solution.py:302
  96.0 3.8 %collective-permute-start.15 = (bf16[8,32,512]{2,1,0:T(8,128)(2,1)S(1)}, bf16[8,32,512]{2,1,0:T(8,128)(2,1)S(1)}, u32[]{:S(2)}, u32[]{:S(2)}) collective-permute-start(bf16[8,32,512]{2,1,0:T(8,128)(2,1)S(1)} %all_to_all.23.mine_ref), channel_id=1, source_target_pairs={{0,4},{4,0},{1,5},{5,1},{2,6},{6,2},{3,7},{7,3},{8,12},{12,8},{9,1... | collective-permute-start | bytes 786440 | tf_op jit(solution)/shard_map/ppermute | solution.py:261
  101.0 1.5 %far_rows.1 = (bf16[256,2048]{1,0:T(8,128)(2,1)S(1)}, bf16[256,2048]{1,0:T(8,128)(2,1)S(1)}, bf16[4,128,256]{2,1,0:T(8,128)(2,1)S(1)}, bf16[4,128,256]{2,1,0:T(8,128)(2,1)S(1)}) custom-call(s32[1]{0:T(128)} %bitcast.core_ref, f32[256,2048]{1,0:T(8,128)S(1)} %product.3.prod, bf16[8,32,512]{2,1,0:T(8,128)(2,1)S(1)} %collective-permute-done.15.other_ref, ...), custom_call_target="tpu_custom_call" | custom-call | flops 1342177280 | bytes 7340032 | tf_op jit(solution)/shard_map/far_rows/pallas_call | solution.py:437
  103.4 2.0 %collective-permute-start.20 = (bf16[4,128,256]{2,1,0:T(8,128)(2,1)S(1)}, bf16[4,128,256]{2,1,0:T(8,128)(2,1)S(1)}, u32[]{:S(2)}, u32[]{:S(2)}) collective-permute-start(bf16[4,128,256]{2,1,0:T(8,128)(2,1)S(1)} %get-tuple-element.105), channel_id=1, source_target_pairs={{0,3},{1,0},{2,1},{3,2},{4,7},{5,4},{6,5},{7,6},{8,11},{9,8},{10,9... | collective-permute-start | bytes 786440 | tf_op jit(solution)/shard_map/ppermute | solution.py:512
  108.0 3.6 %collective-permute-done.17 = bf16[4,128,256]{2,1,0:T(8,128)(2,1)S(1)} collective-permute-done((bf16[4,128,256]{2,1,0:T(8,128)(2,1)S(1)}, bf16[4,128,256]{2,1,0:T(8,128)(2,1)S(1)}, u32[]{:S(2)}, u32[]{:S(2)}) %collective-permute-start.17) | collective-permute-done | bytes 262176 | tf_op jit(solution)/shard_map/ppermute | solution.py:508
  111.9 2.7 %collective-permute-start.21 = (bf16[4,128,256]{2,1,0:T(8,128)(2,1)S(1)}, bf16[4,128,256]{2,1,0:T(8,128)(2,1)S(1)}, u32[]{:S(2)}, u32[]{:S(2)}) collective-permute-start(bf16[4,128,256]{2,1,0:T(8,128)(2,1)S(1)} %add_convert_fusion), channel_id=1, source_target_pairs={{0,3},{1,0},{2,1},{3,2},{4,7},{5,4},{6,5},{7,6},{8,11},{9,8},{10,9... | collective-permute-start | bytes 786440 | tf_op jit(solution)/shard_map/ppermute | solution.py:512
  114.6 1.7 %collective-permute-done.16.near_a = bf16[4,128,256]{2,1,0:T(8,128)(2,1)S(1)} collective-permute-done((bf16[4,128,256]{2,1,0:T(8,128)(2,1)S(1)}, bf16[4,128,256]{2,1,0:T(8,128)(2,1)S(1)}, u32[]{:S(2)}, u32[]{:S(2)}) %collective-permute-start.16) | collective-permute-done | bytes 262176 | tf_op jit(solution)/shard_map/ppermute | solution.py:512
  117.3 5.6 %collective-permute-done.18.far_a = bf16[4,128,256]{2,1,0:T(8,128)(2,1)S(1)} collective-permute-done((bf16[4,128,256]{2,1,0:T(8,128)(2,1)S(1)}, bf16[4,128,256]{2,1,0:T(8,128)(2,1)S(1)}, u32[]{:S(2)}, u32[]{:S(2)}) %collective-permute-start.18) | collective-permute-done | bytes 262176 | tf_op jit(solution)/shard_map/ppermute | solution.py:508
  122.9 1.1 finish.1
  (40 shorter events, 11.3 us)
Async XLA Ops:
  1.9 8.4 %collective-permute-start = (bf16[4,128,256]{2,1,0:T(8,128)(2,1)S(1)}, bf16[4,128,256]{2,1,0:T(8,128)(2,1)S(1)}, u32[]{:S(2)}, u32[]{:S(2)}) collective-permute-start(bf16[4,128,256]{2,1,0:T(8,128)(2,1)S(1)} %get-tuple-element.55.refs_0_), channel_id=1, source_target_pairs={{0,1},{1,2},{2,3},{3,0},{4,5},{5,6},{6,7},{7,4},{8,9},{9,10},{10,1... | collective-permute-start | bytes 786440 | tf_op jit(solution)/shard_map/ppermute | solution.py:508
  4.1 6.6 %collective-permute-start.1 = (bf16[4,128,256]{2,1,0:T(8,128)(2,1)S(1)}, bf16[4,128,256]{2,1,0:T(8,128)(2,1)S(1)}, u32[]{:S(2)}, u32[]{:S(2)}) collective-permute-start(bf16[4,128,256]{2,1,0:T(8,128)(2,1)S(1)} %get-tuple-element.56.refs_1_), channel_id=1, source_target_pairs={{0,3},{1,0},{2,1},{3,2},{4,7},{5,4},{6,5},{7,6},{8,11},{9,8},{10,9... | collective-permute-start | bytes 786440 | tf_op jit(solution)/shard_map/ppermute | solution.py:512
  5.6 13.5 %collective-permute-start.2 = (bf16[4,128,256]{2,1,0:T(8,128)(2,1)S(1)}, bf16[4,128,256]{2,1,0:T(8,128)(2,1)S(1)}, u32[]{:S(2)}, u32[]{:S(2)}) collective-permute-start(bf16[4,128,256]{2,1,0:T(8,128)(2,1)S(1)} %get-tuple-element.55.refs_0_), channel_id=1, source_target_pairs={{0,3},{1,0},{2,1},{3,2},{4,7},{5,4},{6,5},{7,6},{8,11},{9,8},{10,9... | collective-permute-start | bytes 786440 | tf_op jit(solution)/shard_map/ppermute | solution.py:512
  7.0 12.2 %collective-permute-start.5 = (bf16[4,128,256]{2,1,0:T(8,128)(2,1)S(1)}, bf16[4,128,256]{2,1,0:T(8,128)(2,1)S(1)}, u32[]{:S(2)}, u32[]{:S(2)}) collective-permute-start(bf16[4,128,256]{2,1,0:T(8,128)(2,1)S(1)} %get-tuple-element.56.refs_1_), channel_id=1, source_target_pairs={{0,1},{1,2},{2,3},{3,0},{4,5},{5,6},{6,7},{7,4},{8,9},{9,10},{10,1... | collective-permute-start | bytes 786440 | tf_op jit(solution)/shard_map/ppermute | solution.py:508
  10.7 11.2 %collective-permute-start.4 = (bf16[4,128,256]{2,1,0:T(8,128)(2,1)S(1)}, bf16[4,128,256]{2,1,0:T(8,128)(2,1)S(1)}, u32[]{:S(2)}, u32[]{:S(2)}) collective-permute-start(bf16[4,128,256]{2,1,0:T(8,128)(2,1)S(1)} %collective-permute-done.1.refs_3_), channel_id=1, source_target_pairs={{0,3},{1,0},{2,1},{3,2},{4,7},{5,4},{6,5},{7,6},{8,11},{9,8},{10,9... | collective-permute-start | bytes 786440 | tf_op jit(solution)/shard_map/ppermute | solution.py:512
  13.0 9.0 %collective-permute-start.3 = (bf16[4,128,256]{2,1,0:T(8,128)(2,1)S(1)}, bf16[4,128,256]{2,1,0:T(8,128)(2,1)S(1)}, u32[]{:S(2)}, u32[]{:S(2)}) collective-permute-start(bf16[4,128,256]{2,1,0:T(8,128)(2,1)S(1)} %collective-permute-done.refs_6_), channel_id=1, source_target_pairs={{0,1},{1,2},{2,3},{3,0},{4,5},{5,6},{6,7},{7,4},{8,9},{9,10},{10,1... | collective-permute-start | bytes 786440 | tf_op jit(solution)/shard_map/ppermute | solution.py:508
  23.4 5.8 %collective-permute-start.6 = (bf16[256,512]{1,0:T(8,128)(2,1)S(1)}, bf16[256,512]{1,0:T(8,128)(2,1)S(1)}, u32[]{:S(2)}, u32[]{:S(2)}) collective-permute-start(bf16[256,512]{1,0:T(8,128)(2,1)S(1)} %get-tuple-element.67), channel_id=1, source_target_pairs={{0,4},{4,0},{1,5},{5,1},{2,6},{6,2},{3,7},{7,3},{8,12},{12,8},{9,1... | collective-permute-start | bytes 786440 | tf_op jit(solution)/shard_map/ppermute | solution.py:261
  39.4 8.7 %collective-permute-start.9 = (bf16[1,32,512]{2,1,0:T(8,128)(2,1)S(1)}, bf16[1,32,512]{2,1,0:T(8,128)(2,1)S(1)}, u32[]{:S(2)}, u32[]{:S(2)}) collective-permute-start(bf16[1,32,512]{2,1,0:T(8,128)(2,1)S(1)} %total.4.refs_0_), channel_id=1, source_target_pairs={{0,32},{16,48},{32,0},{48,16},{1,33},{17,49},{33,1},{49,17},{2,34}... | collective-permute-start | bytes 98312 | tf_op jit(solution)/shard_map/ppermute | solution.py:306
  45.5 3.7 %collective-permute-start.8 = (bf16[1,32,512]{2,1,0:T(8,128)(2,1)S(1)}, bf16[1,32,512]{2,1,0:T(8,128)(2,1)S(1)}, u32[]{:S(2)}, u32[]{:S(2)}) collective-permute-start(bf16[1,32,512]{2,1,0:T(8,128)(2,1)S(1)} %total.4.refs_0_), channel_id=1, source_target_pairs={{0,48},{16,0},{32,16},{48,32},{1,49},{17,1},{33,17},{49,33},{2,50}... | collective-permute-start | bytes 98312 | tf_op jit(solution)/shard_map/ppermute | solution.py:306
  45.8 5.2 %collective-permute-start.7 = (bf16[1,32,512]{2,1,0:T(8,128)(2,1)S(1)}, bf16[1,32,512]{2,1,0:T(8,128)(2,1)S(1)}, u32[]{:S(2)}, u32[]{:S(2)}) collective-permute-start(bf16[1,32,512]{2,1,0:T(8,128)(2,1)S(1)} %total.4.refs_0_), channel_id=1, source_target_pairs={{0,16},{16,32},{32,48},{48,0},{1,17},{17,33},{33,49},{49,1},{2,18}... | collective-permute-start | bytes 98312 | tf_op jit(solution)/shard_map/ppermute | solution.py:306
  59.7 5.2 %copy-start = (f32[2,2048]{1,0:T(2,128)S(1)}, f32[2,2048]{1,0:T(2,128)}, u32[]{:S(2)}) copy-start(f32[2,2048]{1,0:T(2,128)} %b_ref.3) | copy-start | bytes 49156
  59.7 5.2 %collective-permute-start.10 = (bf16[8,32,512]{2,1,0:T(8,128)(2,1)S(1)}, bf16[8,32,512]{2,1,0:T(8,128)(2,1)S(1)}, u32[]{:S(2)}, u32[]{:S(2)}) collective-permute-start(bf16[8,32,512]{2,1,0:T(8,128)(2,1)S(1)} %all_to_all.21.mine_ref), channel_id=1, source_target_pairs={{0,4},{4,0},{1,5},{5,1},{2,6},{6,2},{3,7},{7,3},{8,12},{12,8},{9,1... | collective-permute-start | bytes 786440 | tf_op jit(solution)/shard_map/ppermute | solution.py:261
  66.7 1.7 %collective-permute-start.11 = (bf16[256,512]{1,0:T(8,128)(2,1)S(1)}, bf16[256,512]{1,0:T(8,128)(2,1)S(1)}, u32[]{:S(2)}, u32[]{:S(2)}) collective-permute-start(bf16[256,512]{1,0:T(8,128)(2,1)S(1)} %get-tuple-element.82), channel_id=1, source_target_pairs={{0,4},{4,0},{1,5},{5,1},{2,6},{6,2},{3,7},{7,3},{8,12},{12,8},{9,1... | collective-permute-start | bytes 786440 | tf_op jit(solution)/shard_map/ppermute | solution.py:261
  77.5 7.1 %collective-permute-start.14 = (bf16[1,32,512]{2,1,0:T(8,128)(2,1)S(1)}, bf16[1,32,512]{2,1,0:T(8,128)(2,1)S(1)}, u32[]{:S(2)}, u32[]{:S(2)}) collective-permute-start(bf16[1,32,512]{2,1,0:T(8,128)(2,1)S(1)} %total.6.refs_0_), channel_id=1, source_target_pairs={{0,32},{16,48},{32,0},{48,16},{1,33},{17,49},{33,1},{49,17},{2,34}... | collective-permute-start | bytes 98312 | tf_op jit(solution)/shard_map/ppermute | solution.py:306
  81.8 4.0 %collective-permute-start.13 = (bf16[1,32,512]{2,1,0:T(8,128)(2,1)S(1)}, bf16[1,32,512]{2,1,0:T(8,128)(2,1)S(1)}, u32[]{:S(2)}, u32[]{:S(2)}) collective-permute-start(bf16[1,32,512]{2,1,0:T(8,128)(2,1)S(1)} %total.6.refs_0_), channel_id=1, source_target_pairs={{0,48},{16,0},{32,16},{48,32},{1,49},{17,1},{33,17},{49,33},{2,50}... | collective-permute-start | bytes 98312 | tf_op jit(solution)/shard_map/ppermute | solution.py:306
  81.8 5.0 %collective-permute-start.12 = (bf16[1,32,512]{2,1,0:T(8,128)(2,1)S(1)}, bf16[1,32,512]{2,1,0:T(8,128)(2,1)S(1)}, u32[]{:S(2)}, u32[]{:S(2)}) collective-permute-start(bf16[1,32,512]{2,1,0:T(8,128)(2,1)S(1)} %total.6.refs_0_), channel_id=1, source_target_pairs={{0,16},{16,32},{32,48},{48,0},{1,17},{17,33},{33,49},{49,1},{2,18}... | collective-permute-start | bytes 98312 | tf_op jit(solution)/shard_map/ppermute | solution.py:306
  96.0 5.0 %collective-permute-start.15 = (bf16[8,32,512]{2,1,0:T(8,128)(2,1)S(1)}, bf16[8,32,512]{2,1,0:T(8,128)(2,1)S(1)}, u32[]{:S(2)}, u32[]{:S(2)}) collective-permute-start(bf16[8,32,512]{2,1,0:T(8,128)(2,1)S(1)} %all_to_all.23.mine_ref), channel_id=1, source_target_pairs={{0,4},{4,0},{1,5},{5,1},{2,6},{6,2},{3,7},{7,3},{8,12},{12,8},{9,1... | collective-permute-start | bytes 786440 | tf_op jit(solution)/shard_map/ppermute | solution.py:261
  102.5 9.1 %collective-permute-start.17 = (bf16[4,128,256]{2,1,0:T(8,128)(2,1)S(1)}, bf16[4,128,256]{2,1,0:T(8,128)(2,1)S(1)}, u32[]{:S(2)}, u32[]{:S(2)}) collective-permute-start(bf16[4,128,256]{2,1,0:T(8,128)(2,1)S(1)} %get-tuple-element.102), channel_id=1, source_target_pairs={{0,1},{1,2},{2,3},{3,0},{4,5},{5,6},{6,7},{7,4},{8,9},{9,10},{10,1... | collective-permute-start | bytes 786440 | tf_op jit(solution)/shard_map/ppermute | solution.py:508
  103.4 8.4 %collective-permute-start.20 = (bf16[4,128,256]{2,1,0:T(8,128)(2,1)S(1)}, bf16[4,128,256]{2,1,0:T(8,128)(2,1)S(1)}, u32[]{:S(2)}, u32[]{:S(2)}) collective-permute-start(bf16[4,128,256]{2,1,0:T(8,128)(2,1)S(1)} %get-tuple-element.105), channel_id=1, source_target_pairs={{0,3},{1,0},{2,1},{3,2},{4,7},{5,4},{6,5},{7,6},{8,11},{9,8},{10,9... | collective-permute-start | bytes 786440 | tf_op jit(solution)/shard_map/ppermute | solution.py:512
  106.5 9.9 %collective-permute-start.16 = (bf16[4,128,256]{2,1,0:T(8,128)(2,1)S(1)}, bf16[4,128,256]{2,1,0:T(8,128)(2,1)S(1)}, u32[]{:S(2)}, u32[]{:S(2)}) collective-permute-start(bf16[4,128,256]{2,1,0:T(8,128)(2,1)S(1)} %get-tuple-element.100), channel_id=1, source_target_pairs={{0,3},{1,0},{2,1},{3,2},{4,7},{5,4},{6,5},{7,6},{8,11},{9,8},{10,9... | collective-permute-start | bytes 786440 | tf_op jit(solution)/shard_map/ppermute | solution.py:512
  107.5 9.8 %collective-permute-start.19 = (bf16[4,128,256]{2,1,0:T(8,128)(2,1)S(1)}, bf16[4,128,256]{2,1,0:T(8,128)(2,1)S(1)}, u32[]{:S(2)}, u32[]{:S(2)}) collective-permute-start(bf16[4,128,256]{2,1,0:T(8,128)(2,1)S(1)} %get-tuple-element.103), channel_id=1, source_target_pairs={{0,1},{1,2},{2,3},{3,0},{4,5},{5,6},{6,7},{7,4},{8,9},{9,10},{10,1... | collective-permute-start | bytes 786440 | tf_op jit(solution)/shard_map/ppermute | solution.py:508
  111.7 11.2 %collective-permute-start.18 = (bf16[4,128,256]{2,1,0:T(8,128)(2,1)S(1)}, bf16[4,128,256]{2,1,0:T(8,128)(2,1)S(1)}, u32[]{:S(2)}, u32[]{:S(2)}) collective-permute-start(bf16[4,128,256]{2,1,0:T(8,128)(2,1)S(1)} %add_convert_fusion.1), channel_id=1, source_target_pairs={{0,1},{1,2},{2,3},{3,0},{4,5},{5,6},{6,7},{7,4},{8,9},{9,10},{10,1... | collective-permute-start | bytes 786440 | tf_op jit(solution)/shard_map/ppermute | solution.py:508
  111.9 11.0 %collective-permute-start.21 = (bf16[4,128,256]{2,1,0:T(8,128)(2,1)S(1)}, bf16[4,128,256]{2,1,0:T(8,128)(2,1)S(1)}, u32[]{:S(2)}, u32[]{:S(2)}) collective-permute-start(bf16[4,128,256]{2,1,0:T(8,128)(2,1)S(1)} %add_convert_fusion), channel_id=1, source_target_pairs={{0,3},{1,0},{2,1},{3,2},{4,7},{5,4},{6,5},{7,6},{8,11},{9,8},{10,9... | collective-permute-start | bytes 786440 | tf_op jit(solution)/shard_map/ppermute | solution.py:512

commit v10 on v8

--- a/solution.py
+++ b/solution.py
@@ -362,7 +362,7 @@
     shape = pltpu.VMEM((CHUNKS,) + CHUNK, BF16)
     parts = swap_all(small(cut_kernel, shape, "cut", keep, got))
     own, counts = lax.optimization_barrier((total(1, parts), counts))
-    near = (turn(own, 1), turn(own, 3), turn(own, 2), turned_counts(counts))
+    near = (turn(own, 2), turn(own, 1), turn(own, 3), turned_counts(counts))
     *near, turned = lax.optimization_barrier(near)
     mine = swap_all(total(CHUNKS, own, *near))
     prod, other = lax.optimization_barrier((product(core, mine, v, u, layer), swap(mine, "c")))

time: 124 us -> 126 us (1.016)
  waiting for transfers between devices: 20.9 us -> 23.6 us
    ppermute x6, waiting for transfers between devices: 5.11 us -> 7.35 us  [turn(): return lax.ppermute(arr, 'zh', [(i, i + k & 3) for i in range(4)])]
  transfers between devices with their start and end apart: 22 -> 22, of which waited for: 13 -> 13; matrix products, arithmetic and copies ran while one was open for 0% -> 0% of each run, Pallas kernels for 12% -> 11%
where the time goes in v10:
time: 126 us
  starting transfers between devices  42.6 us (34%)
  blocking collectives  36.7 us (29%)
  waiting for transfers between devices  23.6 us (19%)
  Pallas kernels  21.5 us (17%)
    all_to_all x4, blocking collectives, swap_all(): return lax.all_to_all(arr, ('x', 'zl'), 0, 0, tiled=True)  36.7 us
    ppermute x6, starting transfers between devices, turn(): return lax.ppermute(arr, 'zh', [(i, i + k & 3) for i in range(4)])  14.8 us
    ppermute x4, starting transfers between devices, swap(): return lax.ppermute(arr, axis, [(0, 1), (1, 0)])  12.8 us
    ppermute x6, starting transfers between devices, left(): return lax.ppermute(arr, 'row', [(i, i + 3 & 3) for i in range(4)])  11.3 us
    ppermute x6, waiting for transfers between devices, right(): return lax.ppermute(arr, 'row', [(i, i + 1 & 3) for i in range(4)])  10.1 us
    pallas_call x2, Pallas kernels, make_counts(): pl.pallas_call(functools.partial(counts_kernel, first_table=0 if edges is...  9.38 us
    ppermute x6, waiting for transfers between devices, turn(): return lax.ppermute(arr, 'zh', [(i, i + k & 3) for i in range(4)])  7.35 us
    ppermute x6, waiting for transfers between devices, left(): return lax.ppermute(arr, 'row', [(i, i + 3 & 3) for i in range(4)])  4.5 us
  transfers between devices with their start and end apart: 22, of which 13 were waited for; matrix products, arithmetic and copies ran while one was open for 0% of the time, Pallas kernels for 11%

profile of v10, /device:TPU:1, one launch (start us, length us, event | category | flops | bytes accessed | tf_op | source)
XLA Modules:
  0.0 125.6 jit_solution(10579805493212318854)
XLA Ops:
  0.6 1.2 cast.1
  1.9 2.2 %collective-permute-start = (bf16[4,128,256]{2,1,0:T(8,128)(2,1)S(1)}, bf16[4,128,256]{2,1,0:T(8,128)(2,1)S(1)}, u32[]{:S(2)}, u32[]{:S(2)}) collective-permute-start(bf16[4,128,256]{2,1,0:T(8,128)(2,1)S(1)} %get-tuple-element.55.refs_0_), channel_id=1, source_target_pairs={{0,1},{1,2},{2,3},{3,0},{4,5},{5,6},{6,7},{7,4},{8,9},{9,10},{10,1... | collective-permute-start | bytes 786440 | tf_op jit(solution)/shard_map/ppermute | solution.py:501
  4.1 1.5 %collective-permute-start.1 = (bf16[4,128,256]{2,1,0:T(8,128)(2,1)S(1)}, bf16[4,128,256]{2,1,0:T(8,128)(2,1)S(1)}, u32[]{:S(2)}, u32[]{:S(2)}) collective-permute-start(bf16[4,128,256]{2,1,0:T(8,128)(2,1)S(1)} %get-tuple-element.56.refs_1_), channel_id=1, source_target_pairs={{0,3},{1,0},{2,1},{3,2},{4,7},{5,4},{6,5},{7,6},{8,11},{9,8},{10,9... | collective-permute-start | bytes 786440 | tf_op jit(solution)/shard_map/ppermute | solution.py:505
  5.6 1.4 %collective-permute-start.2 = (bf16[4,128,256]{2,1,0:T(8,128)(2,1)S(1)}, bf16[4,128,256]{2,1,0:T(8,128)(2,1)S(1)}, u32[]{:S(2)}, u32[]{:S(2)}) collective-permute-start(bf16[4,128,256]{2,1,0:T(8,128)(2,1)S(1)} %get-tuple-element.55.refs_0_), channel_id=1, source_target_pairs={{0,3},{1,0},{2,1},{3,2},{4,7},{5,4},{6,5},{7,6},{8,11},{9,8},{10,9... | collective-permute-start | bytes 786440 | tf_op jit(solution)/shard_map/ppermute | solution.py:505
  7.1 4.9 %counts.2 = (bf16[4,256,512]{2,1,0:T(8,128)(2,1)S(1)}, s32[16]{0:T(128)S(1)}) custom-call(s32[1]{0:T(128)} %bitcast.1.mine_ref, s32[8,4096]{1,0:T(8,128)} %ids_ref.3, s32[8,4096]{1,0:T(8,128)} %own_ref.3), custom_call_target="tpu_custom_call" | custom-call | flops 1610612736 | bytes 3145728 | tf_op jit(solution)/shard_map/counts/pallas_call | solution.py:140
  12.0 2.7 %collective-permute-start.4 = (bf16[4,128,256]{2,1,0:T(8,128)(2,1)S(1)}, bf16[4,128,256]{2,1,0:T(8,128)(2,1)S(1)}, u32[]{:S(2)}, u32[]{:S(2)}) collective-permute-start(bf16[4,128,256]{2,1,0:T(8,128)(2,1)S(1)} %collective-permute-done.1.refs_3_), channel_id=1, source_target_pairs={{0,3},{1,0},{2,1},{3,2},{4,7},{5,4},{6,5},{7,6},{8,11},{9,8},{10,9... | collective-permute-start | bytes 786440 | tf_op jit(solution)/shard_map/ppermute | solution.py:505
  14.7 4.5 %counts.3 = (bf16[4,256,512]{2,1,0:T(8,128)(2,1)S(1)}, bf16[256,2048]{1,0:T(8,128)(2,1)S(1)}, bf16[2,2048,512]{2,1,0:T(8,128)(2,1)S(1)}, bf16[2,512,2048]{2,1,0:T(8,128)(2,1)S(1)}) custom-call(s32[1]{0:T(128)} %bitcast.1.mine_ref, s32[8,4096]{1,0:T(8,128)} %ids_ref.3, s32[8,4096]{1,0:T(8,128)} %own_ref.3, s32[16]{0:T(128)S(1)} %get-tuple-element.58.refs_0_, ...), custom_call_target="tpu_custom_call" | custom-call | flops 1610612736 | bytes 3145728 | tf_op jit(solution)/shard_map/counts/pallas_call | solution.py:140
  19.2 2.7 %collective-permute-done.4.refs_5_ = bf16[4,128,256]{2,1,0:T(8,128)(2,1)S(1)} collective-permute-done((bf16[4,128,256]{2,1,0:T(8,128)(2,1)S(1)}, bf16[4,128,256]{2,1,0:T(8,128)(2,1)S(1)}, u32[]{:S(2)}, u32[]{:S(2)}) %collective-permute-start.4) | collective-permute-done | bytes 262176 | tf_op jit(solution)/shard_map/ppermute | solution.py:505
  21.9 1.5 %first_sums.1 = (bf16[256,2048]{1,0:T(8,128)(2,1)S(1)}, bf16[256,2048]{1,0:T(8,128)(2,1)S(1)}, bf16[256,512]{1,0:T(8,128)(2,1)S(1)}) custom-call(s32[1]{0:T(128)} %bitcast.core_ref, bf16[4,256,512]{2,1,0:T(8,128)(2,1)S(1)} %get-tuple-element.73.counts_a.in_ref, bf16[4,256,512]{2,1,0:T(8,128)(2,1)S(1)} %get-tuple-element.88.counts_b.in_ref, ...), custom_call_target="tpu_custom_call" | custom-call | flops 1610612736 | bytes 10485760 | tf_op jit(solution)/shard_map/first_sums/pallas_call | solution.py:240
  23.4 4.4 %collective-permute-start.6 = (bf16[256,512]{1,0:T(8,128)(2,1)S(1)}, bf16[256,512]{1,0:T(8,128)(2,1)S(1)}, u32[]{:S(2)}, u32[]{:S(2)}) collective-permute-start(bf16[256,512]{1,0:T(8,128)(2,1)S(1)} %get-tuple-element.67), channel_id=1, source_target_pairs={{0,4},{4,0},{1,5},{5,1},{2,6},{6,2},{3,7},{7,3},{8,12},{12,8},{9,1... | collective-permute-start | bytes 786440 | tf_op jit(solution)/shard_map/ppermute | solution.py:256
  29.0 10.4 %all_to_all.20.refs_0_ = bf16[8,32,512]{2,1,0:T(8,128)(2,1)S(1)} all-to-all(bf16[8,32,512]{2,1,0:T(8,128)(2,1)S(1)} %cut.2), channel_id=1, replica_groups=mesh['x'=4,'zh'=4,'zl'=2,'c'=2,'row'=4] {'x','zl'}, dimensions={0} | all-to-all | bytes 524288 | tf_op jit(solution)/shard_map/all_to_all | solution.py:297
  39.4 5.2 %collective-permute-start.9 = (bf16[1,32,512]{2,1,0:T(8,128)(2,1)S(1)}, bf16[1,32,512]{2,1,0:T(8,128)(2,1)S(1)}, u32[]{:S(2)}, u32[]{:S(2)}) collective-permute-start(bf16[1,32,512]{2,1,0:T(8,128)(2,1)S(1)} %total.4.refs_0_), channel_id=1, source_target_pairs={{0,48},{16,0},{32,16},{48,32},{1,49},{17,1},{33,17},{49,33},{2,50}... | collective-permute-start | bytes 98312 | tf_op jit(solution)/shard_map/ppermute | solution.py:301
  44.6 3.3 %collective-permute-start.7 = (bf16[1,32,512]{2,1,0:T(8,128)(2,1)S(1)}, bf16[1,32,512]{2,1,0:T(8,128)(2,1)S(1)}, u32[]{:S(2)}, u32[]{:S(2)}) collective-permute-start(bf16[1,32,512]{2,1,0:T(8,128)(2,1)S(1)} %total.4.refs_0_), channel_id=1, source_target_pairs={{0,32},{16,48},{32,0},{48,16},{1,33},{17,49},{33,1},{49,17},{2,34}... | collective-permute-start | bytes 98312 | tf_op jit(solution)/shard_map/ppermute | solution.py:301
  48.2 1.3 %collective-permute-done.8.refs_2_ = bf16[1,32,512]{2,1,0:T(8,128)(2,1)S(1)} collective-permute-done((bf16[1,32,512]{2,1,0:T(8,128)(2,1)S(1)}, bf16[1,32,512]{2,1,0:T(8,128)(2,1)S(1)}, u32[]{:S(2)}, u32[]{:S(2)}) %collective-permute-start.8) | collective-permute-done | bytes 32800 | tf_op jit(solution)/shard_map/ppermute | solution.py:301
  49.5 2.0 %collective-permute-done.7.refs_1_ = bf16[1,32,512]{2,1,0:T(8,128)(2,1)S(1)} collective-permute-done((bf16[1,32,512]{2,1,0:T(8,128)(2,1)S(1)}, bf16[1,32,512]{2,1,0:T(8,128)(2,1)S(1)}, u32[]{:S(2)}, u32[]{:S(2)}) %collective-permute-start.7) | collective-permute-done | bytes 32800 | tf_op jit(solution)/shard_map/ppermute | solution.py:301
  51.5 8.5 %all_to_all.21.mine_ref = bf16[8,32,512]{2,1,0:T(8,128)(2,1)S(1)} all-to-all(bf16[8,32,512]{2,1,0:T(8,128)(2,1)S(1)} %total.5), channel_id=1, replica_groups=mesh['x'=4,'zh'=4,'zl'=2,'c'=2,'row'=4] {'x','zl'}, dimensions={0} | all-to-all | bytes 524288 | tf_op jit(solution)/shard_map/all_to_all | solution.py:297
  60.1 4.0 %collective-permute-start.10 = (bf16[8,32,512]{2,1,0:T(8,128)(2,1)S(1)}, bf16[8,32,512]{2,1,0:T(8,128)(2,1)S(1)}, u32[]{:S(2)}, u32[]{:S(2)}) collective-permute-start(bf16[8,32,512]{2,1,0:T(8,128)(2,1)S(1)} %all_to_all.21.mine_ref), channel_id=1, source_target_pairs={{0,4},{4,0},{1,5},{5,1},{2,6},{6,2},{3,7},{7,3},{8,12},{12,8},{9,1... | collective-permute-start | bytes 786440 | tf_op jit(solution)/shard_map/ppermute | solution.py:256
  65.3 1.8 %middle.1 = (bf16[256,2048]{1,0:T(8,128)(2,1)S(1)}, bf16[256,2048]{1,0:T(8,128)(2,1)S(1)}, bf16[256,2048]{1,0:T(8,128)(2,1)S(1)}, bf16[256,512]{1,0:T(8,128)(2,1)S(1)}) custom-call(s32[1]{0:T(128)} %bitcast.core_ref, f32[256,2048]{1,0:T(8,128)S(1)} %product.2.prod, bf16[8,32,512]{2,1,0:T(8,128)(2,1)S(1)} %collective-permute-done.10.other_ref, ...), custom_call_target="tpu_custom_call" | custom-call | flops 2147483648 | bytes 8388608 | tf_op jit(solution)/shard_map/middle/pallas_call | solution.py:392
  68.8 9.0 %all_to_all.22.refs_0_ = bf16[8,32,512]{2,1,0:T(8,128)(2,1)S(1)} all-to-all(bf16[8,32,512]{2,1,0:T(8,128)(2,1)S(1)} %cut.3), channel_id=1, replica_groups=mesh['x'=4,'zh'=4,'zl'=2,'c'=2,'row'=4] {'x','zl'}, dimensions={0} | all-to-all | bytes 524288 | tf_op jit(solution)/shard_map/all_to_all | solution.py:297
  77.8 3.9 %collective-permute-start.14 = (bf16[1,32,512]{2,1,0:T(8,128)(2,1)S(1)}, bf16[1,32,512]{2,1,0:T(8,128)(2,1)S(1)}, u32[]{:S(2)}, u32[]{:S(2)}) collective-permute-start(bf16[1,32,512]{2,1,0:T(8,128)(2,1)S(1)} %total.6.refs_0_), channel_id=1, source_target_pairs={{0,48},{16,0},{32,16},{48,32},{1,49},{17,1},{33,17},{49,33},{2,50}... | collective-permute-start | bytes 98312 | tf_op jit(solution)/shard_map/ppermute | solution.py:301
  81.7 2.4 %collective-permute-start.12 = (bf16[1,32,512]{2,1,0:T(8,128)(2,1)S(1)}, bf16[1,32,512]{2,1,0:T(8,128)(2,1)S(1)}, u32[]{:S(2)}, u32[]{:S(2)}) collective-permute-start(bf16[1,32,512]{2,1,0:T(8,128)(2,1)S(1)} %total.6.refs_0_), channel_id=1, source_target_pairs={{0,32},{16,48},{32,0},{48,16},{1,33},{17,49},{33,1},{49,17},{2,34}... | collective-permute-start | bytes 98312 | tf_op jit(solution)/shard_map/ppermute | solution.py:301
  84.5 2.2 %collective-permute-done.13.refs_2_ = bf16[1,32,512]{2,1,0:T(8,128)(2,1)S(1)} collective-permute-done((bf16[1,32,512]{2,1,0:T(8,128)(2,1)S(1)}, bf16[1,32,512]{2,1,0:T(8,128)(2,1)S(1)}, u32[]{:S(2)}, u32[]{:S(2)}) %collective-permute-start.13) | collective-permute-done | bytes 32800 | tf_op jit(solution)/shard_map/ppermute | solution.py:301
  86.6 1.9 %collective-permute-done.12.refs_1_ = bf16[1,32,512]{2,1,0:T(8,128)(2,1)S(1)} collective-permute-done((bf16[1,32,512]{2,1,0:T(8,128)(2,1)S(1)}, bf16[1,32,512]{2,1,0:T(8,128)(2,1)S(1)}, u32[]{:S(2)}, u32[]{:S(2)}) %collective-permute-start.12) | collective-permute-done | bytes 32800 | tf_op jit(solution)/shard_map/ppermute | solution.py:301
  88.5 8.8 %all_to_all.23.mine_ref = bf16[8,32,512]{2,1,0:T(8,128)(2,1)S(1)} all-to-all(bf16[8,32,512]{2,1,0:T(8,128)(2,1)S(1)} %total.7), channel_id=1, replica_groups=mesh['x'=4,'zh'=4,'zl'=2,'c'=2,'row'=4] {'x','zl'}, dimensions={0} | all-to-all | bytes 524288 | tf_op jit(solution)/shard_map/all_to_all | solution.py:297
  97.4 3.9 %collective-permute-start.15 = (bf16[8,32,512]{2,1,0:T(8,128)(2,1)S(1)}, bf16[8,32,512]{2,1,0:T(8,128)(2,1)S(1)}, u32[]{:S(2)}, u32[]{:S(2)}) collective-permute-start(bf16[8,32,512]{2,1,0:T(8,128)(2,1)S(1)} %all_to_all.23.mine_ref), channel_id=1, source_target_pairs={{0,4},{4,0},{1,5},{5,1},{2,6},{6,2},{3,7},{7,3},{8,12},{12,8},{9,1... | collective-permute-start | bytes 786440 | tf_op jit(solution)/shard_map/ppermute | solution.py:256
  102.5 1.8 %far_rows.1 = (bf16[256,2048]{1,0:T(8,128)(2,1)S(1)}, bf16[256,2048]{1,0:T(8,128)(2,1)S(1)}, bf16[4,128,256]{2,1,0:T(8,128)(2,1)S(1)}, bf16[4,128,256]{2,1,0:T(8,128)(2,1)S(1)}) custom-call(s32[1]{0:T(128)} %bitcast.core_ref, f32[256,2048]{1,0:T(8,128)S(1)} %product.3.prod, bf16[8,32,512]{2,1,0:T(8,128)(2,1)S(1)} %collective-permute-done.15.other_ref, ...), custom_call_target="tpu_custom_call" | custom-call | flops 1342177280 | bytes 7340032 | tf_op jit(solution)/shard_map/far_rows/pallas_call | solution.py:431
  104.9 2.0 %collective-permute-start.20 = (bf16[4,128,256]{2,1,0:T(8,128)(2,1)S(1)}, bf16[4,128,256]{2,1,0:T(8,128)(2,1)S(1)}, u32[]{:S(2)}, u32[]{:S(2)}) collective-permute-start(bf16[4,128,256]{2,1,0:T(8,128)(2,1)S(1)} %get-tuple-element.105), channel_id=1, source_target_pairs={{0,3},{1,0},{2,1},{3,2},{4,7},{5,4},{6,5},{7,6},{8,11},{9,8},{10,9... | collective-permute-start | bytes 786440 | tf_op jit(solution)/shard_map/ppermute | solution.py:505
  109.5 3.6 %collective-permute-done.17 = bf16[4,128,256]{2,1,0:T(8,128)(2,1)S(1)} collective-permute-done((bf16[4,128,256]{2,1,0:T(8,128)(2,1)S(1)}, bf16[4,128,256]{2,1,0:T(8,128)(2,1)S(1)}, u32[]{:S(2)}, u32[]{:S(2)}) %collective-permute-start.17) | collective-permute-done | bytes 262176 | tf_op jit(solution)/shard_map/ppermute | solution.py:501
  113.4 2.7 %collective-permute-start.21 = (bf16[4,128,256]{2,1,0:T(8,128)(2,1)S(1)}, bf16[4,128,256]{2,1,0:T(8,128)(2,1)S(1)}, u32[]{:S(2)}, u32[]{:S(2)}) collective-permute-start(bf16[4,128,256]{2,1,0:T(8,128)(2,1)S(1)} %add_convert_fusion), channel_id=1, source_target_pairs={{0,3},{1,0},{2,1},{3,2},{4,7},{5,4},{6,5},{7,6},{8,11},{9,8},{10,9... | collective-permute-start | bytes 786440 | tf_op jit(solution)/shard_map/ppermute | solution.py:505
  116.1 1.8 %collective-permute-done.16.near_a = bf16[4,128,256]{2,1,0:T(8,128)(2,1)S(1)} collective-permute-done((bf16[4,128,256]{2,1,0:T(8,128)(2,1)S(1)}, bf16[4,128,256]{2,1,0:T(8,128)(2,1)S(1)}, u32[]{:S(2)}, u32[]{:S(2)}) %collective-permute-start.16) | collective-permute-done | bytes 262176 | tf_op jit(solution)/shard_map/ppermute | solution.py:505
  118.8 5.6 %collective-permute-done.18.far_a = bf16[4,128,256]{2,1,0:T(8,128)(2,1)S(1)} collective-permute-done((bf16[4,128,256]{2,1,0:T(8,128)(2,1)S(1)}, bf16[4,128,256]{2,1,0:T(8,128)(2,1)S(1)}, u32[]{:S(2)}, u32[]{:S(2)}) %collective-permute-start.18) | collective-permute-done | bytes 262176 | tf_op jit(solution)/shard_map/ppermute | solution.py:501
  124.4 1.1 finish.1
  (40 shorter events, 10.4 us)
Async XLA Ops:
  1.9 10.1 %collective-permute-start = (bf16[4,128,256]{2,1,0:T(8,128)(2,1)S(1)}, bf16[4,128,256]{2,1,0:T(8,128)(2,1)S(1)}, u32[]{:S(2)}, u32[]{:S(2)}) collective-permute-start(bf16[4,128,256]{2,1,0:T(8,128)(2,1)S(1)} %get-tuple-element.55.refs_0_), channel_id=1, source_target_pairs={{0,1},{1,2},{2,3},{3,0},{4,5},{5,6},{6,7},{7,4},{8,9},{9,10},{10,1... | collective-permute-start | bytes 786440 | tf_op jit(solution)/shard_map/ppermute | solution.py:501
  4.1 7.9 %collective-permute-start.1 = (bf16[4,128,256]{2,1,0:T(8,128)(2,1)S(1)}, bf16[4,128,256]{2,1,0:T(8,128)(2,1)S(1)}, u32[]{:S(2)}, u32[]{:S(2)}) collective-permute-start(bf16[4,128,256]{2,1,0:T(8,128)(2,1)S(1)} %get-tuple-element.56.refs_1_), channel_id=1, source_target_pairs={{0,3},{1,0},{2,1},{3,2},{4,7},{5,4},{6,5},{7,6},{8,11},{9,8},{10,9... | collective-permute-start | bytes 786440 | tf_op jit(solution)/shard_map/ppermute | solution.py:505
  5.6 13.6 %collective-permute-start.2 = (bf16[4,128,256]{2,1,0:T(8,128)(2,1)S(1)}, bf16[4,128,256]{2,1,0:T(8,128)(2,1)S(1)}, u32[]{:S(2)}, u32[]{:S(2)}) collective-permute-start(bf16[4,128,256]{2,1,0:T(8,128)(2,1)S(1)} %get-tuple-element.55.refs_0_), channel_id=1, source_target_pairs={{0,3},{1,0},{2,1},{3,2},{4,7},{5,4},{6,5},{7,6},{8,11},{9,8},{10,9... | collective-permute-start | bytes 786440 | tf_op jit(solution)/shard_map/ppermute | solution.py:505
  7.0 12.2 %collective-permute-start.5 = (bf16[4,128,256]{2,1,0:T(8,128)(2,1)S(1)}, bf16[4,128,256]{2,1,0:T(8,128)(2,1)S(1)}, u32[]{:S(2)}, u32[]{:S(2)}) collective-permute-start(bf16[4,128,256]{2,1,0:T(8,128)(2,1)S(1)} %get-tuple-element.56.refs_1_), channel_id=1, source_target_pairs={{0,1},{1,2},{2,3},{3,0},{4,5},{5,6},{6,7},{7,4},{8,9},{9,10},{10,1... | collective-permute-start | bytes 786440 | tf_op jit(solution)/shard_map/ppermute | solution.py:501
  12.0 9.9 %collective-permute-start.4 = (bf16[4,128,256]{2,1,0:T(8,128)(2,1)S(1)}, bf16[4,128,256]{2,1,0:T(8,128)(2,1)S(1)}, u32[]{:S(2)}, u32[]{:S(2)}) collective-permute-start(bf16[4,128,256]{2,1,0:T(8,128)(2,1)S(1)} %collective-permute-done.1.refs_3_), channel_id=1, source_target_pairs={{0,3},{1,0},{2,1},{3,2},{4,7},{5,4},{6,5},{7,6},{8,11},{9,8},{10,9... | collective-permute-start | bytes 786440 | tf_op jit(solution)/shard_map/ppermute | solution.py:505
  14.7 7.2 %collective-permute-start.3 = (bf16[4,128,256]{2,1,0:T(8,128)(2,1)S(1)}, bf16[4,128,256]{2,1,0:T(8,128)(2,1)S(1)}, u32[]{:S(2)}, u32[]{:S(2)}) collective-permute-start(bf16[4,128,256]{2,1,0:T(8,128)(2,1)S(1)} %collective-permute-done.refs_6_), channel_id=1, source_target_pairs={{0,1},{1,2},{2,3},{3,0},{4,5},{5,6},{6,7},{7,4},{8,9},{9,10},{10,1... | collective-permute-start | bytes 786440 | tf_op jit(solution)/shard_map/ppermute | solution.py:501
  23.4 5.6 %collective-permute-start.6 = (bf16[256,512]{1,0:T(8,128)(2,1)S(1)}, bf16[256,512]{1,0:T(8,128)(2,1)S(1)}, u32[]{:S(2)}, u32[]{:S(2)}) collective-permute-start(bf16[256,512]{1,0:T(8,128)(2,1)S(1)} %get-tuple-element.67), channel_id=1, source_target_pairs={{0,4},{4,0},{1,5},{5,1},{2,6},{6,2},{3,7},{7,3},{8,12},{12,8},{9,1... | collective-permute-start | bytes 786440 | tf_op jit(solution)/shard_map/ppermute | solution.py:256
  39.4 8.8 %collective-permute-start.9 = (bf16[1,32,512]{2,1,0:T(8,128)(2,1)S(1)}, bf16[1,32,512]{2,1,0:T(8,128)(2,1)S(1)}, u32[]{:S(2)}, u32[]{:S(2)}) collective-permute-start(bf16[1,32,512]{2,1,0:T(8,128)(2,1)S(1)} %total.4.refs_0_), channel_id=1, source_target_pairs={{0,48},{16,0},{32,16},{48,32},{1,49},{17,1},{33,17},{49,33},{2,50}... | collective-permute-start | bytes 98312 | tf_op jit(solution)/shard_map/ppermute | solution.py:301
  44.6 4.9 %collective-permute-start.8 = (bf16[1,32,512]{2,1,0:T(8,128)(2,1)S(1)}, bf16[1,32,512]{2,1,0:T(8,128)(2,1)S(1)}, u32[]{:S(2)}, u32[]{:S(2)}) collective-permute-start(bf16[1,32,512]{2,1,0:T(8,128)(2,1)S(1)} %total.4.refs_0_), channel_id=1, source_target_pairs={{0,16},{16,32},{32,48},{48,0},{1,17},{17,33},{33,49},{49,1},{2,18}... | collective-permute-start | bytes 98312 | tf_op jit(solution)/shard_map/ppermute | solution.py:301
  44.6 6.9 %collective-permute-start.7 = (bf16[1,32,512]{2,1,0:T(8,128)(2,1)S(1)}, bf16[1,32,512]{2,1,0:T(8,128)(2,1)S(1)}, u32[]{:S(2)}, u32[]{:S(2)}) collective-permute-start(bf16[1,32,512]{2,1,0:T(8,128)(2,1)S(1)} %total.4.refs_0_), channel_id=1, source_target_pairs={{0,32},{16,48},{32,0},{48,16},{1,33},{17,49},{33,1},{49,17},{2,34}... | collective-permute-start | bytes 98312 | tf_op jit(solution)/shard_map/ppermute | solution.py:301
  60.1 5.2 %copy-start = (f32[2,2048]{1,0:T(2,128)S(1)}, f32[2,2048]{1,0:T(2,128)}, u32[]{:S(2)}) copy-start(f32[2,2048]{1,0:T(2,128)} %b_ref.3) | copy-start | bytes 49156
  60.1 5.2 %collective-permute-start.10 = (bf16[8,32,512]{2,1,0:T(8,128)(2,1)S(1)}, bf16[8,32,512]{2,1,0:T(8,128)(2,1)S(1)}, u32[]{:S(2)}, u32[]{:S(2)}) collective-permute-start(bf16[8,32,512]{2,1,0:T(8,128)(2,1)S(1)} %all_to_all.21.mine_ref), channel_id=1, source_target_pairs={{0,4},{4,0},{1,5},{5,1},{2,6},{6,2},{3,7},{7,3},{8,12},{12,8},{9,1... | collective-permute-start | bytes 786440 | tf_op jit(solution)/shard_map/ppermute | solution.py:256
  67.0 1.6 %collective-permute-start.11 = (bf16[256,512]{1,0:T(8,128)(2,1)S(1)}, bf16[256,512]{1,0:T(8,128)(2,1)S(1)}, u32[]{:S(2)}, u32[]{:S(2)}) collective-permute-start(bf16[256,512]{1,0:T(8,128)(2,1)S(1)} %get-tuple-element.82), channel_id=1, source_target_pairs={{0,4},{4,0},{1,5},{5,1},{2,6},{6,2},{3,7},{7,3},{8,12},{12,8},{9,1... | collective-permute-start | bytes 786440 | tf_op jit(solution)/shard_map/ppermute | solution.py:256
  77.8 6.6 %collective-permute-start.14 = (bf16[1,32,512]{2,1,0:T(8,128)(2,1)S(1)}, bf16[1,32,512]{2,1,0:T(8,128)(2,1)S(1)}, u32[]{:S(2)}, u32[]{:S(2)}) collective-permute-start(bf16[1,32,512]{2,1,0:T(8,128)(2,1)S(1)} %total.6.refs_0_), channel_id=1, source_target_pairs={{0,48},{16,0},{32,16},{48,32},{1,49},{17,1},{33,17},{49,33},{2,50}... | collective-permute-start | bytes 98312 | tf_op jit(solution)/shard_map/ppermute | solution.py:301
  81.7 4.9 %collective-permute-start.13 = (bf16[1,32,512]{2,1,0:T(8,128)(2,1)S(1)}, bf16[1,32,512]{2,1,0:T(8,128)(2,1)S(1)}, u32[]{:S(2)}, u32[]{:S(2)}) collective-permute-start(bf16[1,32,512]{2,1,0:T(8,128)(2,1)S(1)} %total.6.refs_0_), channel_id=1, source_target_pairs={{0,16},{16,32},{32,48},{48,0},{1,17},{17,33},{33,49},{49,1},{2,18}... | collective-permute-start | bytes 98312 | tf_op jit(solution)/shard_map/ppermute | solution.py:301
  81.7 6.8 %collective-permute-start.12 = (bf16[1,32,512]{2,1,0:T(8,128)(2,1)S(1)}, bf16[1,32,512]{2,1,0:T(8,128)(2,1)S(1)}, u32[]{:S(2)}, u32[]{:S(2)}) collective-permute-start(bf16[1,32,512]{2,1,0:T(8,128)(2,1)S(1)} %total.6.refs_0_), channel_id=1, source_target_pairs={{0,32},{16,48},{32,0},{48,16},{1,33},{17,49},{33,1},{49,17},{2,34}... | collective-permute-start | bytes 98312 | tf_op jit(solution)/shard_map/ppermute | solution.py:301
  97.4 5.1 %collective-permute-start.15 = (bf16[8,32,512]{2,1,0:T(8,128)(2,1)S(1)}, bf16[8,32,512]{2,1,0:T(8,128)(2,1)S(1)}, u32[]{:S(2)}, u32[]{:S(2)}) collective-permute-start(bf16[8,32,512]{2,1,0:T(8,128)(2,1)S(1)} %all_to_all.23.mine_ref), channel_id=1, source_target_pairs={{0,4},{4,0},{1,5},{5,1},{2,6},{6,2},{3,7},{7,3},{8,12},{12,8},{9,1... | collective-permute-start | bytes 786440 | tf_op jit(solution)/shard_map/ppermute | solution.py:256
  104.2 8.9 %collective-permute-start.17 = (bf16[4,128,256]{2,1,0:T(8,128)(2,1)S(1)}, bf16[4,128,256]{2,1,0:T(8,128)(2,1)S(1)}, u32[]{:S(2)}, u32[]{:S(2)}) collective-permute-start(bf16[4,128,256]{2,1,0:T(8,128)(2,1)S(1)} %get-tuple-element.102), channel_id=1, source_target_pairs={{0,1},{1,2},{2,3},{3,0},{4,5},{5,6},{6,7},{7,4},{8,9},{9,10},{10,1... | collective-permute-start | bytes 786440 | tf_op jit(solution)/shard_map/ppermute | solution.py:501
  104.9 8.4 %collective-permute-start.20 = (bf16[4,128,256]{2,1,0:T(8,128)(2,1)S(1)}, bf16[4,128,256]{2,1,0:T(8,128)(2,1)S(1)}, u32[]{:S(2)}, u32[]{:S(2)}) collective-permute-start(bf16[4,128,256]{2,1,0:T(8,128)(2,1)S(1)} %get-tuple-element.105), channel_id=1, source_target_pairs={{0,3},{1,0},{2,1},{3,2},{4,7},{5,4},{6,5},{7,6},{8,11},{9,8},{10,9... | collective-permute-start | bytes 786440 | tf_op jit(solution)/shard_map/ppermute | solution.py:505
  108.0 9.9 %collective-permute-start.16 = (bf16[4,128,256]{2,1,0:T(8,128)(2,1)S(1)}, bf16[4,128,256]{2,1,0:T(8,128)(2,1)S(1)}, u32[]{:S(2)}, u32[]{:S(2)}) collective-permute-start(bf16[4,128,256]{2,1,0:T(8,128)(2,1)S(1)} %get-tuple-element.100), channel_id=1, source_target_pairs={{0,3},{1,0},{2,1},{3,2},{4,7},{5,4},{6,5},{7,6},{8,11},{9,8},{10,9... | collective-permute-start | bytes 786440 | tf_op jit(solution)/shard_map/ppermute | solution.py:505
  108.9 9.8 %collective-permute-start.19 = (bf16[4,128,256]{2,1,0:T(8,128)(2,1)S(1)}, bf16[4,128,256]{2,1,0:T(8,128)(2,1)S(1)}, u32[]{:S(2)}, u32[]{:S(2)}) collective-permute-start(bf16[4,128,256]{2,1,0:T(8,128)(2,1)S(1)} %get-tuple-element.103), channel_id=1, source_target_pairs={{0,1},{1,2},{2,3},{3,0},{4,5},{5,6},{6,7},{7,4},{8,9},{9,10},{10,1... | collective-permute-start | bytes 786440 | tf_op jit(solution)/shard_map/ppermute | solution.py:501
  113.2 11.2 %collective-permute-start.18 = (bf16[4,128,256]{2,1,0:T(8,128)(2,1)S(1)}, bf16[4,128,256]{2,1,0:T(8,128)(2,1)S(1)}, u32[]{:S(2)}, u32[]{:S(2)}) collective-permute-start(bf16[4,128,256]{2,1,0:T(8,128)(2,1)S(1)} %add_convert_fusion.1), channel_id=1, source_target_pairs={{0,1},{1,2},{2,3},{3,0},{4,5},{5,6},{6,7},{7,4},{8,9},{9,10},{10,1... | collective-permute-start | bytes 786440 | tf_op jit(solution)/shard_map/ppermute | solution.py:501
  113.4 11.0 %collective-permute-start.21 = (bf16[4,128,256]{2,1,0:T(8,128)(2,1)S(1)}, bf16[4,128,256]{2,1,0:T(8,128)(2,1)S(1)}, u32[]{:S(2)}, u32[]{:S(2)}) collective-permute-start(bf16[4,128,256]{2,1,0:T(8,128)(2,1)S(1)} %add_convert_fusion), channel_id=1, source_target_pairs={{0,3},{1,0},{2,1},{3,2},{4,7},{5,4},{6,5},{7,6},{8,11},{9,8},{10,9... | collective-permute-start | bytes 786440 | tf_op jit(solution)/shard_map/ppermute | solution.py:505

commit v11 on v8

--- a/solution.py
+++ b/solution.py
@@ -220,26 +220,52 @@
     return pl.BlockSpec(memory_space=pl.ANY)
 
 
-def first_kernel(core_ref, counts_a, counts_b, *refs):
-    embs, (cot, v_ref, u_ref, pooled_ref, wide_ref, send_ref) = refs[:8], refs[8:]
-    half, _, emb = embs[0].shape
+def near_kernel_pool(counts_a, counts_b, oa, ob, ra, rb, la, lb, out_ref):
+    half, rows, emb = oa.shape
     for t in range(2 * half):
         side, i = divmod(t, half)
-        rows = jnp.concatenate([embs[2 * k + side][i] for k in range(4)], axis=0)
-        pooled = jnp.dot((counts_a, counts_b)[side][i], rows, preferred_element_type=F32).astype(BF16)
+        counts = (counts_a, counts_b)[side]
+        own, right_rows, left_rows = ((oa, ra, la), (ob, rb, lb))[side]
+        two = jnp.concatenate([own[i], right_rows[i]], axis=0)
+        part = jnp.dot(counts[i, :, : 2 * rows], two, preferred_element_type=F32)
+        part += jnp.dot(counts[i, :, 3 * rows :], left_rows[i], preferred_element_type=F32)
+        out_ref[:, t * emb : (t + 1) * emb] = part.astype(BF16)
+
+
+def near_pooled(counts, embs):
+    half, samp, _ = counts[0].shape
+    emb = embs[0].shape[-1]
+    return pl.pallas_call(
+        near_kernel_pool,
+        in_specs=[vmem()] * 8,
+        out_specs=vmem(),
+        out_shape=pltpu.VMEM((samp, 2 * half * emb), BF16),
+        compiler_params=params(4),
+        cost_estimate=cost(1 << 29, 4 << 20),
+        name="near_pooled",
+    )(*kept(*counts), *embs)
+
+
+def first_kernel(core_ref, counts_a, counts_b, part, far_a, far_b, cot, v_ref, u_ref, pooled_ref, wide_ref, send_ref):
+    half, rows, emb = far_a.shape
+    for t in range(2 * half):
+        side, i = divmod(t, half)
         at = slice(t * emb, (t + 1) * emb)
+        far = (counts_a, counts_b)[side][i, :, 2 * rows : 3 * rows]
+        pooled = jnp.dot(far, (far_a, far_b)[side][i], preferred_element_type=F32)
+        pooled = (pooled + part[:, at].astype(F32)).astype(BF16)
         pooled_ref[:, at] = pooled
         wide_ref[:, at] = (cot[:, at].astype(F32) * pooled.astype(F32)).astype(BF16)
     one_sum(core_ref[0] != 0, pooled_ref, wide_ref, v_ref, u_ref, 0, send_ref)
 
 
-def first_sums(core, counts, embs, cot, v, u):
+def first_sums(core, counts, part, far, cot, v, u):
     half, samp, rows = counts[0].shape
-    emb = embs[0].shape[-1]
+    emb = far[0].shape[-1]
     rank = v.shape[-1]
     return pl.pallas_call(
         first_kernel,
-        in_specs=[smem()] + [vmem()] * 13,
+        in_specs=[smem()] + [vmem()] * 8,
         out_specs=[vmem()] * 3,
         out_shape=[
             pltpu.VMEM((samp, 2 * half * emb), BF16),
@@ -249,7 +275,7 @@
         compiler_params=params(8),
         cost_estimate=cost(3 << 29, 10 << 20),
         name="first_sums",
-    )(core, *kept(*counts), *embs, *kept(cot, v, u))
+    )(core, *kept(*counts, part), *far, *kept(cot, v, u))
 
 
 def swap(arr, axis):
@@ -525,8 +551,9 @@
     far_a, far_b = right(left_a), left(right_b)
     loads = (cotangent, cross_v, cross_u)
     counts_b, cot, v, u = make_counts(mine, entry_ids, entry_sample, samp, rows, edges, loads)
-    embs = (own_a, own_b, right_a, right_b, far_a, far_b, left_a, left_b)
-    pooled, wide, send = first_sums(core, (counts_a, counts_b), embs, cot, v, u)
+    counts = (counts_a, counts_b)
+    part = near_pooled(counts, (own_a, own_b, right_a, right_b, left_a, left_b))
+    pooled, wide, send = first_sums(core, counts, part, (far_a, far_b), cot, v, u)
     prod, other, turned_a = sum_all(core, send, pooled, wide, v, u, 0, counts_a)
     x1, a, wide, send = middle(core, prod, other, cross_bias, pooled, cot, u, v)
     prod, other, turned_b = sum_all(core, send, x1, wide, v, u, 1, counts_b)

time: 124 us -> 124 us (level)
    pallas_call x2, Pallas kernels: 9.86 us -> 8.42 us  [make_counts(): pl.pallas_call(functools.partial(counts_kernel, first_table=0 if edges is...]
  transfers between devices with their start and end apart: 22 -> 22, of which waited for: 13 -> 13; matrix products, arithmetic and copies ran while one was open for 0% -> 0% of each run, Pallas kernels for 12% -> 11%
where the time goes in v11:
time: 124 us
  starting transfers between devices  43.3 us (35%)
  blocking collectives  37.2 us (30%)
  Pallas kernels  21.2 us (17%)
  waiting for transfers between devices  21.1 us (17%)
    all_to_all x4, blocking collectives, swap_all(): return lax.all_to_all(arr, ('x', 'zl'), 0, 0, tiled=True)  37.2 us
    ppermute x6, starting transfers between devices, turn(): return lax.ppermute(arr, 'zh', [(i, i + k & 3) for i in range(4)])  15.1 us
    ppermute x4, starting transfers between devices, swap(): return lax.ppermute(arr, axis, [(0, 1), (1, 0)])  12.7 us
    ppermute x6, starting transfers between devices, left(): return lax.ppermute(arr, 'row', [(i, i + 3 & 3) for i in range(4)])  11.8 us
    ppermute x6, waiting for transfers between devices, right(): return lax.ppermute(arr, 'row', [(i, i + 1 & 3) for i in range(4)])  10.2 us
    pallas_call x2, Pallas kernels, make_counts(): pl.pallas_call(functools.partial(counts_kernel, first_table=0 if edges is...  8.42 us
    ppermute x6, waiting for transfers between devices, turn(): return lax.ppermute(arr, 'zh', [(i, i + k & 3) for i in range(4)])  5.11 us
    ppermute x6, waiting for transfers between devices, left(): return lax.ppermute(arr, 'row', [(i, i + 3 & 3) for i in range(4)])  4.26 us
  transfers between devices with their start and end apart: 22, of which 13 were waited for; matrix products, arithmetic and copies ran while one was open for 0% of the time, Pallas kernels for 11%

profile of v11, /device:TPU:1, one launch (start us, length us, event | category | flops | bytes accessed | tf_op | source)
XLA Modules:
  0.0 124.0 jit_solution(3087630396046138162)
XLA Ops:
  0.6 1.2 %cast.1 = (bf16[4,128,256]{2,1,0:T(8,128)(2,1)S(1)}, bf16[4,128,256]{2,1,0:T(8,128)(2,1)S(1)}) custom-call(f32[8,128,256]{2,1,0:T(8,128)} %in_ref.1), custom_call_target="tpu_custom_call" | custom-call | flops 262144 | bytes 1572864 | tf_op jit(solution)/shard_map/cast/pallas_call | solution.py:57
  1.9 2.2 %collective-permute-start = (bf16[4,128,256]{2,1,0:T(8,128)(2,1)S(1)}, bf16[4,128,256]{2,1,0:T(8,128)(2,1)S(1)}, u32[]{:S(2)}, u32[]{:S(2)}) collective-permute-start(bf16[4,128,256]{2,1,0:T(8,128)(2,1)S(1)} %get-tuple-element.55.oa), channel_id=1, source_target_pairs={{0,1},{1,2},{2,3},{3,0},{4,5},{5,6},{6,7},{7,4},{8,9},{9,10},{10,1... | collective-permute-start | bytes 786440 | tf_op jit(solution)/shard_map/ppermute | solution.py:527
  4.1 1.5 %collective-permute-start.1 = (bf16[4,128,256]{2,1,0:T(8,128)(2,1)S(1)}, bf16[4,128,256]{2,1,0:T(8,128)(2,1)S(1)}, u32[]{:S(2)}, u32[]{:S(2)}) collective-permute-start(bf16[4,128,256]{2,1,0:T(8,128)(2,1)S(1)} %get-tuple-element.56.ob), channel_id=1, source_target_pairs={{0,3},{1,0},{2,1},{3,2},{4,7},{5,4},{6,5},{7,6},{8,11},{9,8},{10,9... | collective-permute-start | bytes 786440 | tf_op jit(solution)/shard_map/ppermute | solution.py:531
  5.6 1.4 %collective-permute-start.2 = (bf16[4,128,256]{2,1,0:T(8,128)(2,1)S(1)}, bf16[4,128,256]{2,1,0:T(8,128)(2,1)S(1)}, u32[]{:S(2)}, u32[]{:S(2)}) collective-permute-start(bf16[4,128,256]{2,1,0:T(8,128)(2,1)S(1)} %get-tuple-element.55.oa), channel_id=1, source_target_pairs={{0,3},{1,0},{2,1},{3,2},{4,7},{5,4},{6,5},{7,6},{8,11},{9,8},{10,9... | collective-permute-start | bytes 786440 | tf_op jit(solution)/shard_map/ppermute | solution.py:531
  7.1 3.9 %counts.2 = (bf16[4,256,512]{2,1,0:T(8,128)(2,1)S(1)}, s32[16]{0:T(128)S(1)}) custom-call(s32[1]{0:T(128)} %bitcast.1.mine_ref, s32[8,4096]{1,0:T(8,128)} %ids_ref.3, s32[8,4096]{1,0:T(8,128)} %own_ref.3), custom_call_target="tpu_custom_call" | custom-call | flops 1610612736 | bytes 3145728 | tf_op jit(solution)/shard_map/counts/pallas_call | solution.py:140
  11.0 3.1 %collective-permute-start.5 = (bf16[4,128,256]{2,1,0:T(8,128)(2,1)S(1)}, bf16[4,128,256]{2,1,0:T(8,128)(2,1)S(1)}, u32[]{:S(2)}, u32[]{:S(2)}) collective-permute-start(bf16[4,128,256]{2,1,0:T(8,128)(2,1)S(1)} %collective-permute-done.1.rb), channel_id=1, source_target_pairs={{0,3},{1,0},{2,1},{3,2},{4,7},{5,4},{6,5},{7,6},{8,11},{9,8},{10,9... | collective-permute-start | bytes 786440 | tf_op jit(solution)/shard_map/ppermute | solution.py:531
  14.2 4.5 %counts.3 = (bf16[4,256,512]{2,1,0:T(8,128)(2,1)S(1)}, bf16[256,2048]{1,0:T(8,128)(2,1)S(1)}, bf16[2,2048,512]{2,1,0:T(8,128)(2,1)S(1)}, bf16[2,512,2048]{2,1,0:T(8,128)(2,1)S(1)}) custom-call(s32[1]{0:T(128)} %bitcast.1.mine_ref, s32[8,4096]{1,0:T(8,128)} %ids_ref.3, s32[8,4096]{1,0:T(8,128)} %own_ref.3, s32[16]{0:T(128)S(1)} %get-tuple-element.58.refs_0_, ...), custom_call_target="tpu_custom_call" | custom-call | flops 1610612736 | bytes 3145728 | tf_op jit(solution)/shard_map/counts/pallas_call | solution.py:140
  19.4 2.5 %collective-permute-done.5.far_b = bf16[4,128,256]{2,1,0:T(8,128)(2,1)S(1)} collective-permute-done((bf16[4,128,256]{2,1,0:T(8,128)(2,1)S(1)}, bf16[4,128,256]{2,1,0:T(8,128)(2,1)S(1)}, u32[]{:S(2)}, u32[]{:S(2)}) %collective-permute-start.5) | collective-permute-done | bytes 262176 | tf_op jit(solution)/shard_map/ppermute | solution.py:531
  21.9 1.3 %first_sums.1 = (bf16[256,2048]{1,0:T(8,128)(2,1)S(1)}, bf16[256,2048]{1,0:T(8,128)(2,1)S(1)}, bf16[256,512]{1,0:T(8,128)(2,1)S(1)}) custom-call(s32[1]{0:T(128)} %bitcast.core_ref, bf16[4,256,512]{2,1,0:T(8,128)(2,1)S(1)} %get-tuple-element.73.counts_a.in_ref, bf16[4,256,512]{2,1,0:T(8,128)(2,1)S(1)} %get-tuple-element.88.counts_b.in_ref, ...), custom_call_target="tpu_custom_call" | custom-call | flops 1610612736 | bytes 10485760 | tf_op jit(solution)/shard_map/first_sums/pallas_call | solution.py:266
  23.3 4.4 %collective-permute-start.6 = (bf16[256,512]{1,0:T(8,128)(2,1)S(1)}, bf16[256,512]{1,0:T(8,128)(2,1)S(1)}, u32[]{:S(2)}, u32[]{:S(2)}) collective-permute-start(bf16[256,512]{1,0:T(8,128)(2,1)S(1)} %get-tuple-element.67), channel_id=1, source_target_pairs={{0,4},{4,0},{1,5},{5,1},{2,6},{6,2},{3,7},{7,3},{8,12},{12,8},{9,1... | collective-permute-start | bytes 786440 | tf_op jit(solution)/shard_map/ppermute | solution.py:282
  28.9 10.4 %all_to_all.20.refs_0_ = bf16[8,32,512]{2,1,0:T(8,128)(2,1)S(1)} all-to-all(bf16[8,32,512]{2,1,0:T(8,128)(2,1)S(1)} %cut.2), channel_id=1, replica_groups=mesh['x'=4,'zh'=4,'zl'=2,'c'=2,'row'=4] {'x','zl'}, dimensions={0} | all-to-all | bytes 524288 | tf_op jit(solution)/shard_map/all_to_all | solution.py:323
  39.3 6.1 %collective-permute-start.9 = (bf16[1,32,512]{2,1,0:T(8,128)(2,1)S(1)}, bf16[1,32,512]{2,1,0:T(8,128)(2,1)S(1)}, u32[]{:S(2)}, u32[]{:S(2)}) collective-permute-start(bf16[1,32,512]{2,1,0:T(8,128)(2,1)S(1)} %total.4.refs_0_), channel_id=1, source_target_pairs={{0,32},{16,48},{32,0},{48,16},{1,33},{17,49},{33,1},{49,17},{2,34}... | collective-permute-start | bytes 98312 | tf_op jit(solution)/shard_map/ppermute | solution.py:327
  45.6 2.1 %collective-permute-start.7 = (bf16[1,32,512]{2,1,0:T(8,128)(2,1)S(1)}, bf16[1,32,512]{2,1,0:T(8,128)(2,1)S(1)}, u32[]{:S(2)}, u32[]{:S(2)}) collective-permute-start(bf16[1,32,512]{2,1,0:T(8,128)(2,1)S(1)} %total.4.refs_0_), channel_id=1, source_target_pairs={{0,16},{16,32},{32,48},{48,0},{1,17},{17,33},{33,49},{49,1},{2,18}... | collective-permute-start | bytes 98312 | tf_op jit(solution)/shard_map/ppermute | solution.py:327
  48.1 1.0 collective-permute-done.8.refs_2_
  49.1 1.8 %collective-permute-done.7.refs_1_ = bf16[1,32,512]{2,1,0:T(8,128)(2,1)S(1)} collective-permute-done((bf16[1,32,512]{2,1,0:T(8,128)(2,1)S(1)}, bf16[1,32,512]{2,1,0:T(8,128)(2,1)S(1)}, u32[]{:S(2)}, u32[]{:S(2)}) %collective-permute-start.7) | collective-permute-done | bytes 32800 | tf_op jit(solution)/shard_map/ppermute | solution.py:327
  50.9 8.7 %all_to_all.21.mine_ref = bf16[8,32,512]{2,1,0:T(8,128)(2,1)S(1)} all-to-all(bf16[8,32,512]{2,1,0:T(8,128)(2,1)S(1)} %total.5), channel_id=1, replica_groups=mesh['x'=4,'zh'=4,'zl'=2,'c'=2,'row'=4] {'x','zl'}, dimensions={0} | all-to-all | bytes 524288 | tf_op jit(solution)/shard_map/all_to_all | solution.py:323
  59.6 4.0 %collective-permute-start.10 = (bf16[8,32,512]{2,1,0:T(8,128)(2,1)S(1)}, bf16[8,32,512]{2,1,0:T(8,128)(2,1)S(1)}, u32[]{:S(2)}, u32[]{:S(2)}) collective-permute-start(bf16[8,32,512]{2,1,0:T(8,128)(2,1)S(1)} %all_to_all.21.mine_ref), channel_id=1, source_target_pairs={{0,4},{4,0},{1,5},{5,1},{2,6},{6,2},{3,7},{7,3},{8,12},{12,8},{9,1... | collective-permute-start | bytes 786440 | tf_op jit(solution)/shard_map/ppermute | solution.py:282
  64.8 1.8 %middle.1 = (bf16[256,2048]{1,0:T(8,128)(2,1)S(1)}, bf16[256,2048]{1,0:T(8,128)(2,1)S(1)}, bf16[256,2048]{1,0:T(8,128)(2,1)S(1)}, bf16[256,512]{1,0:T(8,128)(2,1)S(1)}) custom-call(s32[1]{0:T(128)} %bitcast.core_ref, f32[256,2048]{1,0:T(8,128)S(1)} %product.2.prod, bf16[8,32,512]{2,1,0:T(8,128)(2,1)S(1)} %collective-permute-done.10.other_ref, ...), custom_call_target="tpu_custom_call" | custom-call | flops 2147483648 | bytes 8388608 | tf_op jit(solution)/shard_map/middle/pallas_call | solution.py:418
  68.3 9.0 %all_to_all.22.refs_0_ = bf16[8,32,512]{2,1,0:T(8,128)(2,1)S(1)} all-to-all(bf16[8,32,512]{2,1,0:T(8,128)(2,1)S(1)} %cut.3), channel_id=1, replica_groups=mesh['x'=4,'zh'=4,'zl'=2,'c'=2,'row'=4] {'x','zl'}, dimensions={0} | all-to-all | bytes 524288 | tf_op jit(solution)/shard_map/all_to_all | solution.py:323
  77.3 4.3 %collective-permute-start.14 = (bf16[1,32,512]{2,1,0:T(8,128)(2,1)S(1)}, bf16[1,32,512]{2,1,0:T(8,128)(2,1)S(1)}, u32[]{:S(2)}, u32[]{:S(2)}) collective-permute-start(bf16[1,32,512]{2,1,0:T(8,128)(2,1)S(1)} %total.6.refs_0_), channel_id=1, source_target_pairs={{0,32},{16,48},{32,0},{48,16},{1,33},{17,49},{33,1},{49,17},{2,34}... | collective-permute-start | bytes 98312 | tf_op jit(solution)/shard_map/ppermute | solution.py:327
  81.7 2.4 %collective-permute-start.12 = (bf16[1,32,512]{2,1,0:T(8,128)(2,1)S(1)}, bf16[1,32,512]{2,1,0:T(8,128)(2,1)S(1)}, u32[]{:S(2)}, u32[]{:S(2)}) collective-permute-start(bf16[1,32,512]{2,1,0:T(8,128)(2,1)S(1)} %total.6.refs_0_), channel_id=1, source_target_pairs={{0,16},{16,32},{32,48},{48,0},{1,17},{17,33},{33,49},{49,1},{2,18}... | collective-permute-start | bytes 98312 | tf_op jit(solution)/shard_map/ppermute | solution.py:327
  84.3 1.3 %collective-permute-done.13.refs_2_ = bf16[1,32,512]{2,1,0:T(8,128)(2,1)S(1)} collective-permute-done((bf16[1,32,512]{2,1,0:T(8,128)(2,1)S(1)}, bf16[1,32,512]{2,1,0:T(8,128)(2,1)S(1)}, u32[]{:S(2)}, u32[]{:S(2)}) %collective-permute-start.13) | collective-permute-done | bytes 32800 | tf_op jit(solution)/shard_map/ppermute | solution.py:327
  85.6 1.0 collective-permute-done.12.refs_1_
  86.7 9.1 %all_to_all.23.mine_ref = bf16[8,32,512]{2,1,0:T(8,128)(2,1)S(1)} all-to-all(bf16[8,32,512]{2,1,0:T(8,128)(2,1)S(1)} %total.7), channel_id=1, replica_groups=mesh['x'=4,'zh'=4,'zl'=2,'c'=2,'row'=4] {'x','zl'}, dimensions={0} | all-to-all | bytes 524288 | tf_op jit(solution)/shard_map/all_to_all | solution.py:323
  95.8 3.8 %collective-permute-start.15 = (bf16[8,32,512]{2,1,0:T(8,128)(2,1)S(1)}, bf16[8,32,512]{2,1,0:T(8,128)(2,1)S(1)}, u32[]{:S(2)}, u32[]{:S(2)}) collective-permute-start(bf16[8,32,512]{2,1,0:T(8,128)(2,1)S(1)} %all_to_all.23.mine_ref), channel_id=1, source_target_pairs={{0,4},{4,0},{1,5},{5,1},{2,6},{6,2},{3,7},{7,3},{8,12},{12,8},{9,1... | collective-permute-start | bytes 786440 | tf_op jit(solution)/shard_map/ppermute | solution.py:282
  100.8 1.8 %far_rows.1 = (bf16[256,2048]{1,0:T(8,128)(2,1)S(1)}, bf16[256,2048]{1,0:T(8,128)(2,1)S(1)}, bf16[4,128,256]{2,1,0:T(8,128)(2,1)S(1)}, bf16[4,128,256]{2,1,0:T(8,128)(2,1)S(1)}) custom-call(s32[1]{0:T(128)} %bitcast.core_ref, f32[256,2048]{1,0:T(8,128)S(1)} %product.3.prod, bf16[8,32,512]{2,1,0:T(8,128)(2,1)S(1)} %collective-permute-done.15.other_ref, ...), custom_call_target="tpu_custom_call" | custom-call | flops 1342177280 | bytes 7340032 | tf_op jit(solution)/shard_map/far_rows/pallas_call | solution.py:457
  103.3 2.0 %collective-permute-start.20 = (bf16[4,128,256]{2,1,0:T(8,128)(2,1)S(1)}, bf16[4,128,256]{2,1,0:T(8,128)(2,1)S(1)}, u32[]{:S(2)}, u32[]{:S(2)}) collective-permute-start(bf16[4,128,256]{2,1,0:T(8,128)(2,1)S(1)} %get-tuple-element.105), channel_id=1, source_target_pairs={{0,3},{1,0},{2,1},{3,2},{4,7},{5,4},{6,5},{7,6},{8,11},{9,8},{10,9... | collective-permute-start | bytes 786440 | tf_op jit(solution)/shard_map/ppermute | solution.py:531
  107.9 3.6 %collective-permute-done.17 = bf16[4,128,256]{2,1,0:T(8,128)(2,1)S(1)} collective-permute-done((bf16[4,128,256]{2,1,0:T(8,128)(2,1)S(1)}, bf16[4,128,256]{2,1,0:T(8,128)(2,1)S(1)}, u32[]{:S(2)}, u32[]{:S(2)}) %collective-permute-start.17) | collective-permute-done | bytes 262176 | tf_op jit(solution)/shard_map/ppermute | solution.py:527
  111.8 2.7 %collective-permute-start.21 = (bf16[4,128,256]{2,1,0:T(8,128)(2,1)S(1)}, bf16[4,128,256]{2,1,0:T(8,128)(2,1)S(1)}, u32[]{:S(2)}, u32[]{:S(2)}) collective-permute-start(bf16[4,128,256]{2,1,0:T(8,128)(2,1)S(1)} %add_convert_fusion), channel_id=1, source_target_pairs={{0,3},{1,0},{2,1},{3,2},{4,7},{5,4},{6,5},{7,6},{8,11},{9,8},{10,9... | collective-permute-start | bytes 786440 | tf_op jit(solution)/shard_map/ppermute | solution.py:531
  114.5 1.7 %collective-permute-done.16.near_a = bf16[4,128,256]{2,1,0:T(8,128)(2,1)S(1)} collective-permute-done((bf16[4,128,256]{2,1,0:T(8,128)(2,1)S(1)}, bf16[4,128,256]{2,1,0:T(8,128)(2,1)S(1)}, u32[]{:S(2)}, u32[]{:S(2)}) %collective-permute-start.16) | collective-permute-done | bytes 262176 | tf_op jit(solution)/shard_map/ppermute | solution.py:531
  117.1 5.6 %collective-permute-done.18.far_a = bf16[4,128,256]{2,1,0:T(8,128)(2,1)S(1)} collective-permute-done((bf16[4,128,256]{2,1,0:T(8,128)(2,1)S(1)}, bf16[4,128,256]{2,1,0:T(8,128)(2,1)S(1)}, u32[]{:S(2)}, u32[]{:S(2)}) %collective-permute-start.18) | collective-permute-done | bytes 262176 | tf_op jit(solution)/shard_map/ppermute | solution.py:527
  122.8 1.1 finish.1
  (41 shorter events, 11.4 us)
Async XLA Ops:
  1.9 9.1 %collective-permute-start = (bf16[4,128,256]{2,1,0:T(8,128)(2,1)S(1)}, bf16[4,128,256]{2,1,0:T(8,128)(2,1)S(1)}, u32[]{:S(2)}, u32[]{:S(2)}) collective-permute-start(bf16[4,128,256]{2,1,0:T(8,128)(2,1)S(1)} %get-tuple-element.55.oa), channel_id=1, source_target_pairs={{0,1},{1,2},{2,3},{3,0},{4,5},{5,6},{6,7},{7,4},{8,9},{9,10},{10,1... | collective-permute-start | bytes 786440 | tf_op jit(solution)/shard_map/ppermute | solution.py:527
  4.1 7.0 %collective-permute-start.1 = (bf16[4,128,256]{2,1,0:T(8,128)(2,1)S(1)}, bf16[4,128,256]{2,1,0:T(8,128)(2,1)S(1)}, u32[]{:S(2)}, u32[]{:S(2)}) collective-permute-start(bf16[4,128,256]{2,1,0:T(8,128)(2,1)S(1)} %get-tuple-element.56.ob), channel_id=1, source_target_pairs={{0,3},{1,0},{2,1},{3,2},{4,7},{5,4},{6,5},{7,6},{8,11},{9,8},{10,9... | collective-permute-start | bytes 786440 | tf_op jit(solution)/shard_map/ppermute | solution.py:531
  5.6 13.1 %collective-permute-start.2 = (bf16[4,128,256]{2,1,0:T(8,128)(2,1)S(1)}, bf16[4,128,256]{2,1,0:T(8,128)(2,1)S(1)}, u32[]{:S(2)}, u32[]{:S(2)}) collective-permute-start(bf16[4,128,256]{2,1,0:T(8,128)(2,1)S(1)} %get-tuple-element.55.oa), channel_id=1, source_target_pairs={{0,3},{1,0},{2,1},{3,2},{4,7},{5,4},{6,5},{7,6},{8,11},{9,8},{10,9... | collective-permute-start | bytes 786440 | tf_op jit(solution)/shard_map/ppermute | solution.py:531
  7.0 11.7 %collective-permute-start.3 = (bf16[4,128,256]{2,1,0:T(8,128)(2,1)S(1)}, bf16[4,128,256]{2,1,0:T(8,128)(2,1)S(1)}, u32[]{:S(2)}, u32[]{:S(2)}) collective-permute-start(bf16[4,128,256]{2,1,0:T(8,128)(2,1)S(1)} %get-tuple-element.56.ob), channel_id=1, source_target_pairs={{0,1},{1,2},{2,3},{3,0},{4,5},{5,6},{6,7},{7,4},{8,9},{9,10},{10,1... | collective-permute-start | bytes 786440 | tf_op jit(solution)/shard_map/ppermute | solution.py:527
  11.0 10.9 %collective-permute-start.5 = (bf16[4,128,256]{2,1,0:T(8,128)(2,1)S(1)}, bf16[4,128,256]{2,1,0:T(8,128)(2,1)S(1)}, u32[]{:S(2)}, u32[]{:S(2)}) collective-permute-start(bf16[4,128,256]{2,1,0:T(8,128)(2,1)S(1)} %collective-permute-done.1.rb), channel_id=1, source_target_pairs={{0,3},{1,0},{2,1},{3,2},{4,7},{5,4},{6,5},{7,6},{8,11},{9,8},{10,9... | collective-permute-start | bytes 786440 | tf_op jit(solution)/shard_map/ppermute | solution.py:531
  14.2 7.7 %collective-permute-start.4 = (bf16[4,128,256]{2,1,0:T(8,128)(2,1)S(1)}, bf16[4,128,256]{2,1,0:T(8,128)(2,1)S(1)}, u32[]{:S(2)}, u32[]{:S(2)}) collective-permute-start(bf16[4,128,256]{2,1,0:T(8,128)(2,1)S(1)} %collective-permute-done.la), channel_id=1, source_target_pairs={{0,1},{1,2},{2,3},{3,0},{4,5},{5,6},{6,7},{7,4},{8,9},{9,10},{10,1... | collective-permute-start | bytes 786440 | tf_op jit(solution)/shard_map/ppermute | solution.py:527
  23.3 5.6 %collective-permute-start.6 = (bf16[256,512]{1,0:T(8,128)(2,1)S(1)}, bf16[256,512]{1,0:T(8,128)(2,1)S(1)}, u32[]{:S(2)}, u32[]{:S(2)}) collective-permute-start(bf16[256,512]{1,0:T(8,128)(2,1)S(1)} %get-tuple-element.67), channel_id=1, source_target_pairs={{0,4},{4,0},{1,5},{5,1},{2,6},{6,2},{3,7},{7,3},{8,12},{12,8},{9,1... | collective-permute-start | bytes 786440 | tf_op jit(solution)/shard_map/ppermute | solution.py:282
  39.3 8.8 %collective-permute-start.9 = (bf16[1,32,512]{2,1,0:T(8,128)(2,1)S(1)}, bf16[1,32,512]{2,1,0:T(8,128)(2,1)S(1)}, u32[]{:S(2)}, u32[]{:S(2)}) collective-permute-start(bf16[1,32,512]{2,1,0:T(8,128)(2,1)S(1)} %total.4.refs_0_), channel_id=1, source_target_pairs={{0,32},{16,48},{32,0},{48,16},{1,33},{17,49},{33,1},{49,17},{2,34}... | collective-permute-start | bytes 98312 | tf_op jit(solution)/shard_map/ppermute | solution.py:327
  45.4 3.7 %collective-permute-start.8 = (bf16[1,32,512]{2,1,0:T(8,128)(2,1)S(1)}, bf16[1,32,512]{2,1,0:T(8,128)(2,1)S(1)}, u32[]{:S(2)}, u32[]{:S(2)}) collective-permute-start(bf16[1,32,512]{2,1,0:T(8,128)(2,1)S(1)} %total.4.refs_0_), channel_id=1, source_target_pairs={{0,48},{16,0},{32,16},{48,32},{1,49},{17,1},{33,17},{49,33},{2,50}... | collective-permute-start | bytes 98312 | tf_op jit(solution)/shard_map/ppermute | solution.py:327
  45.6 5.2 %collective-permute-start.7 = (bf16[1,32,512]{2,1,0:T(8,128)(2,1)S(1)}, bf16[1,32,512]{2,1,0:T(8,128)(2,1)S(1)}, u32[]{:S(2)}, u32[]{:S(2)}) collective-permute-start(bf16[1,32,512]{2,1,0:T(8,128)(2,1)S(1)} %total.4.refs_0_), channel_id=1, source_target_pairs={{0,16},{16,32},{32,48},{48,0},{1,17},{17,33},{33,49},{49,1},{2,18}... | collective-permute-start | bytes 98312 | tf_op jit(solution)/shard_map/ppermute | solution.py:327
  59.6 5.2 %copy-start = (f32[2,2048]{1,0:T(2,128)S(1)}, f32[2,2048]{1,0:T(2,128)}, u32[]{:S(2)}) copy-start(f32[2,2048]{1,0:T(2,128)} %b_ref.3) | copy-start | bytes 49156
  59.6 5.2 %collective-permute-start.10 = (bf16[8,32,512]{2,1,0:T(8,128)(2,1)S(1)}, bf16[8,32,512]{2,1,0:T(8,128)(2,1)S(1)}, u32[]{:S(2)}, u32[]{:S(2)}) collective-permute-start(bf16[8,32,512]{2,1,0:T(8,128)(2,1)S(1)} %all_to_all.21.mine_ref), channel_id=1, source_target_pairs={{0,4},{4,0},{1,5},{5,1},{2,6},{6,2},{3,7},{7,3},{8,12},{12,8},{9,1... | collective-permute-start | bytes 786440 | tf_op jit(solution)/shard_map/ppermute | solution.py:282
  66.6 1.7 %collective-permute-start.11 = (bf16[256,512]{1,0:T(8,128)(2,1)S(1)}, bf16[256,512]{1,0:T(8,128)(2,1)S(1)}, u32[]{:S(2)}, u32[]{:S(2)}) collective-permute-start(bf16[256,512]{1,0:T(8,128)(2,1)S(1)} %get-tuple-element.82), channel_id=1, source_target_pairs={{0,4},{4,0},{1,5},{5,1},{2,6},{6,2},{3,7},{7,3},{8,12},{12,8},{9,1... | collective-permute-start | bytes 786440 | tf_op jit(solution)/shard_map/ppermute | solution.py:282
  77.3 7.0 %collective-permute-start.14 = (bf16[1,32,512]{2,1,0:T(8,128)(2,1)S(1)}, bf16[1,32,512]{2,1,0:T(8,128)(2,1)S(1)}, u32[]{:S(2)}, u32[]{:S(2)}) collective-permute-start(bf16[1,32,512]{2,1,0:T(8,128)(2,1)S(1)} %total.6.refs_0_), channel_id=1, source_target_pairs={{0,32},{16,48},{32,0},{48,16},{1,33},{17,49},{33,1},{49,17},{2,34}... | collective-permute-start | bytes 98312 | tf_op jit(solution)/shard_map/ppermute | solution.py:327
  81.6 4.0 %collective-permute-start.13 = (bf16[1,32,512]{2,1,0:T(8,128)(2,1)S(1)}, bf16[1,32,512]{2,1,0:T(8,128)(2,1)S(1)}, u32[]{:S(2)}, u32[]{:S(2)}) collective-permute-start(bf16[1,32,512]{2,1,0:T(8,128)(2,1)S(1)} %total.6.refs_0_), channel_id=1, source_target_pairs={{0,48},{16,0},{32,16},{48,32},{1,49},{17,1},{33,17},{49,33},{2,50}... | collective-permute-start | bytes 98312 | tf_op jit(solution)/shard_map/ppermute | solution.py:327
  81.7 5.0 %collective-permute-start.12 = (bf16[1,32,512]{2,1,0:T(8,128)(2,1)S(1)}, bf16[1,32,512]{2,1,0:T(8,128)(2,1)S(1)}, u32[]{:S(2)}, u32[]{:S(2)}) collective-permute-start(bf16[1,32,512]{2,1,0:T(8,128)(2,1)S(1)} %total.6.refs_0_), channel_id=1, source_target_pairs={{0,16},{16,32},{32,48},{48,0},{1,17},{17,33},{33,49},{49,1},{2,18}... | collective-permute-start | bytes 98312 | tf_op jit(solution)/shard_map/ppermute | solution.py:327
  95.8 5.0 %collective-permute-start.15 = (bf16[8,32,512]{2,1,0:T(8,128)(2,1)S(1)}, bf16[8,32,512]{2,1,0:T(8,128)(2,1)S(1)}, u32[]{:S(2)}, u32[]{:S(2)}) collective-permute-start(bf16[8,32,512]{2,1,0:T(8,128)(2,1)S(1)} %all_to_all.23.mine_ref), channel_id=1, source_target_pairs={{0,4},{4,0},{1,5},{5,1},{2,6},{6,2},{3,7},{7,3},{8,12},{12,8},{9,1... | collective-permute-start | bytes 786440 | tf_op jit(solution)/shard_map/ppermute | solution.py:282
  102.6 8.9 %collective-permute-start.17 = (bf16[4,128,256]{2,1,0:T(8,128)(2,1)S(1)}, bf16[4,128,256]{2,1,0:T(8,128)(2,1)S(1)}, u32[]{:S(2)}, u32[]{:S(2)}) collective-permute-start(bf16[4,128,256]{2,1,0:T(8,128)(2,1)S(1)} %get-tuple-element.102), channel_id=1, source_target_pairs={{0,1},{1,2},{2,3},{3,0},{4,5},{5,6},{6,7},{7,4},{8,9},{9,10},{10,1... | collective-permute-start | bytes 786440 | tf_op jit(solution)/shard_map/ppermute | solution.py:527
  103.3 8.4 %collective-permute-start.20 = (bf16[4,128,256]{2,1,0:T(8,128)(2,1)S(1)}, bf16[4,128,256]{2,1,0:T(8,128)(2,1)S(1)}, u32[]{:S(2)}, u32[]{:S(2)}) collective-permute-start(bf16[4,128,256]{2,1,0:T(8,128)(2,1)S(1)} %get-tuple-element.105), channel_id=1, source_target_pairs={{0,3},{1,0},{2,1},{3,2},{4,7},{5,4},{6,5},{7,6},{8,11},{9,8},{10,9... | collective-permute-start | bytes 786440 | tf_op jit(solution)/shard_map/ppermute | solution.py:531
  106.3 9.9 %collective-permute-start.16 = (bf16[4,128,256]{2,1,0:T(8,128)(2,1)S(1)}, bf16[4,128,256]{2,1,0:T(8,128)(2,1)S(1)}, u32[]{:S(2)}, u32[]{:S(2)}) collective-permute-start(bf16[4,128,256]{2,1,0:T(8,128)(2,1)S(1)} %get-tuple-element.100), channel_id=1, source_target_pairs={{0,3},{1,0},{2,1},{3,2},{4,7},{5,4},{6,5},{7,6},{8,11},{9,8},{10,9... | collective-permute-start | bytes 786440 | tf_op jit(solution)/shard_map/ppermute | solution.py:531
  107.3 9.8 %collective-permute-start.19 = (bf16[4,128,256]{2,1,0:T(8,128)(2,1)S(1)}, bf16[4,128,256]{2,1,0:T(8,128)(2,1)S(1)}, u32[]{:S(2)}, u32[]{:S(2)}) collective-permute-start(bf16[4,128,256]{2,1,0:T(8,128)(2,1)S(1)} %get-tuple-element.103), channel_id=1, source_target_pairs={{0,1},{1,2},{2,3},{3,0},{4,5},{5,6},{6,7},{7,4},{8,9},{9,10},{10,1... | collective-permute-start | bytes 786440 | tf_op jit(solution)/shard_map/ppermute | solution.py:527
  111.6 11.2 %collective-permute-start.18 = (bf16[4,128,256]{2,1,0:T(8,128)(2,1)S(1)}, bf16[4,128,256]{2,1,0:T(8,128)(2,1)S(1)}, u32[]{:S(2)}, u32[]{:S(2)}) collective-permute-start(bf16[4,128,256]{2,1,0:T(8,128)(2,1)S(1)} %add_convert_fusion.1), channel_id=1, source_target_pairs={{0,1},{1,2},{2,3},{3,0},{4,5},{5,6},{6,7},{7,4},{8,9},{9,10},{10,1... | collective-permute-start | bytes 786440 | tf_op jit(solution)/shard_map/ppermute | solution.py:527
  111.8 11.0 %collective-permute-start.21 = (bf16[4,128,256]{2,1,0:T(8,128)(2,1)S(1)}, bf16[4,128,256]{2,1,0:T(8,128)(2,1)S(1)}, u32[]{:S(2)}, u32[]{:S(2)}) collective-permute-start(bf16[4,128,256]{2,1,0:T(8,128)(2,1)S(1)} %add_convert_fusion), channel_id=1, source_target_pairs={{0,3},{1,0},{2,1},{3,2},{4,7},{5,4},{6,5},{7,6},{8,11},{9,8},{10,9... | collective-permute-start | bytes 786440 | tf_op jit(solution)/shard_map/ppermute | solution.py:531
